TPU v7x, 32 devices: a whole 2x2x4 slice. The times are simulated.
32 devices in a mesh: dp: 8 (over z, core), seq: 4 (over y, x).
Axes of the slice: x: 2, y: 2, z: 4, core: 2. Of those that a mesh axis runs over, the one named last changes fastest.
Arguments:
- tokens: bfloat16 [8, 4096, 1024], P('dp', 'seq'), may hold values from -6 to 6
- cotangent: bfloat16 [8, 4096, 1024], P('dp', 'seq'), may hold values from -6 to 6
- lengths: int32 [8], P('dp'), may hold values from 512 to 4096, as said below
- norm_one: float32 [1024], replicated, may hold values from 0.5 to 1.5
- w_query: bfloat16 [1024, 512], replicated, may hold values from -0.1875 to 0.1875
- w_key: bfloat16 [1024, 128], replicated, may hold values from -0.1875 to 0.1875
- w_value: bfloat16 [1024, 128], replicated, may hold values from -0.1875 to 0.1875
- w_gatez: bfloat16 [1024, 1536], replicated, may hold values from -0.1875 to 0.1875
- w_conv_in: bfloat16 [1024, 1792], replicated, may hold values from -0.1875 to 0.1875
- w_step: bfloat16 [1024, 24], replicated, may hold values from -0.1875 to 0.1875
- conv_weight: float32 [4, 1792], replicated, may hold values from -3 to 3
- conv_bias: float32 [1792], replicated, may hold values from -3 to 3
- step_bias: float32 [24], replicated, may hold values from -2 to 0
- decay_log: float32 [24], replicated, may hold values from -12 to 0
- skip_gain: float32 [24], replicated, may hold values from 0.5 to 1.5
- gated_gain: float32 [1536], replicated, may hold values from 0.5 to 1.5
- w_attn_out: bfloat16 [512, 1024], replicated, may hold values from -1 to 1
- w_mix_out: bfloat16 [1536, 1024], replicated, may hold values from -0.15625 to 0.15625
- norm_two: float32 [1024], replicated, may hold values from 0.5 to 1.5
- w_gate: bfloat16 [1024, 2048], replicated, may hold values from -0.1875 to 0.1875
- w_up: bfloat16 [1024, 2048], replicated, may hold values from -0.1875 to 0.1875
- w_down: bfloat16 [2048, 1024], replicated, may hold values from -0.125 to 0.125
Outputs:
- output: bfloat16 [8, 4096, 1024], P('dp', 'seq')
- grad_tokens: float32 [8, 4096, 1024], P('dp', 'seq')
- grad_norm_one: float32 [1024], P('seq')
- grad_w_query: float32 [1024, 512], P('seq')
- grad_w_key: float32 [1024, 128], P('seq')
- grad_w_value: float32 [1024, 128], P('seq')
- grad_w_gatez: float32 [1024, 1536], P('seq')
- grad_w_conv_in: float32 [1024, 1792], P('seq')
- grad_w_step: float32 [1024, 24], P('seq')
- grad_conv_weight: float32 [4, 1792], replicated
- grad_conv_bias: float32 [1792], replicated
- grad_step_bias: float32 [24], replicated
- grad_decay_log: float32 [24], replicated
- grad_skip_gain: float32 [24], replicated
- grad_gated_gain: float32 [1536], P('seq')
- grad_w_attn_out: float32 [512, 1024], P('seq')
- grad_w_mix_out: float32 [1536, 1024], P('seq')
- grad_norm_two: float32 [1024], P('seq')
- grad_w_gate: float32 [1024, 2048], P('seq')
- grad_w_up: float32 [1024, 2048], P('seq')
- grad_w_down: float32 [2048, 1024], P('seq')
Inputs may be any that keep to these rules, and one draw needn't show every extreme that they name: `lengths`: in every group of 1 sequence of one index of dp, one sequence, drawn from the seed, has length 4096; the others are drawn evenly.
All inputs are finite; a program needn't handle non-finite values.
Results may differ from a plain program's by a relative error of at most 0.02.
Values may be sent and summed in bfloat16 or wider, within the bound.
No kernel may reach another device: no remote copies, remote signals or barrier semaphores. Data moves between devices by JAX's collectives and lax.ppermute only.
A program may use at most 576 MiB of HBM per device.

v0:
```python
import jax
import jax.numpy as jnp
from jax import lax
from jax.sharding import PartitionSpec as P

HEADS = 8
KV_HEADS = 2
HEAD = 64
SSM_HEADS = 24
SSM_HEAD = 64
STATE = 128


highest = lax.Precision.HIGHEST
epsilon = 1e-05
rope_base = 100000000000.0
lowest_score = -1e30


def from_behind(value, axis, steps):
    count = lax.axis_size(axis)
    initial, last = (max(0, -steps), min(count, count - steps))
    return lax.ppermute(value, axis, [(source, source + steps) for source in range(initial, last)])


def entering(x, axis, join, neutral):
    place = lax.axis_index(axis)
    gathered = jax.tree.map(
        lambda a, kind: lax.all_gather(a.astype(kind), axis), x, (jnp.bfloat16, jnp.bfloat16)
    )
    state = jax.tree.map(lambda a, e: jnp.zeros_like(a) + jnp.asarray(e, a.dtype), x, neutral)

    def one(turn, state):
        return join(
            state,
            jax.tree.map(
                lambda a, own: lax.dynamic_index_in_dim(a, turn, 0, False).astype(own.dtype),
                gathered,
                x,
            ),
        )

    return lax.fori_loop(0, place, one, state)


def entering_2(x, axis, join, neutral):
    count = lax.axis_size(axis)
    place = lax.axis_index(axis)
    ahead = count - 1 - place
    gathered = jax.tree.map(
        lambda a, kind: lax.all_gather(a.astype(kind), axis),
        x,
        jax.tree.map(lambda a: jnp.bfloat16 if a.dtype == jnp.float32 else a.dtype, x),
    )
    state = jax.tree.map(lambda a, e: jnp.zeros_like(a) + jnp.asarray(e, a.dtype), x, neutral)

    def one(turn, state):
        source = count - 1 - turn
        return join(
            state,
            jax.tree.map(
                lambda a, own: lax.dynamic_index_in_dim(a, source, 0, False).astype(own.dtype),
                gathered,
                x,
            ),
        )

    return lax.fori_loop(0, ahead, one, state)


def as_sent(x):
    return jax.tree.map(lambda a: a.astype(jnp.bfloat16) if a.dtype == jnp.float32 else a, x)


def to_low(value):
    return value.astype(jnp.bfloat16)


def project(left, weight):
    return jnp.einsum("sck,km->scm", left, weight, preferred_element_type=jnp.float32)


def project_back(grad, weight):
    return jnp.einsum("scm,km->sck", grad, weight, preferred_element_type=jnp.float32)


def weight_grad(left, grad):
    return jnp.einsum("sck,scm->km", left, grad, preferred_element_type=jnp.float32)


def normed(value, gain):
    return value * lax.rsqrt(jnp.mean(value * value, -1, keepdims=True) + epsilon) * gain


def gated_norm(mixed, gatez, gain):
    return normed(mixed * jax.nn.silu(gatez), gain)


def swiglu(gate_lin, up_lin):
    return jax.nn.silu(gate_lin) * up_lin


def rope_tables(positions, head_size):
    inverse = 1.0 / rope_base ** (jnp.arange(0, head_size, 2).astype(jnp.float32) / head_size)
    angles = positions.astype(jnp.float32)[:, None] * inverse[None, :]
    return (jnp.cos(angles)[:, None, :], jnp.sin(angles)[:, None, :])


def rotate(value, cosine, sine):
    half_size = value.shape[-1] // 2
    former, latter = (value[..., :half_size], value[..., half_size:])
    return jnp.concatenate([former * cosine - latter * sine, latter * cosine + former * sine], -1)


def convolve(extended, conv_weight, conv_bias):
    taps = conv_weight.shape[0]
    rows_here = extended.shape[1] - taps + 1
    summed = conv_bias
    for offset in range(taps):
        summed = summed + conv_weight[offset] * extended[:, offset : offset + rows_here]
    return jax.nn.silu(summed)


def lower_ones(rows_here):
    return (jnp.arange(rows_here)[None, :] <= jnp.arange(rows_here)[:, None]).astype(jnp.float32)


def span_terms(ssm_in, in_keys, steps, decay_log):
    lower_tri = lower_ones(steps.shape[1])
    log_decay = steps * -jnp.exp(decay_log)
    cumulative = jnp.einsum("tu,suh->sth", lower_tri, log_decay, precision=highest)
    final_log = cumulative[:, -1]
    weights = jnp.exp(final_log[:, None] - cumulative) * steps
    state_part = jnp.einsum("suh,suhp,sun->shpn", weights, ssm_in, in_keys, precision=highest)
    return (state_part, jnp.exp(final_log))


def span_out(ssm_in, in_keys, in_queries, steps, decay_log, skip_gain, state_in):
    lower_tri = lower_ones(steps.shape[1])
    log_decay = steps * -jnp.exp(decay_log)
    cumulative = jnp.einsum("tu,suh->sth", lower_tri, log_decay, precision=highest)
    differ = cumulative[:, :, None, :] - cumulative[:, None, :, :]
    mixing = (
        jnp.exp(jnp.where(lower_tri[None, :, :, None] > 0, differ, lowest_score))
        * steps[:, None, :, :]
    )
    intersection = jnp.einsum("stn,sun->stu", in_queries, in_keys, precision=highest)
    combined = intersection[..., None] * mixing
    inner = jnp.einsum("stuh,suhp->sthp", combined, ssm_in, precision=highest)
    carried = (
        jnp.einsum("stn,shpn->sthp", in_queries, state_in, precision=highest)
        * jnp.exp(cumulative)[..., None]
    )
    return inner + carried + skip_gain[:, None] * ssm_in


def combine_states(earlier, later):
    return (earlier[0] * later[0], later[0][:, :, None, None] * earlier[1] + later[1])


def allowed_keys(query_pos, key_pos, lengths):
    causal = key_pos[None, :] <= query_pos[:, None]
    inside = key_pos[None, :] < lengths[:, None]
    return (causal[None, :, :] & inside[:, None, :])[:, :, None, None, :]


def on_device(
    tokens,
    cotangent,
    lengths,
    norm_one,
    w_query,
    w_key,
    w_value,
    w_gatez,
    w_conv_in,
    w_step,
    conv_weight,
    conv_bias,
    step_bias,
    decay_log,
    skip_gain,
    gated_gain,
    w_attn_out,
    w_mix_out,
    norm_two,
    w_gate,
    w_up,
    w_down,
):
    seqs_here, rows_here, width = tokens.shape
    grouped = HEADS // KV_HEADS
    ssm_width = SSM_HEADS * SSM_HEAD
    taps = conv_weight.shape[0]
    positions = lax.axis_index("seq") * rows_here + jnp.arange(rows_here)
    live = (positions[None, :] < lengths[:, None]).astype(jnp.float32)[..., None]
    cosine, sine = rope_tables(positions, HEAD)
    inputs = tokens.astype(jnp.float32)
    hidden = to_low(normed(inputs, norm_one))
    query_lin = project(hidden, w_query)
    key_lin = project(hidden, w_key)
    values_low = to_low(project(hidden, w_value)).reshape(seqs_here, rows_here, KV_HEADS, HEAD)
    queries = to_low(rotate(query_lin.reshape(seqs_here, rows_here, HEADS, HEAD), cosine, sine))
    queries = queries.reshape(seqs_here, rows_here, KV_HEADS, grouped, HEAD)
    keys_rot = to_low(rotate(key_lin.reshape(seqs_here, rows_here, KV_HEADS, HEAD), cosine, sine))

    def piece_scores(key_piece):
        scores = (
            jnp.einsum("scjqd,srjd->scjqr", queries, key_piece, preferred_element_type=jnp.float32)
            * 0.125
        )
        key_pos = jnp.arange(key_piece.shape[1])
        return (scores, allowed_keys(positions, key_pos, lengths))

    stat_shape = (seqs_here, rows_here, KV_HEADS, grouped)
    best = jnp.full(stat_shape, lowest_score, jnp.float32)
    key_piece = lax.all_gather(keys_rot, "seq", axis=1, tiled=True)
    value_piece = lax.all_gather(values_low, "seq", axis=1, tiled=True)
    scores, allowed = piece_scores(key_piece)
    scores = jnp.where(allowed, scores, lowest_score)
    newest = jnp.maximum(best, jnp.max(scores, -1))
    weights = jnp.where(allowed, jnp.exp(scores - newest[..., None]), 0.0)
    accum = jnp.einsum(
        "scjqr,srjd->scjqd", weights, value_piece.astype(jnp.float32), precision=highest
    )
    totals = jnp.sum(weights, -1)
    accum, best, totals = (accum, newest, totals)
    attn_full = accum / totals[..., None]
    log_total = best + jnp.log(totals)
    attn_low = to_low(attn_full.reshape(seqs_here, rows_here, HEADS * HEAD))
    conv_lin = project(hidden, w_conv_in)
    gatez = project(hidden, w_gatez)
    step_lin = project(hidden, w_step)
    earlier_rows = from_behind(
        conv_lin[:, rows_here - taps + 1 :].astype(jnp.bfloat16), "seq", 1
    ).astype(jnp.float32)
    extended = jnp.concatenate([earlier_rows, conv_lin], 1)
    activated = convolve(extended, conv_weight, conv_bias)
    ssm_in = (
        to_low(activated[..., :ssm_width])
        .astype(jnp.float32)
        .reshape(seqs_here, rows_here, SSM_HEADS, SSM_HEAD)
    )
    in_keys = to_low(activated[..., ssm_width : ssm_width + STATE]).astype(jnp.float32)
    in_queries = to_low(activated[..., ssm_width + STATE :]).astype(jnp.float32)
    step_raw = step_lin + step_bias
    steps = jax.nn.softplus(step_raw) * live
    state_part, decay_total = span_terms(ssm_in, in_keys, steps, decay_log)
    identity = (jnp.ones_like(decay_total), jnp.zeros_like(state_part))
    unused, state_in = entering((decay_total, state_part), "seq", combine_states, identity)
    mixed = span_out(ssm_in, in_keys, in_queries, steps, decay_log, skip_gain, state_in)
    mixed_flat = mixed.reshape(seqs_here, rows_here, ssm_width)
    mix_low = to_low(gated_norm(mixed_flat, gatez, gated_gain))
    branch = project(attn_low, w_attn_out) + project(mix_low, w_mix_out)
    after_mix = inputs + live * branch
    hidden_two = to_low(normed(after_mix, norm_two))
    gate_lin = project(hidden_two, w_gate)
    up_lin = project(hidden_two, w_up)
    act_low = to_low(swiglu(gate_lin, up_lin))
    output = to_low(after_mix + live * project(act_low, w_down))
    grad_out = cotangent.astype(jnp.float32)
    grad_ffn = to_low(live * grad_out)
    g_down = weight_grad(act_low, grad_ffn)
    unused_value, swiglu_pull = jax.vjp(swiglu, gate_lin, up_lin)
    grad_gate, grad_up = swiglu_pull(project_back(grad_ffn, w_down))
    grad_gate = to_low(grad_gate)
    grad_up = to_low(grad_up)
    g_gate = weight_grad(hidden_two, grad_gate)
    g_up = weight_grad(hidden_two, grad_up)
    unused_value, norm_pull_two = jax.vjp(normed, after_mix, norm_two)
    grad_mid, g_norm_two = norm_pull_two(
        project_back(grad_gate, w_gate) + project_back(grad_up, w_up)
    )
    grad_mid = grad_mid + grad_out
    grad_branch = to_low(live * grad_mid)
    g_attn_out = weight_grad(attn_low, grad_branch)
    g_mix_out = weight_grad(mix_low, grad_branch)
    grad_attn = to_low(project_back(grad_branch, w_attn_out)).reshape(
        seqs_here, rows_here, KV_HEADS, grouped, HEAD
    )
    unused_value, gated_pull = jax.vjp(gated_norm, mixed_flat, gatez, gated_gain)
    grad_mixed, grad_gatez, g_gated = gated_pull(project_back(grad_branch, w_mix_out))
    grad_gatez = to_low(grad_gatez)
    grad_mixed = grad_mixed.reshape(seqs_here, rows_here, SSM_HEADS, SSM_HEAD)
    unused_value, out_pull = jax.vjp(
        span_out, ssm_in, in_keys, in_queries, steps, decay_log, skip_gain, state_in
    )
    g_in_one, g_keys_one, g_queries, g_steps_one, g_decay_one, g_skip, g_state_in = out_pull(
        grad_mixed
    )
    unused, later_grad = entering_2((decay_total, g_state_in), "seq", combine_states, identity)
    g_total = jnp.sum(later_grad * state_in, (2, 3))
    unused_value, terms_pull = jax.vjp(span_terms, ssm_in, in_keys, steps, decay_log)
    g_in_two, g_keys_two, g_steps_two, g_decay_two = terms_pull((later_grad, g_total))
    grad_steps = (g_steps_one + g_steps_two) * live * jax.nn.sigmoid(step_raw)
    g_step_bias = jnp.sum(grad_steps, (0, 1))
    grad_step_low = to_low(grad_steps)
    grad_activated = jnp.concatenate(
        [
            (g_in_one + g_in_two).reshape(seqs_here, rows_here, ssm_width),
            g_keys_one + g_keys_two,
            g_queries,
        ],
        -1,
    )
    unused_value, conv_pull = jax.vjp(convolve, extended, conv_weight, conv_bias)
    grad_extended, g_conv_weight, g_conv_bias = conv_pull(grad_activated)
    returned = from_behind(as_sent(grad_extended[:, : taps - 1]), "seq", -1)
    grad_conv = grad_extended[:, taps - 1 :]
    grad_conv = jnp.concatenate(
        [grad_conv[:, : rows_here - taps + 1], grad_conv[:, rows_here - taps + 1 :] + returned], 1
    )
    grad_conv_low = to_low(grad_conv)
    delta = jnp.sum(grad_attn.astype(jnp.float32) * attn_full, -1)
    grad_attn_wide = grad_attn.astype(jnp.float32)
    key_piece = lax.all_gather(keys_rot, "seq", axis=1, tiled=True)
    value_piece = lax.all_gather(values_low, "seq", axis=1, tiled=True)
    scores, allowed = piece_scores(key_piece)
    weights = jnp.where(allowed, jnp.exp(scores - log_total[..., None]), 0.0)
    grad_weights = jnp.einsum(
        "scjqd,srjd->scjqr", grad_attn, value_piece, preferred_element_type=jnp.float32
    )
    grad_scores = to_low(weights * (grad_weights - delta[..., None]))
    grad_query = (
        jnp.einsum("scjqr,srjd->scjqd", grad_scores, key_piece, preferred_element_type=jnp.float32)
        * 0.125
    )
    key_part = (
        jnp.einsum("scjqr,scjqd->srjd", grad_scores, queries, preferred_element_type=jnp.float32)
        * 0.125
    )
    value_part = jnp.einsum("scjqr,scjqd->srjd", weights, grad_attn_wide, precision=highest)
    grad_keys = key_part
    grad_values = value_part
    grad_query, grad_keys, grad_values = (grad_query, grad_keys, grad_values)
    grad_keys, grad_values = (
        lax.psum_scatter(
            grad_keys.astype(jnp.bfloat16), "seq", scatter_dimension=1, tiled=True
        ).astype(jnp.float32),
        lax.psum_scatter(
            grad_values.astype(jnp.bfloat16), "seq", scatter_dimension=1, tiled=True
        ).astype(jnp.float32),
    )
    grad_query_low = to_low(
        rotate(grad_query.reshape(seqs_here, rows_here, HEADS, HEAD), cosine, -sine).reshape(
            seqs_here, rows_here, HEADS * HEAD
        )
    )
    grad_key_low = to_low(
        rotate(grad_keys, cosine, -sine).reshape(seqs_here, rows_here, KV_HEADS * HEAD)
    )
    grad_value_low = to_low(grad_values.reshape(seqs_here, rows_here, KV_HEADS * HEAD))
    g_query = weight_grad(hidden, grad_query_low)
    g_key = weight_grad(hidden, grad_key_low)
    g_value = weight_grad(hidden, grad_value_low)
    g_gatez = weight_grad(hidden, grad_gatez)
    g_conv_in = weight_grad(hidden, grad_conv_low)
    g_step = weight_grad(hidden, grad_step_low)
    grad_hidden = (
        project_back(grad_query_low, w_query)
        + project_back(grad_key_low, w_key)
        + project_back(grad_value_low, w_value)
    )
    grad_hidden = (
        grad_hidden
        + project_back(grad_gatez, w_gatez)
        + project_back(grad_conv_low, w_conv_in)
        + project_back(grad_step_low, w_step)
    )
    unused_value, norm_pull_one = jax.vjp(normed, inputs, norm_one)
    grad_inputs, g_norm_one = norm_pull_one(grad_hidden)
    grad_tokens = grad_inputs + grad_mid
    (
        p_norm_one,
        p_query,
        p_key,
        p_value,
        p_gatez,
        p_conv_in,
        p_step,
        p_gated,
        p_attn_out,
        p_mix_out,
        p_norm_two,
        p_gate,
        p_up,
        p_down,
    ) = (
        lax.psum_scatter(
            g_norm_one.astype(jnp.bfloat16), "seq", scatter_dimension=0, tiled=True
        ).astype(jnp.float32),
        lax.psum_scatter(
            g_query.astype(jnp.bfloat16), "seq", scatter_dimension=0, tiled=True
        ).astype(jnp.float32),
        lax.psum_scatter(g_key.astype(jnp.bfloat16), "seq", scatter_dimension=0, tiled=True).astype(
            jnp.float32
        ),
        lax.psum_scatter(
            g_value.astype(jnp.bfloat16), "seq", scatter_dimension=0, tiled=True
        ).astype(jnp.float32),
        lax.psum_scatter(
            g_gatez.astype(jnp.bfloat16), "seq", scatter_dimension=0, tiled=True
        ).astype(jnp.float32),
        lax.psum_scatter(
            g_conv_in.astype(jnp.bfloat16), "seq", scatter_dimension=0, tiled=True
        ).astype(jnp.float32),
        lax.psum_scatter(
            g_step.astype(jnp.bfloat16), "seq", scatter_dimension=0, tiled=True
        ).astype(jnp.float32),
        lax.psum_scatter(
            g_gated.astype(jnp.bfloat16), "seq", scatter_dimension=0, tiled=True
        ).astype(jnp.float32),
        lax.psum_scatter(
            g_attn_out.astype(jnp.bfloat16), "seq", scatter_dimension=0, tiled=True
        ).astype(jnp.float32),
        lax.psum_scatter(
            g_mix_out.astype(jnp.bfloat16), "seq", scatter_dimension=0, tiled=True
        ).astype(jnp.float32),
        lax.psum_scatter(
            g_norm_two.astype(jnp.bfloat16), "seq", scatter_dimension=0, tiled=True
        ).astype(jnp.float32),
        lax.psum_scatter(
            g_gate.astype(jnp.bfloat16), "seq", scatter_dimension=0, tiled=True
        ).astype(jnp.float32),
        lax.psum_scatter(g_up.astype(jnp.bfloat16), "seq", scatter_dimension=0, tiled=True).astype(
            jnp.float32
        ),
        lax.psum_scatter(
            g_down.astype(jnp.bfloat16), "seq", scatter_dimension=0, tiled=True
        ).astype(jnp.float32),
    )
    summed = (
        lax.psum(p_norm_one.astype(jnp.bfloat16), "dp").astype(jnp.float32),
        lax.psum(p_query.astype(jnp.bfloat16), "dp").astype(jnp.float32),
        lax.psum(p_key.astype(jnp.bfloat16), "dp").astype(jnp.float32),
        lax.psum(p_value.astype(jnp.bfloat16), "dp").astype(jnp.float32),
        lax.psum(p_gatez.astype(jnp.bfloat16), "dp").astype(jnp.float32),
        lax.psum(p_conv_in.astype(jnp.bfloat16), "dp").astype(jnp.float32),
        lax.psum(p_step.astype(jnp.bfloat16), "dp").astype(jnp.float32),
        lax.psum(p_gated.astype(jnp.bfloat16), "dp").astype(jnp.float32),
        lax.psum(p_attn_out.astype(jnp.bfloat16), "dp").astype(jnp.float32),
        lax.psum(p_mix_out.astype(jnp.bfloat16), "dp").astype(jnp.float32),
        lax.psum(p_norm_two.astype(jnp.bfloat16), "dp").astype(jnp.float32),
        lax.psum(p_gate.astype(jnp.bfloat16), "dp").astype(jnp.float32),
        lax.psum(p_up.astype(jnp.bfloat16), "dp").astype(jnp.float32),
        lax.psum(p_down.astype(jnp.bfloat16), "dp").astype(jnp.float32),
    )
    (
        s_norm_one,
        s_query,
        s_key,
        s_value,
        s_gatez,
        s_conv_in,
        s_step,
        s_gated,
        s_attn_out,
        s_mix_out,
        s_norm_two,
        s_gate,
        s_up,
        s_down,
    ) = summed
    small_sums = lax.psum(
        (g_conv_weight, g_conv_bias, g_step_bias, g_decay_one + g_decay_two, g_skip), ("dp", "seq")
    )
    s_conv_weight, s_conv_bias, s_step_bias, s_decay, s_skip = small_sums
    return (
        output,
        grad_tokens,
        s_norm_one,
        s_query,
        s_key,
        s_value,
        s_gatez,
        s_conv_in,
        s_step,
        s_conv_weight,
        s_conv_bias,
        s_step_bias,
        s_decay,
        s_skip,
        s_gated,
        s_attn_out,
        s_mix_out,
        s_norm_two,
        s_gate,
        s_up,
        s_down,
    )


def solution(mesh):
    return jax.shard_map(
        on_device,
        mesh=mesh,
        in_specs=(
            P("dp", "seq", None),
            P("dp", "seq", None),
            P("dp"),
            P(),
            P(),
            P(),
            P(),
            P(),
            P(),
            P(),
            P(),
            P(),
            P(),
            P(),
            P(),
            P(),
            P(),
            P(),
            P(),
            P(),
            P(),
            P(),
        ),
        out_specs=(
            P("dp", "seq", None),
            P("dp", "seq", None),
            P("seq"),
            P("seq", None),
            P("seq", None),
            P("seq", None),
            P("seq", None),
            P("seq", None),
            P("seq", None),
            P(),
            P(),
            P(),
            P(),
            P(),
            P("seq"),
            P("seq", None),
            P("seq", None),
            P("seq"),
            P("seq", None),
            P("seq", None),
            P("seq", None),
        ),
        check_vma=False,
    )
```

profile of v0, /device:TPU:1, one launch (start us, length us, event | category | flops | bytes accessed | tf_op | source)
XLA Modules:
  0.0 1393.6 jit_solution(10505384780612016629)
XLA Ops:
  81.2 17.4 %multiply_convert_fusion.2 = (bf16[1,1024,1792]{2,1,0:T(8,128)(2,1)S(1)}, f32[1,1024,1792]{2,1,0:T(8,128)}) fusion(f32[1024,1792]{1,0:T(8,128)} %copy-done.1, f32[1792]{0:T(1024)S(1)} %get-tuple-element.356, f32[1,1024,1792]{2,1,0:T(8,128)} %bitcast.551, f32[1,3,1792]{2,1,0:T(4,128)S(1)} %convert_element_type.429, f32[1792]{0:T(1024)S(1)} %get-tuple-element.357, ...), kind=kLoop, calls=%fused_computation.90 | loop fusion | flops 29360128 | bytes 25747456 | tf_op jit(solution)/shard_map/convert.14
  124.5 49.0 %fusion.8 = (f32[1024,2,4]{0,2,1:T(4,128)S(1)}, f32[2,4096,1024,4]{2,1,3,0:T(8,128)}) fusion(pred[1024,4096]{0,1:T(8,128)(4,1)} %fusion.41, bf16[1024,2,4,32]{0,3,2,1:T(8,128)(2,1)} %bitcast.577, bf16[1024,2,4,32]{0,3,2,1:T(8,128)(2,1)} %bitcast.575, bf16[1,4096,2,64]{1,3,2,0:T(8,128)(2,1)} %all-gather.9.cloned.1.call-done), kind=kOutput, calls=%fused_computation.16 | convolution fusion | flops 4397719552 | bytes 140541952 | tf_op jit(solution)/shard_map/scjqd,srjd->scjqr/dot_general | solution.py:209
  173.6 42.5 %fusion.13 = f32[1024,2,4]{0,2,1:T(4,128)S(1)} fusion(f32[2,4096,1024,4]{2,1,3,0:T(8,128)} %get-tuple-element.443, f32[1024,2,4]{0,2,1:T(4,128)S(1)} %broadcast_maximum_fusion, pred[1024,4096]{0,1:T(8,128)(4,1)} %fusion.41), kind=kLoop, calls=%fused_computation.26 | loop fusion | flops 167763968 | bytes 138477568 | tf_op jit(solution)/shard_map/reduce_sum | solution.py:226
  216.1 95.2 %fusion.252 = (bf16[1,1024,2,4,64]{1,4,3,2,0:T(8,128)(2,1)}, f32[1,1024,2,4,64]{1,4,3,2,0:T(8,128)}) fusion(f32[1024,2,4]{0,2,1:T(4,128)S(1)} %fusion.13, f32[2,4096,1024,4]{2,1,3,0:T(8,128)} %get-tuple-element.443, f32[1024,2,4]{0,2,1:T(4,128)S(1)} %broadcast_maximum_fusion, pred[1024,4096]{0,1:T(8,128)(4,1)} %fusion.41, ...), kind=kOutput, calls=%fused_computation.342 | convolution fusion | flops 25905070080 | bytes 142671872 | tf_op jit(solution)/shard_map/scjqr,srjd->scjqd/dot_general | solution.py:223
  319.5 78.5 %fusion.57 = f32[1,1024,24,64]{1,3,2,0:T(8,128)} fusion(f32[1,1024,24,64]{1,3,2,0:T(8,128)} %bitcast.565, f32[1024,24,64]{0,2,1:T(8,128)} %fusion.171, f32[24]{0:T(128)S(1)} %copy-done.117, f32[1024,24]{0,1:T(8,128)S(1)} %copy-done.53, bf16[1024,24,64]{0,2,1:T(8,128)(2,1)} %bitcast.556, f32[1024,24]{0,1:T(8,128)S(1)} %copy-done.64, ...), kind=kOutput, calls=%fused_computation.99 | convolution fusion | flops 19434307584 | bytes 27557984 | tf_op jit(solution)/shard_map/stuh,suhp->sthp/dot_general | solution.py:149
  438.6 15.3 %multiply_convert_fusion = (bf16[1024,2048]{1,0:T(8,128)(2,1)}, bf16[1024,2048]{1,0:T(8,128)(2,1)}, bf16[1024,2048]{1,0:T(8,128)(2,1)}) fusion(f32[1024,2048]{1,0:T(8,128)} %fusion.253, f32[1024,2048]{1,0:T(8,128)} %fusion.254, bf16[2048,1024]{1,0:T(8,128)(2,1)} %param.47, bf16[1,1024,1024]{1,2,0:T(8,128)(2,1)S(1)} %copy-done.15, f32[1024]{0:T(1024)S(1)} %copy-done.62), kind=kOutput, calls=%fused_computation.65 | convolution fusion | flops 4331667456 | bytes 35655680 | tf_op jit(solution)/shard_map/scm,km->sck/dot_general | solution.py:84
  472.9 75.4 %fusion.1 = bf16[1,1024,2,4,4096]{1,4,3,2,0:T(8,128)(2,1)} fusion(f32[2,4096,1024,4]{2,1,3,0:T(8,128)} %get-tuple-element.443, bf16[1024,2,4,64]{0,3,2,1:T(8,128)(2,1)} %bitcast.580, f32[1024,2,4]{0,2,1:T(4,128)S(1)} %fusion.103, f32[1024,2,4]{0,2,1:T(4,128)S(1)} %copy-done.94, pred[1024,4096]{0,1:T(8,128)(4,1)} %fusion.41, ...), kind=kOutput, calls=%fused_computation.6 | convolution fusion | flops 4496293888 | bytes 207683584 | tf_op jit(solution)/shard_map/scjqd,srjd->scjqr/dot_general | solution.py:320
  548.3 28.6 %fusion.81 = bf16[1,4096,2,64]{1,3,2,0:T(8,128)(2,1)} fusion(bf16[1,1024,2,4,4096]{1,4,3,2,0:T(8,128)(2,1)} %fusion.1, bf16[1024,2,4,32]{0,3,2,1:T(8,128)(2,1)} %bitcast.578, bf16[1024,2,4,32]{0,3,2,1:T(8,128)(2,1)} %bitcast.576), kind=kOutput, calls=%fused_computation.123 | convolution fusion | flops 4298113024 | bytes 69206016 | tf_op jit(solution)/shard_map/scjqr,scjqd->srjd/dot_general | solution.py:329
  576.9 104.2 %fusion.72 = bf16[1,4096,2,64]{1,3,2,0:T(8,128)(2,1)} fusion(bf16[1024,2,4,64]{0,3,2,1:T(8,128)(2,1)} %bitcast.581, f32[2,4096,1024,4]{2,1,3,0:T(8,128)} %get-tuple-element.443, f32[1024,2,4]{0,2,1:T(4,128)S(1)} %copy-done.94, pred[1024,4096]{0,1:T(8,128)(4,1)} %fusion.41), kind=kOutput, calls=%fused_computation.120 | convolution fusion | flops 25870991360 | bytes 140541952 | tf_op jit(solution)/shard_map/scjqr,scjqd->srjd/dot_general | solution.py:332
  681.2 11.7 multiply_reduce_fusion.5
  692.9 10.2 fusion.58
  730.4 26.9 %broadcast_multiply_fusion.4 = f32[2,64,1024,4]{2,1,3,0:T(8,128)} fusion(bf16[1,1024,2,4,4096]{1,4,3,2,0:T(8,128)(2,1)} %fusion.1, bf16[1,4096,2,64]{1,3,2,0:T(8,128)(2,1)} %all-gather.9.cloned.1.call-done), kind=kOutput, calls=%fused_computation.222 | convolution fusion | flops 4295491584 | bytes 70254592 | tf_op jit(solution)/shard_map/scjqr,srjd->scjqd/dot_general | solution.py:325
  780.0 11.0 fusion.55
  824.5 100.9 %fusion.28 = (f32[1024,24]{0,1:T(8,128)}, f32[1024,24]{0,1:T(8,128)}, f32[1024,24]{0,1:T(8,128)}, f32[1024,1024]{1,0:T(8,128)S(1)}) fusion(f32[1024,1024]{1,0:T(8,128)} %fusion.196, f32[1024,24]{0,1:T(8,128)S(1)} %copy-done.65, f32[1024,24]{0,1:T(8,128)S(1)} %copy-done.67, pred[1024,1024]{1,0:T(8,128)(4,1)} %convert_compare_fusion, ...), kind=kOutput, calls=%fused_computation.41 | convolution fusion | flops 19653386240 | bytes 19365888 | tf_op jit(solution)/shard_map/transpose(jvp(stuh,suhp->sthp))/dot_general | solution.py:149
  930.7 12.4 convolution_bitcast_fusion
  971.3 90.1 %fusion.56 = f32[1,1024,24,64]{1,3,2,0:T(8,128)} fusion(f32[24,64,1024]{2,1,0:T(8,128)} %get-tuple-element.451, f32[1,1024,24,64]{1,3,2,0:T(8,128)} %bitcast.562, f32[24]{0:T(128)S(1)} %copy-done.118, f32[1024,24]{0,1:T(8,128)S(1)} %copy-done.51, f32[24,64,1024]{2,1,0:T(8,128)} %bitcast.561, f32[1024,24]{0,1:T(8,128)S(1)} %copy-done.65, ...), kind=kOutput, calls=%fused_computation.97 | convolution fusion | flops 19434307584 | bytes 30703712 | tf_op jit(solution)/shard_map/transpose(jvp(stuh,suhp->sthp))/dot_general | solution.py:149
  1068.0 12.4 fusion.139
  1080.5 18.6 %multiply_reduce_fusion.3 = (f32[1792]{0:T(1024)S(1)}, f32[1792]{0:T(1024)S(1)}, f32[1792]{0:T(1024)S(1)}, f32[1792]{0:T(1024)S(1)}, f32[1792]{0:T(1024)S(1)}, /*index=5*/f32[1,1024,1792]{2,1,0:T(8,128)S(1)}) fusion(f32[1,1024,1792]{2,1,0:T(8,128)} %bitcast.552, f32[1,3,1792]{2,1,0:T(4,128)S(1)} %copy-done.60, f32[1024,1792]{1,0:T(8,128)} %copy-done.1, ...), kind=kLoop, calls=%fused_computation.88 | loop fusion | flops 42196224 | bytes 36757504 | tf_op jit(solution)/shard_map/transpose(jvp())/reduce_sum | solution.py:120
  1107.2 12.4 fusion.248
  1145.3 10.6 fusion.92
  1188.2 42.5 %all-reduce.12 = (f32[4,1792]{1,0:T(4,128)}, f32[1792]{0:T(1024)}, f32[24]{0:T(128)}, f32[24]{0:T(128)}, f32[24]{0:T(128)}) all-reduce(f32[4,1792]{1,0:T(4,128)S(1)} %pad_add_fusion.1, f32[1792]{0:T(1024)S(1)} %get-tuple-element.348, f32[24]{0:T(128)} %get-tuple-element.426, ...), channel_id=1, replica_groups=mesh['dp'=8,'seq'=4] {'dp','seq'}, use_global_device_ids=true, to_apply=%region_41.42 | all-reduce | flops 9032 | bytes 72256 | tf_op jit(solution)/shard_map/psum | solution.py:464
  1232.5 15.7 %fusion.85 = (bf16[1024]{0:T(1024)(128)(2,1)S(1)}, f32[1024]{0:T(1024)S(1)}, f32[1024,1024]{0,1:T(8,128)}) fusion(bf16[1,1024,1024]{1,2,0:T(8,128)(2,1)S(1)} %copy-done.12, f32[1024]{0:T(1024)S(1)} %copy-done.101, f32[1024]{0:T(1024)S(1)} %copy-done.107, f32[1024,1024]{0,1:T(8,128)S(1)} %fusion.189, bf16[1024,1792]{1,0:T(8,128)(2,1)} %param.34, ...), kind=kOutput, calls=%fused_computation.125 | convolution fusion | flops 3778017280 | bytes 34617344 | tf_op jit(solution)/shard_map/scm,km->sck/dot_general | solution.py:84
  1271.1 27.6 %all-reduce.13 = (bf16[256]{0:T(256)(128)(2,1)S(1)}, bf16[256,24]{0,1:T(8,128)(2,1)S(1)}, bf16[384]{0:T(512)(128)(2,1)S(1)}, bf16[256]{0:T(256)(128)(2,1)S(1)}) all-reduce(bf16[256]{0:T(256)(128)(2,1)S(1)} %dynamic-slice.1, bf16[256,24]{0,1:T(8,128)(2,1)} %reduce-scatter.28.cloned.1.call-done, ...), channel_id=1, replica_groups=mesh['dp'=8,'seq'=4] {'dp'}, use_global_device_ids=true, to_apply=%region_24.25 | all-reduce | flops 7040 | bytes 28160 | tf_op jit(solution)/shard_map/psum | solution.py:433
  1301.1 71.0 %all-reduce.18.cloned.1.call-done = (bf16[256,512]{1,0:T(8,128)(2,1)}, bf16[256,128]{1,0:T(8,128)(2,1)}, bf16[256,128]{1,0:T(8,128)(2,1)}, bf16[256,1536]{1,0:T(...) async-done(((bf16[256,512]{1,0:T(8,128)(2,1)}, ...) | async-done | bytes 6291472 | tf_op jit(solution)/shard_map/psum | solution.py:434
  (452 shorter events, 404.5 us)
Async XLA Ops:
  7.2 397.4 %copy-start = (bf16[1024,1536]{1,0:T(8,128)(2,1)S(1)}, bf16[1024,1536]{1,0:T(8,128)(2,1)}, u32[]{:S(2)}) copy-start(bf16[1024,1536]{1,0:T(8,128)(2,1)} %param.33) | copy-start | bytes 9437188
  7.2 117.3 %all-gather.9.cloned.1.call-start = ((), (), s32[]{:S(2)}) async-start(), calls=%async_computation.14 | async-start | bytes 1310720 | tf_op jit(solution)/shard_map/all_gather | solution.py:217
  19.3 196.8 %all-gather.7.cloned.1.call-start = ((), (), s32[]{:S(2)}) async-start(), calls=%async_computation.13 | async-start | bytes 1310720 | tf_op jit(solution)/shard_map/all_gather | solution.py:218
  29.2 51.9 %collective-permute-start = (bf16[1,3,1792]{2,1,0:T(4,128)(2,1)S(1)}, bf16[1,3,1792]{2,1,0:T(4,128)(2,1)S(1)}, u32[]{:S(2)}, u32[]{:S(2)}) collective-permute-start(bf16[1,3,1792]{2,1,0:T(4,128)(2,1)S(1)} %slice.220), channel_id=1, source_target_pairs={{0,1},{1,2},{2,3},{4,5},{5,6},{6,7},{8,9},{9,10},{10,11},{12,13},{... | collective-permute-start | bytes 32264 | tf_op jit(solution)/shard_map/ppermute | solution.py:23
  34.7 277.3 %all-gather.11.cloned.1.call-start = ((), (), s32[]{:S(2)}) async-start(), calls=%async_computation.28 | async-start | bytes 1966080 | tf_op jit(solution)/shard_map/all_gather | solution.py:29
  63.9 50.9 %copy-start.50 = (f32[1024,24]{0,1:T(8,128)}, f32[1024,24]{0,1:T(8,128)S(1)}, u32[]{:S(2)}) copy-start(f32[1024,24]{0,1:T(8,128)S(1)} %copy.264) | copy-start | bytes 294916
  124.5 638.6 %reduce-scatter.14.cloned.1.call-start = ((), (), s32[]{:S(2)}) async-start(), calls=%async_computation.15 | async-start | bytes 1310720 | tf_op jit(solution)/shard_map/reduce_scatter | solution.py:337
  576.9 104.3 %copy-start.84 = (f32[1024]{0:T(1024)S(1)}, f32[1024]{0:T(1024)}, u32[]{:S(2)}) copy-start(f32[1024]{0:T(1024)} %copy-done.83) | copy-start | bytes 12292
  576.9 104.3 %copy-start.92 = (f32[1536]{0:T(1024)S(1)}, f32[1536]{0:T(1024)}, u32[]{:S(2)}) copy-start(f32[1536]{0:T(1024)} %param.41) | copy-start | bytes 18436
  576.9 191.2 %reduce-scatter.16.cloned.1.call-start = ((), (), s32[]{:S(2)}) async-start(), calls=%async_computation.16 | async-start | bytes 1310720 | tf_op jit(solution)/shard_map/reduce_scatter | solution.py:340
  692.9 260.6 %all-gather.13.cloned.1.call-start = ((), (), s32[]{:S(2)}) async-start(), calls=%async_computation.29 | async-start | bytes 1966080 | tf_op jit(solution)/shard_map/all_gather | solution.py:51
  725.8 504.8 %reduce-scatter.30.cloned.1.call-start = ((), (), s32[]{:S(2)}) async-start(), calls=%async_computation.23 | async-start | bytes 1310720 | tf_op jit(solution)/shard_map/reduce_scatter | solution.py:413
  730.3 500.3 %reduce-scatter.18.cloned.1.call-start = ((), (), s32[]{:S(2)}) async-start(), calls=%async_computation.17 | async-start | bytes 1310720 | tf_op jit(solution)/shard_map/reduce_scatter | solution.py:392
  763.0 467.7 %reduce-scatter.20.cloned.1.call-start = ((), (), s32[]{:S(2)}) async-start(), calls=%async_computation.18 | async-start | bytes 327680 | tf_op jit(solution)/shard_map/reduce_scatter | solution.py:395
  768.0 462.7 %reduce-scatter.22.cloned.1.call-start = ((), (), s32[]{:S(2)}) async-start(), calls=%async_computation.19 | async-start | bytes 327680 | tf_op jit(solution)/shard_map/reduce_scatter | solution.py:398
  771.1 459.5 %reduce-scatter.32.cloned.1.call-start = ((), (), s32[]{:S(2)}) async-start(), calls=%async_computation.24 | async-start | bytes 3932160 | tf_op jit(solution)/shard_map/reduce_scatter | solution.py:416
  780.0 450.7 %reduce-scatter.24.cloned.1.call-start = ((), (), s32[]{:S(2)}) async-start(), calls=%async_computation.20 | async-start | bytes 3932160 | tf_op jit(solution)/shard_map/reduce_scatter | solution.py:401
  797.9 432.9 %reduce-scatter.34.cloned.1.call-start = ((), (), s32[]{:S(2)}) async-start(), calls=%async_computation.25 | async-start | bytes 5242880 | tf_op jit(solution)/shard_map/reduce_scatter | solution.py:422
  807.3 423.5 %reduce-scatter.36.cloned.1.call-start = ((), (), s32[]{:S(2)}) async-start(), calls=%async_computation.26 | async-start | bytes 5242880 | tf_op jit(solution)/shard_map/reduce_scatter | solution.py:425
  823.6 407.2 %reduce-scatter.38.cloned.1.call-start = ((), (), s32[]{:S(2)}) async-start(), calls=%async_computation.27 | async-start | bytes 5242880 | tf_op jit(solution)/shard_map/reduce_scatter | solution.py:428
  953.4 277.4 %reduce-scatter.26.cloned.1.call-start = ((), (), s32[]{:S(2)}) async-start(), calls=%async_computation.21 | async-start | bytes 4587520 | tf_op jit(solution)/shard_map/reduce_scatter | solution.py:404
  1119.6 4.7 collective-permute-start.1
  1131.0 140.1 %reduce-scatter.28.cloned.1.call-start = ((), (), s32[]{:S(2)}) async-start(), calls=%async_computation.22 | async-start | bytes 61440 | tf_op jit(solution)/shard_map/reduce_scatter | solution.py:407
  1187.4 184.7 %all-reduce.18.cloned.1.call-start = ((), (), s32[]{:S(2)}) async-start(), calls=%async_computation.30 | async-start | bytes 12582912 | tf_op jit(solution)/shard_map/psum | solution.py:434
  (121 other events, 1147.5 us)
Sparse Core Ops, SparseCore 0:
  19.4 28.6 all-gather.8
  50.6 26.6 all-gather.6
  124.6 33.8 all-gather.10
  577.0 39.4 reduce-scatter.13
  693.0 39.4 reduce-scatter.15
  734.2 34.4 all-gather.12
  771.6 27.7 reduce-scatter.29
  803.1 27.7 reduce-scatter.17
  833.6 23.6 reduce-scatter.19
  860.1 24.0 reduce-scatter.21
  887.1 44.4 reduce-scatter.31
  934.5 43.9 reduce-scatter.23
  981.4 52.6 reduce-scatter.33
  1037.2 52.6 reduce-scatter.35
  1092.7 52.7 reduce-scatter.37
  1148.6 48.3 reduce-scatter.25
  1200.4 22.8 reduce-scatter.27
  1231.0 141.0 all-reduce.17
where the time goes:
time: 1400 us; the launch traced here: 1390 us
  matrix products  909 us (65%)
  other arithmetic  197 us (14%)
  local copies, waits for them, and re-layouts  104 us (7%)
  blocking collectives  85.1 us (6%)
  waiting for transfers between devices  73.9 us (5%)
  between operations  17.9 us (1%)
    dot_general x3, matrix products, span_out(): inner = jnp.einsum('stuh,suhp->sthp', combined, ssm_in, precision=highest)  270 us
    dot_general x1, matrix products, on_device(): jnp.einsum('scjqr,scjqd->srjd', weights, grad_attn_wide, precision=highest)  104 us
    dot_general x1, matrix products, on_device(): jnp.einsum('scjqr,srjd->scjqd', weights, value_piece.astype(jnp.float32),...  95.2 us
    dot_general x1, matrix products, on_device(): jnp.einsum('scjqd,srjd->scjqr', grad_attn, value_piece, preferred_element...  75.4 us
    dot_general x11, matrix products, project_back(): jnp.einsum('scm,km->sck', grad, weight, preferred_element_type=jnp.float32)  74 us
    psum x1, waiting for transfers between devices, on_device(): lax.psum(p_query.astype(jnp.bfloat16), 'dp').astype(jnp.float32)  71 us
    dot_general x11, matrix products, weight_grad(): jnp.einsum('sck,scm->km', left, grad, preferred_element_type=jnp.float32)  59.2 us
    dot_general x11, matrix products, project(): jnp.einsum('sck,km->scm', left, weight, preferred_element_type=jnp.float32)  56.2 us
  transfers between devices with their start and end apart: 20, of which 2 were waited for; matrix products, arithmetic and copies ran while one was open for 65% of the time, Pallas kernels for 0%

commit v1 on v0

v1 whole, which is shorter than its diff:
```python
import functools

import jax
import jax.numpy as jnp
import numpy as np
from jax import lax
from jax.experimental import pallas as pl
from jax.experimental.pallas import tpu as pltpu
from jax.sharding import PartitionSpec as P

HEADS = 8
KV_HEADS = 2
HEAD = 64
SSM_HEADS = 24
SSM_HEAD = 64
STATE = 128
WIDE = SSM_HEADS * SSM_HEAD
CHUNK = 128
EPS = 1e-05
ROPE_BASE = 100000000000.0
LOG2E = 1.4426950408889634
SCORE2 = 0.125 * LOG2E
LOWEST = -1e30
F32 = jnp.float32
BF16 = jnp.bfloat16
NN = (((1,), (0,)), ((), ()))
NT = (((1,), (1,)), ((), ()))
TN = (((0,), (0,)), ((), ()))
VMEM_LIMIT = 60 << 20


def dot(a, b, dims=NN):
    return lax.dot_general(a, b, dims, preferred_element_type=F32)


def dot_exact(a, b, dims=NN):
    return lax.dot_general(a, b, dims, precision=lax.Precision.HIGHEST, preferred_element_type=F32)


def low(v):
    return v.astype(BF16)


def sigmoid(v):
    return 1.0 / (1.0 + jnp.exp(-v))


def softplus(v):
    e = jnp.exp(-jnp.abs(v))
    tail = jnp.where(e < 1e-2, e * (1.0 - e * (0.5 - e * (1.0 / 3.0))), jnp.log(1.0 + e))
    return jnp.maximum(v, 0.0) + tail


def split_low(v):
    high = low(v)
    return high, low(v - high.astype(F32))


def widen(v, expand):
    return dot(jnp.concatenate(split_low(v), 1), expand)


def head_sums(v, expand):
    high, rest = split_low(v)
    ones = expand[:128]
    return dot(high, ones, NT) + dot(rest, ones, NT)


def full_spec(shape):
    return pl.BlockSpec(shape, lambda *_: (0,) * len(shape), pipeline_mode=pl.Buffered(1))


def params(limit=VMEM_LIMIT):
    return pltpu.CompilerParams(
        vmem_limit_bytes=limit, dimension_semantics=("arbitrary", "arbitrary")
    )


def low_rows(rows):
    t = lax.broadcasted_iota(jnp.int32, (rows, rows), 0)
    u = lax.broadcasted_iota(jnp.int32, (rows, rows), 1)
    return t >= u


def swap_halves(v):
    lane = lax.broadcasted_iota(jnp.int32, v.shape, 1)
    return jnp.where((lane & 63) < 32, pltpu.roll(v, 96, 1), pltpu.roll(v, 32, 1))


def pair_rows(v):
    lane = lax.broadcasted_iota(jnp.int32, v.shape, 1)
    none = jnp.zeros_like(v)
    return jnp.concatenate([jnp.where(lane < 64, v, none), jnp.where(lane >= 64, v, none)], 0)


def enter_body(
    pos_ref, len_ref, tok_ref, halo_ref, gain_ref, wq_ref, wk_ref, wv_ref, wz_ref, wc_ref, ws_ref,
    cw_ref, cb_ref, sb_ref, a_ref, cos_ref, sin_ref, exp_ref,
    hid_ref, q_ref, kv_ref, z_ref, cl_ref, pre_ref, x_ref, bk_ref, cq_ref,
    dt_ref, sg_ref, cum_ref, cumt_ref, st_ref, tot_ref,
    prev, state, total, *, rows, blocks,
):
    s = pl.program_id(0)
    b = pl.program_id(1)

    def normed(v):
        v = v.astype(F32)
        return low(v * lax.rsqrt(jnp.mean(v * v, -1, keepdims=True) + EPS) * gain_ref[...])

    @pl.when(b == 0)
    def _():
        prev[...] = dot(normed(halo_ref[0]), wc_ref[...])[8:]
        state[...] = jnp.zeros_like(state)
        total[...] = jnp.zeros_like(total)

    hid = normed(tok_ref[0])
    hid_ref[0] = hid
    cosine, sine = cos_ref[...], sin_ref[...]
    q = dot(hid, wq_ref[...])
    for g in range(4):
        t = q[:, g * 128 : g * 128 + 128]
        q_ref[0, :, g * 128 : g * 128 + 128] = low(t * cosine + swap_halves(t) * sine)
    t = dot(hid, wk_ref[...])
    kv_ref[0, :, :128] = low(t * cosine + swap_halves(t) * sine)
    kv_ref[0, :, 128:] = low(dot(hid, wv_ref[...]))
    z_ref[0] = low(dot(hid, wz_ref[...]))
    conv = dot(hid, wc_ref[...])
    cl_ref[0] = low(conv)
    ext = jnp.concatenate([prev[...], conv], 0)
    prev[...] = conv[rows - 8 :]
    pre = cb_ref[...] + cw_ref[3:4] * conv
    for back in range(1, 4):
        pre = pre + cw_ref[3 - back : 4 - back] * pltpu.roll(ext, back, 0)[8:]
    pre_ref[0] = low(pre)
    act = low(pre * sigmoid(pre))
    x = act[:, :WIDE]
    bk = act[:, WIDE : WIDE + STATE]
    x_ref[0] = x
    bk_ref[0] = bk
    cq_ref[0] = act[:, WIDE + STATE :]
    raw = dot(hid, ws_ref[...]) + sb_ref[...]
    at = pos_ref[0] + b * rows + lax.broadcasted_iota(jnp.int32, raw.shape, 0)
    live = jnp.where(at < len_ref[s], 1.0, 0.0)
    dt = softplus(raw) * live
    dt_ref[0] = dt
    sg_ref[0] = sigmoid(raw) * live
    log_decay = dt * a_ref[...]
    tri = jnp.where(low_rows(CHUNK), 1.0, 0.0)
    for c in range(rows // CHUNK):
        here = slice(c * CHUNK, (c + 1) * CHUNK)
        cum = dot_exact(tri, log_decay[here])
        cum_ref[0, here] = cum
        cumt_ref[0, :, here] = cum.T[:32]
        last = cum[CHUNK - 1 :]
        weight = dt[here] * jnp.exp2(last - cum)
        wide = widen(jnp.concatenate([weight, jnp.broadcast_to(jnp.exp2(last), (16, 128))], 0), exp_ref[...])
        xw = low(x[here].astype(F32) * wide[:CHUNK])
        state[...] = state[...] * wide[CHUNK : CHUNK + 1] + dot(bk[here], xw, TN)
        total[...] = total[...] + last

    @pl.when(b == blocks - 1)
    def _():
        st_ref[0] = low(state[...])
        tot_ref[0] = jnp.broadcast_to(total[...], (8, 128))


def enter(pos, lens, tokens, halo, gain, wq, wk, wv, wz, wc, ws, cw, cb, sb, a, cosine, sine, expand):
    seqs, span, width = tokens.shape
    rows = min(256, span)
    blocks = span // rows
    conv_width = wc.shape[1]

    def row(n):
        return pl.BlockSpec((1, rows, n), lambda s, b, *_: (s, b, 0))

    def shape(n, kind):
        return jax.ShapeDtypeStruct((seqs, span, n), kind)

    table = pl.BlockSpec((rows, 128), lambda s, b, *_: (b, 0))
    return pl.pallas_call(
        functools.partial(enter_body, rows=rows, blocks=blocks),
        grid_spec=pltpu.PrefetchScalarGridSpec(
            num_scalar_prefetch=2,
            grid=(seqs, blocks),
            in_specs=[
                row(width),
                pl.BlockSpec((1, 16, width), lambda s, b, *_: (s, 0, 0)),
                full_spec(gain.shape), full_spec(wq.shape), full_spec(wk.shape), full_spec(wv.shape),
                full_spec(wz.shape), full_spec(wc.shape), full_spec(ws.shape), full_spec(cw.shape),
                full_spec(cb.shape), full_spec(sb.shape), full_spec(a.shape), table, table,
                full_spec(expand.shape),
            ],
            out_specs=[
                row(width), row(512), row(256), row(WIDE), row(conv_width), row(conv_width),
                row(WIDE), row(STATE), row(STATE), row(128), row(128), row(128),
                pl.BlockSpec((1, 32, rows), lambda s, b, *_: (s, 0, b)),
                pl.BlockSpec((1, STATE, WIDE), lambda s, b, *_: (s, 0, 0)),
                pl.BlockSpec((1, 8, 128), lambda s, b, *_: (s, 0, 0)),
            ],
            scratch_shapes=[
                pltpu.VMEM((8, conv_width), F32), pltpu.VMEM((STATE, WIDE), F32), pltpu.VMEM((1, 128), F32),
            ],
        ),
        out_shape=[
            shape(width, BF16), shape(512, BF16), shape(256, BF16), shape(WIDE, BF16),
            shape(conv_width, BF16), shape(conv_width, BF16), shape(WIDE, BF16), shape(STATE, BF16),
            shape(STATE, BF16), shape(128, F32), shape(128, F32), shape(128, F32),
            jax.ShapeDtypeStruct((seqs, 32, span), F32),
            jax.ShapeDtypeStruct((seqs, STATE, WIDE), BF16),
            jax.ShapeDtypeStruct((seqs, 8, 128), F32),
        ],
        compiler_params=params(),
        name="enter",
    )(pos, lens, tokens, halo, gain, wq, wk, wv, wz, wc, ws, cw, cb, sb, a, cosine, sine, expand)


def scan_body(
    x_ref, bk_ref, cq_ref, dt_ref, cum_ref, cumt_ref, sin_ref, skip_ref, z_ref, gain_ref, exp_ref,
    mix_ref, low_ref, st_ref, state, y,
):
    c = pl.program_id(1)

    @pl.when(c == 0)
    def _():
        state[...] = sin_ref[0]

    x = x_ref[0].astype(F32)
    bk, cq = bk_ref[0], cq_ref[0]
    cum = cum_ref[0]
    last = cum[CHUNK - 1 :]
    expand = exp_ref[...]
    xdt = x * widen(dt_ref[0], expand)
    ends = widen(
        jnp.concatenate([jnp.exp2(cum), jnp.exp2(last - cum), jnp.broadcast_to(jnp.exp2(last), (16, 128))], 0),
        expand,
    )
    inter = jnp.where(low_rows(CHUNK), dot(cq, bk, NT), 0.0)
    held = low(state[...])
    st_ref[0, 0] = held
    y[...] = dot(cq, held) * ends[:CHUNK] + skip_ref[...] * x
    state[...] = state[...] * ends[2 * CHUNK : 2 * CHUNK + 1] + dot(bk, low(xdt * ends[CHUNK : 2 * CHUNK]), TN)
    xdt = low(xdt)
    for p in range(SSM_HEADS // 2):
        parts = []
        for h in (2 * p, 2 * p + 1):
            differ = jnp.minimum(cum[:, h : h + 1] - cumt_ref[0, h : h + 1, :], 0.0)
            parts.append(low(inter * jnp.exp2(differ)))
        cols = slice(p * 128, p * 128 + 128)
        y[:, cols] += dot(jnp.concatenate(parts, 1), pair_rows(xdt[:, cols]))
    mixed = y[...]
    mix_ref[0] = mixed
    z = z_ref[0].astype(F32)
    v = mixed * (z * sigmoid(z))
    low_ref[0] = low(v * lax.rsqrt(jnp.mean(v * v, -1, keepdims=True) + EPS) * gain_ref[...])


def scan_forward(x, bk, cq, dt, cum, cumt, state_in, skip, z, gain, expand):
    seqs, span, _ = x.shape
    chunks = span // CHUNK

    def row(n):
        return pl.BlockSpec((1, CHUNK, n), lambda s, c: (s, c, 0))

    return pl.pallas_call(
        scan_body,
        grid=(seqs, chunks),
        in_specs=[
            row(WIDE), row(STATE), row(STATE), row(128), row(128),
            pl.BlockSpec((1, 32, CHUNK), lambda s, c: (s, 0, c)),
            pl.BlockSpec((1, STATE, WIDE), lambda s, c: (s, 0, 0)),
            full_spec(skip.shape), row(WIDE), full_spec(gain.shape), full_spec(expand.shape),
        ],
        out_specs=[row(WIDE), row(WIDE), pl.BlockSpec((1, 1, STATE, WIDE), lambda s, c: (s, c, 0, 0))],
        out_shape=[
            jax.ShapeDtypeStruct((seqs, span, WIDE), F32),
            jax.ShapeDtypeStruct((seqs, span, WIDE), BF16),
            jax.ShapeDtypeStruct((seqs, chunks, STATE, WIDE), BF16),
        ],
        scratch_shapes=[pltpu.VMEM((STATE, WIDE), F32), pltpu.VMEM((CHUNK, WIDE), F32)],
        compiler_params=params(),
        name="scan_forward",
    )(x, bk, cq, dt, cum, cumt, state_in, skip, z, gain, expand)


def middle_body(
    pos_ref, len_ref, attn_ref, mix_ref, tok_ref, cot_ref, mixed_ref, z_ref, cq_ref, cum_ref,
    wao_ref, wmo_ref, wg_ref, wu_ref, wd_ref, gain2_ref, gated_ref, exp_ref,
    out_ref, h2_ref, act_ref, gffn_ref, gg_ref, gu_ref, gmid_ref, gb_ref, gattn_ref, gmixed_ref, gz_ref,
    delta_ref, gn2_ref, ggain_ref, adj_ref,
    gn2_s, ggain_s, adj, offset, *, rows, blocks, seqs,
):
    s = pl.program_id(0)
    b = pl.program_id(1)

    @pl.when((s == 0) & (b == 0))
    def _():
        gn2_s[...] = jnp.zeros_like(gn2_s)
        ggain_s[...] = jnp.zeros_like(ggain_s)

    @pl.when(b == 0)
    def _():
        adj[...] = jnp.zeros_like(adj)
        offset[...] = jnp.zeros_like(offset)

    at = pos_ref[0] + b * rows + lax.broadcasted_iota(jnp.int32, (rows, 1), 0)
    live = jnp.where(at < len_ref[s], 1.0, 0.0)
    attn = attn_ref[0]
    branch = dot(attn, wao_ref[...]) + dot(mix_ref[0], wmo_ref[...])
    after = tok_ref[0].astype(F32) + live * branch
    scale = lax.rsqrt(jnp.mean(after * after, -1, keepdims=True) + EPS)
    unit = after * scale
    gain = gain2_ref[...]
    h2 = low(unit * gain)
    h2_ref[0] = h2
    gate = dot(h2, wg_ref[...])
    up = dot(h2, wu_ref[...])
    sg = sigmoid(gate)
    silu = gate * sg
    act = low(silu * up)
    act_ref[0] = act
    out_ref[0] = low(after + live * dot(act, wd_ref[...]))
    cot = cot_ref[0].astype(F32)
    gffn = low(live * cot)
    gffn_ref[0] = gffn
    gact = dot(gffn, wd_ref[...], NT)
    gg = low(gact * up * (sg * (1.0 + gate * (1.0 - sg))))
    gu = low(gact * silu)
    gg_ref[0] = gg
    gu_ref[0] = gu
    gh2 = dot(gg, wg_ref[...], NT) + dot(gu, wu_ref[...], NT)
    gn2_s[...] += jnp.sum(gh2 * unit, 0, keepdims=True)
    g = gh2 * gain
    gmid = cot + scale * (g - unit * jnp.mean(g * unit, -1, keepdims=True))
    gmid_ref[0] = gmid
    gb = low(live * gmid)
    gb_ref[0] = gb
    gattn = low(dot(gb, wao_ref[...], NT))
    gattn_ref[0] = gattn
    prod = gattn.astype(F32) * attn.astype(F32)
    col = lax.broadcasted_iota(jnp.int32, (8, 512), 1) // HEAD
    ones = low(jnp.where(col == lax.broadcasted_iota(jnp.int32, (8, 512), 0), 1.0, 0.0))
    high, rest = split_low(prod)
    delta_ref[0] = dot(ones, high, NT) + dot(ones, rest, NT)
    gn = low(dot(gb, wmo_ref[...], NT)).astype(F32)
    mixed = mixed_ref[0]
    z = z_ref[0].astype(F32)
    sg = sigmoid(z)
    silu = z * sg
    v = mixed * silu
    scale = lax.rsqrt(jnp.mean(v * v, -1, keepdims=True) + EPS)
    unit = v * scale
    ggain_s[...] += jnp.sum(gn * unit, 0, keepdims=True)
    g = gn * gated_ref[...]
    g = scale * (g - unit * jnp.mean(g * unit, -1, keepdims=True))
    gmixed = g * silu
    gmixed_ref[0] = low(gmixed)
    gz_ref[0] = low(g * mixed * (sg * (1.0 + z * (1.0 - sg))))
    cum = cum_ref[0]
    logs = []
    for c in range(rows // CHUNK):
        here = cum[c * CHUNK : (c + 1) * CHUNK]
        logs.append(here + offset[...])
        offset[...] += here[CHUNK - 1 :]
    wide = widen(jnp.exp2(jnp.concatenate(logs, 0)), exp_ref[...])
    adj[...] += dot(cq_ref[0], low(gmixed * wide), TN)

    @pl.when(b == blocks - 1)
    def _():
        adj_ref[0] = low(adj[...])

    @pl.when((s == seqs - 1) & (b == blocks - 1))
    def _():
        gn2_ref[...] = gn2_s[...]
        ggain_ref[...] = ggain_s[...]


def middle(pos, lens, attn, mix, tokens, cot, mixed, z, cq, cum, wao, wmo, wg, wu, wd, gain2, gated, expand):
    seqs, span, width = tokens.shape
    rows = min(256, span)
    blocks = span // rows
    ff = wg.shape[1]

    def row(n):
        return pl.BlockSpec((1, rows, n), lambda s, b, *_: (s, b, 0))

    def shape(n, kind):
        return jax.ShapeDtypeStruct((seqs, span, n), kind)

    def once(n):
        return pl.BlockSpec((1, n), lambda s, b, *_: (0, 0))

    return pl.pallas_call(
        functools.partial(middle_body, rows=rows, blocks=blocks, seqs=seqs),
        grid_spec=pltpu.PrefetchScalarGridSpec(
            num_scalar_prefetch=2,
            grid=(seqs, blocks),
            in_specs=[
                row(512), row(WIDE), row(width), row(width), row(WIDE), row(WIDE), row(STATE), row(128),
                full_spec(wao.shape), full_spec(wmo.shape), full_spec(wg.shape), full_spec(wu.shape),
                full_spec(wd.shape), full_spec(gain2.shape), full_spec(gated.shape), full_spec(expand.shape),
            ],
            out_specs=[
                row(width), row(width), row(ff), row(width), row(ff), row(ff), row(width), row(width),
                row(512), row(WIDE), row(WIDE),
                pl.BlockSpec((1, 8, rows), lambda s, b, *_: (s, 0, b)),
                once(width), once(WIDE),
                pl.BlockSpec((1, STATE, WIDE), lambda s, b, *_: (s, 0, 0)),
            ],
            scratch_shapes=[
                pltpu.VMEM((1, width), F32), pltpu.VMEM((1, WIDE), F32), pltpu.VMEM((STATE, WIDE), F32),
                pltpu.VMEM((1, 128), F32),
            ],
        ),
        out_shape=[
            shape(width, BF16), shape(width, BF16), shape(ff, BF16), shape(width, BF16), shape(ff, BF16),
            shape(ff, BF16), shape(width, F32), shape(width, BF16), shape(512, BF16), shape(WIDE, BF16),
            shape(WIDE, BF16),
            jax.ShapeDtypeStruct((seqs, 8, span), F32),
            jax.ShapeDtypeStruct((1, width), F32), jax.ShapeDtypeStruct((1, WIDE), F32),
            jax.ShapeDtypeStruct((seqs, STATE, WIDE), BF16),
        ],
        compiler_params=params(),
        name="middle",
    )(pos, lens, attn, mix, tokens, cot, mixed, z, cq, cum, wao, wmo, wg, wu, wd, gain2, gated, expand)


def scan_back_body(
    x_ref, bk_ref, cq_ref, dt_ref, sg_ref, cum_ref, cumt_ref, dy_ref, mix_ref, st_ref, adj_ref, pre_ref, cl_ref,
    skip_ref, a_ref, cw_ref, exp_ref,
    gc_ref, gs_ref, tail_ref, head_ref, gw_ref, gskip_ref, small_ref,
    adj, after, gact, *, chunks,
):
    s = pl.program_id(0)
    c = pl.program_id(1)

    @pl.when((s == 0) & (c == 0))
    def _():
        gw_ref[...] = jnp.zeros_like(gw_ref)
        gskip_ref[...] = jnp.zeros_like(gskip_ref)
        small_ref[...] = jnp.zeros_like(small_ref)

    @pl.when(c == 0)
    def _():
        adj[...] = adj_ref[0]
        after[...] = jnp.zeros_like(after)

    x = x_ref[0].astype(F32)
    bk, cq = bk_ref[0], cq_ref[0]
    dt = dt_ref[0]
    cum = cum_ref[0]
    last = cum[CHUNK - 1 :]
    expand = exp_ref[...]
    dt_wide = widen(dt, expand)
    ends = widen(
        jnp.concatenate([jnp.exp2(cum), jnp.exp2(last - cum), jnp.broadcast_to(jnp.exp2(last), (16, 128))], 0),
        expand,
    )
    to_end = ends[CHUNK : 2 * CHUNK]
    all_wide = ends[2 * CHUNK : 2 * CHUNK + 1]
    xdt = x * dt_wide
    dy_low = dy_ref[0]
    dy = dy_low.astype(F32)
    dy_in = low(dy * ends[:CHUNK])
    state = st_ref[0, 0]
    gstate = adj[...]
    gstate_low = low(gstate)
    from_end = dot(bk, gstate_low) * to_end
    gb = dot(low(xdt * to_end), gstate_low, NT)
    gc = dot(dy_in, state, NT)
    gfinal = all_wide * jnp.sum(gstate * state.astype(F32), 0, keepdims=True) + jnp.sum(
        xdt * from_end, 0, keepdims=True
    )
    adj[...] = gstate * all_wide + dot(cq, dy_in, TN)
    xdt_low = low(xdt)
    u = lax.broadcasted_iota(jnp.int32, (CHUNK, CHUNK), 0)
    t = lax.broadcasted_iota(jnp.int32, (CHUNK, CHUNK), 1)
    inter = jnp.where(t >= u, dot(bk, cq, NT), 0.0)
    ginter = jnp.zeros((CHUNK, CHUNK), F32)
    for p in range(SSM_HEADS // 2):
        cols = slice(p * 128, p * 128 + 128)
        dy_rows = pair_rows(dy_low[:, cols])
        gmix = dot(xdt_low[:, cols], dy_rows, NT)
        parts = []
        for n, h in enumerate((2 * p, 2 * p + 1)):
            decay = jnp.exp2(jnp.minimum(cumt_ref[0, h : h + 1, :] - cum[:, h : h + 1], 0.0))
            parts.append(low(inter * decay))
            ginter = ginter + gmix[:, n * CHUNK : (n + 1) * CHUNK] * decay
        gact[:, cols] = dot(jnp.concatenate(parts, 1), dy_rows)
    ginter = low(jnp.where(t >= u, ginter, 0.0))
    gact[:, WIDE : WIDE + STATE] = gb + dot(ginter, cq)
    gact[:, WIDE + STATE :] = gc + dot(ginter, bk, TN)
    gxdt = gact[:, :WIDE] + from_end
    skip = skip_ref[...]
    gact[:, :WIDE] = dt_wide * gxdt + skip * dy
    gskip_ref[...] += jnp.sum(dy * x, 0, keepdims=True)
    sums = head_sums(
        jnp.concatenate([x * gxdt, dy * (mix_ref[0] - skip * x), jnp.broadcast_to(gfinal, (16, WIDE))], 0), expand
    )
    direct = sums[:CHUNK]
    gcum = sums[CHUNK : 2 * CHUNK] - dt * direct
    gld = dot_exact(jnp.where(t >= u, 1.0, 0.0), gcum) + sums[2 * CHUNK : 2 * CHUNK + 1]
    a = a_ref[...]
    gstep = (direct + a * gld) * sg_ref[0]
    gs_ref[0] = low(gstep)
    small_ref[0:1] += jnp.sum(dt * gld, 0, keepdims=True) * a
    small_ref[1:2] += jnp.sum(gstep, 0, keepdims=True)
    pre = pre_ref[0].astype(F32)
    sg = sigmoid(pre)
    gpre = gact[...] * (sg * (1.0 + pre * (1.0 - sg)))
    ext = jnp.concatenate([gpre, after[...]], 0)
    after[...] = gpre[:8]
    conv = cl_ref[0].astype(F32)
    gconv = cw_ref[3:4] * gpre
    gw_ref[3:4] += jnp.sum(conv * gpre, 0, keepdims=True)
    gw_ref[4:5] += jnp.sum(gpre, 0, keepdims=True)
    for ahead in range(1, 4):
        moved = pltpu.roll(ext, CHUNK + 8 - ahead, 0)[:CHUNK]
        gconv = gconv + cw_ref[3 - ahead : 4 - ahead] * moved
        gw_ref[3 - ahead : 4 - ahead] += jnp.sum(conv * moved, 0, keepdims=True)
    gc_ref[0] = low(gconv)

    @pl.when(c == 0)
    def _():
        tail_ref[0] = gconv[CHUNK - 8 :]

    @pl.when(c == chunks - 1)
    def _():
        head_ref[0] = gpre[:8]


def scan_backward(x, bk, cq, dt, sg, cum, cumt, dy, mixed, states, adj_in, pre, conv, skip, a, cw, expand):
    seqs, span, _ = x.shape
    chunks = span // CHUNK
    conv_width = pre.shape[2]

    def row(n):
        return pl.BlockSpec((1, CHUNK, n), lambda s, c: (s, chunks - 1 - c, 0))

    def once(m, n):
        return pl.BlockSpec((m, n), lambda s, c: (0, 0))

    edge = pl.BlockSpec((1, 8, conv_width), lambda s, c: (s, 0, 0))
    return pl.pallas_call(
        functools.partial(scan_back_body, chunks=chunks),
        grid=(seqs, chunks),
        in_specs=[
            row(WIDE), row(STATE), row(STATE), row(128), row(128), row(128),
            pl.BlockSpec((1, 32, CHUNK), lambda s, c: (s, 0, chunks - 1 - c)),
            row(WIDE), row(WIDE),
            pl.BlockSpec((1, 1, STATE, WIDE), lambda s, c: (s, chunks - 1 - c, 0, 0)),
            pl.BlockSpec((1, STATE, WIDE), lambda s, c: (s, 0, 0)),
            row(conv_width), row(conv_width),
            full_spec(skip.shape), full_spec(a.shape), full_spec(cw.shape), full_spec(expand.shape),
        ],
        out_specs=[row(conv_width), row(128), edge, edge, once(8, conv_width), once(1, WIDE), once(8, 128)],
        out_shape=[
            jax.ShapeDtypeStruct((seqs, span, conv_width), BF16),
            jax.ShapeDtypeStruct((seqs, span, 128), BF16),
            jax.ShapeDtypeStruct((seqs, 8, conv_width), F32),
            jax.ShapeDtypeStruct((seqs, 8, conv_width), F32),
            jax.ShapeDtypeStruct((8, conv_width), F32),
            jax.ShapeDtypeStruct((1, WIDE), F32),
            jax.ShapeDtypeStruct((8, 128), F32),
        ],
        scratch_shapes=[
            pltpu.VMEM((STATE, WIDE), F32), pltpu.VMEM((8, conv_width), F32), pltpu.VMEM((CHUNK, conv_width), F32),
        ],
        compiler_params=params(),
        name="scan_backward",
    )(x, bk, cq, dt, sg, cum, cumt, dy, mixed, states, adj_in, pre, conv, skip, a, cw, expand)


def leave_body(
    tok_ref, gmid_ref, gq_ref, gk_ref, gv_ref, gz_ref, gc_ref, gs_ref, gain_ref,
    wq_ref, wk_ref, wv_ref, wz_ref, wc_ref, ws_ref,
    gt_ref, gn_ref,
):
    @pl.when((pl.program_id(0) == 0) & (pl.program_id(1) == 0))
    def _():
        gn_ref[...] = jnp.zeros_like(gn_ref)

    gh = dot(gq_ref[0], wq_ref[...], NT) + dot(gk_ref[0], wk_ref[...], NT) + dot(gv_ref[0], wv_ref[...], NT)
    gh = gh + dot(gz_ref[0], wz_ref[...], NT) + dot(gc_ref[0], wc_ref[...], NT) + dot(gs_ref[0], ws_ref[...], NT)
    v = tok_ref[0].astype(F32)
    scale = lax.rsqrt(jnp.mean(v * v, -1, keepdims=True) + EPS)
    unit = v * scale
    gn_ref[...] += jnp.sum(gh * unit, 0, keepdims=True)
    g = gh * gain_ref[...]
    gt_ref[0] = gmid_ref[0] + scale * (g - unit * jnp.mean(g * unit, -1, keepdims=True))


def leave(tokens, gmid, gq, gk, gv, gz, gc, gs, gain, wq, wk, wv, wz, wc, ws):
    seqs, span, width = tokens.shape
    rows = min(256, span)

    def row(a):
        return pl.BlockSpec((1, rows, a.shape[2]), lambda s, b: (s, b, 0))

    return pl.pallas_call(
        leave_body,
        grid=(seqs, span // rows),
        in_specs=[row(v) for v in (tokens, gmid, gq, gk, gv, gz, gc, gs)]
        + [full_spec(v.shape) for v in (gain, wq, wk, wv, wz, wc, ws)],
        out_specs=[row(tokens), pl.BlockSpec((1, width), lambda s, b: (0, 0))],
        out_shape=[jax.ShapeDtypeStruct((seqs, span, width), F32), jax.ShapeDtypeStruct((1, width), F32)],
        compiler_params=params(),
        name="leave",
    )(tokens, gmid, gq, gk, gv, gz, gc, gs, gain, wq, wk, wv, wz, wc, ws)


def dup_halves(v):
    lane = lax.broadcasted_iota(jnp.int32, v.shape, 1)
    other = pltpu.roll(v, 64, 1)
    return low(jnp.where(lane < 64, v, other)), low(jnp.where(lane < 64, other, v))


def head_rows(ref, rows):
    lane = lax.broadcasted_iota(jnp.int32, (rows, 128), 1)
    heads = []
    for h in range(HEADS):
        t = ref[0, :, (h // 2) * 128 : (h // 2) * 128 + 128]
        heads.append(jnp.where((lane < 64) if h % 2 == 0 else (lane >= 64), t, jnp.zeros_like(t)))
    return heads


def key_range(first, length, rows, keys):
    whole = jnp.minimum((first + 1) // keys, length // keys)
    some = jnp.minimum((first + rows + keys - 1) // keys, (length + keys - 1) // keys)
    return whole, some


def seen(i, first, length, rows, keys):
    key_at = i * keys + lax.broadcasted_iota(jnp.int32, (keys, rows), 0)
    query_at = first + lax.broadcasted_iota(jnp.int32, (keys, rows), 1)
    return (key_at <= query_at) & (key_at < length)


def attend_body(
    pos_ref, len_ref, q_ref, kv_ref, o_ref, lse_ref, kd, vt, top, acc, score_a, score_b, top_a, top_b,
    *, rows, keys, total, prep,
):
    s = pl.program_id(0)
    b = pl.program_id(1)

    @pl.when(b == 0)
    def _():
        def one(i, _):
            at = pl.ds(pl.multiple_of(i * prep, prep), prep)
            kd[0, at, :], kd[1, at, :] = dup_halves(kv_ref[0, at, :128].astype(F32))
            t = kv_ref[0, at, 128:].astype(F32).T
            ones = jnp.ones((16, prep), F32)
            vt[0, :, at] = low(jnp.concatenate([t[:64], ones], 0))
            vt[1, :, at] = low(jnp.concatenate([t[64:], ones], 0))
            return 0

        lax.fori_loop(0, total // prep, one, 0)

    first = pos_ref[b]
    length = len_ref[s]
    heads = head_rows(q_ref, rows)
    top[...] = jnp.full_like(top, LOWEST)
    acc[...] = jnp.zeros_like(acc)
    whole, some = key_range(first, length, rows, keys)

    def scores(i, buffer, tops, h, mask=None):
        at = pl.ds(pl.multiple_of(i * keys, keys), keys)
        t = dot(kd[h // 4, at, :], heads[h], NT)
        if mask is not None:
            t = jnp.where(mask, t, LOWEST)
        buffer[h] = t
        tops[h] = jnp.max(t, 0, keepdims=True)

    def add(i, buffer, tops, h):
        at = pl.ds(pl.multiple_of(i * keys, keys), keys)
        before = top[h]
        now = jnp.maximum(before, tops[h])
        p = low(jnp.exp2((buffer[h] - now) * SCORE2))
        acc[h] = acc[h] * jnp.exp2((before - now) * SCORE2) + dot(vt[h // 4, :, at], p)
        top[h] = now

    def edge(i, _):
        mask = seen(i, first, length, rows, keys)
        for h in range(HEADS):
            scores(i, score_a, top_a, h, mask)
        for h in range(HEADS):
            add(i, score_a, top_a, h)
        return 0

    lax.fori_loop(whole, some, edge, 0)
    last = jnp.maximum(whole - 1, 0)
    for h in range(HEADS):
        scores(0, score_a, top_a, h)

    def two(i, _):
        for h in range(HEADS):
            scores(2 * i + 1, score_b, top_b, h)
            add(2 * i, score_a, top_a, h)
        following = jnp.minimum(2 * i + 2, last)
        for h in range(HEADS):
            scores(following, score_a, top_a, h)
            add(2 * i + 1, score_b, top_b, h)
        return 0

    lax.fori_loop(0, whole // 2, two, 0)

    @pl.when(whole % 2 == 1)
    def _():
        for h in range(HEADS):
            add(last, score_a, top_a, h)

    outs = []
    for h in range(HEADS):
        t = acc[h]
        weight = t[64:65]
        outs.append(t[:64] / weight)
        lse_ref[0, h : h + 1, :] = top[h] * SCORE2 + jnp.log2(weight)
    for g in range(HEADS // 2):
        o_ref[0, :, g * 128 : g * 128 + 128] = low(jnp.concatenate(outs[2 * g : 2 * g + 2], 0).T)


def attend(pos, lens, q, kv):
    seqs, span, _ = q.shape
    total = kv.shape[1]
    rows = min(256, span)
    keys = 256
    blocks = span // rows
    return pl.pallas_call(
        functools.partial(attend_body, rows=rows, keys=keys, total=total, prep=512),
        grid_spec=pltpu.PrefetchScalarGridSpec(
            num_scalar_prefetch=2,
            grid=(seqs, blocks),
            in_specs=[
                pl.BlockSpec((1, rows, 512), lambda s, b, *_: (s, b, 0)),
                pl.BlockSpec((1, total, 256), lambda s, b, *_: (s, 0, 0)),
            ],
            out_specs=[
                pl.BlockSpec((1, rows, 512), lambda s, b, *_: (s, b, 0)),
                pl.BlockSpec((1, 8, rows), lambda s, b, *_: (s, 0, b)),
            ],
            scratch_shapes=[
                pltpu.VMEM((2, total, 128), BF16), pltpu.VMEM((2, 80, total), BF16),
                pltpu.VMEM((8, 1, rows), F32), pltpu.VMEM((8, 80, rows), F32),
                pltpu.VMEM((8, keys, rows), F32), pltpu.VMEM((8, keys, rows), F32),
                pltpu.VMEM((8, 1, rows), F32), pltpu.VMEM((8, 1, rows), F32),
            ],
        ),
        out_shape=[
            jax.ShapeDtypeStruct((seqs, span, 512), BF16),
            jax.ShapeDtypeStruct((seqs, 8, span), F32),
        ],
        compiler_params=params(),
        name="attend",
    )(pos, lens, q, kv)


def attend_back_body(
    pos_ref, len_ref, q_ref, do_ref, lse_ref, delta_ref, cos_ref, sin_ref, kv_ref, dq_ref, dkv_ref,
    kd, vd, kt, dk, dv, dq, *, rows, keys, total, blocks, prep,
):
    s = pl.program_id(0)
    b = pl.program_id(1)

    @pl.when(b == 0)
    def _():
        def one(i, _):
            at = pl.ds(pl.multiple_of(i * prep, prep), prep)
            k = kv_ref[0, at, :128].astype(F32)
            kd[0, at, :], kd[1, at, :] = dup_halves(k)
            vd[0, at, :], vd[1, at, :] = dup_halves(kv_ref[0, at, 128:].astype(F32))
            kt[:, at] = low(k.T)
            return 0

        lax.fori_loop(0, total // prep, one, 0)
        dk[...] = jnp.zeros_like(dk)
        dv[...] = jnp.zeros_like(dv)

    first = pos_ref[b]
    length = len_ref[s]
    heads = head_rows(q_ref, rows)
    grads = head_rows(do_ref, rows)
    dq[...] = jnp.zeros_like(dq)
    whole, some = key_range(first, length, rows, keys)

    def step(i, masked):
        at = pl.ds(pl.multiple_of(i * keys, keys), keys)
        mask = seen(i, first, length, rows, keys) if masked else None
        for j in range(KV_HEADS):
            dv_sum = dk_sum = None
            for h in range(4 * j, 4 * j + 4):
                x = dot(kd[j, at, :], heads[h], NT) * SCORE2 - lse_ref[0, h : h + 1, :]
                dp = dot(vd[j, at, :], grads[h], NT)
                if masked:
                    x = jnp.where(mask, x, LOWEST)
                p = jnp.exp2(x)
                ds = low(p * (dp - delta_ref[0, h : h + 1, :]))
                dv_part = dot(low(p), grads[h])
                dk_part = dot(ds, heads[h])
                dv_sum = dv_part if dv_sum is None else dv_sum + dv_part
                dk_sum = dk_part if dk_sum is None else dk_sum + dk_part
                dq[h] += dot(kt[64 * j : 64 * j + 64, at], ds)
            dv[j, at, :] += dv_sum
            dk[j, at, :] += dk_sum

    lax.fori_loop(0, whole, lambda i, _: (step(i, False), 0)[1], 0)
    lax.fori_loop(whole, some, lambda i, _: (step(i, True), 0)[1], 0)
    cosine, sine = cos_ref[...], sin_ref[...]
    for g in range(HEADS // 2):
        parts = []
        for h in (2 * g, 2 * g + 1):
            t = dq[h] * 0.125
            former, latter = t[:32], t[32:]
            parts += [former * cosine + latter * sine, latter * cosine - former * sine]
        dq_ref[0, :, g * 128 : g * 128 + 128] = low(jnp.concatenate(parts, 0).T)

    @pl.when(b == blocks - 1)
    def _():
        def one(i, _):
            at = pl.ds(pl.multiple_of(i * prep, prep), prep)
            lane = lax.broadcasted_iota(jnp.int32, (prep, 128), 1)
            for source, columns, scale in ((dk, slice(0, 128), 0.125), (dv, slice(128, 256), 1.0)):
                pair = [source[j, at, :] for j in range(2)]
                pair = [t + pltpu.roll(t, 64, 1) for t in pair]
                dkv_ref[0, at, columns] = low(jnp.where(lane < 64, pair[0], pair[1]) * scale)
            return 0

        lax.fori_loop(0, total // prep, one, 0)


def attend_backward(pos, lens, q, do, lse, delta, cosine, sine, kv):
    seqs, span, _ = q.shape
    total = kv.shape[1]
    rows = min(256, span)
    keys = 512
    blocks = span // rows
    row = pl.BlockSpec((1, rows, 512), lambda s, b, *_: (s, b, 0))
    stat = pl.BlockSpec((1, 8, rows), lambda s, b, *_: (s, 0, b))
    table = pl.BlockSpec((32, rows), lambda s, b, *_: (0, b))
    every = pl.BlockSpec((1, total, 256), lambda s, b, *_: (s, 0, 0))
    return pl.pallas_call(
        functools.partial(attend_back_body, rows=rows, keys=keys, total=total, blocks=blocks, prep=512),
        grid_spec=pltpu.PrefetchScalarGridSpec(
            num_scalar_prefetch=2,
            grid=(seqs, blocks),
            in_specs=[row, row, stat, stat, table, table, every],
            out_specs=[row, every],
            scratch_shapes=[
                pltpu.VMEM((2, total, 128), BF16), pltpu.VMEM((2, total, 128), BF16), pltpu.VMEM((128, total), BF16),
                pltpu.VMEM((2, total, 128), F32), pltpu.VMEM((2, total, 128), F32), pltpu.VMEM((8, 64, rows), F32),
            ],
        ),
        out_shape=[
            jax.ShapeDtypeStruct((seqs, span, 512), BF16),
            jax.ShapeDtypeStruct((seqs, total, 256), BF16),
        ],
        compiler_params=params(),
        name="attend_backward",
    )(pos, lens, q, do, lse, delta, cosine, sine, kv)


def from_behind(value, axis, steps):
    count = lax.axis_size(axis)
    initial, last = (max(0, -steps), min(count, count - steps))
    return lax.ppermute(value, axis, [(source, source + steps) for source in range(initial, last)])


def weight_grad(left, grad):
    return low(jnp.einsum("sck,scm->km", left, grad, preferred_element_type=F32))


def joined(states, totals, between, taken):
    logs = jnp.einsum("ij,jsh->ish", between.astype(F32), totals, precision=lax.Precision.HIGHEST)
    weights = jnp.where(taken[:, None, None], jnp.exp2(logs), 0.0)[..., :SSM_HEADS]
    weights = jnp.repeat(weights, SSM_HEAD, -1)[:, :, None, :]
    return jnp.sum(states.astype(F32) * weights, 0)


def on_device(
    tokens, cotangent, lengths, norm_one, w_query, w_key, w_value, w_gatez, w_conv_in, w_step, conv_weight,
    conv_bias, step_bias, decay_log, skip_gain, gated_gain, w_attn_out, w_mix_out, norm_two, w_gate, w_up, w_down,
):
    seqs, span, width = tokens.shape
    taps = conv_weight.shape[0]
    count = lax.axis_size("seq")
    place = lax.axis_index("seq")
    first = place * span
    positions = first + jnp.arange(span)
    inverse = 1.0 / ROPE_BASE ** (jnp.arange(0, HEAD, 2).astype(F32) / HEAD)
    angles = positions.astype(F32)[:, None] * inverse[None, :]
    cosine, sine = jnp.cos(angles), jnp.sin(angles)
    cos_row = jnp.concatenate([cosine] * 4, 1)
    sin_row = jnp.concatenate([-sine, sine] * 2, 1)
    rate = -jnp.exp(decay_log)
    pad = (0, 128 - SSM_HEADS)
    rate_row = jnp.pad(rate, pad)[None]
    step_row = jnp.pad(step_bias, pad)[None]
    w_step_wide = jnp.pad(w_step, ((0, 0), pad))
    skip_row = jnp.repeat(skip_gain, SSM_HEAD)[None]
    ones = (np.arange(WIDE)[None, :] // SSM_HEAD == np.arange(128)[:, None]).astype(np.float32)
    expand = jnp.asarray(np.concatenate([ones, ones], 0), BF16)
    pos = first[None].astype(jnp.int32)
    blocks = first + jnp.arange(0, span, min(256, span), dtype=jnp.int32)

    halo = from_behind(tokens[:, span - 16 :], "seq", 1)
    (hidden, q, kv, z, conv, pre, x, bk, cq, dt, sg, cum, cumt, state, total) = enter(
        pos, lengths, tokens, halo, norm_one[None], w_query, w_key, w_value, w_gatez, w_conv_in, w_step_wide,
        conv_weight, conv_bias[None], step_row, rate_row * LOG2E, cos_row, sin_row, expand,
    )
    kv_all = lax.all_gather(kv, "seq", axis=1, tiled=True)
    states = lax.all_gather(state, "seq")
    totals = lax.all_gather(total[:, 0], "seq")
    i = jnp.arange(count)
    state_in = joined(states, totals, (i[None, :] > i[:, None]) & (i[None, :] < place), i < place)
    mixed, mix_low, held = scan_forward(
        x, bk, cq, dt, cum, cumt, state_in, skip_row, z, gated_gain[None], expand
    )
    attn, lse = attend(blocks, lengths, q, kv_all)
    (
        output, hidden_two, act, grad_ffn, grad_gate, grad_up, grad_mid, grad_branch, grad_attn, grad_mixed,
        grad_z, delta, g_norm_two, g_gated, adjoint,
    ) = middle(
        pos, lengths, attn, mix_low, tokens, cotangent, mixed, z, cq, cum, w_attn_out, w_mix_out, w_gate, w_up,
        w_down, norm_two[None], gated_gain[None], expand,
    )
    adjoints = lax.all_gather(adjoint, "seq")
    g_down = weight_grad(act, grad_ffn)
    g_gate = weight_grad(hidden_two, grad_gate)
    g_up = weight_grad(hidden_two, grad_up)
    g_attn_out = weight_grad(attn, grad_branch)
    g_mix_out = weight_grad(mix_low, grad_branch)
    grad_q, grad_kv = attend_backward(blocks, lengths, q, grad_attn, lse, delta, cosine.T, sine.T, kv_all)
    grad_kv = lax.psum_scatter(grad_kv, "seq", scatter_dimension=1, tiled=True)
    adjoint_in = joined(adjoints, totals, (i[None, :] < i[:, None]) & (i[None, :] > place), i > place)
    grad_conv, grad_step, tail, head, g_conv_small, g_skip, g_small = scan_backward(
        x, bk, cq, dt, sg, cum, cumt, grad_mixed, mixed, held, adjoint_in, pre, conv, skip_row, rate_row,
        conv_weight, expand,
    )
    returned = from_behind(low(head), "seq", -1).astype(F32)[:, : taps - 1]
    g_conv_weight = g_conv_small[:taps]
    for ahead in range(1, taps):
        tap = taps - 1 - ahead
        rows = jnp.pad(returned[:, :ahead], ((0, 0), (8 - ahead, 0), (0, 0)))
        tail = tail + conv_weight[tap] * rows
        g_conv_weight = g_conv_weight.at[tap].add(jnp.sum(rows * conv[:, span - 8 :].astype(F32), (0, 1)))
    grad_conv = lax.dynamic_update_slice(grad_conv, low(tail), (0, span - 8, 0))
    grad_key = grad_kv[:, :, :128].astype(F32).reshape(seqs, span, KV_HEADS, 2, HEAD // 2)
    c4, s4 = cosine[None, :, None, :], sine[None, :, None, :]
    former, latter = grad_key[:, :, :, 0], grad_key[:, :, :, 1]
    grad_key = jnp.concatenate([former * c4 + latter * s4, latter * c4 - former * s4], -1)
    grad_key = low(grad_key.reshape(seqs, span, 128))
    grad_value = grad_kv[:, :, 128:]
    grad_tokens, g_norm_one = leave(
        tokens, grad_mid, grad_q, grad_key, grad_value, grad_z, grad_conv, grad_step, norm_one[None],
        w_query, w_key, w_value, w_gatez, w_conv_in, w_step_wide,
    )
    g_query = weight_grad(hidden, grad_q)
    g_key = weight_grad(hidden, grad_key)
    g_value = weight_grad(hidden, grad_value)
    g_gatez = weight_grad(hidden, grad_z)
    g_conv_in = weight_grad(hidden, grad_conv)
    g_step = weight_grad(hidden, grad_step)

    def reduced(g):
        part = lax.psum_scatter(g, "seq", scatter_dimension=0, tiled=True)
        return lax.psum(part, "dp").astype(F32)

    small = [
        g_norm_one[0], g_norm_two[0], g_gated[0], g_conv_weight.reshape(-1), g_conv_small[taps], g_skip[0],
        g_small[0], g_small[1],
    ]
    sizes = [v.shape[0] for v in small]
    flat = lax.psum(jnp.concatenate(small), ("dp", "seq"))
    starts = np.cumsum([0] + sizes)
    small = [flat[a:b] for a, b in zip(starts[:-1], starts[1:])]

    def mine(v):
        n = v.shape[0] // count
        return lax.dynamic_slice(v, (place * n,), (n,))

    s_norm_one, s_norm_two, s_gated = [mine(v) for v in small[:3]]
    s_skip = jnp.sum(small[5].reshape(SSM_HEADS, SSM_HEAD), 1)
    return (
        output,
        grad_tokens,
        s_norm_one,
        reduced(g_query),
        reduced(g_key),
        reduced(g_value),
        reduced(g_gatez),
        reduced(g_conv_in),
        reduced(g_step)[:, :SSM_HEADS],
        small[3].reshape(taps, -1),
        small[4],
        small[7][:SSM_HEADS],
        small[6][:SSM_HEADS],
        s_skip,
        s_gated,
        reduced(g_attn_out),
        reduced(g_mix_out),
        s_norm_two,
        reduced(g_gate),
        reduced(g_up),
        reduced(g_down),
    )


def solution(mesh):
    copied = (P(),) * 19
    return jax.shard_map(
        on_device,
        mesh=mesh,
        in_specs=(P("dp", "seq", None), P("dp", "seq", None), P("dp")) + copied,
        out_specs=(
            P("dp", "seq", None), P("dp", "seq", None), P("seq"),
            P("seq", None), P("seq", None), P("seq", None), P("seq", None), P("seq", None), P("seq", None),
            P(), P(), P(), P(), P(),
            P("seq"), P("seq", None), P("seq", None), P("seq"), P("seq", None), P("seq", None), P("seq", None),
        ),
        check_vma=False,
    )
```

time: 1400 us -> 990 us (0.71)
  matrix products: 909 us -> 65.1 us
  waiting for transfers between devices: 73.9 us -> 601 us
  Pallas kernels: 0 us -> 197 us
  other arithmetic: 197 us -> 33.6 us
  local copies, waits for them, and re-layouts: 104 us -> 15.1 us
  blocking collectives: 85.1 us -> 47.5 us
    dot_general x54 -> x13, matrix products: 909 us -> 65.1 us  [the longest x11 64.8 us: weight_grad(): jnp.einsum('sck,scm->km', left, grad, preferred_element_type=F32)]
    reduce_scatter x13 -> x12, waiting for transfers between devices: 0.15 us -> 456 us  [the longest x11 392 us: reduced(): part = lax.psum_scatter(g, 'seq', scatter_dimension=0, tiled=True)]
    pallas_call x0 -> x7, Pallas kernels: none -> 197 us  [the longest x1 58.8 us: middle(): pl.pallas_call(functools.partial(middle_body, rows=rows, blocks=blocks, s...]
    reduce_sum x9 -> x4, other arithmetic: 83.6 us -> 6.82 us  [the longest x2 5.37 us: joined(): return jnp.sum(states.astype(F32) * weights, 0)]
    all_gather x4 -> x3, waiting for transfers between devices: 0.06 us -> 63.4 us  [the longest x1 22.2 us: on_device(): adjoints = lax.all_gather(adjoint, 'seq')]
    unnamed x260 -> x47, local copies, waits for them, and re-layouts: 40 us -> 4.37 us
    another operation x7 -> x1, other arithmetic: 32.8 us -> 0.07 us
    psum x2 -> x1, blocking collectives: 70.1 us -> 41.4 us  [on_device(): flat = lax.psum(jnp.concatenate(small), ('dp', 'seq'))]
  transfers between devices with their start and end apart: 20 -> 18, of which waited for: 2 -> 15; matrix products, arithmetic and copies ran while one was open for 65% -> 9% of each run, Pallas kernels for 0% -> 10%
where the time goes in v1:
time: 990 us; the launch traced here: 982 us
  waiting for transfers between devices  601 us (61%)
  Pallas kernels  197 us (20%)
  matrix products  65.1 us (7%)
  blocking collectives  47.5 us (5%)
  other arithmetic  33.6 us (3%)
  between operations  15.4 us (2%)
  local copies, waits for them, and re-layouts  15.1 us (2%)
    reduce_scatter x11, waiting for transfers between devices, reduced(): part = lax.psum_scatter(g, 'seq', scatter_dimension=0, tiled=True)  392 us
    psum x1, waiting for transfers between devices, reduced(): return lax.psum(part, 'dp').astype(F32)  77.8 us
    dot_general x11, matrix products, weight_grad(): jnp.einsum('sck,scm->km', left, grad, preferred_element_type=F32)  64.8 us
    reduce_scatter x1, waiting for transfers between devices, on_device(): grad_kv = lax.psum_scatter(grad_kv, 'seq', scatter_dimension=1, tiled=True)  63.8 us
    pallas_call x1, Pallas kernels, middle(): pl.pallas_call(functools.partial(middle_body, rows=rows, blocks=blocks, s...  58.8 us
    psum x1, blocking collectives, on_device(): flat = lax.psum(jnp.concatenate(small), ('dp', 'seq'))  41.4 us
    pallas_call x1, Pallas kernels, scan_backward(): pl.pallas_call(functools.partial(scan_back_body, chunks=chunks), grid=(se...  35.3 us
    pallas_call x1, Pallas kernels, attend_backward(): pl.pallas_call(functools.partial(attend_back_body, rows=rows, keys=keys,...  28.6 us
  transfers between devices with their start and end apart: 18, of which 15 were waited for; matrix products, arithmetic and copies ran while one was open for 9% of the time, Pallas kernels for 10%

profile of v1, /device:TPU:1, one launch (start us, length us, event | category | flops | bytes accessed | tf_op | source)
XLA Modules:
  0.0 981.5 jit_solution(14352138831348478949)
XLA Ops:
  19.8 26.3 %enter.1 = (bf16[1,1024,1024]{2,1,0:T(8,128)(2,1)}, bf16[1,1024,512]{2,1,0:T(8,128)(2,1)}, bf16[1,1024,256]{2,1,0:T(8,128)(2,1)}, bf16[1,1024,1536]{2,1,0:T(8,12...) custom-call(s32[1]{0:T(128)} %bitcast.pos_ref, ...), custom_call_target="tpu_custom_call" | custom-call | tf_op jit(solution)/shard_map/enter/pallas_call | solution.py:180
  56.0 22.0 %all-gather.8.cloned.1.call-done = bf16[4,128,1536]{2,1,0:T(8,128)(2,1)} async-done(((bf16[1,128,1536]{2,1,0:T(8,128)(2,1)}), bf16[4,128,1536]{2,1,0:T(8,128)(2,1)}) %all-gather.8.cloned.1.call-update) | async-done | bytes 1572880 | tf_op jit(solution)/shard_map/all_gather | solution.py:909
  80.7 15.8 %scan_forward.1 = (f32[1,1024,1536]{2,1,0:T(8,128)}, bf16[1,1024,1536]{2,1,0:T(8,128)(2,1)}, bf16[1,8,128,1536]{3,2,1,0:T(8,128)(2,1)}) custom-call(bf16[1,1024,1536]{2,1,0:T(8,128)(2,1)} %get-tuple-element.106.x_ref, bf16[1,1024,128]{2,1,0:T(8,128)(2,1)} %get-tuple-element.107.bk_ref, bf16[1,1024,128]{2,1,0:T(8,128)(2,1)} %get-tuple-element.108.cq_ref, ...), custom_call_target="tpu_custom_call" | custom-call | tf_op jit(solution)/shard_map/scan_forward/pallas_call | solution.py:264
  96.5 19.3 %all-gather.6.cloned.1.call-done.kv_ref = bf16[1,4096,256]{2,1,0:T(8,128)(2,1)} async-done(((bf16[1,1024,256]{2,1,0:T(8,128)(2,1)}), bf16[1,4096,256]{2,1,0:T(8,128)(2,1)}) %all-gather.6.cloned.1.call-update) | async-done | bytes 2097168 | tf_op jit(solution)/shard_map/all_gather | solution.py:908
  115.7 14.1 %attend.1 = (bf16[1,1024,512]{2,1,0:T(8,128)(2,1)}, f32[1,8,1024]{2,1,0:T(8,128)}) custom-call(s32[4]{0:T(128)} %multiply_add_fusion.pos_ref, s32[1]{0:T(128)S(6)} %copy.107.len_ref, bf16[1,1024,512]{2,1,0:T(8,128)(2,1)} %get-tuple-element.103.q_ref, bf16[1,4096,256]{2,1,0:T(8,128)(2,1)} %all-gather.6.cloned.1.call-done.kv_ref), custom_call_target="tpu_custom_call" | custom-call | tf_op jit(solution)/shard_map/attend/pallas_call | solution.py:727
  129.9 58.8 %middle.1 = (bf16[1,1024,1024]{2,1,0:T(8,128)(2,1)}, bf16[1,1024,1024]{2,1,0:T(8,128)(2,1)}, bf16[1,1024,2048]{2,1,0:T(8,128)(2,1)}, bf16[1,1024,1024]{2,1,0:T(8...) custom-call(s32[1]{0:T(128)} %bitcast.pos_ref, ...), custom_call_target="tpu_custom_call" | custom-call | tf_op jit(solution)/shard_map/middle/pallas_call | solution.py:392
  190.0 28.6 %attend_backward.1 = (bf16[1,1024,512]{2,1,0:T(8,128)(2,1)}, bf16[1,4096,256]{2,1,0:T(8,128)(2,1)}) custom-call(s32[4]{0:T(128)} %multiply_add_fusion.pos_ref, s32[1]{0:T(128)S(6)} %copy.107.len_ref, bf16[1,1024,512]{2,1,0:T(8,128)(2,1)} %get-tuple-element.103.q_ref, bf16[1,1024,512]{2,1,0:T(8,128)(2,1)} %get-tuple-element.119.do_ref, ...), custom_call_target="tpu_custom_call" | custom-call | tf_op jit(solution)/shard_map/attend_backward/pallas_call | solution.py:839
  227.3 22.2 %all-gather.10.cloned.1.call-done = bf16[4,128,1536]{2,1,0:T(8,128)(2,1)} async-done(((bf16[1,128,1536]{2,1,0:T(8,128)(2,1)}), bf16[4,128,1536]{2,1,0:T(8,128)(2,1)}) %all-gather.10.cloned.1.call-update) | async-done | bytes 1572880 | tf_op jit(solution)/shard_map/all_gather | solution.py:924
  252.2 35.3 %scan_backward.1 = (bf16[1,1024,1792]{2,1,0:T(8,128)(2,1)}, bf16[1,1024,128]{2,1,0:T(8,128)(2,1)}, f32[1,8,1792]{2,1,0:T(8,128)}, f32[1,8,1792]{2,1,0:T(8,128)},...) custom-call(bf16[1,1024,1536]{2,1,0:T(8,128)(2,1)} %get-tuple-element.106.x_ref, ...), custom_call_target="tpu_custom_call" | custom-call | tf_op jit(solution)/shard_map/scan_backward/pallas_call | solution.py:543
  290.1 63.8 %reduce-scatter.13.cloned.1.call-done = bf16[1,1024,256]{2,1,0:T(8,128)(2,1)} async-done(((bf16[1,4096,256]{2,1,0:T(8,128)(2,1)}), bf16[1,1024,256]{2,1,0:T(8,128)(2,1)}) %reduce-scatter.13.cloned.1.call-update) | async-done | bytes 524304 | tf_op jit(solution)/shard_map/reduce_scatter | solution.py:931
  384.4 9.4 fusion.6
  394.1 9.7 fusion.12
  419.3 23.6 %reduce-scatter.25.cloned.1.call-done = bf16[256,128]{1,0:T(8,128)(2,1)} async-done(((bf16[1024,128]{1,0:T(8,128)(2,1)}), bf16[256,128]{1,0:T(8,128)(2,1)}) %reduce-scatter.25.cloned.1.call-update) | async-done | bytes 65552 | tf_op jit(solution)/shard_map/reduce_scatter | solution.py:963
  443.0 27.4 %reduce-scatter.19.cloned.1.call-done = bf16[256,128]{1,0:T(8,128)(2,1)} async-done(((bf16[1024,128]{1,0:T(8,128)(2,1)}), bf16[256,128]{1,0:T(8,128)(2,1)}) %reduce-scatter.19.cloned.1.call-update) | async-done | bytes 65552 | tf_op jit(solution)/shard_map/reduce_scatter | solution.py:963
  470.4 27.7 %reduce-scatter.17.cloned.1.call-done = bf16[256,128]{1,0:T(8,128)(2,1)} async-done(((bf16[1024,128]{1,0:T(8,128)(2,1)}), bf16[256,128]{1,0:T(8,128)(2,1)}) %reduce-scatter.17.cloned.1.call-update) | async-done | bytes 65552 | tf_op jit(solution)/shard_map/reduce_scatter | solution.py:963
  498.1 47.3 %reduce-scatter.29.cloned.1.call-done = bf16[384,1024]{1,0:T(8,128)(2,1)} async-done(((bf16[1536,1024]{1,0:T(8,128)(2,1)}), bf16[384,1024]{1,0:T(8,128)(2,1)}) %reduce-scatter.29.cloned.1.call-update) | async-done | bytes 786448 | tf_op jit(solution)/shard_map/reduce_scatter | solution.py:963
  545.4 47.0 %reduce-scatter.21.cloned.1.call-done = bf16[256,1536]{1,0:T(8,128)(2,1)} async-done(((bf16[1024,1536]{1,0:T(8,128)(2,1)}), bf16[256,1536]{1,0:T(8,128)(2,1)}) %reduce-scatter.21.cloned.1.call-update) | async-done | bytes 786448 | tf_op jit(solution)/shard_map/reduce_scatter | solution.py:963
  592.3 55.5 %reduce-scatter.33.cloned.1.call-done = bf16[256,2048]{1,0:T(8,128)(2,1)} async-done(((bf16[1024,2048]{1,0:T(8,128)(2,1)}), bf16[256,2048]{1,0:T(8,128)(2,1)}) %reduce-scatter.33.cloned.1.call-update) | async-done | bytes 1048592 | tf_op jit(solution)/shard_map/reduce_scatter | solution.py:963
  647.9 56.0 %reduce-scatter.31.cloned.1.call-done = bf16[256,2048]{1,0:T(8,128)(2,1)} async-done(((bf16[1024,2048]{1,0:T(8,128)(2,1)}), bf16[256,2048]{1,0:T(8,128)(2,1)}) %reduce-scatter.31.cloned.1.call-update) | async-done | bytes 1048592 | tf_op jit(solution)/shard_map/reduce_scatter | solution.py:963
  703.8 55.5 %reduce-scatter.35.cloned.1.call-done = bf16[512,1024]{1,0:T(8,128)(2,1)} async-done(((bf16[2048,1024]{1,0:T(8,128)(2,1)}), bf16[512,1024]{1,0:T(8,128)(2,1)}) %reduce-scatter.35.cloned.1.call-update) | async-done | bytes 1048592 | tf_op jit(solution)/shard_map/reduce_scatter | solution.py:963
  759.4 52.0 %reduce-scatter.23.cloned.1.call-done = bf16[256,1792]{1,0:T(8,128)(2,1)} async-done(((bf16[1024,1792]{1,0:T(8,128)(2,1)}), bf16[256,1792]{1,0:T(8,128)(2,1)}) %reduce-scatter.23.cloned.1.call-update) | async-done | bytes 917520 | tf_op jit(solution)/shard_map/reduce_scatter | solution.py:963
  812.8 17.9 %leave.1 = (f32[1,1024,1024]{2,1,0:T(8,128)}, f32[1,1024]{1,0:T(1,128)}) custom-call(bf16[1,1024,1024]{2,1,0:T(8,128)(2,1)} %tok_ref.5, f32[1,1024,1024]{2,1,0:T(8,128)} %get-tuple-element.118.gmid_ref, bf16[1,1024,512]{2,1,0:T(8,128)(2,1)} %get-tuple-element.122.gq_ref, bf16[1,1024,128]{2,1,0:T(8,128)(2,1)} %copy.80.gk_ref, ...), custom_call_target="tpu_custom_call" | custom-call | tf_op jit(solution)/shard_map/leave/pallas_call | solution.py:599
  832.8 41.4 %psum.84 = f32[14336]{0:T(1024)S(1)} all-reduce(f32[14336]{0:T(1024)S(1)} %constant_dynamic-update-slice_fusion), channel_id=1, replica_groups=mesh['dp'=8,'seq'=4] {'dp','seq'}, use_global_device_ids=true, to_apply=%region_6.7 | all-reduce | flops 14336 | bytes 114688 | tf_op jit(solution)/shard_map/psum | solution.py:971
  878.6 77.8 %all-reduce.9.cloned.1.call-done = (bf16[256,512]{1,0:T(8,128)(2,1)}, bf16[256,128]{1,0:T(8,128)(2,1)}, bf16[256,128]{1,0:T(8,128)(2,1)}, bf16[256,1536]{1,0:T(8...) async-done(((bf16[256,512]{1,0:T(8,128)(2,1)}, ...) | async-done | bytes 6357008 | tf_op jit(solution)/shard_map/psum | solution.py:964
  (170 shorter events, 111.5 us)
Async XLA Ops:
  7.2 10.4 %copy-start.13 = (f32[1792]{0:T(1024)S(1)}, f32[1792]{0:T(1024)}, u32[]{:S(2)}) copy-start(f32[1792]{0:T(1024)} %param.40) | copy-start | bytes 21508
  7.2 11.0 %copy-start.9 = (bf16[1024,24]{0,1:T(8,128)(2,1)S(1)}, bf16[1024,24]{0,1:T(8,128)(2,1)}, u32[]{:S(2)}) copy-start(bf16[1024,24]{0,1:T(8,128)(2,1)} %param.38) | copy-start | bytes 147460
  7.2 70.7 %all-gather.8.cloned.1.call-start = ((), (), s32[]{:S(2)}) async-start(), calls=%async_computation.25 | async-start | bytes 1966080 | tf_op jit(solution)/shard_map/all_gather | solution.py:909
  8.0 11.1 %collective-permute-start = (bf16[1,16,1024]{2,1,0:T(8,128)(2,1)S(1)}, bf16[1,16,1024]{2,1,0:T(8,128)(2,1)S(1)}, u32[]{:S(2)}, u32[]{:S(2)}) collective-permute-start(bf16[1,16,1024]{2,1,0:T(8,128)(2,1)S(1)} %slice.169), channel_id=1, source_target_pairs={{0,1},{1,2},{2,3},{4,5},{5,6},{6,7},{8,9},{9,10},{10,11},{12,13},{... | collective-permute-start | bytes 98312 | tf_op jit(solution)/shard_map/ppermute | solution.py:863
  19.8 27.2 %copy-start.12 = (f32[1536]{0:T(1024)S(1)}, f32[1536]{0:T(1024)}, u32[]{:S(2)}) copy-start(f32[1536]{0:T(1024)} %param.44) | copy-start | bytes 18436
  19.8 27.8 %copy-start.18 = (f32[24]{0:T(128)S(1)}, f32[24]{0:T(128)}, u32[]{:S(2)}) copy-start(f32[24]{0:T(128)} %param.43) | copy-start | bytes 292
  46.1 69.6 %all-gather.6.cloned.1.call-start = ((), (), s32[]{:S(2)}) async-start(), calls=%async_computation.12 | async-start | bytes 2621440 | tf_op jit(solution)/shard_map/all_gather | solution.py:908
  46.9 202.6 %all-gather.10.cloned.1.call-start = ((), (), s32[]{:S(2)}) async-start(), calls=%async_computation.26 | async-start | bytes 1966080 | tf_op jit(solution)/shard_map/all_gather | solution.py:924
  188.7 165.1 %reduce-scatter.13.cloned.1.call-start = ((), (), s32[]{:S(2)}) async-start(), calls=%async_computation.13 | async-start | bytes 2621440 | tf_op jit(solution)/shard_map/reduce_scatter | solution.py:931
  218.7 200.6 %reduce-scatter.27.cloned.1.call-start = ((), (), s32[]{:S(2)}) async-start(), calls=%async_computation.20 | async-start | bytes 1310720 | tf_op jit(solution)/shard_map/reduce_scatter | solution.py:963
  223.1 196.3 %reduce-scatter.15.cloned.1.call-start = ((), (), s32[]{:S(2)}) async-start(), calls=%async_computation.14 | async-start | bytes 1310720 | tf_op jit(solution)/shard_map/reduce_scatter | solution.py:963
  226.6 216.3 %reduce-scatter.25.cloned.1.call-start = ((), (), s32[]{:S(2)}) async-start(), calls=%async_computation.19 | async-start | bytes 327680 | tf_op jit(solution)/shard_map/reduce_scatter | solution.py:963
  290.0 180.4 %reduce-scatter.19.cloned.1.call-start = ((), (), s32[]{:S(2)}) async-start(), calls=%async_computation.16 | async-start | bytes 327680 | tf_op jit(solution)/shard_map/reduce_scatter | solution.py:963
  358.3 139.8 %reduce-scatter.17.cloned.1.call-start = ((), (), s32[]{:S(2)}) async-start(), calls=%async_computation.15 | async-start | bytes 327680 | tf_op jit(solution)/shard_map/reduce_scatter | solution.py:963
  359.9 185.4 %reduce-scatter.29.cloned.1.call-start = ((), (), s32[]{:S(2)}) async-start(), calls=%async_computation.21 | async-start | bytes 3932160 | tf_op jit(solution)/shard_map/reduce_scatter | solution.py:963
  367.7 224.6 %reduce-scatter.21.cloned.1.call-start = ((), (), s32[]{:S(2)}) async-start(), calls=%async_computation.17 | async-start | bytes 3932160 | tf_op jit(solution)/shard_map/reduce_scatter | solution.py:963
  374.7 273.2 %reduce-scatter.33.cloned.1.call-start = ((), (), s32[]{:S(2)}) async-start(), calls=%async_computation.23 | async-start | bytes 5242880 | tf_op jit(solution)/shard_map/reduce_scatter | solution.py:963
  384.3 319.5 %reduce-scatter.31.cloned.1.call-start = ((), (), s32[]{:S(2)}) async-start(), calls=%async_computation.22 | async-start | bytes 5242880 | tf_op jit(solution)/shard_map/reduce_scatter | solution.py:963
  393.8 365.6 %reduce-scatter.35.cloned.1.call-start = ((), (), s32[]{:S(2)}) async-start(), calls=%async_computation.24 | async-start | bytes 5242880 | tf_op jit(solution)/shard_map/reduce_scatter | solution.py:963
  403.8 407.6 %reduce-scatter.23.cloned.1.call-start = ((), (), s32[]{:S(2)}) async-start(), calls=%async_computation.18 | async-start | bytes 4587520 | tf_op jit(solution)/shard_map/reduce_scatter | solution.py:963
  404.6 4.6 collective-permute-start.1
  417.6 538.8 %all-reduce.9.cloned.1.call-start = ((), (), s32[]{:S(2)}) async-start(), calls=%async_computation.27 | async-start | bytes 12713984 | tf_op jit(solution)/shard_map/psum | solution.py:964
  812.8 18.6 %copy-start.16 = (f32[1,1024]{1,0:T(1,128)S(1)}, f32[1,1024]{1,0:T(1,128)}, u32[]{:S(2)}) copy-start(f32[1,1024]{1,0:T(1,128)} %get-tuple-element.137) | copy-start | bytes 12292
  956.4 10.8 %copy-start.5 = (bf16[384,1024]{1,0:T(8,128)(2,1)S(1)}, bf16[384,1024]{1,0:T(8,128)(2,1)}, u32[]{:S(2)}) copy-start(bf16[384,1024]{1,0:T(8,128)(2,1)} %get-tuple-element.267) | copy-start | bytes 2359300
  (13 other events, 41.1 us)
Sparse Core Ops, SparseCore 0:
  46.3 31.6 all-gather.7
  80.4 35.2 all-gather.5
  188.8 60.6 all-gather.9
  252.3 101.4 reduce-scatter.12
  357.4 27.7 reduce-scatter.26
  388.6 27.7 reduce-scatter.14
  419.3 23.5 reduce-scatter.24
  446.3 24.0 reduce-scatter.18
  473.9 24.0 reduce-scatter.16
  500.9 44.4 reduce-scatter.28
  548.4 43.9 reduce-scatter.20
  595.1 52.6 reduce-scatter.32
  651.1 52.6 reduce-scatter.30
  706.7 52.6 reduce-scatter.34
  763.1 48.2 reduce-scatter.22
  815.0 141.4 all-reduce.8

commit v2 on v1

v2 whole, which is shorter than its diff:
```python
import functools

import jax
import jax.numpy as jnp
import numpy as np
from jax import lax
from jax.experimental import pallas as pl
from jax.experimental.pallas import tpu as pltpu
from jax.sharding import PartitionSpec as P

HEADS = 8
KV_HEADS = 2
HEAD = 64
SSM_HEADS = 24
SSM_HEAD = 64
STATE = 128
WIDE = SSM_HEADS * SSM_HEAD
CHUNK = 128
EPS = 1e-05
ROPE_BASE = 100000000000.0
LOG2E = 1.4426950408889634
SCORE2 = 0.125 * LOG2E
LOWEST = -1e30
F32 = jnp.float32
BF16 = jnp.bfloat16
NN = (((1,), (0,)), ((), ()))
NT = (((1,), (1,)), ((), ()))
TN = (((0,), (0,)), ((), ()))
VMEM_LIMIT = 60 << 20


def dot(a, b, dims=NN):
    return lax.dot_general(a, b, dims, preferred_element_type=F32)


def dot_exact(a, b, dims=NN):
    return lax.dot_general(a, b, dims, precision=lax.Precision.HIGHEST, preferred_element_type=F32)


def low(v):
    return v.astype(BF16)


def sigmoid(v):
    return 1.0 / (1.0 + jnp.exp(-v))


def softplus(v):
    e = jnp.exp(-jnp.abs(v))
    tail = jnp.where(e < 1e-2, e * (1.0 - e * (0.5 - e * (1.0 / 3.0))), jnp.log(1.0 + e))
    return jnp.maximum(v, 0.0) + tail


def split_low(v):
    high = low(v)
    return high, low(v - high.astype(F32))


def widen(v, expand):
    return dot(jnp.concatenate(split_low(v), 1), expand)


def head_sums(v, expand):
    high, rest = split_low(v)
    ones = expand[:128]
    return dot(high, ones, NT) + dot(rest, ones, NT)


def cost(micros):
    return pl.CostEstimate(flops=int(micros * 3e9), bytes_accessed=int(micros * 1e5), transcendentals=0)


def full_spec(shape):
    return pl.BlockSpec(shape, lambda *_: (0,) * len(shape), pipeline_mode=pl.Buffered(1))


def params(limit=VMEM_LIMIT):
    return pltpu.CompilerParams(
        vmem_limit_bytes=limit, dimension_semantics=("arbitrary", "arbitrary")
    )


def low_rows(rows):
    t = lax.broadcasted_iota(jnp.int32, (rows, rows), 0)
    u = lax.broadcasted_iota(jnp.int32, (rows, rows), 1)
    return t >= u


def swap_halves(v):
    lane = lax.broadcasted_iota(jnp.int32, v.shape, 1)
    return jnp.where((lane & 63) < 32, pltpu.roll(v, 96, 1), pltpu.roll(v, 32, 1))


def pair_rows(v):
    lane = lax.broadcasted_iota(jnp.int32, v.shape, 1)
    none = jnp.zeros_like(v)
    return jnp.concatenate([jnp.where(lane < 64, v, none), jnp.where(lane >= 64, v, none)], 0)


def first_norm(v, gain):
    v = v.astype(F32)
    return low(v * lax.rsqrt(jnp.mean(v * v, -1, keepdims=True) + EPS) * gain)


def enter_body(tok_ref, gain_ref, wq_ref, wk_ref, wv_ref, cos_ref, sin_ref, hid_ref, q_ref, kv_ref):
    hid = first_norm(tok_ref[0], gain_ref[...])
    hid_ref[0] = hid
    cosine, sine = cos_ref[...], sin_ref[...]
    t = dot(hid, wk_ref[...])
    kv_ref[0, :, :128] = low(t * cosine + swap_halves(t) * sine)
    kv_ref[0, :, 128:] = low(dot(hid, wv_ref[...]))
    q = dot(hid, wq_ref[...])
    for g in range(4):
        t = q[:, g * 128 : g * 128 + 128]
        q_ref[0, :, g * 128 : g * 128 + 128] = low(t * cosine + swap_halves(t) * sine)


def enter(tokens, gain, wq, wk, wv, cosine, sine):
    seqs, span, width = tokens.shape
    rows = min(256, span)

    def row(n):
        return pl.BlockSpec((1, rows, n), lambda s, b: (s, b, 0))

    table = pl.BlockSpec((rows, 128), lambda s, b: (b, 0))
    return pl.pallas_call(
        enter_body,
        grid=(seqs, span // rows),
        in_specs=[row(width)] + [full_spec(v.shape) for v in (gain, wq, wk, wv)] + [table, table],
        out_specs=[row(width), row(512), row(256)],
        out_shape=[jax.ShapeDtypeStruct((seqs, span, n), BF16) for n in (width, 512, 256)],
        compiler_params=params(),
        cost_estimate=cost(8),
        name="enter",
    )(tokens, gain, wq, wk, wv, cosine, sine)


def mixer_body(
    pos_ref, len_ref, hid_ref, halo_ref, gain_ref, wz_ref, wc_ref, ws_ref, cw_ref, cb_ref, sb_ref, a_ref, exp_ref,
    z_ref, cl_ref, pre_ref, x_ref, bk_ref, cq_ref, dt_ref, sg_ref, cum_ref, cumt_ref, st_ref,
    prev, state, total, *, rows, blocks,
):
    s = pl.program_id(0)
    b = pl.program_id(1)

    @pl.when(b == 0)
    def _():
        prev[...] = dot(first_norm(halo_ref[0], gain_ref[...]), wc_ref[...])[8:]
        state[...] = jnp.zeros_like(state)
        total[...] = jnp.zeros_like(total)

    hid = hid_ref[0]
    conv = dot(hid, wc_ref[...])
    raw = dot(hid, ws_ref[...]) + sb_ref[...]
    z_ref[0] = low(dot(hid, wz_ref[...]))
    cl_ref[0] = low(conv)
    ext = jnp.concatenate([prev[...], conv], 0)
    prev[...] = conv[rows - 8 :]
    pre = cb_ref[...] + cw_ref[3:4] * conv
    for back in range(1, 4):
        pre = pre + cw_ref[3 - back : 4 - back] * pltpu.roll(ext, back, 0)[8:]
    pre_ref[0] = low(pre)
    act = low(pre * sigmoid(pre))
    x = act[:, :WIDE]
    bk = act[:, WIDE : WIDE + STATE]
    x_ref[0] = x
    bk_ref[0] = bk
    cq_ref[0] = act[:, WIDE + STATE :]
    at = pos_ref[0] + b * rows + lax.broadcasted_iota(jnp.int32, raw.shape, 0)
    live = jnp.where(at < len_ref[s], 1.0, 0.0)
    dt = softplus(raw) * live
    dt_ref[0] = dt
    sg_ref[0] = sigmoid(raw) * live
    log_decay = dt * a_ref[...]
    tri = jnp.where(low_rows(CHUNK), 1.0, 0.0)
    for c in range(rows // CHUNK):
        here = slice(c * CHUNK, (c + 1) * CHUNK)
        cum = dot_exact(tri, log_decay[here])
        cum_ref[0, here] = cum
        cumt_ref[0, :, here] = cum.T[:32]
        last = cum[CHUNK - 1 :]
        weight = dt[here] * jnp.exp2(last - cum)
        wide = widen(
            jnp.concatenate([weight, jnp.broadcast_to(jnp.exp2(last), (16, 128))], 0), exp_ref[...]
        )
        xw = low(x[here].astype(F32) * wide[:CHUNK])
        state[...] = state[...] * wide[CHUNK : CHUNK + 1] + dot(bk[here], xw, TN)
        total[...] = total[...] + last

    @pl.when(b == blocks - 1)
    def _():
        st_ref[0, :STATE] = low(state[...])
        st_ref[0, STATE:] = total_rows(total[...], exp_ref[...])


def total_rows(total, expand):
    wide = widen(jnp.broadcast_to(total, (8, 128)), expand)
    high = wide.astype(BF16).astype(F32)
    return low(jnp.concatenate([high, wide - high], 0))


def mixer(pos, lens, hid, halo, gain, wz, wc, ws, cw, cb, sb, a, expand):
    seqs, span, width = hid.shape
    rows = min(256, span)
    blocks = span // rows
    conv_width = wc.shape[1]

    def row(n):
        return pl.BlockSpec((1, rows, n), lambda s, b, *_: (s, b, 0))

    def shape(n, kind):
        return jax.ShapeDtypeStruct((seqs, span, n), kind)

    return pl.pallas_call(
        functools.partial(mixer_body, rows=rows, blocks=blocks),
        grid_spec=pltpu.PrefetchScalarGridSpec(
            num_scalar_prefetch=2,
            grid=(seqs, blocks),
            in_specs=[row(width), pl.BlockSpec((1, 16, width), lambda s, b, *_: (s, 0, 0))]
            + [full_spec(v.shape) for v in (gain, wz, wc, ws, cw, cb, sb, a, expand)],
            out_specs=[
                row(WIDE), row(conv_width), row(conv_width), row(WIDE), row(STATE), row(STATE),
                row(128), row(128), row(128),
                pl.BlockSpec((1, 32, rows), lambda s, b, *_: (s, 0, b)),
                pl.BlockSpec((1, STATE + 16, WIDE), lambda s, b, *_: (s, 0, 0)),
            ],
            scratch_shapes=[
                pltpu.VMEM((8, conv_width), F32), pltpu.VMEM((STATE, WIDE), F32), pltpu.VMEM((1, 128), F32),
            ],
        ),
        out_shape=[
            shape(WIDE, BF16), shape(conv_width, BF16), shape(conv_width, BF16), shape(WIDE, BF16),
            shape(STATE, BF16), shape(STATE, BF16), shape(128, F32), shape(128, F32), shape(128, F32),
            jax.ShapeDtypeStruct((seqs, 32, span), F32),
            jax.ShapeDtypeStruct((seqs, STATE + 16, WIDE), BF16),
        ],
        compiler_params=params(),
        cost_estimate=cost(20),
        name="mixer",
    )(pos, lens, hid, halo, gain, wz, wc, ws, cw, cb, sb, a, expand)


def joined(place, ref):
    state = jnp.zeros((STATE, WIDE), F32)
    for i in range(ref.shape[0]):
        logs = ref[i, 0, STATE : STATE + 1].astype(F32) + ref[i, 0, STATE + 8 : STATE + 9].astype(F32)
        state = jnp.where(i < place, state * jnp.exp2(logs) + ref[i, 0, :STATE].astype(F32), state)
    return state


def joined_later(refs):
    state = jnp.zeros((STATE, WIDE), F32)
    for ref in reversed(refs):
        logs = ref[0, STATE : STATE + 1].astype(F32) + ref[0, STATE + 8 : STATE + 9].astype(F32)
        state = state * jnp.exp2(logs) + ref[0, :STATE].astype(F32)
    return state


def gathered_spec(states):
    return pl.BlockSpec((states.shape[0], 1) + states.shape[2:], lambda s, c: (0, s, 0, 0), pipeline_mode=pl.Buffered(1))


SCALARS = pl.BlockSpec(memory_space=pltpu.SMEM)


def scan_body(
    place_ref, x_ref, bk_ref, cq_ref, dt_ref, cum_ref, cumt_ref, skip_ref, z_ref, gain_ref, exp_ref, all_ref,
    mix_ref, low_ref, st_ref, state, y,
):
    c = pl.program_id(1)

    @pl.when(c == 0)
    def _():
        state[...] = joined(place_ref[0], all_ref)

    x = x_ref[0].astype(F32)
    bk, cq = bk_ref[0], cq_ref[0]
    cum = cum_ref[0]
    last = cum[CHUNK - 1 :]
    expand = exp_ref[...]
    xdt = x * widen(dt_ref[0], expand)
    ends = widen(
        jnp.concatenate([jnp.exp2(cum), jnp.exp2(last - cum), jnp.broadcast_to(jnp.exp2(last), (16, 128))], 0),
        expand,
    )
    inter = jnp.where(low_rows(CHUNK), dot(cq, bk, NT), 0.0)
    held = low(state[...])
    st_ref[0, 0] = held
    y[...] = dot(cq, held) * ends[:CHUNK] + skip_ref[...] * x
    state[...] = state[...] * ends[2 * CHUNK : 2 * CHUNK + 1] + dot(bk, low(xdt * ends[CHUNK : 2 * CHUNK]), TN)
    xdt = low(xdt)
    for p in range(SSM_HEADS // 2):
        parts = []
        for h in (2 * p, 2 * p + 1):
            differ = jnp.minimum(cum[:, h : h + 1] - cumt_ref[0, h : h + 1, :], 0.0)
            parts.append(low(inter * jnp.exp2(differ)))
        cols = slice(p * 128, p * 128 + 128)
        y[:, cols] += dot(jnp.concatenate(parts, 1), pair_rows(xdt[:, cols]))
    mixed = y[...]
    mix_ref[0] = mixed
    z = z_ref[0].astype(F32)
    v = mixed * (z * sigmoid(z))
    low_ref[0] = low(v * lax.rsqrt(jnp.mean(v * v, -1, keepdims=True) + EPS) * gain_ref[...])


def scan_forward(place, x, bk, cq, dt, cum, cumt, skip, z, gain, expand, states):
    seqs, span, _ = x.shape
    chunks = span // CHUNK

    def row(n):
        return pl.BlockSpec((1, CHUNK, n), lambda s, c: (s, c, 0))

    return pl.pallas_call(
        scan_body,
        grid=(seqs, chunks),
        in_specs=[
            SCALARS, row(WIDE), row(STATE), row(STATE), row(128), row(128),
            pl.BlockSpec((1, 32, CHUNK), lambda s, c: (s, 0, c)),
            full_spec(skip.shape), row(WIDE), full_spec(gain.shape), full_spec(expand.shape), gathered_spec(states),
        ],
        out_specs=[row(WIDE), row(WIDE), pl.BlockSpec((1, 1, STATE, WIDE), lambda s, c: (s, c, 0, 0))],
        out_shape=[
            jax.ShapeDtypeStruct((seqs, span, WIDE), F32),
            jax.ShapeDtypeStruct((seqs, span, WIDE), BF16),
            jax.ShapeDtypeStruct((seqs, chunks, STATE, WIDE), BF16),
        ],
        scratch_shapes=[pltpu.VMEM((STATE, WIDE), F32), pltpu.VMEM((CHUNK, WIDE), F32)],
        compiler_params=params(),
        cost_estimate=cost(16),
        name="scan_forward",
    )(place, x, bk, cq, dt, cum, cumt, skip, z, gain, expand, states)


def middle_body(
    pos_ref, len_ref, near_ref, far_ref, mix_ref, tok_ref, cot_ref, mixed_ref, z_ref, cq_ref, cum_ref,
    wao_ref, wmo_ref, wg_ref, wu_ref, wd_ref, gain2_ref, gated_ref, exp_ref,
    out_ref, h2_ref, act_ref, gffn_ref, gg_ref, gu_ref, gmid_ref, gb_ref, gnear_ref, gfar_ref, gmixed_ref,
    gz_ref, attn_ref, gn2_ref, ggain_ref, adj_ref,
    gn2_s, ggain_s, adj, offset, *, rows, blocks, seqs,
):
    s = pl.program_id(0)
    b = pl.program_id(1)

    @pl.when((s == 0) & (b == 0))
    def _():
        gn2_s[...] = jnp.zeros_like(gn2_s)
        ggain_s[...] = jnp.zeros_like(ggain_s)

    @pl.when(b == 0)
    def _():
        adj[...] = jnp.zeros_like(adj)
        offset[...] = jnp.zeros_like(offset)

    at = pos_ref[0] + b * rows + lax.broadcasted_iota(jnp.int32, (rows, 1), 0)
    live = jnp.where(at < len_ref[s], 1.0, 0.0)
    attn = jnp.where(b < blocks // 2, near_ref[0], far_ref[0])
    attn_ref[0] = attn
    branch = dot(attn, wao_ref[...]) + dot(mix_ref[0], wmo_ref[...])
    after = tok_ref[0].astype(F32) + live * branch
    scale = lax.rsqrt(jnp.mean(after * after, -1, keepdims=True) + EPS)
    unit = after * scale
    gain = gain2_ref[...]
    h2 = low(unit * gain)
    h2_ref[0] = h2
    gate = dot(h2, wg_ref[...])
    up = dot(h2, wu_ref[...])
    sg = sigmoid(gate)
    silu = gate * sg
    act = low(silu * up)
    act_ref[0] = act
    out_ref[0] = low(after + live * dot(act, wd_ref[...]))
    cot = cot_ref[0].astype(F32)
    gffn = low(live * cot)
    gffn_ref[0] = gffn
    gact = dot(gffn, wd_ref[...], NT)
    gg = low(gact * up * (sg * (1.0 + gate * (1.0 - sg))))
    gu = low(gact * silu)
    gg_ref[0] = gg
    gu_ref[0] = gu
    gh2 = dot(gg, wg_ref[...], NT) + dot(gu, wu_ref[...], NT)
    gn2_s[...] += jnp.sum(gh2 * unit, 0, keepdims=True)
    g = gh2 * gain
    gmid = cot + scale * (g - unit * jnp.mean(g * unit, -1, keepdims=True))
    gmid_ref[0] = gmid
    gb = low(live * gmid)
    gb_ref[0] = gb
    gattn = low(dot(gb, wao_ref[...], NT))

    @pl.when(b < blocks // 2)
    def _():
        gnear_ref[0] = gattn

    @pl.when(b >= blocks // 2)
    def _():
        gfar_ref[0] = gattn

    gn = low(dot(gb, wmo_ref[...], NT)).astype(F32)
    mixed = mixed_ref[0]
    z = z_ref[0].astype(F32)
    sg = sigmoid(z)
    silu = z * sg
    v = mixed * silu
    scale = lax.rsqrt(jnp.mean(v * v, -1, keepdims=True) + EPS)
    unit = v * scale
    ggain_s[...] += jnp.sum(gn * unit, 0, keepdims=True)
    g = gn * gated_ref[...]
    g = scale * (g - unit * jnp.mean(g * unit, -1, keepdims=True))
    gmixed = g * silu
    gmixed_ref[0] = low(gmixed)
    gz_ref[0] = low(g * mixed * (sg * (1.0 + z * (1.0 - sg))))
    cum = cum_ref[0]
    logs = []
    for c in range(rows // CHUNK):
        here = cum[c * CHUNK : (c + 1) * CHUNK]
        logs.append(here + offset[...])
        offset[...] += here[CHUNK - 1 :]
    wide = widen(jnp.exp2(jnp.concatenate(logs, 0)), exp_ref[...])
    adj[...] += dot(cq_ref[0], low(gmixed * wide), TN)

    @pl.when(b == blocks - 1)
    def _():
        adj_ref[0, :STATE] = low(adj[...])
        adj_ref[0, STATE:] = total_rows(offset[...], exp_ref[...])

    @pl.when((s == seqs - 1) & (b == blocks - 1))
    def _():
        gn2_ref[...] = gn2_s[...]
        ggain_ref[...] = ggain_s[...]


def middle(pos, lens, near, far, mix, tokens, cot, mixed, z, cq, cum, wao, wmo, wg, wu, wd, gain2, gated, expand):
    seqs, span, width = tokens.shape
    rows = min(256, span // 2)
    blocks = span // rows
    ff = wg.shape[1]
    lower = pl.BlockSpec((1, rows, 512), lambda s, b, *_: (s, jnp.minimum(b, blocks // 2 - 1), 0))
    upper = pl.BlockSpec((1, rows, 512), lambda s, b, *_: (s, jnp.maximum(b - blocks // 2, 0), 0))

    def row(n):
        return pl.BlockSpec((1, rows, n), lambda s, b, *_: (s, b, 0))

    def shape(n, kind):
        return jax.ShapeDtypeStruct((seqs, span, n), kind)

    def once(n):
        return pl.BlockSpec((1, n), lambda s, b, *_: (0, 0))

    return pl.pallas_call(
        functools.partial(middle_body, rows=rows, blocks=blocks, seqs=seqs),
        grid_spec=pltpu.PrefetchScalarGridSpec(
            num_scalar_prefetch=2,
            grid=(seqs, blocks),
            in_specs=[
                lower, upper, row(WIDE), row(width), row(width), row(WIDE), row(WIDE), row(STATE), row(128),
                full_spec(wao.shape), full_spec(wmo.shape), full_spec(wg.shape), full_spec(wu.shape),
                full_spec(wd.shape), full_spec(gain2.shape), full_spec(gated.shape), full_spec(expand.shape),
            ],
            out_specs=[
                row(width), row(width), row(ff), row(width), row(ff), row(ff), row(width), row(width),
                lower, upper, row(WIDE), row(WIDE), row(512),
                once(width), once(WIDE),
                pl.BlockSpec((1, STATE + 16, WIDE), lambda s, b, *_: (s, 0, 0)),
            ],
            scratch_shapes=[
                pltpu.VMEM((1, width), F32), pltpu.VMEM((1, WIDE), F32), pltpu.VMEM((STATE, WIDE), F32),
                pltpu.VMEM((1, 128), F32),
            ],
        ),
        out_shape=[
            shape(width, BF16), shape(width, BF16), shape(ff, BF16), shape(width, BF16), shape(ff, BF16),
            shape(ff, BF16), shape(width, F32), shape(width, BF16),
            jax.ShapeDtypeStruct((seqs, span // 2, 512), BF16), jax.ShapeDtypeStruct((seqs, span // 2, 512), BF16),
            shape(WIDE, BF16), shape(WIDE, BF16), shape(512, BF16),
            jax.ShapeDtypeStruct((1, width), F32), jax.ShapeDtypeStruct((1, WIDE), F32),
            jax.ShapeDtypeStruct((seqs, STATE + 16, WIDE), BF16),
        ],
        compiler_params=params(),
        cost_estimate=cost(60),
        name="middle",
    )(pos, lens, near, far, mix, tokens, cot, mixed, z, cq, cum, wao, wmo, wg, wu, wd, gain2, gated, expand)


def scan_back_body(
    x_ref, bk_ref, cq_ref, dt_ref, sg_ref, cum_ref, cumt_ref, dy_ref, mix_ref, st_ref, pre_ref, cl_ref,
    skip_ref, a_ref, cw_ref, exp_ref, *rest, chunks, conv_width,
):
    *later, gc_ref, tail_ref, head_ref, gw_ref, gskip_ref, small_ref, adj, after, gact = rest
    s = pl.program_id(0)
    c = pl.program_id(1)

    @pl.when((s == 0) & (c == 0))
    def _():
        gw_ref[...] = jnp.zeros_like(gw_ref)
        gskip_ref[...] = jnp.zeros_like(gskip_ref)
        small_ref[...] = jnp.zeros_like(small_ref)

    @pl.when(c == 0)
    def _():
        adj[...] = joined_later(later)
        after[...] = jnp.zeros_like(after)

    x = x_ref[0].astype(F32)
    bk, cq = bk_ref[0], cq_ref[0]
    dt = dt_ref[0]
    cum = cum_ref[0]
    last = cum[CHUNK - 1 :]
    expand = exp_ref[...]
    dt_wide = widen(dt, expand)
    ends = widen(
        jnp.concatenate([jnp.exp2(cum), jnp.exp2(last - cum), jnp.broadcast_to(jnp.exp2(last), (16, 128))], 0),
        expand,
    )
    to_end = ends[CHUNK : 2 * CHUNK]
    all_wide = ends[2 * CHUNK : 2 * CHUNK + 1]
    xdt = x * dt_wide
    dy_low = dy_ref[0]
    dy = dy_low.astype(F32)
    dy_in = low(dy * ends[:CHUNK])
    state = st_ref[0, 0]
    gstate = adj[...]
    gstate_low = low(gstate)
    from_end = dot(bk, gstate_low) * to_end
    gb = dot(low(xdt * to_end), gstate_low, NT)
    gc = dot(dy_in, state, NT)
    gfinal = all_wide * jnp.sum(gstate * state.astype(F32), 0, keepdims=True) + jnp.sum(
        xdt * from_end, 0, keepdims=True
    )
    adj[...] = gstate * all_wide + dot(cq, dy_in, TN)
    xdt_low = low(xdt)
    u = lax.broadcasted_iota(jnp.int32, (CHUNK, CHUNK), 0)
    t = lax.broadcasted_iota(jnp.int32, (CHUNK, CHUNK), 1)
    inter = jnp.where(t >= u, dot(bk, cq, NT), 0.0)
    ginter = jnp.zeros((CHUNK, CHUNK), F32)
    for p in range(SSM_HEADS // 2):
        cols = slice(p * 128, p * 128 + 128)
        dy_rows = pair_rows(dy_low[:, cols])
        gmix = dot(xdt_low[:, cols], dy_rows, NT)
        parts = []
        for n, h in enumerate((2 * p, 2 * p + 1)):
            decay = jnp.exp2(jnp.minimum(cumt_ref[0, h : h + 1, :] - cum[:, h : h + 1], 0.0))
            parts.append(low(inter * decay))
            ginter = ginter + gmix[:, n * CHUNK : (n + 1) * CHUNK] * decay
        gact[:, cols] = dot(jnp.concatenate(parts, 1), dy_rows)
    ginter = low(jnp.where(t >= u, ginter, 0.0))
    gact[:, WIDE : WIDE + STATE] = gb + dot(ginter, cq)
    gact[:, WIDE + STATE :] = gc + dot(ginter, bk, TN)
    gxdt = gact[:, :WIDE] + from_end
    skip = skip_ref[...]
    gact[:, :WIDE] = dt_wide * gxdt + skip * dy
    gskip_ref[...] += jnp.sum(dy * x, 0, keepdims=True)
    sums = head_sums(
        jnp.concatenate([x * gxdt, dy * (mix_ref[0] - skip * x), jnp.broadcast_to(gfinal, (16, WIDE))], 0), expand
    )
    direct = sums[:CHUNK]
    gcum = sums[CHUNK : 2 * CHUNK] - dt * direct
    gld = dot_exact(jnp.where(t >= u, 1.0, 0.0), gcum) + sums[2 * CHUNK : 2 * CHUNK + 1]
    a = a_ref[...]
    gstep = (direct + a * gld) * sg_ref[0]
    gc_ref[0, :, conv_width : conv_width + 128] = low(gstep)
    gc_ref[0, :, conv_width + 128 :] = jnp.zeros((CHUNK, 128), BF16)
    small_ref[0:1] += jnp.sum(dt * gld, 0, keepdims=True) * a
    small_ref[1:2] += jnp.sum(gstep, 0, keepdims=True)
    pre = pre_ref[0].astype(F32)
    sg = sigmoid(pre)
    gpre = gact[...] * (sg * (1.0 + pre * (1.0 - sg)))
    ext = jnp.concatenate([gpre, after[...]], 0)
    after[...] = gpre[:8]
    conv = cl_ref[0].astype(F32)
    gconv = cw_ref[3:4] * gpre
    gw_ref[3:4] += jnp.sum(conv * gpre, 0, keepdims=True)
    gw_ref[4:5] += jnp.sum(gpre, 0, keepdims=True)
    for ahead in range(1, 4):
        moved = pltpu.roll(ext, CHUNK + 8 - ahead, 0)[:CHUNK]
        gconv = gconv + cw_ref[3 - ahead : 4 - ahead] * moved
        gw_ref[3 - ahead : 4 - ahead] += jnp.sum(conv * moved, 0, keepdims=True)
    gc_ref[0, :, :conv_width] = low(gconv)

    @pl.when(c == 0)
    def _():
        tail_ref[0] = gconv[CHUNK - 8 :]

    @pl.when(c == chunks - 1)
    def _():
        head_ref[0] = gpre[:8]


def scan_backward(x, bk, cq, dt, sg, cum, cumt, dy, mixed, states, pre, conv, skip, a, cw, expand, adjoints):
    seqs, span, _ = x.shape
    chunks = span // CHUNK
    conv_width = pre.shape[2]

    def row(n):
        return pl.BlockSpec((1, CHUNK, n), lambda s, c: (s, chunks - 1 - c, 0))

    def once(m, n):
        return pl.BlockSpec((m, n), lambda s, c: (0, 0))

    edge = pl.BlockSpec((1, 8, conv_width), lambda s, c: (s, 0, 0))
    return pl.pallas_call(
        functools.partial(scan_back_body, chunks=chunks, conv_width=conv_width),
        grid=(seqs, chunks),
        in_specs=[
            row(WIDE), row(STATE), row(STATE), row(128), row(128), row(128),
            pl.BlockSpec((1, 32, CHUNK), lambda s, c: (s, 0, chunks - 1 - c)),
            row(WIDE), row(WIDE),
            pl.BlockSpec((1, 1, STATE, WIDE), lambda s, c: (s, chunks - 1 - c, 0, 0)),
            row(conv_width), row(conv_width),
            full_spec(skip.shape), full_spec(a.shape), full_spec(cw.shape), full_spec(expand.shape),
        ]
        + [
            pl.BlockSpec((1, STATE + 16, WIDE), lambda s, c: (s, 0, 0), pipeline_mode=pl.Buffered(1))
            for _ in adjoints
        ],
        out_specs=[row(conv_width + 256), edge, edge, once(8, conv_width), once(1, WIDE), once(8, 128)],
        out_shape=[
            jax.ShapeDtypeStruct((seqs, span, conv_width + 256), BF16),
            jax.ShapeDtypeStruct((seqs, 8, conv_width), F32),
            jax.ShapeDtypeStruct((seqs, 8, conv_width), F32),
            jax.ShapeDtypeStruct((8, conv_width), F32),
            jax.ShapeDtypeStruct((1, WIDE), F32),
            jax.ShapeDtypeStruct((8, 128), F32),
        ],
        scratch_shapes=[
            pltpu.VMEM((STATE, WIDE), F32), pltpu.VMEM((8, conv_width), F32), pltpu.VMEM((CHUNK, conv_width), F32),
        ],
        compiler_params=params(),
        cost_estimate=cost(35),
        name="scan_backward",
    )(x, bk, cq, dt, sg, cum, cumt, dy, mixed, states, pre, conv, skip, a, cw, expand, *adjoints)


def leave_mixer_body(gz_ref, gc_ref, wz_ref, wc_ref, ws_ref, gh_ref, *, conv_width):
    gh = dot(gz_ref[0], wz_ref[...], NT) + dot(gc_ref[0, :, :conv_width], wc_ref[...], NT)
    gh_ref[0] = gh + dot(gc_ref[0, :, conv_width : conv_width + 128], ws_ref[...], NT)


def leave_mixer(gz, gc, wz, wc, ws):
    seqs, span, _ = gz.shape
    rows = min(256, span)

    def row(n):
        return pl.BlockSpec((1, rows, n), lambda s, b: (s, b, 0))

    width = wz.shape[0]
    return pl.pallas_call(
        functools.partial(leave_mixer_body, conv_width=wc.shape[1]),
        grid=(seqs, span // rows),
        in_specs=[row(gz.shape[2]), row(gc.shape[2])] + [full_spec(v.shape) for v in (wz, wc, ws)],
        out_specs=row(width),
        out_shape=jax.ShapeDtypeStruct((seqs, span, width), F32),
        compiler_params=params(),
        cost_estimate=cost(0),
        name="leave_mixer",
    )(gz, gc, wz, wc, ws)


def leave_body(tok_ref, gmid_ref, gh_ref, gain_ref, wq_ref, wk_ref, wv_ref, cos_ref, sin_ref, *rest, blocks, count):
    near, far = rest[:2], rest[2:4]
    pieces = rest[4 : 4 + 2 * count]
    gt_ref, gn_ref, gq_ref, gkv_ref = rest[4 + 2 * count :]
    b = pl.program_id(1)

    @pl.when((pl.program_id(0) == 0) & (b == 0))
    def _():
        gn_ref[...] = jnp.zeros_like(gn_ref)

    for j in range(2):
        gq_ref[0, :, 256 * j : 256 * j + 256] = jnp.where(b < blocks // 2, near[j][0], far[j][0])
    sums = []
    for j in range(2):
        t = pieces[j * count][0].astype(F32)
        for r in range(1, count):
            t = t + pieces[j * count + r][0].astype(F32)
        sums.append(t)
    lane = lax.broadcasted_iota(jnp.int32, sums[0].shape, 1)
    gk = jnp.where(lane < 64, sums[0], pltpu.roll(sums[1], 64, 1))
    gv = low(jnp.where(lane < 64, pltpu.roll(sums[0], 64, 1), sums[1]))
    gk = low(gk * cos_ref[...] - swap_halves(gk) * sin_ref[...])
    gkv_ref[0, :, :128] = gk
    gkv_ref[0, :, 128:] = gv
    gh = gh_ref[0] + dot(gq_ref[0], wq_ref[...], NT) + dot(gk, wk_ref[...], NT) + dot(gv, wv_ref[...], NT)
    v = tok_ref[0].astype(F32)
    scale = lax.rsqrt(jnp.mean(v * v, -1, keepdims=True) + EPS)
    unit = v * scale
    gn_ref[...] += jnp.sum(gh * unit, 0, keepdims=True)
    g = gh * gain_ref[...]
    gt_ref[0] = gmid_ref[0] + scale * (g - unit * jnp.mean(g * unit, -1, keepdims=True))


def leave(tokens, gmid, gh, gain, wq, wk, wv, cosine, sine, near, far, pieces):
    seqs, span, width = tokens.shape
    rows = min(256, span // 2)
    blocks = span // rows
    count = len(pieces) // 2

    def row(n):
        return pl.BlockSpec((1, rows, n), lambda s, b: (s, b, 0))

    table = pl.BlockSpec((rows, 128), lambda s, b: (b, 0))
    lower = pl.BlockSpec((1, rows, 256), lambda s, b: (s, jnp.minimum(b, blocks // 2 - 1), 0))
    upper = pl.BlockSpec((1, rows, 256), lambda s, b: (s, jnp.maximum(b - blocks // 2, 0), 0))
    return pl.pallas_call(
        functools.partial(leave_body, blocks=blocks, count=count),
        grid=(seqs, blocks),
        in_specs=[row(width)] * 3
        + [full_spec(v.shape) for v in (gain, wq, wk, wv)]
        + [table, table, lower, lower, upper, upper]
        + [row(128)] * (2 * count),
        out_specs=[row(width), pl.BlockSpec((1, width), lambda s, b: (0, 0)), row(512), row(256)],
        out_shape=[
            jax.ShapeDtypeStruct((seqs, span, width), F32), jax.ShapeDtypeStruct((1, width), F32),
            jax.ShapeDtypeStruct((seqs, span, 512), BF16), jax.ShapeDtypeStruct((seqs, span, 256), BF16),
        ],
        compiler_params=params(),
        cost_estimate=cost(10),
        name="leave",
    )(tokens, gmid, gh, gain, wq, wk, wv, cosine, sine, *near, *far, *pieces)


def dup_halves(v):
    lane = lax.broadcasted_iota(jnp.int32, v.shape, 1)
    other = pltpu.roll(v, 64, 1)
    return low(jnp.where(lane < 64, v, other)), low(jnp.where(lane < 64, other, v))


def head_rows(v):
    lane = lax.broadcasted_iota(jnp.int32, (v.shape[0], 128), 1)
    heads = []
    for h in range(v.shape[1] // HEAD):
        t = v[:, (h // 2) * 128 : (h // 2) * 128 + 128]
        heads.append(jnp.where((lane < 64) if h % 2 == 0 else (lane >= 64), t, jnp.zeros_like(t)))
    return heads


def key_range(first, length, rows, keys):
    whole = jnp.minimum((first + 1) // keys, length // keys)
    some = jnp.minimum((first + rows + keys - 1) // keys, (length + keys - 1) // keys)
    return whole, some


def seen(i, first, length, rows, keys):
    key_at = i * keys + lax.broadcasted_iota(jnp.int32, (keys, rows), 0)
    query_at = first + lax.broadcasted_iota(jnp.int32, (keys, rows), 1)
    return (key_at <= query_at) & (key_at < length)


def attend_body(
    pos_ref, len_ref, from_ref, q_ref, other_ref, *rest, rows, keys, blocks, count, span,
):
    kv_refs = rest[:count]
    near_ref, far_ref, lse_ref, kd, vt, top, acc, score_a, score_b, top_a, top_b = rest[count:]
    s = pl.program_id(0)
    b = pl.program_id(1)
    prep = min(512, span)

    @pl.when(b == 0)
    def _():
        ones = jnp.ones((16, prep), F32)
        for r, kv_ref in enumerate(kv_refs):
            for i in range(span // prep):
                here = slice(i * prep, (i + 1) * prep)
                at = pl.ds(pl.multiple_of(from_ref[r] * span + i * prep, prep), prep)
                kd[0, at, :], kd[1, at, :] = dup_halves(kv_ref[0, here, :128].astype(F32))
                t = kv_ref[0, here, 128:].astype(F32).T
                vt[0, :, at] = low(jnp.concatenate([t[:64], ones], 0))
                vt[1, :, at] = low(jnp.concatenate([t[64:], ones], 0))

    first = pos_ref[b]
    length = len_ref[s]
    heads = head_rows(jnp.where(b < blocks // 2, q_ref[0], other_ref[0]))
    top[...] = jnp.full_like(top, LOWEST)
    acc[...] = jnp.zeros_like(acc)
    whole, some = key_range(first, length, rows, keys)

    def scores(i, buffer, tops, h, mask=None):
        at = pl.ds(pl.multiple_of(i * keys, keys), keys)
        t = dot(kd[h // 4, at, :], heads[h], NT)
        if mask is not None:
            t = jnp.where(mask, t, LOWEST)
        buffer[h] = t
        tops[h] = jnp.max(t, 0, keepdims=True)

    def add(i, buffer, tops, h):
        at = pl.ds(pl.multiple_of(i * keys, keys), keys)
        before = top[h]
        now = jnp.maximum(before, tops[h])
        p = low(jnp.exp2((buffer[h] - now) * SCORE2))
        acc[h] = acc[h] * jnp.exp2((before - now) * SCORE2) + dot(vt[h // 4, :, at], p)
        top[h] = now

    def edge(i, _):
        mask = seen(i, first, length, rows, keys)
        for h in range(HEADS):
            scores(i, score_a, top_a, h, mask)
        for h in range(HEADS):
            add(i, score_a, top_a, h)
        return 0

    lax.fori_loop(whole, some, edge, 0)
    last = jnp.maximum(whole - 1, 0)
    for h in range(HEADS):
        scores(0, score_a, top_a, h)

    def two(i, _):
        for h in range(HEADS):
            scores(2 * i + 1, score_b, top_b, h)
            add(2 * i, score_a, top_a, h)
        following = jnp.minimum(2 * i + 2, last)
        for h in range(HEADS):
            scores(following, score_a, top_a, h)
            add(2 * i + 1, score_b, top_b, h)
        return 0

    lax.fori_loop(0, whole // 2, two, 0)

    @pl.when(whole % 2 == 1)
    def _():
        for h in range(HEADS):
            add(last, score_a, top_a, h)

    outs = []
    for h in range(HEADS):
        t = acc[h]
        weight = t[64:65]
        outs.append(t[:64] / weight)
        lse_ref[0, h : h + 1, :] = top[h] * SCORE2 + jnp.log2(weight)
    result = low(jnp.concatenate(outs, 0).T)

    @pl.when(b < blocks // 2)
    def _():
        near_ref[0] = result

    @pl.when(b >= blocks // 2)
    def _():
        far_ref[0] = result


def halves_specs(rows, blocks, columns):
    lower = pl.BlockSpec((1, rows, columns), lambda s, b, *_: (s, jnp.minimum(b, blocks // 2 - 1), 0))
    upper = pl.BlockSpec((1, rows, columns), lambda s, b, *_: (s, jnp.maximum(b - blocks // 2, 0), 0))
    return lower, upper


def attend(pos, lens, sources, q, other, kvs):
    seqs, span, _ = q.shape
    count = len(kvs)
    total = count * span
    rows = min(256, span // 2)
    keys = 256
    blocks = span // rows
    lower, upper = halves_specs(rows, blocks, 512)
    half = jax.ShapeDtypeStruct((seqs, span // 2, 512), BF16)
    return pl.pallas_call(
        functools.partial(attend_body, rows=rows, keys=keys, blocks=blocks, count=count, span=span),
        grid_spec=pltpu.PrefetchScalarGridSpec(
            num_scalar_prefetch=3,
            grid=(seqs, blocks),
            in_specs=[lower, upper]
            + [pl.BlockSpec((1, span, 256), lambda s, b, *_: (s, 0, 0), pipeline_mode=pl.Buffered(1))] * count,
            out_specs=[lower, upper, pl.BlockSpec((1, 8, rows), lambda s, b, *_: (s, 0, b))],
            scratch_shapes=[
                pltpu.VMEM((2, total, 128), BF16), pltpu.VMEM((2, 80, total), BF16),
                pltpu.VMEM((8, 1, rows), F32), pltpu.VMEM((8, 80, rows), F32),
                pltpu.VMEM((8, keys, rows), F32), pltpu.VMEM((8, keys, rows), F32),
                pltpu.VMEM((8, 1, rows), F32), pltpu.VMEM((8, 1, rows), F32),
            ],
        ),
        out_shape=[half, half, jax.ShapeDtypeStruct((seqs, 8, span), F32)],
        compiler_params=params(),
        cost_estimate=cost(26),
        name="attend",
    )(pos, lens, sources, q, other, *kvs)


def attend_back_body(
    pos_ref, len_ref, from_ref, q_ref, other_ref, do_near_ref, do_far_ref, o_near_ref, o_far_ref, lse_ref,
    cos_ref, sin_ref, *rest, rows, keys, blocks, count, span, group,
):
    kv_refs = rest[:count]
    dq_near_ref, dq_far_ref = rest[count : count + 2]
    dkv_refs = rest[count + 2 : 2 * count + 2]
    kd, vd, kt, dk, dv, dq = rest[2 * count + 2 :]
    s = pl.program_id(0)
    b = pl.program_id(1)
    prep = min(512, span)

    @pl.when(b == 0)
    def _():
        for r, kv_ref in enumerate(kv_refs):
            for i in range(span // prep):
                here = slice(i * prep, (i + 1) * prep)
                at = pl.ds(pl.multiple_of(from_ref[r] * span + i * prep, prep), prep)
                k = kv_ref[0, here, :128].astype(F32)
                kd[at, :] = dup_halves(k)[group]
                vd[at, :] = dup_halves(kv_ref[0, here, 128:].astype(F32))[group]
                kt[:, at] = low(k.T[64 * group : 64 * group + 64])
        dk[...] = jnp.zeros_like(dk)
        dv[...] = jnp.zeros_like(dv)

    first = pos_ref[b]
    length = len_ref[s]
    is_near = b < blocks // 2
    heads = head_rows(jnp.where(is_near, q_ref[0], other_ref[0]))
    do = jnp.where(is_near, do_near_ref[0], do_far_ref[0])
    grads = head_rows(do)
    prod = do.astype(F32) * jnp.where(is_near, o_near_ref[0], o_far_ref[0]).astype(F32)
    col = lax.broadcasted_iota(jnp.int32, (8, 256), 1) // HEAD
    ones = low(jnp.where(col == lax.broadcasted_iota(jnp.int32, (8, 256), 0), 1.0, 0.0))
    high, remain = split_low(prod)
    delta = dot(ones, high, NT) + dot(ones, remain, NT)
    dq[...] = jnp.zeros_like(dq)
    whole, some = key_range(first, length, rows, keys)

    def step(i, masked):
        at = pl.ds(pl.multiple_of(i * keys, keys), keys)
        mask = seen(i, first, length, rows, keys) if masked else None
        dv_sum = dk_sum = None
        for h in range(4):
            x = dot(kd[at, :], heads[h], NT) * SCORE2 - lse_ref[0, 4 * group + h : 4 * group + h + 1, :]
            dp = dot(vd[at, :], grads[h], NT)
            if masked:
                x = jnp.where(mask, x, LOWEST)
            p = jnp.exp2(x)
            ds = low(p * (dp - delta[h : h + 1]))
            dv_part = dot(low(p), grads[h])
            dk_part = dot(ds, heads[h])
            dv_sum = dv_part if dv_sum is None else dv_sum + dv_part
            dk_sum = dk_part if dk_sum is None else dk_sum + dk_part
            dq[h] += dot(kt[:, at], ds)
        dv[at, :] += dv_sum
        dk[at, :] += dk_sum

    lax.fori_loop(0, whole, lambda i, _: (step(i, False), 0)[1], 0)
    lax.fori_loop(whole, some, lambda i, _: (step(i, True), 0)[1], 0)
    cosine, sine = cos_ref[...], sin_ref[...]
    parts = []
    for h in range(4):
        t = dq[h] * 0.125
        former, latter = t[:32], t[32:]
        parts += [former * cosine + latter * sine, latter * cosine - former * sine]
    result = low(jnp.concatenate(parts, 0).T)

    @pl.when(is_near)
    def _():
        dq_near_ref[0] = result

    @pl.when(jnp.logical_not(is_near))
    def _():
        dq_far_ref[0] = result

    @pl.when(b == blocks - 1)
    def _():
        lane = lax.broadcasted_iota(jnp.int32, (prep, 128), 1)
        for r, dkv_ref in enumerate(dkv_refs):
            for i in range(span // prep):
                at = pl.ds(pl.multiple_of(from_ref[r] * span + i * prep, prep), prep)
                k, v = dk[at, :], dv[at, :]
                k = (k + pltpu.roll(k, 64, 1)) * 0.125
                v = v + pltpu.roll(v, 64, 1)
                dkv_ref[0, i * prep : (i + 1) * prep] = low(jnp.where(lane < 64, k, v))


def attend_backward(group, pos, lens, sources, q, other, do_near, do_far, o_near, o_far, lse, cosine, sine, kvs):
    seqs, span, _ = q.shape
    count = len(kvs)
    total = count * span
    rows = min(256, span // 2)
    keys = 512
    blocks = span // rows
    lower = pl.BlockSpec((1, rows, 256), lambda s, b, *_: (s, jnp.minimum(b, blocks // 2 - 1), group))
    upper = pl.BlockSpec((1, rows, 256), lambda s, b, *_: (s, jnp.maximum(b - blocks // 2, 0), group))
    out_lower, out_upper = halves_specs(rows, blocks, 256)
    stat = pl.BlockSpec((1, 8, rows), lambda s, b, *_: (s, 0, b))
    table = pl.BlockSpec((32, rows), lambda s, b, *_: (0, b))
    half = jax.ShapeDtypeStruct((seqs, span // 2, 256), BF16)
    outs = pl.pallas_call(
        functools.partial(
            attend_back_body, rows=rows, keys=keys, blocks=blocks, count=count, span=span, group=group
        ),
        grid_spec=pltpu.PrefetchScalarGridSpec(
            num_scalar_prefetch=3,
            grid=(seqs, blocks),
            in_specs=[lower, upper, lower, upper, lower, upper, stat, table, table]
            + [pl.BlockSpec((1, span, 256), lambda s, b, *_: (s, 0, 0), pipeline_mode=pl.Buffered(1))] * count,
            out_specs=[out_lower, out_upper]
            + [pl.BlockSpec((1, span, 128), lambda s, b, *_: (s, 0, 0))] * count,
            scratch_shapes=[
                pltpu.VMEM((total, 128), BF16), pltpu.VMEM((total, 128), BF16), pltpu.VMEM((64, total), BF16),
                pltpu.VMEM((total, 128), F32), pltpu.VMEM((total, 128), F32), pltpu.VMEM((4, 64, rows), F32),
            ],
        ),
        out_shape=[half, half] + [jax.ShapeDtypeStruct((seqs, span, 128), BF16)] * count,
        compiler_params=params(),
        cost_estimate=cost(4 if group else 4),
        name="attend_backward",
    )(pos, lens, sources, q, other, do_near, do_far, o_near, o_far, lse, cosine, sine, *kvs)
    return outs[0], outs[1], outs[2:]


def tall_body(sel_ref, left_ref, *rest, n, widths, with_got, square):
    rights = rest[: len(widths)]
    rest = rest[len(widths) :]
    got_ref = rest[0] if with_got else None
    outs = rest[1:] if with_got else rest
    rows = left_ref.shape[1] // n
    i = pl.program_id(0)
    start = 0
    for part, (right, steps) in enumerate(zip(rights, widths)):

        @pl.when((i >= start) & (i < start + steps))
        def _(part=part, right=right):
            if square:
                if square == "hops":
                    own, to_x, keep_x, to_y, keep_y = outs
                    first, keep = ((to_x, keep_x), (to_y, keep_y))[part]
                for k in range(4):
                    block = jnp.bitwise_xor(sel_ref[1], k)
                    columns = pl.ds(pl.multiple_of(block * rows, rows), rows)
                    value = dot(left_ref[:, columns], right[...], TN)
                    if with_got:
                        value = value + got_ref[block].astype(F32)
                    value = low(value)
                    if square == "direct":
                        outs[k][...] = value
                    elif k == 0:
                        own[...] = value
                    elif k == 3:
                        first[1] = value
                    elif k == part + 1:
                        first[0] = value
                    else:
                        keep[...] = value
            else:
                value = dot(left_ref[...], right[...], TN)
                for j in range(n):
                    here = value[j * rows : (j + 1) * rows]
                    outs[0][j] = low(here + got_ref[j].astype(F32) if with_got else here)

        start += steps


def tall_grad(sel, left, rights, chunk, n, got=None, square="", micros=0.0, name="grad"):
    tokens, width = left.shape
    widths = [v.shape[1] // 2 // chunk for v in rights]
    steps = sum(widths)
    rows = width // n
    starts = [0, widths[0]]

    def within(k, i):
        return jnp.clip(i - starts[k], 0, widths[k] - 1)

    def right_spec(k):
        return pl.BlockSpec((tokens, chunk), lambda i, sel: (0, sel[0] * widths[k] + within(k, i)))

    whole = pl.BlockSpec((n, rows, chunk), lambda i, sel: (0, i, 0))
    extra = () if got is None else (got,)
    if square == "direct":
        out_specs = [pl.BlockSpec((rows, chunk), lambda i, sel: (i, 0))] * 4
        out_shape = [jax.ShapeDtypeStruct((steps * rows, chunk), BF16)] * 4
    elif square:
        out_specs = [pl.BlockSpec((rows, chunk), lambda i, sel: (i, 0))]
        out_shape = [jax.ShapeDtypeStruct((steps * rows, chunk), BF16)]
        for k in range(2):
            out_specs.append(pl.BlockSpec((2, rows, chunk), lambda i, sel, k=k: (0, within(k, i), 0)))
            out_specs.append(pl.BlockSpec((rows, chunk), lambda i, sel, k=k: (within(k, i), 0)))
            out_shape.append(jax.ShapeDtypeStruct((2, widths[k] * rows, chunk), BF16))
            out_shape.append(jax.ShapeDtypeStruct((widths[k] * rows, chunk), BF16))
    else:
        out_specs = whole
        out_shape = jax.ShapeDtypeStruct((n, steps * rows, chunk), BF16)
    return pl.pallas_call(
        functools.partial(tall_body, n=n, widths=widths, with_got=bool(extra), square=square),
        grid_spec=pltpu.PrefetchScalarGridSpec(
            num_scalar_prefetch=1,
            grid=(steps,),
            in_specs=[full_spec(left.shape)] + [right_spec(k) for k in range(2)] + [whole] * len(extra),
            out_specs=out_specs,
        ),
        out_shape=out_shape,
        compiler_params=pltpu.CompilerParams(vmem_limit_bytes=VMEM_LIMIT),
        cost_estimate=cost(micros),
        name=name,
    )(sel, left, *rights, *extra)


def wide_body(sel_ref, *rest, parts, group, with_got, square):
    lefts, rights = rest[:parts], rest[parts : 2 * parts]
    rest = rest[2 * parts :]
    got_ref = rest[0] if with_got else None
    outs = rest[1:] if with_got else rest
    values = [dot(left[...], right[...], TN) for left, right in zip(lefts, rights)]
    if square:
        own, to_x, keep_x, to_y, keep_y = outs
        value = jnp.concatenate(values, 0)
        if with_got:
            value = value + got_ref[0].astype(F32)
        value = low(value)
        split = values[0].shape[0]
        for k in range(4):

            @pl.when(pl.program_id(0) == k)
            def _(k=k):
                if k == 0:
                    own[...] = value
                    return
                for part, (first, keep) in enumerate(((to_x, keep_x), (to_y, keep_y))):
                    here = value[split:] if part else value[:split]
                    if k == 3:
                        first[1] = here
                    elif k == part + 1:
                        first[0] = here
                    else:
                        keep[...] = here
    else:
        for j in range(group):
            start = 0
            for v in values:
                rows = v.shape[0] // group
                here = v[j * rows : (j + 1) * rows]
                at = slice(start, start + rows)
                outs[0][j, at] = low(here + got_ref[j, at].astype(F32) if with_got else here)
                start += rows


def wide_grad(sel, lefts, rights, n, got=None, square="", micros=0.0, name="grad"):
    tokens = lefts[0].shape[0]
    chunk = rights[0].shape[1] // 2
    steps = min(n, 4)
    rows = [v.shape[1] // n for v in lefts]
    total = sum(rows)

    def turn(i, sel):
        return jnp.bitwise_xor(sel[1], i) if square else i

    def once(*dims):
        return pl.BlockSpec(dims, lambda i, sel: (0,) * len(dims))

    whole = pl.BlockSpec((n // steps, total, chunk), lambda i, sel: (turn(i, sel), 0, 0))
    extra = () if got is None else (got,)
    if square:
        a, b = rows[0], total - rows[0]
        dims = [(total, chunk), (2, a, chunk), (a, chunk), (2, b, chunk), (b, chunk)]
        out_specs = [once(*d) for d in dims]
        out_shape = [jax.ShapeDtypeStruct(d, BF16) for d in dims]
    else:
        out_specs = whole
        out_shape = jax.ShapeDtypeStruct((n, total, chunk), BF16)
    return pl.pallas_call(
        functools.partial(wide_body, parts=len(lefts), group=n // steps, with_got=bool(extra), square=square),
        grid_spec=pltpu.PrefetchScalarGridSpec(
            num_scalar_prefetch=1,
            grid=(steps,),
            in_specs=[pl.BlockSpec((tokens, v.shape[1] // steps), lambda i, sel: (0, turn(i, sel))) for v in lefts]
            + [pl.BlockSpec((tokens, chunk), lambda i, sel: (0, sel[0])) for _ in rights]
            + [whole] * len(extra),
            out_specs=out_specs,
        ),
        out_shape=out_shape,
        compiler_params=pltpu.CompilerParams(vmem_limit_bytes=VMEM_LIMIT),
        cost_estimate=cost(micros),
        name=name,
    )(sel, *lefts, *rights, *extra)


def ring(value, steps):
    n = lax.axis_size("seq")
    return lax.ppermute(value, "seq", [(i, (i + steps) % n) for i in range(n)])


def along(value, steps):
    n = lax.axis_size("seq")
    return lax.ppermute(value, "seq", [(i, i + steps) for i in range(n) if 0 <= i + steps < n])


def mirror(value):
    n = lax.axis_size("seq")
    return lax.ppermute(value, "seq", [(i, n - 1 - i) for i in range(n)])


def flip_dp(value, bit):
    n = lax.axis_size("dp")
    return lax.ppermute(value, "dp", [(i, i ^ bit) for i in range(n)])


def other_core(value):
    return flip_dp(value, 1)


def after(value, *done):
    return lax.optimization_barrier((value, done))[0]


def add_low(*values):
    total = values[0].astype(F32)
    for v in values[1:]:
        total = total + v.astype(F32)
    return low(total)


def scatter_seq(value):
    return lax.psum_scatter(value, "seq", scatter_dimension=0, tiled=True)[0]


def flip_seq(value, bit):
    n = lax.axis_size("seq")
    return lax.ppermute(value, "seq", [(i, i ^ bit) for i in range(n)])


def direct_sum(pieces):
    return add_low(pieces[0], *[flip_seq(v, k) for k, v in enumerate(pieces) if k])


def first_hop(pieces):
    own, to_x, keep_x, to_y, keep_y = pieces
    from_x, from_y = flip_seq(to_x, 1), flip_seq(to_y, 2)
    split = keep_x.shape[0]
    return (
        add_low(keep_x, from_x[1]), add_low(keep_y, from_y[1]),
        own[:split], own[split:], from_x[0], from_y[0],
    )


def second_hop(held):
    to_y, to_x, own_a, own_b, from_x, from_y = held
    return jnp.concatenate(
        [add_low(own_a, from_x, flip_seq(to_y, 2)), add_low(own_b, from_y, flip_seq(to_x, 1))], 0
    )


def offloaded_sum_z(value):
    n = lax.axis_size("dp")
    return lax.psum(value, "dp", axis_index_groups=[list(range(c, n, 2)) for c in range(2)])


def sum_z(value, first=2, last=None):
    bit = first
    while bit < (last or lax.axis_size("dp")):
        value = add_low(value, flip_dp(value, bit))
        bit *= 2
    return value


def both_cores(value):
    other = other_core(value)
    first = lax.axis_index("dp") % 2 == 0
    return jnp.where(first, value, other).astype(F32), jnp.where(first, other, value).astype(F32)


def on_device(
    tokens, cotangent, lengths, norm_one, w_query, w_key, w_value, w_gatez, w_conv_in, w_step, conv_weight,
    conv_bias, step_bias, decay_log, skip_gain, gated_gain, w_attn_out, w_mix_out, norm_two, w_gate, w_up, w_down,
):
    seqs, span, width = tokens.shape
    half = span // 2
    taps, conv_width = conv_weight.shape
    count = lax.axis_size("seq")
    place = lax.axis_index("seq").astype(jnp.int32)
    core = (lax.axis_index("dp") % 2).astype(jnp.int32)
    first = place * span
    mirrored = (count - 1 - place) * span + half
    inverse = 1.0 / ROPE_BASE ** (jnp.arange(0, HEAD, 2).astype(F32) / HEAD)

    def tables(positions):
        angles = positions.astype(F32)[:, None] * inverse[None, :]
        return jnp.cos(angles), jnp.sin(angles)

    cosine, sine = tables(first + jnp.arange(span))
    cos_row = jnp.concatenate([cosine] * 4, 1)
    sin_row = jnp.concatenate([-sine, sine] * 2, 1)
    cos_back, sin_back = tables(jnp.concatenate([first + jnp.arange(half), mirrored + jnp.arange(half)]))
    rate = -jnp.exp(decay_log)
    pad = (0, 128 - SSM_HEADS)
    rate_row = jnp.pad(rate, pad)[None]
    step_row = jnp.pad(step_bias, pad)[None]
    w_step_wide = jnp.pad(w_step, ((0, 0), pad))
    skip_row = jnp.repeat(skip_gain, SSM_HEAD)[None]
    ones = (np.arange(WIDE)[None, :] // SSM_HEAD == np.arange(128)[:, None]).astype(np.float32)
    expand = jnp.asarray(np.concatenate([ones, ones], 0), BF16)
    pos = first[None]
    rows = min(256, half)
    blocks = jnp.concatenate([base + jnp.arange(0, half, rows, dtype=jnp.int32) for base in (first, mirrored)])
    sources = lax.rem(place - jnp.arange(count, dtype=jnp.int32) + count, count)
    here = place[None]

    halo = along(tokens[:, span - 16 :], 1)
    hidden, q, kv = enter(after(tokens, halo), norm_one[None], w_query, w_key, w_value, cos_row, sin_row)
    kvs = [kv] + [ring(kv, r) for r in range(1, count)]
    q_other = mirror(q[:, half:])
    z, conv, pre, x, bk, cq, dt, sg, cum, cumt, state = mixer(
        pos, lengths, hidden, halo, norm_one[None], w_gatez, w_conv_in, w_step_wide, conv_weight, conv_bias[None],
        step_row, rate_row * LOG2E, expand,
    )
    states = lax.all_gather(state, "seq")
    o_near, o_far, lse = attend(blocks, lengths, sources, after(q, state), q_other, kvs)
    o_back = mirror(o_far)
    mixed, mix_low, held = scan_forward(
        here, after(x, o_near), bk, cq, dt, cum, cumt, skip_row, z, gated_gain[None], expand, states
    )
    (
        output, hidden_two, act, grad_ffn, grad_gate, grad_up, grad_mid, grad_branch, do_near, do_far, grad_mixed,
        grad_z, attn, g_norm_two, g_gated, adjoint,
    ) = middle(
        pos, lengths, o_near, o_back, mix_low, tokens, cotangent, mixed, z, cq, cum, w_attn_out, w_mix_out, w_gate,
        w_up, w_down, norm_two[None], gated_gain[None], expand,
    )
    adjoints = [along(adjoint, -r) for r in range(1, count)]
    do_other = mirror(do_far)

    def flat(v):
        return v.reshape(seqs * span, v.shape[2])

    mine = jnp.stack([core, place])
    yours = jnp.stack([1 - core, place])
    hid = flat(hidden)
    ffn = (flat(hidden_two), (flat(grad_gate), flat(grad_up)), 512, count)
    outs = ((flat(act), flat(attn), flat(mix_low)), (flat(grad_ffn), flat(grad_branch), flat(grad_branch)), count)

    square = "hops" if count == 4 else ""
    sent_out = wide_grad(yours, *outs, name="grad_outs")
    got_out = other_core(sent_out)
    sent_ffn = tall_grad(after(yours, sent_out), *ffn, name="grad_ffn_in")
    got_ffn = other_core(sent_ffn)
    part_out = wide_grad(after(mine, sent_ffn), *outs, got_out, square, name="grad_outs")
    part_ffn = tall_grad(after(mine, part_out), *ffn, got_ffn, name="grad_ffn_in")
    ffn_sum = scatter_seq(part_ffn)
    grad_conv, tail, head, g_conv_small, g_skip, g_small = scan_backward(
        after(x, part_ffn), bk, cq, dt, sg, cum, cumt, grad_mixed, mixed, held, pre, conv, skip_row, rate_row,
        conv_weight, expand, adjoints,
    )
    out_held = first_hop(part_out) if square else scatter_seq(part_out)
    head = after(head, out_held)
    returned = along(low(head), -1).astype(F32)[:, : taps - 1]
    g_conv_weight = g_conv_small[:taps]
    for ahead in range(1, taps):
        tap = taps - 1 - ahead
        fill = jnp.pad(returned[:, :ahead], ((0, 0), (8 - ahead, 0), (0, 0)))
        tail = tail + conv_weight[tap] * fill
        g_conv_weight = g_conv_weight.at[tap].add(jnp.sum(fill * conv[:, span - 8 :].astype(F32), (0, 1)))
    grad_conv = lax.dynamic_update_slice(grad_conv, low(tail), (0, span - 8, 0))
    inside = (hid, (flat(grad_z), flat(grad_conv)), 256, count)
    sent_in = tall_grad(yours, *inside, name="grad_mixer_in")
    got_in = other_core(sent_in)
    gh = leave_mixer(after(grad_z, sent_in), grad_conv, w_gatez, w_conv_in, w_step_wide)
    out_sum = second_hop(out_held) if square else out_held
    part_in = tall_grad(
        after(mine, gh, out_sum, ffn_sum), *inside, got_in, "direct" if square else "", name="grad_mixer_in"
    )
    ffn_sum, out_sum = offloaded_sum_z((ffn_sum, out_sum))

    def back(group, order):
        near, far, parts = attend_backward(
            group, blocks, lengths, sources, after(q, *order), q_other, do_near, do_other, o_near, o_far, lse,
            cos_back.T, sin_back.T, kvs,
        )
        return near, mirror(far), [parts[0]] + [ring(parts[r], -r) for r in range(1, count)]

    dq_near, dq_far, pieces = back(0, (part_in[0],))
    in_sum = direct_sum(part_in) if square else scatter_seq(part_in)
    results = back(1, (dq_near, in_sum))
    in_sum = sum_z(in_sum, 2, 4)
    grad_tokens, g_norm_one, grad_q, grad_kv = leave(
        tokens, grad_mid, after(gh, in_sum, ffn_sum), norm_one[None], w_query, w_key, w_value, cos_row, sin_row,
        (dq_near, results[0]), (dq_far, results[1]), pieces + results[2],
    )
    in_sum = sum_z(in_sum, 4)
    heads = (hid, (flat(grad_q), flat(grad_kv)), 128, count)
    sent_qkv = tall_grad(yours, *heads, name="grad_qkv")
    part_qkv = tall_grad(mine, *heads, other_core(sent_qkv), square, name="grad_qkv")
    qkv_sum = sum_z(second_hop(first_hop(part_qkv)) if square else scatter_seq(part_qkv))

    def spread(value, chunk_rows, chunks):
        return [
            [v[(a * chunk_rows) : (b * chunk_rows)].reshape(b - a, chunk_rows, -1) for a, b in chunks]
            for v in both_cores(value)
        ]

    def columns(pair):
        return jnp.concatenate([v[i] for v in pair for i in range(v.shape[0])], 1)

    block = width // count
    s_gate, s_up = [columns(p) for p in zip(*spread(ffn_sum, block, ((0, 2), (2, 4))))]
    z_steps, c_steps = WIDE // 512, (conv_width + 256) // 512
    s_gatez, s_conv = [columns(p) for p in zip(*spread(in_sum, block, ((0, z_steps), (z_steps, z_steps + c_steps))))]
    s_query, s_kv = [columns(p) for p in zip(*spread(qkv_sum, block, ((0, 2), (2, 3))))]
    out_all = jnp.concatenate(both_cores(out_sum), 1)
    a, b = w_down.shape[0] // count, w_attn_out.shape[0] // count
    s_down, s_attn_out, s_mix_out = out_all[:a], out_all[a : a + b], out_all[a + b :]

    small = [
        g_norm_one[0], g_norm_two[0], g_gated[0], g_conv_weight.reshape(-1), g_conv_small[taps], g_skip[0],
        g_small[0], g_small[1],
    ]
    sizes = [v.shape[0] for v in small]
    total = jnp.concatenate(small)
    bit = 1
    while bit < lax.axis_size("dp"):
        total = total + flip_dp(total, bit)
        bit *= 2
    bit = 1
    while bit < count:
        total = total + lax.ppermute(total, "seq", [(i, i ^ bit) for i in range(count)])
        bit *= 2
    starts = np.cumsum([0] + sizes)
    small = [total[a:b] for a, b in zip(starts[:-1], starts[1:])]

    def own(v):
        n = v.shape[0] // count
        return lax.dynamic_slice(v, (place * n,), (n,))

    s_norm_one, s_norm_two, s_gated = [own(v) for v in small[:3]]
    s_skip = jnp.sum(small[5].reshape(SSM_HEADS, SSM_HEAD), 1)
    return (
        output,
        grad_tokens,
        s_norm_one,
        s_query,
        s_kv[:, :128],
        s_kv[:, 128:],
        s_gatez,
        s_conv[:, :conv_width],
        s_conv[:, conv_width : conv_width + SSM_HEADS],
        small[3].reshape(taps, -1),
        small[4],
        small[7][:SSM_HEADS],
        small[6][:SSM_HEADS],
        s_skip,
        s_gated,
        s_attn_out,
        s_mix_out,
        s_norm_two,
        s_gate,
        s_up,
        s_down,
    )


def solution(mesh):
    copied = (P(),) * 19
    return jax.shard_map(
        on_device,
        mesh=mesh,
        in_specs=(P("dp", "seq", None), P("dp", "seq", None), P("dp")) + copied,
        out_specs=(
            P("dp", "seq", None), P("dp", "seq", None), P("seq"),
            P("seq", None), P("seq", None), P("seq", None), P("seq", None), P("seq", None), P("seq", None),
            P(), P(), P(), P(), P(),
            P("seq"), P("seq", None), P("seq", None), P("seq"), P("seq", None), P("seq", None), P("seq", None),
        ),
        check_vma=False,
    )
```

time: 990 us -> 560 us (0.57)
  waiting for transfers between devices: 601 us -> 77.1 us
  Pallas kernels: 197 us -> 340 us
  matrix products: 65.1 us -> 0 us
  starting transfers between devices: 6.34 us -> 66.9 us
  blocking collectives: 47.5 us -> 0 us
    reduce_scatter x12 -> x0, waiting for transfers between devices: 456 us -> none  [the longest x11 392 us: reduced(): part = lax.psum_scatter(g, 'seq', scatter_dimension=0, tiled=True)]
    pallas_call x5 -> x15, Pallas kernels: 110 us -> 208 us  [the longest x6 53.9 us: tall_grad(): pl.pallas_call(functools.partial(tall_body, n=n, widths=widths, with_got=...]
    psum x1, waiting for transfers between devices: 77.8 us -> 0.02 us  [offloaded_sum_z(): lax.psum(value, 'dp', axis_index_groups=[list(range(c, n, 2)) for c in ra...]
    ppermute x2 -> x47, waiting for transfers between devices: 3.24 us -> 77 us  [the longest x15 46.4 us: flip_dp(): return lax.ppermute(value, 'dp', [(i, i ^ bit) for i in range(n)])]
    dot_general x13 -> x0, matrix products: 65.1 us -> none  [the longest x11 64.8 us: weight_grad(): jnp.einsum('sck,scm->km', left, grad, preferred_element_type=F32)]
    ppermute x2 -> x47, starting transfers between devices: 5.21 us -> 66.5 us  [the longest x15 27.7 us: flip_dp(): return lax.ppermute(value, 'dp', [(i, i ^ bit) for i in range(n)])]
    pallas_call x1 -> x2, Pallas kernels: 28.6 us -> 71.8 us  [attend_backward(): pl.pallas_call(functools.partial(attend_back_body, rows=rows, keys=keys,...]
    all_gather x2 -> x0, waiting for transfers between devices: 41.4 us -> none  [the longest x1 22.2 us: on_device(): adjoints = lax.all_gather(adjoint, 'seq')]
  transfers between devices with their start and end apart: 18 -> 50, of which waited for: 15 -> 15; matrix products, arithmetic and copies ran while one was open for 9% -> 8% of each run, Pallas kernels for 10% -> 45%
where the time goes in v2:
time: 560 us; the launch traced here: 552 us
  Pallas kernels  340 us (61%)
  waiting for transfers between devices  77.1 us (14%)
  starting transfers between devices  66.9 us (12%)
  other arithmetic  31.3 us (6%)
  local copies, waits for them, and re-layouts  21.2 us (4%)
  between operations  15.4 us (3%)
    pallas_call x2, Pallas kernels, attend_backward(): pl.pallas_call(functools.partial(attend_back_body, rows=rows, keys=keys,...  71.8 us
    pallas_call x1, Pallas kernels, middle(): pl.pallas_call(functools.partial(middle_body, rows=rows, blocks=blocks, s...  59.8 us
    pallas_call x6, Pallas kernels, tall_grad(): pl.pallas_call(functools.partial(tall_body, n=n, widths=widths, with_got=...  53.9 us
    ppermute x15, waiting for transfers between devices, flip_dp(): return lax.ppermute(value, 'dp', [(i, i ^ bit) for i in range(n)])  46.4 us
    pallas_call x1, Pallas kernels, scan_backward(): pl.pallas_call(functools.partial(scan_back_body, chunks=chunks, conv_widt...  35.6 us
    pallas_call x1, Pallas kernels, attend(): pl.pallas_call(functools.partial(attend_body, rows=rows, keys=keys, block...  28.8 us
    ppermute x15, starting transfers between devices, flip_dp(): return lax.ppermute(value, 'dp', [(i, i ^ bit) for i in range(n)])  27.7 us
    pallas_call x2, Pallas kernels, wide_grad(): pl.pallas_call(functools.partial(wide_body, parts=len(lefts), group=n //...  22.1 us
  transfers between devices with their start and end apart: 50, of which 15 were waited for; matrix products, arithmetic and copies ran while one was open for 8% of the time, Pallas kernels for 45%

profile of v2, /device:TPU:1, one launch (start us, length us, event | category | flops | bytes accessed | tf_op | source)
XLA Modules:
  0.0 551.5 jit_solution(18061693559336324092)
XLA Ops:
  22.9 7.2 %enter.1 = (bf16[1,1024,1024]{2,1,0:T(8,128)(2,1)}, bf16[1,1024,512]{2,1,0:T(8,128)(2,1)}, bf16[1,1024,256]{2,1,0:T(8,128)(2,1)}) custom-call(bf16[1,1024,1024]{2,1,0:T(8,128)(2,1)} %tok_ref.4, f32[1,1024]{1,0:T(1,128)} %bitcast.107, bf16[1024,512]{1,0:T(8,128)(2,1)} %wq_ref.3, bf16[1024,128]{1,0:T(8,128)(2,1)} %wk_ref.3, bf16[1024,128]{1,0:T(8,128)(2,1)} %wv_ref.3, ...), custom_call_target="tpu_custom_call" | custom-call | flops 24000000000 | bytes 800000 | tf_op jit(solution)/shard_map/enter/pallas_call | solution.py:126
  35.1 21.0 %mixer.1 = (bf16[1,1024,1536]{2,1,0:T(8,128)(2,1)}, bf16[1,1024,1792]{2,1,0:T(8,128)(2,1)}, bf16[1,1024,1792]{2,1,0:T(8,128)(2,1)}, bf16[1,1024,1536]{2,1,0:T(8,...) custom-call(s32[1]{0:T(128)} %bitcast.pos_ref, ...), custom_call_target="tpu_custom_call" | custom-call | flops 60000002048 | bytes 2000000 | tf_op jit(solution)/shard_map/mixer/pallas_call | solution.py:214
  57.6 8.6 %collective-permute-done.1.other_ref = bf16[1,512,512]{2,1,0:T(8,128)(2,1)S(1)} collective-permute-done((bf16[1,512,512]{2,1,0:T(8,128)(2,1)S(1)}, bf16[1,512,512]{2,1,0:T(8,128)(2,1)S(1)}, u32[]{:S(2)}, u32[]{:S(2)}) %collective-permute-start.1) | collective-permute-done | bytes 524320 | tf_op jit(solution)/shard_map/ppermute | solution.py:1177
  67.0 28.8 %attend.1 = (bf16[1,512,512]{2,1,0:T(8,128)(2,1)}, bf16[1,512,512]{2,1,0:T(8,128)(2,1)}, f32[1,8,1024]{2,1,0:T(8,128)}) custom-call(s32[4]{0:T(128)} %pad_add_fusion.pos_ref, s32[1]{0:T(128)S(6)} %copy.77.len_ref, s32[4]{0:T(128)} %compare_select_fusion.from_ref, bf16[1,1024,512]{2,1,0:T(8,128)(2,1)} %get-tuple-element.201.q_ref, ...), custom_call_target="tpu_custom_call" | custom-call | flops 77999996928 | bytes 2600000 | tf_op jit(solution)/shard_map/attend/pallas_call | solution.py:853
  97.2 16.5 %scan_forward.1 = (f32[1,1024,1536]{2,1,0:T(8,128)}, bf16[1,1024,1536]{2,1,0:T(8,128)(2,1)}, bf16[1,8,128,1536]{3,2,1,0:T(8,128)(2,1)}) custom-call(s32[1]{0:T(128)} %bitcast.4.place_ref, bf16[1,1024,1536]{2,1,0:T(8,128)(2,1)} %get-tuple-element.178.x_ref, bf16[1,1024,128]{2,1,0:T(8,128)(2,1)} %get-tuple-element.152.bk_ref, ...), custom_call_target="tpu_custom_call" | custom-call | flops 48000000000 | bytes 1600000 | tf_op jit(solution)/shard_map/scan_forward/pallas_call | solution.py:313
  114.5 59.8 %middle.1 = (bf16[1,1024,1024]{2,1,0:T(8,128)(2,1)}, bf16[1,1024,1024]{2,1,0:T(8,128)(2,1)}, bf16[1,1024,2048]{2,1,0:T(8,128)(2,1)}, bf16[1,1024,1024]{2,1,0:T(8...) custom-call(s32[1]{0:T(128)} %bitcast.pos_ref, ...), custom_call_target="tpu_custom_call" | custom-call | flops 179999997952 | bytes 6000000 | tf_op jit(solution)/shard_map/middle/pallas_call | solution.py:448
  174.3 10.2 %grad_outs.2 = bf16[4,1024,512]{2,1,0:T(8,128)(2,1)} custom-call(s32[2]{0:T(128)} %pad_add_fusion.1.sel_ref, bf16[1024,2048]{1,0:T(8,128)(2,1)} %bitcast.88, bf16[1024,512]{1,0:T(8,128)(2,1)} %bitcast.98, bf16[1024,1536]{1,0:T(8,128)(2,1)} %bitcast.90, bf16[1024,1024]{1,0:T(8,128)(2,1)} %bitcast.94, bf16[1024,1024]{1,0:T(8,128)(2,1)} %bitcast.78, ...), custom_call_target="tpu_custom_call" | custom-call | tf_op jit(solution)/shard_map/grad_outs/pallas_call | solution.py:1148
  187.7 9.8 %grad_ffn_in.2 = bf16[4,1024,512]{2,1,0:T(8,128)(2,1)} custom-call(s32[2]{0:T(128)} %pad_add_fusion.1.sel_ref, bf16[1024,1024]{1,0:T(8,128)(2,1)} %bitcast.92, bf16[1024,2048]{1,0:T(8,128)(2,1)} %bitcast.84, bf16[1024,2048]{1,0:T(8,128)(2,1)} %bitcast.86), custom_call_target="tpu_custom_call" | custom-call | tf_op jit(solution)/shard_map/grad_ffn_in/pallas_call | solution.py:1071
  202.0 11.9 %grad_outs.3 = (bf16[1024,512]{1,0:T(8,128)(2,1)}, bf16[2,512,512]{2,1,0:T(8,128)(2,1)}, bf16[512,512]{1,0:T(8,128)(2,1)}, bf16[2,512,512]{2,1,0:T(8,128)(2,1)}, bf16[512,512]{1,0:T(8,128)(2,1)}) custom-call(s32[2]{0:T(128)} %pad_add_fusion.2.sel_ref, bf16[1024,2048]{1,0:T(8,128)(2,1)} %bitcast.89, bf16[1024,512]{1,0:T(8,128)(2,1)} %bitcast.99, ...), custom_call_target="tpu_custom_call" | custom-call | tf_op jit(solution)/shard_map/grad_outs/pallas_call | solution.py:1148
  218.9 10.2 %grad_ffn_in.3 = bf16[4,1024,512]{2,1,0:T(8,128)(2,1)} custom-call(s32[2]{0:T(128)} %pad_add_fusion.2.sel_ref, bf16[1024,1024]{1,0:T(8,128)(2,1)} %bitcast.93, bf16[1024,2048]{1,0:T(8,128)(2,1)} %bitcast.85, bf16[1024,2048]{1,0:T(8,128)(2,1)} %bitcast.87, bf16[4,1024,512]{2,1,0:T(8,128)(2,1)} %collective-permute-done.7.rest_2_), custom_call_target="tpu_custom_call" | custom-call | tf_op jit(solution)/shard_map/grad_ffn_in/pallas_call | solution.py:1071
  230.1 35.6 %scan_backward.1 = (bf16[1,1024,2048]{2,1,0:T(8,128)(2,1)}, f32[1,8,1792]{2,1,0:T(8,128)}, f32[1,8,1792]{2,1,0:T(8,128)}, f32[8,1792]{1,0:T(8,128)}, f32[1,1536]{1,0:T(1,128)}, /*index=5*/f32[8,128]{1,0:T(8,128)}) custom-call(bf16[1,1024,1536]{2,1,0:T(8,128)(2,1)} %get-tuple-element.178.x_ref, bf16[1,1024,128]{2,1,0:T(8,128)(2,1)} %get-tuple-element.152.bk_ref, ...), custom_call_target="tpu_custom_call" | custom-call | flops 105000001536 | bytes 3500000 | tf_op jit(solution)/shard_map/scan_backward/pallas_call | solution.py:599
  273.0 10.8 %grad_mixer_in.2 = bf16[4,1792,256]{2,1,0:T(8,128)(2,1)} custom-call(s32[2]{0:T(128)} %pad_add_fusion.1.sel_ref, bf16[1024,1024]{1,0:T(8,128)(2,1)} %bitcast.74, bf16[1024,1536]{1,0:T(8,128)(2,1)} %bitcast.82, bf16[1024,2048]{1,0:T(8,128)(2,1)} %bitcast.72), custom_call_target="tpu_custom_call" | custom-call | tf_op jit(solution)/shard_map/grad_mixer_in/pallas_call | solution.py:1071
  291.7 13.1 %leave_mixer.1.gh_ref = f32[1,1024,1024]{2,1,0:T(8,128)} custom-call(bf16[1,1024,1536]{2,1,0:T(8,128)(2,1)} %get-tuple-element.189.gz_ref, bf16[1,1024,2048]{2,1,0:T(8,128)(2,1)} %fusion.17.gc_ref, bf16[1024,1536]{1,0:T(8,128)(2,1)} %wz_ref.3, bf16[1024,1792]{1,0:T(8,128)(2,1)} %wc_ref.3, bf16[1024,128]{1,0:T(8,128)(2,1)} %pad.29.ws_ref), custom_call_target="tpu_custom_call" | custom-call | tf_op jit(solution)/shard_map/leave_mixer/pallas_call | solution.py:645
  304.9 7.5 %collective-permute-done.15 = bf16[512,512]{1,0:T(8,128)(2,1)} collective-permute-done((bf16[512,512]{1,0:T(8,128)(2,1)}, bf16[512,512]{1,0:T(8,128)(2,1)}, u32[]{:S(2)}, u32[]{:S(2)}) %collective-permute-start.15) | collective-permute-done | bytes 524320 | tf_op jit(solution)/shard_map/ppermute | solution.py:1206
  316.8 11.2 %grad_mixer_in.3 = (bf16[1792,256]{1,0:T(8,128)(2,1)}, bf16[1792,256]{1,0:T(8,128)(2,1)}, bf16[1792,256]{1,0:T(8,128)(2,1)}, bf16[1792,256]{1,0:T(8,128)(2,1)}) custom-call(s32[2]{0:T(128)} %pad_add_fusion.2.sel_ref, bf16[1024,1024]{1,0:T(8,128)(2,1)} %bitcast.75, bf16[1024,1536]{1,0:T(8,128)(2,1)} %bitcast.83, bf16[1024,2048]{1,0:T(8,128)(2,1)} %bitcast.73, ...), custom_call_target="tpu_custom_call" | custom-call | tf_op jit(solution)/shard_map/grad_mixer_in/pallas_call | solution.py:1071
  330.7 35.8 %attend_backward.2 = (bf16[1,512,256]{2,1,0:T(8,128)(2,1)}, bf16[1,512,256]{2,1,0:T(8,128)(2,1)}, bf16[1,1024,128]{2,1,0:T(8,128)(2,1)}, bf16[1,1024,128]{2,1,0:...) custom-call(s32[4]{0:T(128)} %pad_add_fusion.pos_ref, s32[1]{0:T(128)S(6)} %copy.77.len_ref, ...), custom_call_target="tpu_custom_call" | custom-call | flops 12000000000 | bytes 400000 | tf_op jit(solution)/shard_map/attend_backward/pallas_call | solution.py:976
  373.2 36.0 %attend_backward.3 = (bf16[1,512,256]{2,1,0:T(8,128)(2,1)}, bf16[1,512,256]{2,1,0:T(8,128)(2,1)}, bf16[1,1024,128]{2,1,0:T(8,128)(2,1)}, bf16[1,1024,128]{2,1,0:...) custom-call(s32[4]{0:T(128)} %pad_add_fusion.pos_ref, s32[1]{0:T(128)S(6)} %copy.77.len_ref, ...), custom_call_target="tpu_custom_call" | custom-call | flops 12000000000 | bytes 400000 | tf_op jit(solution)/shard_map/attend_backward/pallas_call | solution.py:976
  413.1 7.0 %collective-permute-done.20 = bf16[1792,256]{1,0:T(8,128)(2,1)S(1)} collective-permute-done((bf16[1792,256]{1,0:T(8,128)(2,1)S(1)}, bf16[1792,256]{1,0:T(8,128)(2,1)S(1)}, u32[]{:S(2)}, u32[]{:S(2)}) %collective-permute-start.20) | collective-permute-done | bytes 917536 | tf_op jit(solution)/shard_map/ppermute | solution.py:1182
  426.5 9.9 %leave.1 = (f32[1,1024,1024]{2,1,0:T(8,128)}, f32[1,1024]{1,0:T(1,128)}, bf16[1,1024,512]{2,1,0:T(8,128)(2,1)}, bf16[1,1024,256]{2,1,0:T(8,128)(2,1)}) custom-call(bf16[1,1024,1024]{2,1,0:T(8,128)(2,1)} %tok_ref.4, f32[1,1024,1024]{2,1,0:T(8,128)} %get-tuple-element.161.gmid_ref, f32[1,1024,1024]{2,1,0:T(8,128)} %leave_mixer.1.gh_ref, f32[1,1024]{1,0:T(1,128)} %bitcast.109, ...), custom_call_target="tpu_custom_call" | custom-call | flops 30000001024 | bytes 1000000 | tf_op jit(solution)/shard_map/leave/pallas_call | solution.py:702
  436.4 5.8 %grad_qkv.2 = bf16[4,768,128]{2,1,0:T(8,128)(2,1)} custom-call(s32[2]{0:T(128)} %pad_add_fusion.1.sel_ref, bf16[1024,1024]{1,0:T(8,128)(2,1)} %bitcast.76, bf16[1024,512]{1,0:T(8,128)(2,1)} %bitcast.96, bf16[1024,256]{1,0:T(8,128)(2,1)} %bitcast.100), custom_call_target="tpu_custom_call" | custom-call | tf_op jit(solution)/shard_map/grad_qkv/pallas_call | solution.py:1071
  442.2 10.3 %collective-permute-start.35 = (bf16[4,768,128]{2,1,0:T(8,128)(2,1)}, bf16[4,768,128]{2,1,0:T(8,128)(2,1)}, u32[]{:S(2)}, u32[]{:S(2)}) collective-permute-start(bf16[4,768,128]{2,1,0:T(8,128)(2,1)} %grad_qkv.2), channel_id=1, source_target_pairs={{0,4},{4,0},{8,12},{12,8},{16,20},{20,16},{24,28},{28,24},{1,5},{5... | collective-permute-start | bytes 2359304 | tf_op jit(solution)/shard_map/ppermute | solution.py:1182
  475.6 6.0 %grad_qkv.3 = (bf16[768,128]{1,0:T(8,128)(2,1)}, bf16[2,512,128]{2,1,0:T(8,128)(2,1)}, bf16[512,128]{1,0:T(8,128)(2,1)}, bf16[2,256,128]{2,1,0:T(8,128)(2,1)}, bf16[256,128]{1,0:T(8,128)(2,1)}) custom-call(s32[2]{0:T(128)} %pad_add_fusion.2.sel_ref, bf16[1024,1024]{1,0:T(8,128)(2,1)} %bitcast.77, bf16[1024,512]{1,0:T(8,128)(2,1)} %bitcast.97, ...), custom_call_target="tpu_custom_call" | custom-call | tf_op jit(solution)/shard_map/grad_qkv/pallas_call | solution.py:1071
  487.9 21.5 %collective-permute-done.43 = bf16[1792,256]{1,0:T(8,128)(2,1)} collective-permute-done((bf16[1792,256]{1,0:T(8,128)(2,1)S(1)}, bf16[1792,256]{1,0:T(8,128)(2,1)}, u32[]{:S(2)}, u32[]{:S(2)}) %collective-permute-start.43) | collective-permute-done | bytes 917536 | tf_op jit(solution)/shard_map/ppermute | solution.py:1182
  527.1 8.1 %collective-permute-done.41 = bf16[768,128]{1,0:T(8,128)(2,1)S(1)} collective-permute-done((bf16[768,128]{1,0:T(8,128)(2,1)S(1)}, bf16[768,128]{1,0:T(8,128)(2,1)S(1)}, u32[]{:S(2)}, u32[]{:S(2)}) %collective-permute-start.41) | collective-permute-done | bytes 196640 | tf_op jit(solution)/shard_map/ppermute | solution.py:1182
  (270 shorter events, 133.6 us)
Async XLA Ops:
  7.2 90.0 %all-gather.3.cloned.1.call-start = ((), (), s32[]{:S(2)}) async-start(), calls=%async_computation.1 | async-start | bytes 2211840 | tf_op jit(solution)/shard_map/all_gather | solution.py:1293
  34.8 31.4 %collective-permute-start.1 = (bf16[1,512,512]{2,1,0:T(8,128)(2,1)S(1)}, bf16[1,512,512]{2,1,0:T(8,128)(2,1)S(1)}, u32[]{:S(2)}, u32[]{:S(2)}) collective-permute-start(bf16[1,512,512]{2,1,0:T(8,128)(2,1)S(1)} %slice.337), channel_id=1, source_target_pairs={{0,3},{1,2},{2,1},{3,0},{4,7},{5,6},{6,5},{7,4},{8,11},{9,10},{10,... | collective-permute-start | bytes 1572872 | tf_op jit(solution)/shard_map/ppermute | solution.py:1177
  56.2 260.6 %reduce-scatter.4.cloned.1.call-start = ((), (), s32[]{:S(2)}) async-start(), calls=%async_computation.2 | async-start | bytes 5242880
  197.6 31.6 %collective-permute-start.10 = (bf16[1,144,1536]{2,1,0:T(8,128)(2,1)S(1)}, bf16[1,144,1536]{2,1,0:T(8,128)(2,1)S(1)}, u32[]{:S(2)}, u32[]{:S(2)}) collective-permute-start(bf16[1,144,1536]{2,1,0:T(8,128)(2,1)S(1)} %copy-done.31), channel_id=1, source_target_pairs={{3,0},{7,4},{11,8},{15,12},{19,16},{23,20},{27,24},{31,28}} | collective-permute-start | bytes 1327112 | tf_op jit(solution)/shard_map/ppermute | solution.py:1172
  198.9 30.4 %collective-permute-start.8 = (bf16[1,144,1536]{2,1,0:T(8,128)(2,1)S(1)}, bf16[1,144,1536]{2,1,0:T(8,128)(2,1)S(1)}, u32[]{:S(2)}, u32[]{:S(2)}) collective-permute-start(bf16[1,144,1536]{2,1,0:T(8,128)(2,1)S(1)} %copy-done.31), channel_id=1, source_target_pairs={{1,0},{2,1},{3,2},{5,4},{6,5},{7,6},{9,8},{10,9},{11,10},{13,12},{... | collective-permute-start | bytes 1327112 | tf_op jit(solution)/shard_map/ppermute | solution.py:1172
  200.2 29.1 %collective-permute-start.9 = (bf16[1,144,1536]{2,1,0:T(8,128)(2,1)S(1)}, bf16[1,144,1536]{2,1,0:T(8,128)(2,1)}, u32[]{:S(2)}, u32[]{:S(2)}) collective-permute-start(bf16[1,144,1536]{2,1,0:T(8,128)(2,1)S(1)} %copy-done.31), channel_id=1, source_target_pairs={{2,0},{3,1},{6,4},{7,5},{10,8},{11,9},{14,12},{15,13},{18,16},{19,... | collective-permute-start | bytes 1327112 | tf_op jit(solution)/shard_map/ppermute | solution.py:1172
  213.9 51.8 %collective-permute-start.12 = (bf16[2,512,512]{2,1,0:T(8,128)(2,1)}, bf16[2,512,512]{2,1,0:T(8,128)(2,1)S(1)}, u32[]{:S(2)}, u32[]{:S(2)}) collective-permute-start(bf16[2,512,512]{2,1,0:T(8,128)(2,1)} %get-tuple-element.175), channel_id=1, source_target_pairs={{0,2},{1,3},{2,0},{3,1},{4,6},{5,7},{6,4},{7,5},{8,10},{9,11},{10,... | collective-permute-start | bytes 3145736 | tf_op jit(solution)/shard_map/ppermute | solution.py:1206
  216.8 49.9 %collective-permute-start.11 = (bf16[2,512,512]{2,1,0:T(8,128)(2,1)}, bf16[2,512,512]{2,1,0:T(8,128)(2,1)S(1)}, u32[]{:S(2)}, u32[]{:S(2)}) collective-permute-start(bf16[2,512,512]{2,1,0:T(8,128)(2,1)} %get-tuple-element.173), channel_id=1, source_target_pairs={{0,1},{1,0},{2,3},{3,2},{4,5},{5,4},{6,7},{7,6},{8,9},{9,8},{10,11... | collective-permute-start | bytes 3145736 | tf_op jit(solution)/shard_map/ppermute | solution.py:1206
  229.1 192.5 %all-reduce.10.cloned.1.call-start = ((), (), s32[]{:S(2)}) async-start(), calls=%async_computation.3 | async-start | bytes 4194304 | tf_op jit(solution)/shard_map/psum | solution.py:1232
  283.8 33.0 %collective-permute-start.16 = (bf16[4,1792,256]{2,1,0:T(8,128)(2,1)}, bf16[4,1792,256]{2,1,0:T(8,128)(2,1)}, u32[]{:S(2)}, u32[]{:S(2)}) collective-permute-start(bf16[4,1792,256]{2,1,0:T(8,128)(2,1)} %grad_mixer_in.2), channel_id=1, source_target_pairs={{0,4},{4,0},{8,12},{12,8},{16,20},{20,16},{24,28},{28,24},{1,5},{5... | collective-permute-start | bytes 11010056 | tf_op jit(solution)/shard_map/ppermute | solution.py:1182
  287.7 42.9 %collective-permute-start.21 = (bf16[1,512,512]{2,1,0:T(8,128)(2,1)}, bf16[1,512,512]{2,1,0:T(8,128)(2,1)}, u32[]{:S(2)}, u32[]{:S(2)}) collective-permute-start(bf16[1,512,512]{2,1,0:T(8,128)(2,1)} %get-tuple-element.198), channel_id=1, source_target_pairs={{0,3},{1,2},{2,1},{3,0},{4,7},{5,6},{6,5},{7,4},{8,11},{9,10},{10,... | collective-permute-start | bytes 1572872 | tf_op jit(solution)/shard_map/ppermute | solution.py:1177
  328.0 40.9 %collective-permute-start.17 = (bf16[1792,256]{1,0:T(8,128)(2,1)}, bf16[1792,256]{1,0:T(8,128)(2,1)S(1)}, u32[]{:S(2)}, u32[]{:S(2)}) collective-permute-start(bf16[1792,256]{1,0:T(8,128)(2,1)} %get-tuple-element.192), channel_id=1, source_target_pairs={{0,1},{1,0},{2,3},{3,2},{4,5},{5,4},{6,7},{7,6},{8,9},{9,8},{10,11... | collective-permute-start | bytes 2752520 | tf_op jit(solution)/shard_map/ppermute | solution.py:1206
  328.7 40.4 %collective-permute-start.18 = (bf16[1792,256]{1,0:T(8,128)(2,1)}, bf16[1792,256]{1,0:T(8,128)(2,1)S(1)}, u32[]{:S(2)}, u32[]{:S(2)}) collective-permute-start(bf16[1792,256]{1,0:T(8,128)(2,1)} %get-tuple-element.193), channel_id=1, source_target_pairs={{0,2},{1,3},{2,0},{3,1},{4,6},{5,7},{6,4},{7,5},{8,10},{9,11},{10,... | collective-permute-start | bytes 2752520 | tf_op jit(solution)/shard_map/ppermute | solution.py:1206
  328.7 41.3 %collective-permute-start.19 = (bf16[1792,256]{1,0:T(8,128)(2,1)}, bf16[1792,256]{1,0:T(8,128)(2,1)}, u32[]{:S(2)}, u32[]{:S(2)}) collective-permute-start(bf16[1792,256]{1,0:T(8,128)(2,1)} %get-tuple-element.194), channel_id=1, source_target_pairs={{0,3},{1,2},{2,1},{3,0},{4,7},{5,6},{6,5},{7,4},{8,11},{9,10},{10,... | collective-permute-start | bytes 2752520 | tf_op jit(solution)/shard_map/ppermute | solution.py:1206
  366.4 42.8 %collective-permute-start.22 = (bf16[1,512,256]{2,1,0:T(8,128)(2,1)}, bf16[1,512,256]{2,1,0:T(8,128)(2,1)S(1)}, u32[]{:S(2)}, u32[]{:S(2)}) collective-permute-start(bf16[1,512,256]{2,1,0:T(8,128)(2,1)} %get-tuple-element.203), channel_id=1, source_target_pairs={{0,3},{1,2},{2,1},{3,0},{4,7},{5,6},{6,5},{7,4},{8,11},{9,10},{10,... | collective-permute-start | bytes 786440 | tf_op jit(solution)/shard_map/ppermute | solution.py:1177
  366.9 43.9 %collective-permute-start.24 = (bf16[1,1024,128]{2,1,0:T(8,128)(2,1)}, bf16[1,1024,128]{2,1,0:T(8,128)(2,1)S(1)}, u32[]{:S(2)}, u32[]{:S(2)}) collective-permute-start(bf16[1,1024,128]{2,1,0:T(8,128)(2,1)} %get-tuple-element.206), channel_id=1, source_target_pairs={{0,3},{1,0},{2,1},{3,2},{4,7},{5,4},{6,5},{7,6},{8,11},{9,8},{10,9... | collective-permute-start | bytes 786440 | tf_op jit(solution)/shard_map/ppermute | solution.py:1167
  368.9 42.8 %collective-permute-start.25 = (bf16[1,1024,128]{2,1,0:T(8,128)(2,1)}, bf16[1,1024,128]{2,1,0:T(8,128)(2,1)}, u32[]{:S(2)}, u32[]{:S(2)}) collective-permute-start(bf16[1,1024,128]{2,1,0:T(8,128)(2,1)} %get-tuple-element.207), channel_id=1, source_target_pairs={{0,2},{1,3},{2,0},{3,1},{4,6},{5,7},{6,4},{7,5},{8,10},{9,11},{10,... | collective-permute-start | bytes 786440 | tf_op jit(solution)/shard_map/ppermute | solution.py:1167
  369.1 52.6 %collective-permute-start.26 = (bf16[1,1024,128]{2,1,0:T(8,128)(2,1)}, bf16[1,1024,128]{2,1,0:T(8,128)(2,1)}, u32[]{:S(2)}, u32[]{:S(2)}) collective-permute-start(bf16[1,1024,128]{2,1,0:T(8,128)(2,1)} %get-tuple-element.208), channel_id=1, source_target_pairs={{0,1},{1,2},{2,3},{3,0},{4,5},{5,6},{6,7},{7,4},{8,9},{9,10},{10,1... | collective-permute-start | bytes 786440 | tf_op jit(solution)/shard_map/ppermute | solution.py:1167
  371.9 48.1 %collective-permute-start.20 = (bf16[1792,256]{1,0:T(8,128)(2,1)S(1)}, bf16[1792,256]{1,0:T(8,128)(2,1)S(1)}, u32[]{:S(2)}, u32[]{:S(2)}) collective-permute-start(bf16[1792,256]{1,0:T(8,128)(2,1)S(1)} %add_convert_fusion.2), channel_id=1, source_target_pairs={{0,8},{4,12},{8,0},{12,4},{16,24},{20,28},{24,16},{28,20},{1,9},{5... | collective-permute-start | bytes 2752520 | tf_op jit(solution)/shard_map/ppermute | solution.py:1182
  442.2 33.4 %collective-permute-start.35 = (bf16[4,768,128]{2,1,0:T(8,128)(2,1)}, bf16[4,768,128]{2,1,0:T(8,128)(2,1)}, u32[]{:S(2)}, u32[]{:S(2)}) collective-permute-start(bf16[4,768,128]{2,1,0:T(8,128)(2,1)} %grad_qkv.2), channel_id=1, source_target_pairs={{0,4},{4,0},{8,12},{12,8},{16,20},{20,16},{24,28},{28,24},{1,5},{5... | collective-permute-start | bytes 2359304 | tf_op jit(solution)/shard_map/ppermute | solution.py:1182
  466.8 42.6 %collective-permute-start.43 = (bf16[1792,256]{1,0:T(8,128)(2,1)S(1)}, bf16[1792,256]{1,0:T(8,128)(2,1)}, u32[]{:S(2)}, u32[]{:S(2)}) collective-permute-start(bf16[1792,256]{1,0:T(8,128)(2,1)S(1)} %add_convert_fusion.1), channel_id=1, source_target_pairs={{0,16},{4,20},{8,24},{12,28},{16,0},{20,4},{24,8},{28,12},{1,17},{... | collective-permute-start | bytes 2752520 | tf_op jit(solution)/shard_map/ppermute | solution.py:1182
  468.2 44.1 %collective-permute-start.46 = (bf16[1024,512]{1,0:T(8,128)(2,1)S(1)}, bf16[1024,512]{1,0:T(8,128)(2,1)}, u32[]{:S(2)}, u32[]{:S(2)}) collective-permute-start(bf16[1024,512]{1,0:T(8,128)(2,1)S(1)} %copy-done.3), channel_id=1, source_target_pairs={{0,4},{4,0},{8,12},{12,8},{16,20},{20,16},{24,28},{28,24},{1,5},{5... | collective-permute-start | bytes 3145736 | tf_op jit(solution)/shard_map/ppermute | solution.py:1182
  471.7 42.4 %collective-permute-start.45 = (bf16[1024,512]{1,0:T(8,128)(2,1)S(1)}, bf16[1024,512]{1,0:T(8,128)(2,1)}, u32[]{:S(2)}, u32[]{:S(2)}) collective-permute-start(bf16[1024,512]{1,0:T(8,128)(2,1)S(1)} %copy-done.2), channel_id=1, source_target_pairs={{0,4},{4,0},{8,12},{12,8},{16,20},{20,16},{24,28},{28,24},{1,5},{5... | collective-permute-start | bytes 3145736 | tf_op jit(solution)/shard_map/ppermute | solution.py:1182
  483.9 27.5 %collective-permute-start.36 = (bf16[2,512,128]{2,1,0:T(8,128)(2,1)}, bf16[2,512,128]{2,1,0:T(8,128)(2,1)S(1)}, u32[]{:S(2)}, u32[]{:S(2)}) collective-permute-start(bf16[2,512,128]{2,1,0:T(8,128)(2,1)} %get-tuple-element.223), channel_id=1, source_target_pairs={{0,1},{1,0},{2,3},{3,2},{4,5},{5,4},{6,7},{7,6},{8,9},{9,8},{10,11... | collective-permute-start | bytes 786440 | tf_op jit(solution)/shard_map/ppermute | solution.py:1206
  (62 other events, 827.9 us)
Sparse Core Ops, SparseCore 0:
  56.3 35.1 all-gather.2
  229.3 58.8 reduce-scatter.3
  316.9 101.3 all-reduce.9

commit v3 on v2

--- a/solution.py
+++ b/solution.py
@@ -26,7 +26,7 @@
 NN = (((1,), (0,)), ((), ()))
 NT = (((1,), (1,)), ((), ()))
 TN = (((0,), (0,)), ((), ()))
-VMEM_LIMIT = 60 << 20
+VMEM_LIMIT = 127 << 19
 
 
 def dot(a, b, dims=NN):
@@ -78,6 +78,25 @@
     return pltpu.CompilerParams(
         vmem_limit_bytes=limit, dimension_semantics=("arbitrary", "arbitrary")
     )
+
+
+SCALARS = pl.BlockSpec(memory_space=pltpu.SMEM)
+
+
+def halves_out(core, values, mine_ref, yours_ref):
+    first = core == 0
+    start = 0
+    for value in values:
+        size = value.shape[1] // 2
+        lower, upper = value[:, :size], value[:, size:]
+        mine_ref[0, :, start : start + size] = jnp.where(first, lower, upper)
+        yours_ref[0, :, start : start + size] = jnp.where(first, upper, lower)
+        start += size
+
+
+def halves_in(core, mine, yours):
+    first = core == 0
+    return jnp.concatenate([jnp.where(first, mine, yours), jnp.where(first, yours, mine)], 1)
 
 
 def low_rows(rows):
@@ -260,9 +279,6 @@
     return pl.BlockSpec((states.shape[0], 1) + states.shape[2:], lambda s, c: (0, s, 0, 0), pipeline_mode=pl.Buffered(1))
 
 
-SCALARS = pl.BlockSpec(memory_space=pltpu.SMEM)
-
-
 def scan_body(
     place_ref, x_ref, bk_ref, cq_ref, dt_ref, cum_ref, cumt_ref, skip_ref, z_ref, gain_ref, exp_ref, all_ref,
     mix_ref, low_ref, st_ref, state, y,
@@ -332,58 +348,104 @@
 
 
 def middle_body(
-    pos_ref, len_ref, near_ref, far_ref, mix_ref, tok_ref, cot_ref, mixed_ref, z_ref, cq_ref, cum_ref,
-    wao_ref, wmo_ref, wg_ref, wu_ref, wd_ref, gain2_ref, gated_ref, exp_ref,
-    out_ref, h2_ref, act_ref, gffn_ref, gg_ref, gu_ref, gmid_ref, gb_ref, gnear_ref, gfar_ref, gmixed_ref,
-    gz_ref, attn_ref, gn2_ref, ggain_ref, adj_ref,
-    gn2_s, ggain_s, adj, offset, *, rows, blocks, seqs,
+    pos_ref, len_ref, near_ref, far_ref, mix_ref, tok_ref, cot_ref,
+    wao_ref, wmo_ref, wg_ref, wu_ref, wd_ref, gain2_ref,
+    out_ref, left_ref, mine_ref, yours_ref, gmid_ref, gn2_ref, *, rows, blocks,
 ):
     s = pl.program_id(0)
     b = pl.program_id(1)
 
     @pl.when((s == 0) & (b == 0))
     def _():
-        gn2_s[...] = jnp.zeros_like(gn2_s)
-        ggain_s[...] = jnp.zeros_like(ggain_s)
-
-    @pl.when(b == 0)
-    def _():
-        adj[...] = jnp.zeros_like(adj)
-        offset[...] = jnp.zeros_like(offset)
+        gn2_ref[...] = jnp.zeros_like(gn2_ref)
 
     at = pos_ref[0] + b * rows + lax.broadcasted_iota(jnp.int32, (rows, 1), 0)
     live = jnp.where(at < len_ref[s], 1.0, 0.0)
     attn = jnp.where(b < blocks // 2, near_ref[0], far_ref[0])
-    attn_ref[0] = attn
+    width, ff = wd_ref.shape[1], wd_ref.shape[0]
+    left_ref[0, :, width + ff :] = attn
     branch = dot(attn, wao_ref[...]) + dot(mix_ref[0], wmo_ref[...])
     after = tok_ref[0].astype(F32) + live * branch
     scale = lax.rsqrt(jnp.mean(after * after, -1, keepdims=True) + EPS)
     unit = after * scale
     gain = gain2_ref[...]
     h2 = low(unit * gain)
-    h2_ref[0] = h2
+    left_ref[0, :, :width] = h2
     gate = dot(h2, wg_ref[...])
     up = dot(h2, wu_ref[...])
     sg = sigmoid(gate)
     silu = gate * sg
     act = low(silu * up)
-    act_ref[0] = act
+    left_ref[0, :, width : width + ff] = act
     out_ref[0] = low(after + live * dot(act, wd_ref[...]))
     cot = cot_ref[0].astype(F32)
     gffn = low(live * cot)
-    gffn_ref[0] = gffn
     gact = dot(gffn, wd_ref[...], NT)
     gg = low(gact * up * (sg * (1.0 + gate * (1.0 - sg))))
     gu = low(gact * silu)
-    gg_ref[0] = gg
-    gu_ref[0] = gu
     gh2 = dot(gg, wg_ref[...], NT) + dot(gu, wu_ref[...], NT)
-    gn2_s[...] += jnp.sum(gh2 * unit, 0, keepdims=True)
+    gn2_ref[...] += jnp.sum(gh2 * unit, 0, keepdims=True)
     g = gh2 * gain
     gmid = cot + scale * (g - unit * jnp.mean(g * unit, -1, keepdims=True))
     gmid_ref[0] = gmid
-    gb = low(live * gmid)
-    gb_ref[0] = gb
+    halves_out(pos_ref[1], (gg, gu, gffn, low(live * gmid)), mine_ref, yours_ref)
+
+
+def middle(pos, lens, near, far, mix, tokens, cot, wao, wmo, wg, wu, wd, gain2):
+    seqs, span, width = tokens.shape
+    rows = min(256, span // 2)
+    blocks = span // rows
+    ff = wg.shape[1]
+    lower = pl.BlockSpec((1, rows, 512), lambda s, b, *_: (s, jnp.minimum(b, blocks // 2 - 1), 0))
+    upper = pl.BlockSpec((1, rows, 512), lambda s, b, *_: (s, jnp.maximum(b - blocks // 2, 0), 0))
+
+    def row(n):
+        return pl.BlockSpec((1, rows, n), lambda s, b, *_: (s, b, 0))
+
+    def shape(n, kind):
+        return jax.ShapeDtypeStruct((seqs, span, n), kind)
+
+    return pl.pallas_call(
+        functools.partial(middle_body, rows=rows, blocks=blocks),
+        grid_spec=pltpu.PrefetchScalarGridSpec(
+            num_scalar_prefetch=2,
+            grid=(seqs, blocks),
+            in_specs=[lower, upper, row(WIDE), row(width), row(width)]
+            + [full_spec(v.shape) for v in (wao, wmo, wg, wu, wd, gain2)],
+            out_specs=[
+                row(width), row(width + ff + 512), row(width + ff), row(width + ff), row(width),
+                pl.BlockSpec((1, width), lambda s, b, *_: (0, 0)),
+            ],
+        ),
+        out_shape=[
+            shape(width, BF16), shape(width + ff + 512, BF16), shape(width + ff, BF16), shape(width + ff, BF16),
+            shape(width, F32),
+            jax.ShapeDtypeStruct((1, width), F32),
+        ],
+        compiler_params=params(),
+        cost_estimate=cost(45),
+        name="middle",
+    )(pos, lens, near, far, mix, tokens, cot, wao, wmo, wg, wu, wd, gain2)
+
+
+def branch_body(
+    core_ref, gb_m, gb_y, mixed_ref, z_ref, cq_ref, cum_ref, wao_ref, wmo_ref, gated_ref, exp_ref,
+    gnear_ref, gfar_ref, gmixed_ref, gz_m, gz_y, ggain_ref, adj_ref, adj, offset, *, rows, blocks,
+):
+    s = pl.program_id(0)
+    b = pl.program_id(1)
+
+    @pl.when((s == 0) & (b == 0))
+    def _():
+        ggain_ref[...] = jnp.zeros_like(ggain_ref)
+
+    @pl.when(b == 0)
+    def _():
+        adj[...] = jnp.zeros_like(adj)
+        offset[...] = jnp.zeros_like(offset)
+
+    core = core_ref[0]
+    gb = halves_in(core, gb_m[0], gb_y[0])
     gattn = low(dot(gb, wao_ref[...], NT))
 
     @pl.when(b < blocks // 2)
@@ -402,12 +464,12 @@
     v = mixed * silu
     scale = lax.rsqrt(jnp.mean(v * v, -1, keepdims=True) + EPS)
     unit = v * scale
-    ggain_s[...] += jnp.sum(gn * unit, 0, keepdims=True)
+    ggain_ref[...] += jnp.sum(gn * unit, 0, keepdims=True)
     g = gn * gated_ref[...]
     g = scale * (g - unit * jnp.mean(g * unit, -1, keepdims=True))
     gmixed = g * silu
     gmixed_ref[0] = low(gmixed)
-    gz_ref[0] = low(g * mixed * (sg * (1.0 + z * (1.0 - sg))))
+    halves_out(core, (low(g * mixed * (sg * (1.0 + z * (1.0 - sg)))),), gz_m, gz_y)
     cum = cum_ref[0]
     logs = []
     for c in range(rows // CHUNK):
@@ -422,69 +484,49 @@
         adj_ref[0, :STATE] = low(adj[...])
         adj_ref[0, STATE:] = total_rows(offset[...], exp_ref[...])
 
-    @pl.when((s == seqs - 1) & (b == blocks - 1))
-    def _():
-        gn2_ref[...] = gn2_s[...]
-        ggain_ref[...] = ggain_s[...]
-
-
-def middle(pos, lens, near, far, mix, tokens, cot, mixed, z, cq, cum, wao, wmo, wg, wu, wd, gain2, gated, expand):
-    seqs, span, width = tokens.shape
+
+def branch_back(core, mine, yours, mixed, z, cq, cum, wao, wmo, gated, expand):
+    seqs, span, packed = mine.shape
+    half_width = wao.shape[1] // 2
+    gb = pl.BlockSpec((1, min(256, span // 2), half_width), lambda s, b: (s, b, packed // half_width - 1))
     rows = min(256, span // 2)
     blocks = span // rows
-    ff = wg.shape[1]
-    lower = pl.BlockSpec((1, rows, 512), lambda s, b, *_: (s, jnp.minimum(b, blocks // 2 - 1), 0))
-    upper = pl.BlockSpec((1, rows, 512), lambda s, b, *_: (s, jnp.maximum(b - blocks // 2, 0), 0))
+    lower = pl.BlockSpec((1, rows, 512), lambda s, b: (s, jnp.minimum(b, blocks // 2 - 1), 0))
+    upper = pl.BlockSpec((1, rows, 512), lambda s, b: (s, jnp.maximum(b - blocks // 2, 0), 0))
 
     def row(n):
-        return pl.BlockSpec((1, rows, n), lambda s, b, *_: (s, b, 0))
+        return pl.BlockSpec((1, rows, n), lambda s, b: (s, b, 0))
 
     def shape(n, kind):
         return jax.ShapeDtypeStruct((seqs, span, n), kind)
 
-    def once(n):
-        return pl.BlockSpec((1, n), lambda s, b, *_: (0, 0))
-
+    half = jax.ShapeDtypeStruct((seqs, span // 2, 512), BF16)
     return pl.pallas_call(
-        functools.partial(middle_body, rows=rows, blocks=blocks, seqs=seqs),
-        grid_spec=pltpu.PrefetchScalarGridSpec(
-            num_scalar_prefetch=2,
-            grid=(seqs, blocks),
-            in_specs=[
-                lower, upper, row(WIDE), row(width), row(width), row(WIDE), row(WIDE), row(STATE), row(128),
-                full_spec(wao.shape), full_spec(wmo.shape), full_spec(wg.shape), full_spec(wu.shape),
-                full_spec(wd.shape), full_spec(gain2.shape), full_spec(gated.shape), full_spec(expand.shape),
-            ],
-            out_specs=[
-                row(width), row(width), row(ff), row(width), row(ff), row(ff), row(width), row(width),
-                lower, upper, row(WIDE), row(WIDE), row(512),
-                once(width), once(WIDE),
-                pl.BlockSpec((1, STATE + 16, WIDE), lambda s, b, *_: (s, 0, 0)),
-            ],
-            scratch_shapes=[
-                pltpu.VMEM((1, width), F32), pltpu.VMEM((1, WIDE), F32), pltpu.VMEM((STATE, WIDE), F32),
-                pltpu.VMEM((1, 128), F32),
-            ],
-        ),
+        functools.partial(branch_body, rows=rows, blocks=blocks),
+        grid=(seqs, blocks),
+        in_specs=[SCALARS, gb, gb, row(WIDE), row(WIDE), row(STATE), row(128)]
+        + [full_spec(v.shape) for v in (wao, wmo, gated, expand)],
+        out_specs=[
+            lower, upper, row(WIDE), row(WIDE // 2), row(WIDE // 2), pl.BlockSpec((1, WIDE), lambda s, b: (0, 0)),
+            pl.BlockSpec((1, STATE + 16, WIDE), lambda s, b: (s, 0, 0)),
+        ],
         out_shape=[
-            shape(width, BF16), shape(width, BF16), shape(ff, BF16), shape(width, BF16), shape(ff, BF16),
-            shape(ff, BF16), shape(width, F32), shape(width, BF16),
-            jax.ShapeDtypeStruct((seqs, span // 2, 512), BF16), jax.ShapeDtypeStruct((seqs, span // 2, 512), BF16),
-            shape(WIDE, BF16), shape(WIDE, BF16), shape(512, BF16),
-            jax.ShapeDtypeStruct((1, width), F32), jax.ShapeDtypeStruct((1, WIDE), F32),
+            half, half, shape(WIDE, BF16), shape(WIDE // 2, BF16), shape(WIDE // 2, BF16),
+            jax.ShapeDtypeStruct((1, WIDE), F32),
             jax.ShapeDtypeStruct((seqs, STATE + 16, WIDE), BF16),
         ],
+        scratch_shapes=[pltpu.VMEM((STATE, WIDE), F32), pltpu.VMEM((1, 128), F32)],
         compiler_params=params(),
-        cost_estimate=cost(60),
-        name="middle",
-    )(pos, lens, near, far, mix, tokens, cot, mixed, z, cq, cum, wao, wmo, wg, wu, wd, gain2, gated, expand)
+        cost_estimate=cost(6),
+        name="branch_back",
+    )(core, mine, yours, mixed, z, cq, cum, wao, wmo, gated, expand)
 
 
 def scan_back_body(
     x_ref, bk_ref, cq_ref, dt_ref, sg_ref, cum_ref, cumt_ref, dy_ref, mix_ref, st_ref, pre_ref, cl_ref,
-    skip_ref, a_ref, cw_ref, exp_ref, *rest, chunks, conv_width,
+    skip_ref, a_ref, cw_ref, exp_ref, core_ref, *rest, chunks, conv_width,
 ):
-    *later, gc_ref, tail_ref, head_ref, gw_ref, gskip_ref, small_ref, adj, after, gact = rest
+    *later, gc_m, gc_y, tail_ref, head_ref, gw_ref, gskip_ref, small_ref, adj, after, gact = rest
     s = pl.program_id(0)
     c = pl.program_id(1)
 
@@ -556,8 +598,6 @@
     gld = dot_exact(jnp.where(t >= u, 1.0, 0.0), gcum) + sums[2 * CHUNK : 2 * CHUNK + 1]
     a = a_ref[...]
     gstep = (direct + a * gld) * sg_ref[0]
-    gc_ref[0, :, conv_width : conv_width + 128] = low(gstep)
-    gc_ref[0, :, conv_width + 128 :] = jnp.zeros((CHUNK, 128), BF16)
     small_ref[0:1] += jnp.sum(dt * gld, 0, keepdims=True) * a
     small_ref[1:2] += jnp.sum(gstep, 0, keepdims=True)
     pre = pre_ref[0].astype(F32)
@@ -573,18 +613,21 @@
         moved = pltpu.roll(ext, CHUNK + 8 - ahead, 0)[:CHUNK]
         gconv = gconv + cw_ref[3 - ahead : 4 - ahead] * moved
         gw_ref[3 - ahead : 4 - ahead] += jnp.sum(conv * moved, 0, keepdims=True)
-    gc_ref[0, :, :conv_width] = low(gconv)
+    everything = jnp.concatenate([low(gconv), low(gstep), jnp.zeros((CHUNK, 128), BF16)], 1)
+    halves_out(core_ref[0], (everything,), gc_m, gc_y)
 
     @pl.when(c == 0)
     def _():
-        tail_ref[0] = gconv[CHUNK - 8 :]
+        tail_ref[0, :, :conv_width] = gconv[CHUNK - 8 :]
+        tail_ref[0, :, conv_width : conv_width + 128] = gstep[CHUNK - 8 :]
+        tail_ref[0, :, conv_width + 128 :] = jnp.zeros((8, 128), F32)
 
     @pl.when(c == chunks - 1)
     def _():
         head_ref[0] = gpre[:8]
 
 
-def scan_backward(x, bk, cq, dt, sg, cum, cumt, dy, mixed, states, pre, conv, skip, a, cw, expand, adjoints):
+def scan_backward(x, bk, cq, dt, sg, cum, cumt, dy, mixed, states, pre, conv, skip, a, cw, expand, core, adjoints):
     seqs, span, _ = x.shape
     chunks = span // CHUNK
     conv_width = pre.shape[2]
@@ -605,16 +648,20 @@
             row(WIDE), row(WIDE),
             pl.BlockSpec((1, 1, STATE, WIDE), lambda s, c: (s, chunks - 1 - c, 0, 0)),
             row(conv_width), row(conv_width),
-            full_spec(skip.shape), full_spec(a.shape), full_spec(cw.shape), full_spec(expand.shape),
+            full_spec(skip.shape), full_spec(a.shape), full_spec(cw.shape), full_spec(expand.shape), SCALARS,
         ]
         + [
             pl.BlockSpec((1, STATE + 16, WIDE), lambda s, c: (s, 0, 0), pipeline_mode=pl.Buffered(1))
             for _ in adjoints
         ],
-        out_specs=[row(conv_width + 256), edge, edge, once(8, conv_width), once(1, WIDE), once(8, 128)],
+        out_specs=[
+            row((conv_width + 256) // 2), row((conv_width + 256) // 2),
+            pl.BlockSpec((1, 8, conv_width + 256), lambda s, c: (s, 0, 0)), edge, once(8, conv_width), once(1, WIDE), once(8, 128),
+        ],
         out_shape=[
-            jax.ShapeDtypeStruct((seqs, span, conv_width + 256), BF16),
-            jax.ShapeDtypeStruct((seqs, 8, conv_width), F32),
+            jax.ShapeDtypeStruct((seqs, span, (conv_width + 256) // 2), BF16),
+            jax.ShapeDtypeStruct((seqs, span, (conv_width + 256) // 2), BF16),
+            jax.ShapeDtypeStruct((seqs, 8, conv_width + 256), F32),
             jax.ShapeDtypeStruct((seqs, 8, conv_width), F32),
             jax.ShapeDtypeStruct((8, conv_width), F32),
             jax.ShapeDtypeStruct((1, WIDE), F32),
@@ -624,18 +671,21 @@
             pltpu.VMEM((STATE, WIDE), F32), pltpu.VMEM((8, conv_width), F32), pltpu.VMEM((CHUNK, conv_width), F32),
         ],
         compiler_params=params(),
-        cost_estimate=cost(35),
+        cost_estimate=cost(4),
         name="scan_backward",
-    )(x, bk, cq, dt, sg, cum, cumt, dy, mixed, states, pre, conv, skip, a, cw, expand, *adjoints)
-
-
-def leave_mixer_body(gz_ref, gc_ref, wz_ref, wc_ref, ws_ref, gh_ref, *, conv_width):
-    gh = dot(gz_ref[0], wz_ref[...], NT) + dot(gc_ref[0, :, :conv_width], wc_ref[...], NT)
-    gh_ref[0] = gh + dot(gc_ref[0, :, conv_width : conv_width + 128], ws_ref[...], NT)
-
-
-def leave_mixer(gz, gc, wz, wc, ws):
-    seqs, span, _ = gz.shape
+    )(x, bk, cq, dt, sg, cum, cumt, dy, mixed, states, pre, conv, skip, a, cw, expand, core, *adjoints)
+
+
+def leave_mixer_body(core_ref, gz_m, gz_y, gc_m, gc_y, wz_ref, wc_ref, ws_ref, gh_ref, *, conv_width):
+    core = core_ref[0]
+    gz = halves_in(core, gz_m[0], gz_y[0])
+    gc = halves_in(core, gc_m[0], gc_y[0])
+    gh = dot(gz, wz_ref[...], NT) + dot(gc[:, :conv_width], wc_ref[...], NT)
+    gh_ref[0] = gh + dot(gc[:, conv_width : conv_width + 128], ws_ref[...], NT)
+
+
+def leave_mixer(core, gz, gc, wz, wc, ws):
+    seqs, span, _ = gz[0].shape
     rows = min(256, span)
 
     def row(n):
@@ -645,27 +695,24 @@
     return pl.pallas_call(
         functools.partial(leave_mixer_body, conv_width=wc.shape[1]),
         grid=(seqs, span // rows),
-        in_specs=[row(gz.shape[2]), row(gc.shape[2])] + [full_spec(v.shape) for v in (wz, wc, ws)],
+        in_specs=[SCALARS]
+        + [row(v.shape[2]) for v in (*gz, *gc)]
+        + [full_spec(v.shape) for v in (wz, wc, ws)],
         out_specs=row(width),
         out_shape=jax.ShapeDtypeStruct((seqs, span, width), F32),
         compiler_params=params(),
         cost_estimate=cost(0),
         name="leave_mixer",
-    )(gz, gc, wz, wc, ws)
-
-
-def leave_body(tok_ref, gmid_ref, gh_ref, gain_ref, wq_ref, wk_ref, wv_ref, cos_ref, sin_ref, *rest, blocks, count):
+    )(core, *gz, *gc, wz, wc, ws)
+
+
+def heads_body(core_ref, cos_ref, sin_ref, *rest, blocks, count):
     near, far = rest[:2], rest[2:4]
     pieces = rest[4 : 4 + 2 * count]
-    gt_ref, gn_ref, gq_ref, gkv_ref = rest[4 + 2 * count :]
+    gq_m, gq_y, gkv_m, gkv_y = rest[4 + 2 * count :]
+    core = core_ref[0]
     b = pl.program_id(1)
-
-    @pl.when((pl.program_id(0) == 0) & (b == 0))
-    def _():
-        gn_ref[...] = jnp.zeros_like(gn_ref)
-
-    for j in range(2):
-        gq_ref[0, :, 256 * j : 256 * j + 256] = jnp.where(b < blocks // 2, near[j][0], far[j][0])
+    halves_out(core, (jnp.concatenate([jnp.where(b < blocks // 2, near[j][0], far[j][0]) for j in range(2)], 1),), gq_m, gq_y)
     sums = []
     for j in range(2):
         t = pieces[j * count][0].astype(F32)
@@ -676,9 +723,44 @@
     gk = jnp.where(lane < 64, sums[0], pltpu.roll(sums[1], 64, 1))
     gv = low(jnp.where(lane < 64, pltpu.roll(sums[0], 64, 1), sums[1]))
     gk = low(gk * cos_ref[...] - swap_halves(gk) * sin_ref[...])
-    gkv_ref[0, :, :128] = gk
-    gkv_ref[0, :, 128:] = gv
-    gh = gh_ref[0] + dot(gq_ref[0], wq_ref[...], NT) + dot(gk, wk_ref[...], NT) + dot(gv, wv_ref[...], NT)
+    halves_out(core, (jnp.concatenate([gk, gv], 1),), gkv_m, gkv_y)
+
+
+def heads_back(core, cosine, sine, near, far, pieces):
+    seqs, half, _ = near[0].shape
+    span = 2 * half
+    rows = min(256, half)
+    blocks = span // rows
+    table = pl.BlockSpec((rows, 128), lambda s, b: (b, 0))
+    lower = pl.BlockSpec((1, rows, 256), lambda s, b: (s, jnp.minimum(b, blocks // 2 - 1), 0))
+    upper = pl.BlockSpec((1, rows, 256), lambda s, b: (s, jnp.maximum(b - blocks // 2, 0), 0))
+
+    def row(n):
+        return pl.BlockSpec((1, rows, n), lambda s, b: (s, b, 0))
+
+    return pl.pallas_call(
+        functools.partial(heads_body, blocks=blocks, count=len(pieces) // 2),
+        grid=(seqs, blocks),
+        in_specs=[SCALARS, table, table, lower, lower, upper, upper] + [row(128)] * len(pieces),
+        out_specs=[row(256), row(256), row(128), row(128)],
+        out_shape=[jax.ShapeDtypeStruct((seqs, span, n), BF16) for n in (256, 256, 128, 128)],
+        compiler_params=params(),
+        cost_estimate=cost(0),
+        name="heads_back",
+    )(core, cosine, sine, *near, *far, *pieces)
+
+
+def leave_body(
+    core_ref, tok_ref, gmid_ref, gh_ref, gq_m, gq_y, gkv_m, gkv_y, gain_ref, wq_ref, wk_ref, wv_ref, gt_ref, gn_ref
+):
+    @pl.when((pl.program_id(0) == 0) & (pl.program_id(1) == 0))
+    def _():
+        gn_ref[...] = jnp.zeros_like(gn_ref)
+
+    core = core_ref[0]
+    gh = gh_ref[0] + dot(halves_in(core, gq_m[0], gq_y[0]), wq_ref[...], NT)
+    gkv = halves_in(core, gkv_m[0], gkv_y[0])
+    gh = gh + dot(gkv[:, :128], wk_ref[...], NT) + dot(gkv[:, 128:], wv_ref[...], NT)
     v = tok_ref[0].astype(F32)
     scale = lax.rsqrt(jnp.mean(v * v, -1, keepdims=True) + EPS)
     unit = v * scale
@@ -687,34 +769,23 @@
     gt_ref[0] = gmid_ref[0] + scale * (g - unit * jnp.mean(g * unit, -1, keepdims=True))
 
 
-def leave(tokens, gmid, gh, gain, wq, wk, wv, cosine, sine, near, far, pieces):
+def leave(core, tokens, gmid, gh, heads, gain, wq, wk, wv):
     seqs, span, width = tokens.shape
-    rows = min(256, span // 2)
-    blocks = span // rows
-    count = len(pieces) // 2
+    rows = min(256, span)
 
     def row(n):
         return pl.BlockSpec((1, rows, n), lambda s, b: (s, b, 0))
 
-    table = pl.BlockSpec((rows, 128), lambda s, b: (b, 0))
-    lower = pl.BlockSpec((1, rows, 256), lambda s, b: (s, jnp.minimum(b, blocks // 2 - 1), 0))
-    upper = pl.BlockSpec((1, rows, 256), lambda s, b: (s, jnp.maximum(b - blocks // 2, 0), 0))
     return pl.pallas_call(
-        functools.partial(leave_body, blocks=blocks, count=count),
-        grid=(seqs, blocks),
-        in_specs=[row(width)] * 3
-        + [full_spec(v.shape) for v in (gain, wq, wk, wv)]
-        + [table, table, lower, lower, upper, upper]
-        + [row(128)] * (2 * count),
-        out_specs=[row(width), pl.BlockSpec((1, width), lambda s, b: (0, 0)), row(512), row(256)],
-        out_shape=[
-            jax.ShapeDtypeStruct((seqs, span, width), F32), jax.ShapeDtypeStruct((1, width), F32),
-            jax.ShapeDtypeStruct((seqs, span, 512), BF16), jax.ShapeDtypeStruct((seqs, span, 256), BF16),
-        ],
+        leave_body,
+        grid=(seqs, span // rows),
+        in_specs=[SCALARS] + [row(width)] * 3 + [row(v.shape[2]) for v in heads] + [full_spec(v.shape) for v in (gain, wq, wk, wv)],
+        out_specs=[row(width), pl.BlockSpec((1, width), lambda s, b: (0, 0))],
+        out_shape=[jax.ShapeDtypeStruct((seqs, span, width), F32), jax.ShapeDtypeStruct((1, width), F32)],
         compiler_params=params(),
-        cost_estimate=cost(10),
+        cost_estimate=cost(0),
         name="leave",
-    )(tokens, gmid, gh, gain, wq, wk, wv, cosine, sine, *near, *far, *pieces)
+    )(core, tokens, gmid, gh, *heads, gain, wq, wk, wv)
 
 
 def dup_halves(v):
@@ -991,18 +1062,24 @@
         ),
         out_shape=[half, half] + [jax.ShapeDtypeStruct((seqs, span, 128), BF16)] * count,
         compiler_params=params(),
-        cost_estimate=cost(4 if group else 4),
+        cost_estimate=cost(1 if group else 20),
         name="attend_backward",
     )(pos, lens, sources, q, other, do_near, do_far, o_near, o_far, lse, cosine, sine, *kvs)
     return outs[0], outs[1], outs[2:]
 
 
-def tall_body(sel_ref, left_ref, *rest, n, widths, with_got, square):
-    rights = rest[: len(widths)]
-    rest = rest[len(widths) :]
-    got_ref = rest[0] if with_got else None
-    outs = rest[1:] if with_got else rest
-    rows = left_ref.shape[1] // n
+def in_hbm(shape):
+    return pltpu.HBM(shape, BF16)
+
+
+def both(left, right):
+    return dot(left[0][...], right[0][...], TN) + dot(left[1][...], right[1][...], TN)
+
+
+def tall_body(place_ref, left_a, left_b, *rest, n, widths, square):
+    rights = [rest[2 * k : 2 * k + 2] for k in range(len(widths))]
+    outs = rest[2 * len(widths) :]
+    rows = left_a.shape[1] // n
     i = pl.program_id(0)
     start = 0
     for part, (right, steps) in enumerate(zip(rights, widths)):
@@ -1014,12 +1091,9 @@
                     own, to_x, keep_x, to_y, keep_y = outs
                     first, keep = ((to_x, keep_x), (to_y, keep_y))[part]
                 for k in range(4):
-                    block = jnp.bitwise_xor(sel_ref[1], k)
+                    block = jnp.bitwise_xor(place_ref[0], k)
                     columns = pl.ds(pl.multiple_of(block * rows, rows), rows)
-                    value = dot(left_ref[:, columns], right[...], TN)
-                    if with_got:
-                        value = value + got_ref[block].astype(F32)
-                    value = low(value)
+                    value = low(both((left_a.at[:, columns], left_b.at[:, columns]), right))
                     if square == "direct":
                         outs[k][...] = value
                     elif k == 0:
@@ -1031,71 +1105,72 @@
                     else:
                         keep[...] = value
             else:
-                value = dot(left_ref[...], right[...], TN)
+                value = low(both((left_a, left_b), right))
                 for j in range(n):
-                    here = value[j * rows : (j + 1) * rows]
-                    outs[0][j] = low(here + got_ref[j].astype(F32) if with_got else here)
+                    outs[0][j] = value[j * rows : (j + 1) * rows]
 
         start += steps
 
 
-def tall_grad(sel, left, rights, chunk, n, got=None, square="", micros=0.0, name="grad"):
-    tokens, width = left.shape
-    widths = [v.shape[1] // 2 // chunk for v in rights]
+def tall_grad(place, left, rights, chunk, n, square="", micros=0.0, name="grad"):
+    tokens, width = left[0].shape[0], left[3]
+    widths = [v[3] // chunk for v in rights]
     steps = sum(widths)
     rows = width // n
     starts = [0, widths[0]]
+    parts = range(len(rights))
 
     def within(k, i):
         return jnp.clip(i - starts[k], 0, widths[k] - 1)
 
     def right_spec(k):
-        return pl.BlockSpec((tokens, chunk), lambda i, sel: (0, sel[0] * widths[k] + within(k, i)))
-
-    whole = pl.BlockSpec((n, rows, chunk), lambda i, sel: (0, i, 0))
-    extra = () if got is None else (got,)
+        return pl.BlockSpec((tokens, chunk), lambda i, place: (0, rights[k][2] // chunk + within(k, i)))
+
+    left_spec = pl.BlockSpec(
+        (tokens, width), lambda i, place: (0, left[2] // width), pipeline_mode=pl.Buffered(1)
+    )
+
     if square == "direct":
-        out_specs = [pl.BlockSpec((rows, chunk), lambda i, sel: (i, 0))] * 4
-        out_shape = [jax.ShapeDtypeStruct((steps * rows, chunk), BF16)] * 4
+        out_specs = [pl.BlockSpec((rows, chunk), lambda i, place: (i, 0))] * 4
+        out_shape = [in_hbm((steps * rows, chunk))] * 4
     elif square:
-        out_specs = [pl.BlockSpec((rows, chunk), lambda i, sel: (i, 0))]
+        out_specs = [pl.BlockSpec((rows, chunk), lambda i, place: (i, 0))]
         out_shape = [jax.ShapeDtypeStruct((steps * rows, chunk), BF16)]
-        for k in range(2):
-            out_specs.append(pl.BlockSpec((2, rows, chunk), lambda i, sel, k=k: (0, within(k, i), 0)))
-            out_specs.append(pl.BlockSpec((rows, chunk), lambda i, sel, k=k: (within(k, i), 0)))
-            out_shape.append(jax.ShapeDtypeStruct((2, widths[k] * rows, chunk), BF16))
+        for k in parts:
+            out_specs.append(pl.BlockSpec((2, rows, chunk), lambda i, place, k=k: (0, within(k, i), 0)))
+            out_specs.append(pl.BlockSpec((rows, chunk), lambda i, place, k=k: (within(k, i), 0)))
+            out_shape.append(in_hbm((2, widths[k] * rows, chunk)))
             out_shape.append(jax.ShapeDtypeStruct((widths[k] * rows, chunk), BF16))
     else:
-        out_specs = whole
+        out_specs = pl.BlockSpec((n, rows, chunk), lambda i, place: (0, i, 0))
         out_shape = jax.ShapeDtypeStruct((n, steps * rows, chunk), BF16)
     return pl.pallas_call(
-        functools.partial(tall_body, n=n, widths=widths, with_got=bool(extra), square=square),
+        functools.partial(tall_body, n=n, widths=widths, square=square),
         grid_spec=pltpu.PrefetchScalarGridSpec(
             num_scalar_prefetch=1,
             grid=(steps,),
-            in_specs=[full_spec(left.shape)] + [right_spec(k) for k in range(2)] + [whole] * len(extra),
+            in_specs=[left_spec] * 2 + [right_spec(k) for k in parts for _ in range(2)],
             out_specs=out_specs,
         ),
         out_shape=out_shape,
         compiler_params=pltpu.CompilerParams(vmem_limit_bytes=VMEM_LIMIT),
         cost_estimate=cost(micros),
         name=name,
-    )(sel, left, *rights, *extra)
-
-
-def wide_body(sel_ref, *rest, parts, group, with_got, square):
-    lefts, rights = rest[:parts], rest[parts : 2 * parts]
-    rest = rest[2 * parts :]
-    got_ref = rest[0] if with_got else None
-    outs = rest[1:] if with_got else rest
-    values = [dot(left[...], right[...], TN) for left, right in zip(lefts, rights)]
+    )(place, *left[:2], *[v for right in rights for v in right[:2]])
+
+
+PIECE = 256
+
+
+def wide_body(place_ref, *rest, parts, group, square, split):
+    lefts = [rest[2 * k : 2 * k + 2] for k in range(parts)]
+    rights = [rest[2 * k : 2 * k + 2] for k in range(parts, 2 * parts)]
+    outs = rest[4 * parts :]
+    values = [low(both(left, right)) for left, right in zip(lefts, rights)]
+    values = [v[:, c : c + PIECE] for v in values for c in range(0, v.shape[1], PIECE)]
     if square:
         own, to_x, keep_x, to_y, keep_y = outs
         value = jnp.concatenate(values, 0)
-        if with_got:
-            value = value + got_ref[0].astype(F32)
-        value = low(value)
-        split = values[0].shape[0]
         for k in range(4):
 
             @pl.when(pl.program_id(0) == k)
@@ -1116,50 +1191,120 @@
             start = 0
             for v in values:
                 rows = v.shape[0] // group
-                here = v[j * rows : (j + 1) * rows]
-                at = slice(start, start + rows)
-                outs[0][j, at] = low(here + got_ref[j, at].astype(F32) if with_got else here)
+                outs[0][j, start : start + rows] = v[j * rows : (j + 1) * rows]
                 start += rows
 
 
-def wide_grad(sel, lefts, rights, n, got=None, square="", micros=0.0, name="grad"):
-    tokens = lefts[0].shape[0]
-    chunk = rights[0].shape[1] // 2
+def wide_grad(place, lefts, rights, n, square="", micros=0.0, name="grad"):
+    tokens = lefts[0][0].shape[0]
     steps = min(n, 4)
-    rows = [v.shape[1] // n for v in lefts]
+    rows = [v[3] // n * (g[3] // PIECE) for v, g in zip(lefts, rights)]
     total = sum(rows)
-
-    def turn(i, sel):
-        return jnp.bitwise_xor(sel[1], i) if square else i
+    split = sum(rows[:2])
+
+    def turn(i, place):
+        return jnp.bitwise_xor(place[0], i) if square else i
 
     def once(*dims):
-        return pl.BlockSpec(dims, lambda i, sel: (0,) * len(dims))
-
-    whole = pl.BlockSpec((n // steps, total, chunk), lambda i, sel: (turn(i, sel), 0, 0))
-    extra = () if got is None else (got,)
+        return pl.BlockSpec(dims, lambda i, place: (0,) * len(dims), pipeline_mode=pl.Buffered(1))
+
+    def left_spec(v):
+        size = v[3] // steps
+        return pl.BlockSpec((tokens, size), lambda i, place: (0, v[2] // size + turn(i, place)))
+
+    def right_spec(v):
+        return pl.BlockSpec((tokens, v[3]), lambda i, place: (0, v[2] // v[3]), pipeline_mode=pl.Buffered(1))
+
     if square:
-        a, b = rows[0], total - rows[0]
-        dims = [(total, chunk), (2, a, chunk), (a, chunk), (2, b, chunk), (b, chunk)]
+        dims = [(total, PIECE)]
+        for size in (split, total - split):
+            dims += [(2, size, PIECE), (size, PIECE)]
         out_specs = [once(*d) for d in dims]
-        out_shape = [jax.ShapeDtypeStruct(d, BF16) for d in dims]
+        out_shape = [in_hbm(d) for d in dims]
     else:
-        out_specs = whole
-        out_shape = jax.ShapeDtypeStruct((n, total, chunk), BF16)
+        out_specs = pl.BlockSpec((n // steps, total, PIECE), lambda i, place: (i, 0, 0))
+        out_shape = jax.ShapeDtypeStruct((n, total, PIECE), BF16)
     return pl.pallas_call(
-        functools.partial(wide_body, parts=len(lefts), group=n // steps, with_got=bool(extra), square=square),
+        functools.partial(wide_body, parts=len(lefts), group=n // steps, square=square, split=split),
         grid_spec=pltpu.PrefetchScalarGridSpec(
             num_scalar_prefetch=1,
             grid=(steps,),
-            in_specs=[pl.BlockSpec((tokens, v.shape[1] // steps), lambda i, sel: (0, turn(i, sel))) for v in lefts]
-            + [pl.BlockSpec((tokens, chunk), lambda i, sel: (0, sel[0])) for _ in rights]
-            + [whole] * len(extra),
+            in_specs=[left_spec(v) for v in lefts for _ in range(2)] + [right_spec(v) for v in rights for _ in range(2)],
             out_specs=out_specs,
         ),
         out_shape=out_shape,
         compiler_params=pltpu.CompilerParams(vmem_limit_bytes=VMEM_LIMIT),
         cost_estimate=cost(micros),
         name=name,
-    )(sel, *lefts, *rights, *extra)
+    )(place, *[v for left in lefts for v in left[:2]], *[v for right in rights for v in right[:2]])
+
+
+def in_place(body, args, outs, name, micros=0):
+    return pl.pallas_call(
+        body,
+        grid=(1,),
+        in_specs=[SCALARS if v.ndim == 1 else full_spec(v.shape) for v in args],
+        out_specs=[full_spec(v.shape) for v in outs],
+        out_shape=outs,
+        compiler_params=pltpu.CompilerParams(vmem_limit_bytes=VMEM_LIMIT),
+        cost_estimate=cost(micros),
+        name=name,
+    )(*args)
+
+
+def like(v):
+    return in_hbm(v.shape)
+
+
+def first_body(keep_x, keep_y, from_x, from_y, to_y, to_x):
+    to_y[...] = low(keep_x[...].astype(F32) + from_x[1].astype(F32))
+    to_x[...] = low(keep_y[...].astype(F32) + from_y[1].astype(F32))
+
+
+def second_body(own, from_x, from_y, late_y, late_x, out):
+    split = late_y.shape[0]
+    for at, first, last in ((slice(0, split), from_x, late_y), (slice(split, None), from_y, late_x)):
+        out[at] = low(own[at].astype(F32) + first[0].astype(F32) + last[...].astype(F32))
+
+
+def sum_body(*refs):
+    total = refs[0][...].astype(F32)
+    for ref in refs[1:-1]:
+        total = total + ref[...].astype(F32)
+    refs[-1][...] = low(total)
+
+
+def square_body(own, one, two, three, out):
+    near = own[...].astype(F32) + one[...].astype(F32)
+    out[...] = low(near + (two[...].astype(F32) + three[...].astype(F32)))
+
+
+def unpack_body(core_ref, own, other, *outs, plan):
+    first = core_ref[0] == 0
+    for out, column, columns, half, start, rows in plan:
+        at = slice(start, start + rows)
+        a, b = (own, other) if half == 0 else (other, own)
+        value = jnp.where(first, a[at], b[at])
+        outs[out][:, column : column + columns] = value[:, :columns].astype(F32)
+
+
+def unpack(core, own, other, matrices):
+    piece = own.shape[1]
+    plan, shapes, start = [], [], 0
+    for rows, pieces, columns in matrices:
+        ends = np.cumsum([0] + list(columns))
+        for half in range(2):
+            for i in range(pieces):
+                column = (half * pieces + i) * piece
+                for k, size in enumerate(columns):
+                    if ends[k] <= column < ends[k + 1]:
+                        offset = int(column - ends[k])
+                        plan.append(
+                            (len(shapes) + k, offset, min(piece, size - offset), half, start + i * rows, rows)
+                        )
+        shapes += [jax.ShapeDtypeStruct((rows, size), F32) for size in columns]
+        start += pieces * rows
+    return in_place(functools.partial(unpack_body, plan=plan), (core, own, other), shapes, "unpack")
 
 
 def ring(value, steps):
@@ -1190,13 +1335,6 @@
     return lax.optimization_barrier((value, done))[0]
 
 
-def add_low(*values):
-    total = values[0].astype(F32)
-    for v in values[1:]:
-        total = total + v.astype(F32)
-    return low(total)
-
-
 def scatter_seq(value):
     return lax.psum_scatter(value, "seq", scatter_dimension=0, tiled=True)[0]
 
@@ -1206,30 +1344,47 @@
     return lax.ppermute(value, "seq", [(i, i ^ bit) for i in range(n)])
 
 
+def add_low(*values):
+    return in_place(sum_body, values, [like(values[0])], "add")[0]
+
+
 def direct_sum(pieces):
     return add_low(pieces[0], *[flip_seq(v, k) for k, v in enumerate(pieces) if k])
 
 
-def first_hop(pieces):
+def first_hop(pieces, *done):
     own, to_x, keep_x, to_y, keep_y = pieces
     from_x, from_y = flip_seq(to_x, 1), flip_seq(to_y, 2)
+    held = in_place(
+        first_body, (after(keep_x, *done), keep_y, from_x, from_y), [like(keep_x), like(keep_y)], "first_hop"
+    )
+    return (*held, own, from_x, from_y)
+
+
+def with_rows(pieces, place, rows):
+    own, to_x, keep_x, to_y, keep_y = pieces
     split = keep_x.shape[0]
-    return (
-        add_low(keep_x, from_x[1]), add_low(keep_y, from_y[1]),
-        own[:split], own[split:], from_x[0], from_y[0],
-    )
-
-
-def second_hop(held):
-    to_y, to_x, own_a, own_b, from_x, from_y = held
-    return jnp.concatenate(
-        [add_low(own_a, from_x, flip_seq(to_y, 2)), add_low(own_b, from_y, flip_seq(to_x, 1))], 0
-    )
-
-
-def offloaded_sum_z(value):
+    mine, beside, below, across = [rows[jnp.bitwise_xor(place, k)] for k in range(4)]
+    own = jnp.concatenate([own[:split], mine, own[split:]], 0)
+    to_x = jnp.concatenate([to_x, jnp.stack([beside, across])], 1)
+    return own, to_x, jnp.concatenate([keep_x, below], 0), to_y, keep_y
+
+
+def second_hop(held, *done):
+    to_y, to_x, own, from_x, from_y = held
+    args = (after(own, *done), from_x, from_y, flip_seq(to_y, 2), flip_seq(to_x, 1))
+    return in_place(second_body, args, [like(own)], "second_hop")[0]
+
+
+def offloaded_sum_z(value, which):
     n = lax.axis_size("dp")
-    return lax.psum(value, "dp", axis_index_groups=[list(range(c, n, 2)) for c in range(2)])
+    groups = [list(range(c, n, 2))[:: -1 if which & 1 else 1] for c in range(2)]
+    return lax.psum(value, "dp", axis_index_groups=groups[:: -1 if which & 2 else 1])
+
+
+def sum_four(value, *done):
+    got = [flip_dp(value, bit) for bit in (2, 4, 6)]
+    return in_place(square_body, (after(value, *done), *got), [like(value)], "add")[0]
 
 
 def sum_z(value, first=2, last=None):
@@ -1238,12 +1393,6 @@
         value = add_low(value, flip_dp(value, bit))
         bit *= 2
     return value
-
-
-def both_cores(value):
-    other = other_core(value)
-    first = lax.axis_index("dp") % 2 == 0
-    return jnp.where(first, value, other).astype(F32), jnp.where(first, other, value).astype(F32)
 
 
 def on_device(
@@ -1276,11 +1425,19 @@
     skip_row = jnp.repeat(skip_gain, SSM_HEAD)[None]
     ones = (np.arange(WIDE)[None, :] // SSM_HEAD == np.arange(128)[:, None]).astype(np.float32)
     expand = jnp.asarray(np.concatenate([ones, ones], 0), BF16)
-    pos = first[None]
+    pos = jnp.stack([first, core])
+    core_here = core[None]
     rows = min(256, half)
     blocks = jnp.concatenate([base + jnp.arange(0, half, rows, dtype=jnp.int32) for base in (first, mirrored)])
     sources = lax.rem(place - jnp.arange(count, dtype=jnp.int32) + count, count)
     here = place[None]
+
+    def flat(v):
+        return v.reshape(seqs * span, v.shape[2])
+
+    def with_other(mine, yours=None):
+        mine, yours = flat(mine), flat(mine if yours is None else yours)
+        return mine, other_core(yours), 0, mine.shape[1]
 
     halo = along(tokens[:, span - 16 :], 1)
     hidden, q, kv = enter(after(tokens, halo), norm_one[None], w_query, w_key, w_value, cos_row, sin_row)
@@ -1296,56 +1453,75 @@
     mixed, mix_low, held = scan_forward(
         here, after(x, o_near), bk, cq, dt, cum, cumt, skip_row, z, gated_gain[None], expand, states
     )
-    (
-        output, hidden_two, act, grad_ffn, grad_gate, grad_up, grad_mid, grad_branch, do_near, do_far, grad_mixed,
-        grad_z, attn, g_norm_two, g_gated, adjoint,
-    ) = middle(
-        pos, lengths, o_near, o_back, mix_low, tokens, cotangent, mixed, z, cq, cum, w_attn_out, w_mix_out, w_gate,
-        w_up, w_down, norm_two[None], gated_gain[None], expand,
+    hid = with_other(hidden)
+    mix_pair = with_other(mix_low)
+    output, lefts, mine, yours, grad_mid, g_norm_two = middle(
+        pos, lengths, o_near, o_back, after(mix_low, hid[1]), tokens, cotangent, w_attn_out, w_mix_out, w_gate, w_up, w_down,
+        norm_two[None],
+    )
+    square = "hops" if count == 4 else ""
+    ff = w_gate.shape[1]
+    lefts, rights = with_other(lefts), with_other(mine, yours)
+    ffn_left = (*lefts[:2], 0, width)
+    ffn_rights = [(*rights[:2], k * ff // 2, ff // 2) for k in range(2)]
+    grad_ffn, grad_branch = [(*rights[:2], ff + k * width // 2, width // 2) for k in range(2)]
+    out_lefts = ((*lefts[:2], width, ff), (*lefts[:2], width + ff, w_attn_out.shape[0]), mix_pair, hid)
+    do_near, do_far, grad_mixed, gz_m, gz_y, g_gated, adjoint = branch_back(
+        core_here, mine, yours, mixed, z, cq, cum, w_attn_out, w_mix_out, gated_gain[None], expand
     )
     adjoints = [along(adjoint, -r) for r in range(1, count)]
     do_other = mirror(do_far)
-
-    def flat(v):
-        return v.reshape(seqs * span, v.shape[2])
-
-    mine = jnp.stack([core, place])
-    yours = jnp.stack([1 - core, place])
-    hid = flat(hidden)
-    ffn = (flat(hidden_two), (flat(grad_gate), flat(grad_up)), 512, count)
-    outs = ((flat(act), flat(attn), flat(mix_low)), (flat(grad_ffn), flat(grad_branch), flat(grad_branch)), count)
-
-    square = "hops" if count == 4 else ""
-    sent_out = wide_grad(yours, *outs, name="grad_outs")
-    got_out = other_core(sent_out)
-    sent_ffn = tall_grad(after(yours, sent_out), *ffn, name="grad_ffn_in")
-    got_ffn = other_core(sent_ffn)
-    part_out = wide_grad(after(mine, sent_ffn), *outs, got_out, square, name="grad_outs")
-    part_ffn = tall_grad(after(mine, part_out), *ffn, got_ffn, name="grad_ffn_in")
-    ffn_sum = scatter_seq(part_ffn)
-    grad_conv, tail, head, g_conv_small, g_skip, g_small = scan_backward(
-        after(x, part_ffn), bk, cq, dt, sg, cum, cumt, grad_mixed, mixed, held, pre, conv, skip_row, rate_row,
-        conv_weight, expand, adjoints,
+    part_ffn = tall_grad(after(here, do_near), ffn_left, ffn_rights, 512, count, square, name="grad_ffn_in")
+    part_out = wide_grad(
+        after(here, part_ffn[0], *adjoints), out_lefts, (grad_ffn, grad_branch, grad_branch, with_other(gz_m, gz_y)), count,
+        square, micros=16, name="grad_outs",
+    )
+    ffn_held = first_hop(part_ffn, part_out[0]) if square else scatter_seq(part_ffn)
+    gc_m, gc_y, tail, head, g_conv_small, g_skip, g_small = scan_backward(
+        after(x, part_out[0]), bk, cq, dt, sg, cum, cumt, grad_mixed, mixed, held, pre, conv, skip_row, rate_row,
+        conv_weight, expand, core_here, adjoints,
     )
     out_held = first_hop(part_out) if square else scatter_seq(part_out)
-    head = after(head, out_held)
+    ffn_sum = second_hop(ffn_held) if square else ffn_held
+    head = after(head, out_held, ffn_sum)
     returned = along(low(head), -1).astype(F32)[:, : taps - 1]
     g_conv_weight = g_conv_small[:taps]
+    beside = ((0, 0), (0, 0), (0, tail.shape[2] - conv_width))
     for ahead in range(1, taps):
         tap = taps - 1 - ahead
         fill = jnp.pad(returned[:, :ahead], ((0, 0), (8 - ahead, 0), (0, 0)))
-        tail = tail + conv_weight[tap] * fill
+        tail = tail + jnp.pad(conv_weight[tap] * fill, beside)
         g_conv_weight = g_conv_weight.at[tap].add(jnp.sum(fill * conv[:, span - 8 :].astype(F32), (0, 1)))
-    grad_conv = lax.dynamic_update_slice(grad_conv, low(tail), (0, span - 8, 0))
-    inside = (hid, (flat(grad_z), flat(grad_conv)), 256, count)
-    sent_in = tall_grad(yours, *inside, name="grad_mixer_in")
-    got_in = other_core(sent_in)
-    gh = leave_mixer(after(grad_z, sent_in), grad_conv, w_gatez, w_conv_in, w_step_wide)
-    out_sum = second_hop(out_held) if square else out_held
+    tail = low(tail)
+    size = tail.shape[2] // 2
+    tails = tail[:, :, :size], tail[:, :, size:]
+    gc_m, gc_y = [
+        lax.dynamic_update_slice(v, jnp.where(core == i, *tails), (0, span - 8, 0)) for i, v in enumerate((gc_m, gc_y))
+    ]
     part_in = tall_grad(
-        after(mine, gh, out_sum, ffn_sum), *inside, got_in, "direct" if square else "", name="grad_mixer_in"
-    )
-    ffn_sum, out_sum = offloaded_sum_z((ffn_sum, out_sum))
+        here, hid, (with_other(gc_m, gc_y),), 256, count, "direct" if square else "", name="grad_conv_in"
+    )
+    ffn_sum = offloaded_sum_z(ffn_sum, 0)
+    out_sum = second_hop(out_held, part_in[0]) if square else out_held
+    order = (part_in[0], out_sum)
+    out_sum = offloaded_sum_z(out_sum, 1)
+
+    small = [
+        g_norm_two[0], g_gated[0], g_conv_weight.reshape(-1), g_conv_small[taps], g_skip[0],
+        g_small[0], g_small[1],
+    ]
+    sizes = [v.shape[0] for v in small]
+    total = jnp.concatenate(small)
+    total = jnp.pad(total, (0, -total.shape[0] % 1024)).reshape(-1, 128)
+    hops = [("seq", 1 << k) for k in range(count.bit_length() - 1)]
+    hops += [("dp", 2 << k) for k in range(lax.axis_size("dp").bit_length() - 2)] + [("dp", 1)]
+
+    def flip(value, axis, bit):
+        return flip_seq(value, bit) if axis == "seq" else flip_dp(value, bit)
+
+    def small_step(total):
+        axis, bit = hops.pop(0)
+        return total + flip(total, axis, bit)
 
     def back(group, order):
         near, far, parts = attend_backward(
@@ -1354,52 +1530,70 @@
         )
         return near, mirror(far), [parts[0]] + [ring(parts[r], -r) for r in range(1, count)]
 
-    dq_near, dq_far, pieces = back(0, (part_in[0],))
-    in_sum = direct_sum(part_in) if square else scatter_seq(part_in)
-    results = back(1, (dq_near, in_sum))
-    in_sum = sum_z(in_sum, 2, 4)
-    grad_tokens, g_norm_one, grad_q, grad_kv = leave(
-        tokens, grad_mid, after(gh, in_sum, ffn_sum), norm_one[None], w_query, w_key, w_value, cos_row, sin_row,
-        (dq_near, results[0]), (dq_far, results[1]), pieces + results[2],
-    )
-    in_sum = sum_z(in_sum, 4)
-    heads = (hid, (flat(grad_q), flat(grad_kv)), 128, count)
-    sent_qkv = tall_grad(yours, *heads, name="grad_qkv")
-    part_qkv = tall_grad(mine, *heads, other_core(sent_qkv), square, name="grad_qkv")
-    qkv_sum = sum_z(second_hop(first_hop(part_qkv)) if square else scatter_seq(part_qkv))
-
-    def spread(value, chunk_rows, chunks):
-        return [
-            [v[(a * chunk_rows) : (b * chunk_rows)].reshape(b - a, chunk_rows, -1) for a, b in chunks]
-            for v in both_cores(value)
-        ]
-
-    def columns(pair):
-        return jnp.concatenate([v[i] for v in pair for i in range(v.shape[0])], 1)
-
+    dq_near, dq_far, pieces = back(0, order)
+    in_sum = direct_sum([after(part_in[0], dq_near), *part_in[1:]]) if square else scatter_seq(part_in)
+    total = small_step(total)
+    results = back(1, (dq_near, in_sum, ffn_sum, total))
+    four = lax.axis_size("dp") == 8
+    in_sum = offloaded_sum_z(in_sum, 2)
+    total = small_step(after(total, dq_near))
+    gh = leave_mixer(
+        core_here, (after(gz_m, results[0], dq_far, total, *pieces), gz_y), (gc_m, gc_y), w_gatez, w_conv_in, w_step_wide
+    )
+    total = small_step(after(total, results[0]))
+    heads = heads_back(
+        core_here, after(cos_row, gh, total), sin_row, (dq_near, results[0]), (dq_far, results[1]), pieces + results[2]
+    )
+    heads_pairs = with_other(*heads[:2]), with_other(*heads[2:])
+    grad_tokens, g_norm_one = leave(
+        core_here, tokens, grad_mid, gh, heads, norm_one[None], w_query, w_key, w_value
+    )
+    total = small_step(after(total, gh))
+    part_qkv = tall_grad(
+        after(here, grad_tokens, out_sum, total), hid, heads_pairs, 128, count, square, name="grad_qkv"
+    )
+    norm_rows = low(g_norm_one.reshape(count, -1))
+    columns = min(128, norm_rows.shape[1])
+    norm_rows = norm_rows.reshape(count, -1, columns)
+    norm_shape = norm_rows.shape[1:]
+    norm_rows = jnp.pad(norm_rows, ((0, 0), (0, -norm_shape[0] % 16), (0, 128 - columns)))
+    norm_at = 2 * width // count if square else part_qkv.shape[1]
+    if square:
+        part_qkv = with_rows(part_qkv, place, norm_rows)
+    else:
+        part_qkv = jnp.concatenate([part_qkv, norm_rows], 1)
+    while hops:
+        total = small_step(total)
+    qkv_held = first_hop(part_qkv, out_sum, in_sum, total) if square else scatter_seq(part_qkv)
+    qkv_sum = second_hop(qkv_held, total) if square else qkv_held
+    ffn_sum, out_sum, in_sum = [after(v, qkv_sum) for v in (ffn_sum, out_sum, in_sum)]
     block = width // count
-    s_gate, s_up = [columns(p) for p in zip(*spread(ffn_sum, block, ((0, 2), (2, 4))))]
-    z_steps, c_steps = WIDE // 512, (conv_width + 256) // 512
-    s_gatez, s_conv = [columns(p) for p in zip(*spread(in_sum, block, ((0, z_steps), (z_steps, z_steps + c_steps))))]
-    s_query, s_kv = [columns(p) for p in zip(*spread(qkv_sum, block, ((0, 2), (2, 3))))]
-    out_all = jnp.concatenate(both_cores(out_sum), 1)
-    a, b = w_down.shape[0] // count, w_attn_out.shape[0] // count
-    s_down, s_attn_out, s_mix_out = out_all[:a], out_all[a : a + b], out_all[a + b :]
-
-    small = [
-        g_norm_one[0], g_norm_two[0], g_gated[0], g_conv_weight.reshape(-1), g_conv_small[taps], g_skip[0],
-        g_small[0], g_small[1],
+
+    def rows_of(*weights):
+        return [(v.shape[0] // count, v.shape[1] // 2 // PIECE, (v.shape[1],)) for v in weights]
+
+    s_gate, s_up = unpack(core_here, ffn_sum, other_core(ffn_sum), [(block, 2, (v.shape[1],)) for v in (w_gate, w_up)])
+    s_down, s_attn_out, s_mix_out, s_gatez = unpack(
+        core_here, out_sum, other_core(out_sum), rows_of(w_down, w_attn_out, w_mix_out, w_gatez)
+    )
+    s_conv, s_step = unpack(
+        core_here, in_sum, other_core(in_sum),
+        [(block, (conv_width + 256) // 2 // PIECE, (conv_width, SSM_HEADS))],
+    )
+    if four:
+        qkv_sum = sum_four(qkv_sum, s_gate, s_down, s_conv)
+    else:
+        qkv_sum = sum_z(qkv_sum)
+    got = other_core(qkv_sum)
+    norm_parts = [v[norm_at : norm_at + norm_shape[0], : norm_shape[1]].astype(F32) for v in (qkv_sum, got)]
+    s_norm_one = (norm_parts[0] + norm_parts[1]).reshape(-1)
+    qkv_sum, got = [
+        jnp.concatenate([v[:norm_at], v[norm_at + norm_rows.shape[1] :]], 0) for v in (qkv_sum, got)
     ]
-    sizes = [v.shape[0] for v in small]
-    total = jnp.concatenate(small)
-    bit = 1
-    while bit < lax.axis_size("dp"):
-        total = total + flip_dp(total, bit)
-        bit *= 2
-    bit = 1
-    while bit < count:
-        total = total + lax.ppermute(total, "seq", [(i, i ^ bit) for i in range(count)])
-        bit *= 2
+    s_query, s_key, s_value = unpack(
+        core_here, qkv_sum, got, [(block, 2, (w_query.shape[1],)), (block, 1, (w_key.shape[1], w_value.shape[1]))]
+    )
+    total = total.reshape(-1)
     starts = np.cumsum([0] + sizes)
     small = [total[a:b] for a, b in zip(starts[:-1], starts[1:])]
 
@@ -1407,22 +1601,22 @@
         n = v.shape[0] // count
         return lax.dynamic_slice(v, (place * n,), (n,))
 
-    s_norm_one, s_norm_two, s_gated = [own(v) for v in small[:3]]
-    s_skip = jnp.sum(small[5].reshape(SSM_HEADS, SSM_HEAD), 1)
+    s_norm_two, s_gated = [own(v) for v in small[:2]]
+    s_skip = jnp.sum(small[4].reshape(SSM_HEADS, SSM_HEAD), 1)
     return (
         output,
         grad_tokens,
         s_norm_one,
         s_query,
-        s_kv[:, :128],
-        s_kv[:, 128:],
+        s_key,
+        s_value,
         s_gatez,
-        s_conv[:, :conv_width],
-        s_conv[:, conv_width : conv_width + SSM_HEADS],
-        small[3].reshape(taps, -1),
-        small[4],
-        small[7][:SSM_HEADS],
+        s_conv,
+        s_step,
+        small[2].reshape(taps, -1),
+        small[3],
         small[6][:SSM_HEADS],
+        small[5][:SSM_HEADS],
         s_skip,
         s_gated,
         s_attn_out,

time: 560 us -> 544 us (0.971)
  waiting for transfers between devices: 77.1 us -> 41.9 us
  Pallas kernels: 340 us -> 363 us
  other arithmetic: 31.3 us -> 17.7 us
  starting transfers between devices: 66.9 us -> 75.1 us
    ppermute x15 -> x18, waiting for transfers between devices: 46.4 us -> 5.13 us  [flip_dp(): return lax.ppermute(value, 'dp', [(i, i ^ bit) for i in range(n)])]
    pallas_call x8 -> x19, Pallas kernels: 124 us -> 146 us  [the longest x1 46 us: middle(): pl.pallas_call(functools.partial(middle_body, rows=rows, blocks=blocks),...]
    ppermute x11 -> x17, waiting for transfers between devices: 10.5 us -> 20.9 us  [flip_seq(): return lax.ppermute(value, 'seq', [(i, i ^ bit) for i in range(n)])]
    convert_element_type x13 -> x3, other arithmetic: 8.12 us -> 0.73 us  [low(): return v.astype(BF16)]
    psum x1 -> x3, waiting for transfers between devices: 0.02 us -> 6.05 us  [offloaded_sum_z(): lax.psum(value, 'dp', axis_index_groups=groups[::-1 if which & 2 else 1])]
    ppermute x9, waiting for transfers between devices: 5.93 us -> 0.02 us  [ring(): return lax.ppermute(value, 'seq', [(i, (i + steps) % n) for i in range(n)])]
    ppermute x11 -> x17, starting transfers between devices: 14.5 us -> 20.1 us  [flip_seq(): return lax.ppermute(value, 'seq', [(i, i ^ bit) for i in range(n)])]
    ppermute x15 -> x18, starting transfers between devices: 27.7 us -> 31.3 us  [flip_dp(): return lax.ppermute(value, 'dp', [(i, i ^ bit) for i in range(n)])]
  transfers between devices with their start and end apart: 50 -> 58, of which waited for: 15 -> 10; matrix products, arithmetic and copies ran while one was open for 8% -> 6% of each run, Pallas kernels for 45% -> 57%
where the time goes in v3:
time: 544 us; the launch traced here: 535 us
  Pallas kernels  363 us (67%)
  starting transfers between devices  75.1 us (14%)
  waiting for transfers between devices  41.9 us (8%)
  local copies, waits for them, and re-layouts  21.2 us (4%)
  other arithmetic  17.7 us (3%)
  between operations  15.6 us (3%)
    pallas_call x2, Pallas kernels, attend_backward(): pl.pallas_call(functools.partial(attend_back_body, rows=rows, keys=keys,...  71.6 us
    pallas_call x1, Pallas kernels, middle(): pl.pallas_call(functools.partial(middle_body, rows=rows, blocks=blocks),...  46 us
    pallas_call x1, Pallas kernels, scan_backward(): pl.pallas_call(functools.partial(scan_back_body, chunks=chunks, conv_widt...  35.3 us
    pallas_call x12, Pallas kernels, in_place(): pl.pallas_call(body, grid=(1,), in_specs=[SCALARS if v.ndim == 1 else ful...  35.2 us
    pallas_call x3, Pallas kernels, tall_grad(): pl.pallas_call(functools.partial(tall_body, n=n, widths=widths, square=sq...  32.6 us
    ppermute x18, starting transfers between devices, flip_dp(): return lax.ppermute(value, 'dp', [(i, i ^ bit) for i in range(n)])  31.3 us
    pallas_call x1, Pallas kernels, attend(): pl.pallas_call(functools.partial(attend_body, rows=rows, keys=keys, block...  29 us
    pallas_call x1, Pallas kernels, wide_grad(): pl.pallas_call(functools.partial(wide_body, parts=len(lefts), group=n //...  22.7 us
  transfers between devices with their start and end apart: 58, of which 10 were waited for; matrix products, arithmetic and copies ran while one was open for 6% of the time, Pallas kernels for 57%

profile of v3, /device:TPU:1, one launch (start us, length us, event | category | flops | bytes accessed | tf_op | source)
XLA Modules:
  0.0 534.5 jit_solution(10525937000312015802)
XLA Ops:
  22.5 7.2 %enter.1 = (bf16[1,1024,1024]{2,1,0:T(8,128)(2,1)}, bf16[1,1024,512]{2,1,0:T(8,128)(2,1)}, bf16[1,1024,256]{2,1,0:T(8,128)(2,1)}) custom-call(bf16[1,1024,1024]{2,1,0:T(8,128)(2,1)} %tok_ref.4, f32[1,1024]{1,0:T(1,128)} %bitcast.72, bf16[1024,512]{1,0:T(8,128)(2,1)} %wq_ref.3, bf16[1024,128]{1,0:T(8,128)(2,1)} %wk_ref.3, bf16[1024,128]{1,0:T(8,128)(2,1)} %wv_ref.3, ...), custom_call_target="tpu_custom_call" | custom-call | flops 24000000000 | bytes 800000 | tf_op jit(solution)/shard_map/enter/pallas_call | solution.py:145
  35.5 21.7 %mixer.1 = (bf16[1,1024,1536]{2,1,0:T(8,128)(2,1)}, bf16[1,1024,1792]{2,1,0:T(8,128)(2,1)}, bf16[1,1024,1792]{2,1,0:T(8,128)(2,1)}, bf16[1,1024,1536]{2,1,0:T(8,...) custom-call(s32[2]{0:T(128)} %pad_add_fusion.pos_ref, ...), custom_call_target="tpu_custom_call" | custom-call | flops 60000002048 | bytes 2000000 | tf_op jit(solution)/shard_map/mixer/pallas_call | solution.py:233
  59.6 6.3 %collective-permute-done.1.other_ref = bf16[1,512,512]{2,1,0:T(8,128)(2,1)} collective-permute-done((bf16[1,512,512]{2,1,0:T(8,128)(2,1)}, bf16[1,512,512]{2,1,0:T(8,128)(2,1)}, u32[]{:S(2)}, u32[]{:S(2)}) %collective-permute-start.1) | collective-permute-done | bytes 524320 | tf_op jit(solution)/shard_map/ppermute | solution.py:1322
  65.9 29.0 %attend.1 = (bf16[1,512,512]{2,1,0:T(8,128)(2,1)}, bf16[1,512,512]{2,1,0:T(8,128)(2,1)}, f32[1,8,1024]{2,1,0:T(8,128)}) custom-call(s32[4]{0:T(128)} %get-tuple-element.387.pos_ref, s32[1]{0:T(128)S(6)} %copy.65.len_ref, s32[4]{0:T(128)} %get-tuple-element.386.from_ref, bf16[1,1024,512]{2,1,0:T(8,128)(2,1)} %get-tuple-element.247.q_ref, ...), custom_call_target="tpu_custom_call" | custom-call | flops 77999996928 | bytes 2600000 | tf_op jit(solution)/shard_map/attend/pallas_call | solution.py:924
  96.1 16.5 %scan_forward.1 = (f32[1,1024,1536]{2,1,0:T(8,128)}, bf16[1,1024,1536]{2,1,0:T(8,128)(2,1)}, bf16[1,8,128,1536]{3,2,1,0:T(8,128)(2,1)}) custom-call(s32[1]{0:T(128)} %bitcast.5.place_ref, bf16[1,1024,1536]{2,1,0:T(8,128)(2,1)} %get-tuple-element.208.x_ref, bf16[1,1024,128]{2,1,0:T(8,128)(2,1)} %get-tuple-element.186.bk_ref, ...), custom_call_target="tpu_custom_call" | custom-call | flops 48000000000 | bytes 1600000 | tf_op jit(solution)/shard_map/scan_forward/pallas_call | solution.py:329
  112.6 46.0 %middle.1 = (bf16[1,1024,1024]{2,1,0:T(8,128)(2,1)}, bf16[1,1024,3584]{2,1,0:T(8,128)(2,1)}, bf16[1,1024,3072]{2,1,0:T(8,128)(2,1)}, bf16[1,1024,3072]{2,1,0:T(8...) custom-call(s32[2]{0:T(128)} %pad_add_fusion.pos_ref, s32[1]{0:T(128)S(6)} %copy.65.len_ref, ...), custom_call_target="tpu_custom_call" | custom-call | flops 134999998464 | bytes 4500000 | tf_op jit(solution)/shard_map/middle/pallas_call | solution.py:408
  161.5 18.5 %branch_back.1 = (bf16[1,512,512]{2,1,0:T(8,128)(2,1)}, bf16[1,512,512]{2,1,0:T(8,128)(2,1)}, bf16[1,1024,1536]{2,1,0:T(8,128)(2,1)}, bf16[1,1024,768]{2,1,0:T(8...) custom-call(s32[1]{0:T(128)} %bitcast.1.core_ref, ...), custom_call_target="tpu_custom_call" | custom-call | flops 17999998976 | bytes 600000 | tf_op jit(solution)/shard_map/branch_back/pallas_call | solution.py:504
  184.2 15.5 %grad_ffn_in.1 = (bf16[1024,512]{1,0:T(8,128)(2,1)}, bf16[2,512,512]{2,1,0:T(8,128)(2,1)}, bf16[512,512]{1,0:T(8,128)(2,1)}, bf16[2,512,512]{2,1,0:T(8,128)(2,1)}, bf16[512,512]{1,0:T(8,128)(2,1)}) custom-call(s32[1]{0:T(128)} %bitcast.5.place_ref, bf16[1024,3584]{1,0:T(8,128)(2,1)} %bitcast.60, ...), custom_call_target="tpu_custom_call" | custom-call | tf_op jit(solution)/shard_map/grad_ffn_in/pallas_call | solution.py:1147
  206.3 22.7 %grad_outs.1 = (bf16[2816,256]{1,0:T(8,128)(2,1)}, bf16[2,1280,256]{2,1,0:T(8,128)(2,1)}, bf16[1280,256]{1,0:T(8,128)(2,1)}, bf16[2,1536,256]{2,1,0:T(8,128)(2,1)}, bf16[1536,256]{1,0:T(8,128)(2,1)}) custom-call(s32[1]{0:T(128)} %bitcast.5.place_ref, bf16[1024,3584]{1,0:T(8,128)(2,1)} %bitcast.61, ...), custom_call_target="tpu_custom_call" | custom-call | flops 48000000000 | bytes 1600000 | tf_op jit(solution)/shard_map/grad_outs/pallas_call | solution.py:1227
  236.4 35.3 %scan_backward.1 = (bf16[1,1024,1024]{2,1,0:T(8,128)(2,1)}, bf16[1,1024,1024]{2,1,0:T(8,128)(2,1)}, f32[1,8,2048]{2,1,0:T(8,128)}, f32[1,8,1792]{2,1,0:T(8,128)}...) custom-call(bf16[1,1024,1536]{2,1,0:T(8,128)(2,1)} %get-tuple-element.208.x_ref, ...), custom_call_target="tpu_custom_call" | custom-call | flops 12000000000 | bytes 400000 | tf_op jit(solution)/shard_map/scan_backward/pallas_call | solution.py:642
  271.7 14.5 %collective-permute-done.18.late_y = bf16[512,512]{1,0:T(8,128)(2,1)} collective-permute-done((bf16[512,512]{1,0:T(8,128)(2,1)}, bf16[512,512]{1,0:T(8,128)(2,1)}, u32[]{:S(2)}, u32[]{:S(2)}) %collective-permute-start.18) | collective-permute-done | bytes 524320 | tf_op jit(solution)/shard_map/ppermute | solution.py:1344
  299.5 4.0 collective-permute-start.21
  308.9 4.9 collective-permute-done.28
  313.8 9.2 %grad_conv_in.1 = (bf16[1024,256]{1,0:T(8,128)(2,1)}, bf16[1024,256]{1,0:T(8,128)(2,1)}, bf16[1024,256]{1,0:T(8,128)(2,1)}, bf16[1024,256]{1,0:T(8,128)(2,1)}) custom-call(s32[1]{0:T(128)} %bitcast.5.place_ref, bf16[1024,1024]{1,0:T(8,128)(2,1)} %bitcast.56, bf16[1024,1024]{1,0:T(8,128)(2,1)} %collective-permute-done.6.rest_7_.left_b, ...), custom_call_target="tpu_custom_call" | custom-call | tf_op jit(solution)/shard_map/grad_conv_in/pallas_call | solution.py:1147
  323.0 4.3 second_hop.4
  330.5 35.9 %attend_backward.2 = (bf16[1,512,256]{2,1,0:T(8,128)(2,1)}, bf16[1,512,256]{2,1,0:T(8,128)(2,1)}, bf16[1,1024,128]{2,1,0:T(8,128)(2,1)}, bf16[1,1024,128]{2,1,0:...) custom-call(s32[4]{0:T(128)} %get-tuple-element.387.pos_ref, s32[1]{0:T(128)S(6)} %copy.65.len_ref, ...), custom_call_target="tpu_custom_call" | custom-call | flops 60000002048 | bytes 2000000 | tf_op jit(solution)/shard_map/attend_backward/pallas_call | solution.py:1047
  373.4 35.6 %attend_backward.3 = (bf16[1,512,256]{2,1,0:T(8,128)(2,1)}, bf16[1,512,256]{2,1,0:T(8,128)(2,1)}, bf16[1,1024,128]{2,1,0:T(8,128)(2,1)}, bf16[1,1024,128]{2,1,0:...) custom-call(s32[4]{0:T(128)} %get-tuple-element.387.pos_ref, s32[1]{0:T(128)S(6)} %copy.65.len_ref, ...), custom_call_target="tpu_custom_call" | custom-call | flops 3000000000 | bytes 100000 | tf_op jit(solution)/shard_map/attend_backward/pallas_call | solution.py:1047
  415.6 13.1 %leave_mixer.1.gh_ref = f32[1,1024,1024]{2,1,0:T(8,128)} custom-call(s32[1]{0:T(128)} %bitcast.1.core_ref, bf16[1,1024,768]{2,1,0:T(8,128)(2,1)} %get-tuple-element.255.gz_m, bf16[1,1024,768]{2,1,0:T(8,128)(2,1)} %get-tuple-element.206.gz_y, bf16[1,1024,1024]{2,1,0:T(8,128)(2,1)} %get-tuple-element.371.gc_m, bf16[1,1024,1024]{2,1,0:T(8,128)(2,1)} %get-tuple-element.370.gc_y, ...), custom_call_target="tpu_custom_call" | custom-call | tf_op jit(solution)/shard_map/leave_mixer/pallas_call | solution.py:695
  428.8 4.4 heads_back.1
  433.2 7.2 %collective-permute-start.40 = (bf16[1024,256]{1,0:T(8,128)(2,1)}, bf16[1024,256]{1,0:T(8,128)(2,1)}, u32[]{:S(2)}, u32[]{:S(2)}) collective-permute-start(bf16[1024,256]{1,0:T(8,128)(2,1)} %bitcast.68), channel_id=1, source_target_pairs={{0,4},{4,0},{8,12},{12,8},{16,20},{20,16},{24,28},{28,24},{1,5},{5... | collective-permute-start | bytes 1572872 | tf_op jit(solution)/shard_map/ppermute | solution.py:1327
  446.1 9.4 %leave.1 = (f32[1,1024,1024]{2,1,0:T(8,128)}, f32[1,1024]{1,0:T(1,128)}) custom-call(s32[1]{0:T(128)} %bitcast.1.core_ref, bf16[1,1024,1024]{2,1,0:T(8,128)(2,1)} %tok_ref.4, f32[1,1024,1024]{2,1,0:T(8,128)} %get-tuple-element.195.gmid_ref, f32[1,1024,1024]{2,1,0:T(8,128)} %leave_mixer.1.gh_ref, bf16[1,1024,256]{2,1,0:T(8,128)(2,1)} %get-tuple-element.263.gq_m, ...), custom_call_target="tpu_custom_call" | custom-call | tf_op jit(solution)/shard_map/leave/pallas_call | solution.py:779
  457.6 7.9 %grad_qkv.1 = (bf16[768,128]{1,0:T(8,128)(2,1)}, bf16[2,512,128]{2,1,0:T(8,128)(2,1)}, bf16[512,128]{1,0:T(8,128)(2,1)}, bf16[2,256,128]{2,1,0:T(8,128)(2,1)}, bf16[256,128]{1,0:T(8,128)(2,1)}) custom-call(s32[1]{0:T(128)} %bitcast.5.place_ref, bf16[1024,1024]{1,0:T(8,128)(2,1)} %bitcast.57, bf16[1024,1024]{1,0:T(8,128)(2,1)} %collective-permute-done.6.rest_7_.left_b, ...), custom_call_target="tpu_custom_call" | custom-call | tf_op jit(solution)/shard_map/grad_qkv/pallas_call | solution.py:1147
  470.7 6.0 %all-reduce.18.cloned.1.call-done.own = bf16[1024,256]{1,0:T(8,128)(2,1)} async-done(((bf16[1024,256]{1,0:T(8,128)(2,1)}), bf16[1024,256]{1,0:T(8,128)(2,1)}) %all-reduce.18.cloned.1.call-update) | async-done | bytes 524304 | tf_op jit(solution)/shard_map/psum | solution.py:1382
  505.7 4.4 unpack.5
  (247 shorter events, 139.5 us)
Async XLA Ops:
  7.2 88.9 %all-gather.3.cloned.1.call-start = ((), (), s32[]{:S(2)}) async-start(), calls=%async_computation.3 | async-start | bytes 2211840 | tf_op jit(solution)/shard_map/all_gather | solution.py:1450
  29.7 29.9 %collective-permute-start.2 = (bf16[1,1024,256]{2,1,0:T(8,128)(2,1)}, bf16[1,1024,256]{2,1,0:T(8,128)(2,1)}, u32[]{:S(2)}, u32[]{:S(2)}) collective-permute-start(bf16[1,1024,256]{2,1,0:T(8,128)(2,1)} %get-tuple-element.181.rest_0_), channel_id=1, source_target_pairs={{0,1},{1,2},{2,3},{3,0},{4,5},{5,6},{6,7},{7,4},{8,9},{9,10},{10,1... | collective-permute-start | bytes 1572872 | tf_op jit(solution)/shard_map/ppermute | solution.py:1312
  31.0 28.7 %collective-permute-start.3 = (bf16[1,1024,256]{2,1,0:T(8,128)(2,1)}, bf16[1,1024,256]{2,1,0:T(8,128)(2,1)}, u32[]{:S(2)}, u32[]{:S(2)}) collective-permute-start(bf16[1,1024,256]{2,1,0:T(8,128)(2,1)} %get-tuple-element.181.rest_0_), channel_id=1, source_target_pairs={{0,2},{1,3},{2,0},{3,1},{4,6},{5,7},{6,4},{7,5},{8,10},{9,11},{10,... | collective-permute-start | bytes 1572872 | tf_op jit(solution)/shard_map/ppermute | solution.py:1312
  31.1 28.6 %collective-permute-start.4 = (bf16[1,1024,256]{2,1,0:T(8,128)(2,1)}, bf16[1,1024,256]{2,1,0:T(8,128)(2,1)}, u32[]{:S(2)}, u32[]{:S(2)}) collective-permute-start(bf16[1,1024,256]{2,1,0:T(8,128)(2,1)} %get-tuple-element.181.rest_0_), channel_id=1, source_target_pairs={{0,3},{1,0},{2,1},{3,2},{4,7},{5,4},{6,5},{7,6},{8,11},{9,8},{10,9... | collective-permute-start | bytes 1572872 | tf_op jit(solution)/shard_map/ppermute | solution.py:1312
  35.2 30.7 %collective-permute-start.1 = (bf16[1,512,512]{2,1,0:T(8,128)(2,1)}, bf16[1,512,512]{2,1,0:T(8,128)(2,1)}, u32[]{:S(2)}, u32[]{:S(2)}) collective-permute-start(bf16[1,512,512]{2,1,0:T(8,128)(2,1)} %slice.170), channel_id=1, source_target_pairs={{0,3},{1,2},{2,1},{3,0},{4,7},{5,6},{6,5},{7,4},{8,11},{9,10},{10,... | collective-permute-start | bytes 1572872 | tf_op jit(solution)/shard_map/ppermute | solution.py:1322
  57.2 316.2 %all-reduce.14.cloned.1.call-start = ((), (), s32[]{:S(2)}) async-start(), calls=%async_computation | async-start | bytes 2097152 | tf_op jit(solution)/shard_map/psum | solution.py:1382
  57.5 55.1 %collective-permute-start.6 = (bf16[1024,1024]{1,0:T(8,128)(2,1)}, bf16[1024,1024]{1,0:T(8,128)(2,1)}, u32[]{:S(2)}, u32[]{:S(2)}) collective-permute-start(bf16[1024,1024]{1,0:T(8,128)(2,1)} %bitcast.54), channel_id=1, source_target_pairs={{0,4},{4,0},{8,12},{12,8},{16,20},{20,16},{24,28},{28,24},{1,5},{5... | collective-permute-start | bytes 6291464 | tf_op jit(solution)/shard_map/ppermute | solution.py:1327
  161.1 45.2 %collective-permute-start.12 = (bf16[1024,1536]{1,0:T(8,128)(2,1)}, bf16[1024,1536]{1,0:T(8,128)(2,1)}, u32[]{:S(2)}, u32[]{:S(2)}) collective-permute-start(bf16[1024,1536]{1,0:T(8,128)(2,1)} %bitcast.77), channel_id=1, source_target_pairs={{0,4},{4,0},{8,12},{12,8},{16,20},{20,16},{24,28},{28,24},{1,5},{5... | collective-permute-start | bytes 9437192 | tf_op jit(solution)/shard_map/ppermute | solution.py:1327
  203.1 28.8 %collective-permute-start.16 = (bf16[2,512,512]{2,1,0:T(8,128)(2,1)}, bf16[2,512,512]{2,1,0:T(8,128)(2,1)}, u32[]{:S(2)}, u32[]{:S(2)}) collective-permute-start(bf16[2,512,512]{2,1,0:T(8,128)(2,1)} %get-tuple-element.223), channel_id=1, source_target_pairs={{0,1},{1,0},{2,3},{3,2},{4,5},{5,4},{6,7},{7,6},{8,9},{9,8},{10,11... | collective-permute-start | bytes 3145736 | tf_op jit(solution)/shard_map/ppermute | solution.py:1344
  229.0 60.7 %collective-permute-start.15 = (bf16[2,1536,256]{2,1,0:T(8,128)(2,1)}, bf16[2,1536,256]{2,1,0:T(8,128)(2,1)}, u32[]{:S(2)}, u32[]{:S(2)}) collective-permute-start(bf16[2,1536,256]{2,1,0:T(8,128)(2,1)} %get-tuple-element.220), channel_id=1, source_target_pairs={{0,2},{1,3},{2,0},{3,1},{4,6},{5,7},{6,4},{7,5},{8,10},{9,11},{10,... | collective-permute-start | bytes 4718600 | tf_op jit(solution)/shard_map/ppermute | solution.py:1344
  229.1 60.5 %collective-permute-start.14 = (bf16[2,1280,256]{2,1,0:T(8,128)(2,1)}, bf16[2,1280,256]{2,1,0:T(8,128)(2,1)}, u32[]{:S(2)}, u32[]{:S(2)}) collective-permute-start(bf16[2,1280,256]{2,1,0:T(8,128)(2,1)} %get-tuple-element.219), channel_id=1, source_target_pairs={{0,1},{1,0},{2,3},{3,2},{4,5},{5,4},{6,7},{7,6},{8,9},{9,8},{10,11... | collective-permute-start | bytes 3932168 | tf_op jit(solution)/shard_map/ppermute | solution.py:1344
  230.7 99.8 %collective-permute-start.24 = (bf16[1,512,512]{2,1,0:T(8,128)(2,1)}, bf16[1,512,512]{2,1,0:T(8,128)(2,1)}, u32[]{:S(2)}, u32[]{:S(2)}) collective-permute-start(bf16[1,512,512]{2,1,0:T(8,128)(2,1)} %get-tuple-element.235), channel_id=1, source_target_pairs={{0,3},{1,2},{2,1},{3,0},{4,7},{5,6},{6,5},{7,4},{8,11},{9,10},{10,... | collective-permute-start | bytes 1572872 | tf_op jit(solution)/shard_map/ppermute | solution.py:1322
  235.0 51.2 %collective-permute-start.18 = (bf16[512,512]{1,0:T(8,128)(2,1)}, bf16[512,512]{1,0:T(8,128)(2,1)}, u32[]{:S(2)}, u32[]{:S(2)}) collective-permute-start(bf16[512,512]{1,0:T(8,128)(2,1)} %get-tuple-element.228), channel_id=1, source_target_pairs={{0,2},{1,3},{2,0},{3,1},{4,6},{5,7},{6,4},{7,5},{8,10},{9,11},{10,... | collective-permute-start | bytes 1572872 | tf_op jit(solution)/shard_map/ppermute | solution.py:1344
  235.2 51.0 %collective-permute-start.19 = (bf16[512,512]{1,0:T(8,128)(2,1)}, bf16[512,512]{1,0:T(8,128)(2,1)}, u32[]{:S(2)}, u32[]{:S(2)}) collective-permute-start(bf16[512,512]{1,0:T(8,128)(2,1)} %get-tuple-element.229), channel_id=1, source_target_pairs={{0,1},{1,0},{2,3},{3,2},{4,5},{5,4},{6,7},{7,6},{8,9},{9,8},{10,11... | collective-permute-start | bytes 1572872 | tf_op jit(solution)/shard_map/ppermute | solution.py:1344
  297.8 159.1 %all-reduce.16.cloned.1.call-start = ((), (), s32[]{:S(2)}) async-start(), calls=%async_computation.1 | async-start | bytes 2883584 | tf_op jit(solution)/shard_map/psum | solution.py:1382
  327.2 40.8 %collective-permute-start.25 = (bf16[1024,256]{1,0:T(8,128)(2,1)}, bf16[1024,256]{1,0:T(8,128)(2,1)}, u32[]{:S(2)}, u32[]{:S(2)}) collective-permute-start(bf16[1024,256]{1,0:T(8,128)(2,1)} %get-tuple-element.239), channel_id=1, source_target_pairs={{0,1},{1,0},{2,3},{3,2},{4,5},{5,4},{6,7},{7,6},{8,9},{9,8},{10,11... | collective-permute-start | bytes 1572872 | tf_op jit(solution)/shard_map/ppermute | solution.py:1344
  328.1 42.3 %collective-permute-start.26 = (bf16[1024,256]{1,0:T(8,128)(2,1)}, bf16[1024,256]{1,0:T(8,128)(2,1)}, u32[]{:S(2)}, u32[]{:S(2)}) collective-permute-start(bf16[1024,256]{1,0:T(8,128)(2,1)} %get-tuple-element.240), channel_id=1, source_target_pairs={{0,2},{1,3},{2,0},{3,1},{4,6},{5,7},{6,4},{7,5},{8,10},{9,11},{10,... | collective-permute-start | bytes 1572872 | tf_op jit(solution)/shard_map/ppermute | solution.py:1344
  329.3 41.2 %collective-permute-start.27 = (bf16[1024,256]{1,0:T(8,128)(2,1)}, bf16[1024,256]{1,0:T(8,128)(2,1)}, u32[]{:S(2)}, u32[]{:S(2)}) collective-permute-start(bf16[1024,256]{1,0:T(8,128)(2,1)} %get-tuple-element.241), channel_id=1, source_target_pairs={{0,3},{1,2},{2,1},{3,0},{4,7},{5,6},{6,5},{7,4},{8,11},{9,10},{10,... | collective-permute-start | bytes 1572872 | tf_op jit(solution)/shard_map/ppermute | solution.py:1344
  330.5 146.3 %all-reduce.18.cloned.1.call-start = ((), (), s32[]{:S(2)}) async-start(), calls=%async_computation.2 | async-start | bytes 1048576 | tf_op jit(solution)/shard_map/psum | solution.py:1382
  366.5 42.5 %collective-permute-start.30 = (f32[104,128]{1,0:T(8,128)S(1)}, f32[104,128]{1,0:T(8,128)S(1)}, u32[]{:S(2)}, u32[]{:S(2)}) collective-permute-start(f32[104,128]{1,0:T(8,128)S(1)} %bitcast_add_fusion), channel_id=1, source_target_pairs={{0,2},{1,3},{2,0},{3,1},{4,6},{5,7},{6,4},{7,5},{8,10},{9,11},{10,... | collective-permute-start | bytes 159752 | tf_op jit(solution)/shard_map/ppermute | solution.py:1344
  368.0 43.2 %collective-permute-start.29 = (bf16[1,512,256]{2,1,0:T(8,128)(2,1)}, bf16[1,512,256]{2,1,0:T(8,128)(2,1)S(1)}, u32[]{:S(2)}, u32[]{:S(2)}) collective-permute-start(bf16[1,512,256]{2,1,0:T(8,128)(2,1)} %get-tuple-element.249), channel_id=1, source_target_pairs={{0,3},{1,2},{2,1},{3,0},{4,7},{5,6},{6,5},{7,4},{8,11},{9,10},{10,... | collective-permute-start | bytes 786440 | tf_op jit(solution)/shard_map/ppermute | solution.py:1322
  368.0 43.4 %collective-permute-start.31 = (bf16[1,1024,128]{2,1,0:T(8,128)(2,1)}, bf16[1,1024,128]{2,1,0:T(8,128)(2,1)}, u32[]{:S(2)}, u32[]{:S(2)}) collective-permute-start(bf16[1,1024,128]{2,1,0:T(8,128)(2,1)} %get-tuple-element.252), channel_id=1, source_target_pairs={{0,3},{1,0},{2,1},{3,2},{4,7},{5,4},{6,5},{7,6},{8,11},{9,8},{10,9... | collective-permute-start | bytes 786440 | tf_op jit(solution)/shard_map/ppermute | solution.py:1312
  370.4 42.3 %collective-permute-start.32 = (bf16[1,1024,128]{2,1,0:T(8,128)(2,1)}, bf16[1,1024,128]{2,1,0:T(8,128)(2,1)}, u32[]{:S(2)}, u32[]{:S(2)}) collective-permute-start(bf16[1,1024,128]{2,1,0:T(8,128)(2,1)} %get-tuple-element.253), channel_id=1, source_target_pairs={{0,2},{1,3},{2,0},{3,1},{4,6},{5,7},{6,4},{7,5},{8,10},{9,11},{10,... | collective-permute-start | bytes 786440 | tf_op jit(solution)/shard_map/ppermute | solution.py:1312
  370.5 43.8 %collective-permute-start.33 = (bf16[1,1024,128]{2,1,0:T(8,128)(2,1)}, bf16[1,1024,128]{2,1,0:T(8,128)(2,1)}, u32[]{:S(2)}, u32[]{:S(2)}) collective-permute-start(bf16[1,1024,128]{2,1,0:T(8,128)(2,1)} %get-tuple-element.254), channel_id=1, source_target_pairs={{0,1},{1,2},{2,3},{3,0},{4,5},{5,6},{6,7},{7,4},{8,9},{9,10},{10,1... | collective-permute-start | bytes 786440 | tf_op jit(solution)/shard_map/ppermute | solution.py:1312
  (57 other events, 723.6 us)
Sparse Core Ops, SparseCore 0:
  57.3 35.1 all-gather.2
  297.9 55.3 all-reduce.13
  356.4 63.0 all-reduce.15
  443.1 33.5 all-reduce.17

commit v4 on v3

--- a/solution.py
+++ b/solution.py
@@ -42,7 +42,7 @@
 
 
 def sigmoid(v):
-    return 1.0 / (1.0 + jnp.exp(-v))
+    return jax.nn.sigmoid(v)
 
 
 def softplus(v):
@@ -105,6 +105,24 @@
     return t >= u
 
 
+def rotation(span, count, order):
+    inverse = (1.0 / np.float64(ROPE_BASE) ** (np.arange(0, HEAD, 2) / HEAD)).astype(np.float32).astype(np.float64)
+    steps = np.arange(span)[:, None] * inverse
+    starts = (np.arange(count) * span)[:, None] * inverse
+    if order == "rows":
+        sign = np.tile(np.repeat([-1.0, 1.0], HEAD // 2), 2)
+        made = [np.tile(np.cos(steps), 4), np.tile(np.sin(steps), 4) * sign]
+        made += [np.tile(np.cos(starts), 4)[:, None], (np.tile(np.sin(starts), 4) * sign)[:, None]]
+    else:
+        made = [np.cos(steps).T, np.sin(steps).T]
+        made += [np.repeat(f(starts)[:, :, None], 128, 2) for f in (np.cos, np.sin)]
+    return [jnp.asarray(v.astype(np.float32)) for v in made]
+
+
+def turned(step_cos, step_sin, start_cos, start_sin):
+    return start_cos * step_cos - start_sin * step_sin, start_sin * step_cos + start_cos * step_sin
+
+
 def swap_halves(v):
     lane = lax.broadcasted_iota(jnp.int32, v.shape, 1)
     return jnp.where((lane & 63) < 32, pltpu.roll(v, 96, 1), pltpu.roll(v, 32, 1))
@@ -121,10 +139,13 @@
     return low(v * lax.rsqrt(jnp.mean(v * v, -1, keepdims=True) + EPS) * gain)
 
 
-def enter_body(tok_ref, gain_ref, wq_ref, wk_ref, wv_ref, cos_ref, sin_ref, hid_ref, q_ref, kv_ref):
+def enter_body(
+    place_ref, tok_ref, gain_ref, wq_ref, wk_ref, wv_ref, cos_ref, sin_ref, cos0_ref, sin0_ref, hid_ref, q_ref, kv_ref
+):
     hid = first_norm(tok_ref[0], gain_ref[...])
     hid_ref[0] = hid
-    cosine, sine = cos_ref[...], sin_ref[...]
+    place = place_ref[0]
+    cosine, sine = turned(cos_ref[...], sin_ref[...], cos0_ref[place], sin0_ref[place])
     t = dot(hid, wk_ref[...])
     kv_ref[0, :, :128] = low(t * cosine + swap_halves(t) * sine)
     kv_ref[0, :, 128:] = low(dot(hid, wv_ref[...]))
@@ -134,7 +155,7 @@
         q_ref[0, :, g * 128 : g * 128 + 128] = low(t * cosine + swap_halves(t) * sine)
 
 
-def enter(tokens, gain, wq, wk, wv, cosine, sine):
+def enter(place, tokens, gain, wq, wk, wv, tables):
     seqs, span, width = tokens.shape
     rows = min(256, span)
 
@@ -145,13 +166,16 @@
     return pl.pallas_call(
         enter_body,
         grid=(seqs, span // rows),
-        in_specs=[row(width)] + [full_spec(v.shape) for v in (gain, wq, wk, wv)] + [table, table],
+        in_specs=[SCALARS, row(width)]
+        + [full_spec(v.shape) for v in (gain, wq, wk, wv)]
+        + [table, table]
+        + [full_spec(v.shape) for v in tables[2:]],
         out_specs=[row(width), row(512), row(256)],
         out_shape=[jax.ShapeDtypeStruct((seqs, span, n), BF16) for n in (width, 512, 256)],
         compiler_params=params(),
         cost_estimate=cost(8),
         name="enter",
-    )(tokens, gain, wq, wk, wv, cosine, sine)
+    )(place, tokens, gain, wq, wk, wv, *tables)
 
 
 def mixer_body(
@@ -347,20 +371,42 @@
     )(place, x, bk, cq, dt, cum, cumt, skip, z, gain, expand, states)
 
 
+def live_rows(pos_ref, len_ref, rows):
+    at = pos_ref[0] + pl.program_id(1) * rows + lax.broadcasted_iota(jnp.int32, (rows, 1), 0)
+    return jnp.where(at < len_ref[pl.program_id(0)], 1.0, 0.0)
+
+
+def grad_act_body(pos_ref, len_ref, cot_ref, wd_ref, out_ref, *, rows):
+    gffn = low(live_rows(pos_ref, len_ref, rows) * cot_ref[0].astype(F32))
+    out_ref[0] = low(dot(gffn, wd_ref[...], NT))
+
+
+def grad_act(pos, lens, cot, wd):
+    seqs, span, width = cot.shape
+    rows = min(256, span)
+    ff = wd.shape[0]
+    return pl.pallas_call(
+        functools.partial(grad_act_body, rows=rows),
+        grid_spec=pltpu.PrefetchScalarGridSpec(
+            num_scalar_prefetch=2,
+            grid=(seqs, span // rows),
+            in_specs=[pl.BlockSpec((1, rows, width), lambda s, b, *_: (s, b, 0)), full_spec(wd.shape)],
+            out_specs=pl.BlockSpec((1, rows, ff), lambda s, b, *_: (s, b, 0)),
+        ),
+        out_shape=jax.ShapeDtypeStruct((seqs, span, ff), BF16),
+        compiler_params=params(),
+        cost_estimate=cost(0),
+        name="grad_act",
+    )(pos, lens, cot, wd)
+
+
 def middle_body(
-    pos_ref, len_ref, near_ref, far_ref, mix_ref, tok_ref, cot_ref,
+    pos_ref, len_ref, near_ref, far_ref, mix_ref, tok_ref, cot_ref, gact_ref,
     wao_ref, wmo_ref, wg_ref, wu_ref, wd_ref, gain2_ref,
-    out_ref, left_ref, mine_ref, yours_ref, gmid_ref, gn2_ref, *, rows, blocks,
+    out_ref, left_ref, mine_ref, yours_ref, gmid_ref, *, rows, blocks,
 ):
-    s = pl.program_id(0)
     b = pl.program_id(1)
-
-    @pl.when((s == 0) & (b == 0))
-    def _():
-        gn2_ref[...] = jnp.zeros_like(gn2_ref)
-
-    at = pos_ref[0] + b * rows + lax.broadcasted_iota(jnp.int32, (rows, 1), 0)
-    live = jnp.where(at < len_ref[s], 1.0, 0.0)
+    live = live_rows(pos_ref, len_ref, rows)
     attn = jnp.where(b < blocks // 2, near_ref[0], far_ref[0])
     width, ff = wd_ref.shape[1], wd_ref.shape[0]
     left_ref[0, :, width + ff :] = attn
@@ -380,18 +426,17 @@
     out_ref[0] = low(after + live * dot(act, wd_ref[...]))
     cot = cot_ref[0].astype(F32)
     gffn = low(live * cot)
-    gact = dot(gffn, wd_ref[...], NT)
+    gact = gact_ref[0].astype(F32)
     gg = low(gact * up * (sg * (1.0 + gate * (1.0 - sg))))
     gu = low(gact * silu)
     gh2 = dot(gg, wg_ref[...], NT) + dot(gu, wu_ref[...], NT)
-    gn2_ref[...] += jnp.sum(gh2 * unit, 0, keepdims=True)
     g = gh2 * gain
     gmid = cot + scale * (g - unit * jnp.mean(g * unit, -1, keepdims=True))
     gmid_ref[0] = gmid
     halves_out(pos_ref[1], (gg, gu, gffn, low(live * gmid)), mine_ref, yours_ref)
 
 
-def middle(pos, lens, near, far, mix, tokens, cot, wao, wmo, wg, wu, wd, gain2):
+def middle(pos, lens, near, far, mix, tokens, cot, gact, wao, wmo, wg, wu, wd, gain2):
     seqs, span, width = tokens.shape
     rows = min(256, span // 2)
     blocks = span // rows
@@ -410,34 +455,27 @@
         grid_spec=pltpu.PrefetchScalarGridSpec(
             num_scalar_prefetch=2,
             grid=(seqs, blocks),
-            in_specs=[lower, upper, row(WIDE), row(width), row(width)]
+            in_specs=[lower, upper, row(WIDE), row(width), row(width), row(ff)]
             + [full_spec(v.shape) for v in (wao, wmo, wg, wu, wd, gain2)],
             out_specs=[
                 row(width), row(width + ff + 512), row(width + ff), row(width + ff), row(width),
-                pl.BlockSpec((1, width), lambda s, b, *_: (0, 0)),
             ],
         ),
         out_shape=[
             shape(width, BF16), shape(width + ff + 512, BF16), shape(width + ff, BF16), shape(width + ff, BF16),
             shape(width, F32),
-            jax.ShapeDtypeStruct((1, width), F32),
         ],
         compiler_params=params(),
         cost_estimate=cost(45),
         name="middle",
-    )(pos, lens, near, far, mix, tokens, cot, wao, wmo, wg, wu, wd, gain2)
+    )(pos, lens, near, far, mix, tokens, cot, gact, wao, wmo, wg, wu, wd, gain2)
 
 
 def branch_body(
     core_ref, gb_m, gb_y, mixed_ref, z_ref, cq_ref, cum_ref, wao_ref, wmo_ref, gated_ref, exp_ref,
-    gnear_ref, gfar_ref, gmixed_ref, gz_m, gz_y, ggain_ref, adj_ref, adj, offset, *, rows, blocks,
+    gnear_ref, gfar_ref, gmixed_ref, gz_m, gz_y, adj_ref, adj, offset, *, rows, blocks,
 ):
-    s = pl.program_id(0)
     b = pl.program_id(1)
-
-    @pl.when((s == 0) & (b == 0))
-    def _():
-        ggain_ref[...] = jnp.zeros_like(ggain_ref)
 
     @pl.when(b == 0)
     def _():
@@ -464,7 +502,6 @@
     v = mixed * silu
     scale = lax.rsqrt(jnp.mean(v * v, -1, keepdims=True) + EPS)
     unit = v * scale
-    ggain_ref[...] += jnp.sum(gn * unit, 0, keepdims=True)
     g = gn * gated_ref[...]
     g = scale * (g - unit * jnp.mean(g * unit, -1, keepdims=True))
     gmixed = g * silu
@@ -507,12 +544,11 @@
         in_specs=[SCALARS, gb, gb, row(WIDE), row(WIDE), row(STATE), row(128)]
         + [full_spec(v.shape) for v in (wao, wmo, gated, expand)],
         out_specs=[
-            lower, upper, row(WIDE), row(WIDE // 2), row(WIDE // 2), pl.BlockSpec((1, WIDE), lambda s, b: (0, 0)),
+            lower, upper, row(WIDE), row(WIDE // 2), row(WIDE // 2),
             pl.BlockSpec((1, STATE + 16, WIDE), lambda s, b: (s, 0, 0)),
         ],
         out_shape=[
             half, half, shape(WIDE, BF16), shape(WIDE // 2, BF16), shape(WIDE // 2, BF16),
-            jax.ShapeDtypeStruct((1, WIDE), F32),
             jax.ShapeDtypeStruct((seqs, STATE + 16, WIDE), BF16),
         ],
         scratch_shapes=[pltpu.VMEM((STATE, WIDE), F32), pltpu.VMEM((1, 128), F32)],
@@ -706,7 +742,7 @@
     )(core, *gz, *gc, wz, wc, ws)
 
 
-def heads_body(core_ref, cos_ref, sin_ref, *rest, blocks, count):
+def heads_body(core_ref, place_ref, cos_ref, sin_ref, cos0_ref, sin0_ref, *rest, blocks, count):
     near, far = rest[:2], rest[2:4]
     pieces = rest[4 : 4 + 2 * count]
     gq_m, gq_y, gkv_m, gkv_y = rest[4 + 2 * count :]
@@ -722,11 +758,13 @@
     lane = lax.broadcasted_iota(jnp.int32, sums[0].shape, 1)
     gk = jnp.where(lane < 64, sums[0], pltpu.roll(sums[1], 64, 1))
     gv = low(jnp.where(lane < 64, pltpu.roll(sums[0], 64, 1), sums[1]))
-    gk = low(gk * cos_ref[...] - swap_halves(gk) * sin_ref[...])
+    place = place_ref[0]
+    cosine, sine = turned(cos_ref[...], sin_ref[...], cos0_ref[place], sin0_ref[place])
+    gk = low(gk * cosine - swap_halves(gk) * sine)
     halves_out(core, (jnp.concatenate([gk, gv], 1),), gkv_m, gkv_y)
 
 
-def heads_back(core, cosine, sine, near, far, pieces):
+def heads_back(core, place, tables, near, far, pieces):
     seqs, half, _ = near[0].shape
     span = 2 * half
     rows = min(256, half)
@@ -741,22 +779,20 @@
     return pl.pallas_call(
         functools.partial(heads_body, blocks=blocks, count=len(pieces) // 2),
         grid=(seqs, blocks),
-        in_specs=[SCALARS, table, table, lower, lower, upper, upper] + [row(128)] * len(pieces),
+        in_specs=[SCALARS, SCALARS, table, table]
+        + [full_spec(v.shape) for v in tables[2:]]
+        + [lower, lower, upper, upper] + [row(128)] * len(pieces),
         out_specs=[row(256), row(256), row(128), row(128)],
         out_shape=[jax.ShapeDtypeStruct((seqs, span, n), BF16) for n in (256, 256, 128, 128)],
         compiler_params=params(),
         cost_estimate=cost(0),
         name="heads_back",
-    )(core, cosine, sine, *near, *far, *pieces)
+    )(core, place, *tables, *near, *far, *pieces)
 
 
 def leave_body(
-    core_ref, tok_ref, gmid_ref, gh_ref, gq_m, gq_y, gkv_m, gkv_y, gain_ref, wq_ref, wk_ref, wv_ref, gt_ref, gn_ref
+    core_ref, tok_ref, gmid_ref, gh_ref, gq_m, gq_y, gkv_m, gkv_y, gain_ref, wq_ref, wk_ref, wv_ref, gt_ref
 ):
-    @pl.when((pl.program_id(0) == 0) & (pl.program_id(1) == 0))
-    def _():
-        gn_ref[...] = jnp.zeros_like(gn_ref)
-
     core = core_ref[0]
     gh = gh_ref[0] + dot(halves_in(core, gq_m[0], gq_y[0]), wq_ref[...], NT)
     gkv = halves_in(core, gkv_m[0], gkv_y[0])
@@ -764,7 +800,6 @@
     v = tok_ref[0].astype(F32)
     scale = lax.rsqrt(jnp.mean(v * v, -1, keepdims=True) + EPS)
     unit = v * scale
-    gn_ref[...] += jnp.sum(gh * unit, 0, keepdims=True)
     g = gh * gain_ref[...]
     gt_ref[0] = gmid_ref[0] + scale * (g - unit * jnp.mean(g * unit, -1, keepdims=True))
 
@@ -780,8 +815,8 @@
         leave_body,
         grid=(seqs, span // rows),
         in_specs=[SCALARS] + [row(width)] * 3 + [row(v.shape[2]) for v in heads] + [full_spec(v.shape) for v in (gain, wq, wk, wv)],
-        out_specs=[row(width), pl.BlockSpec((1, width), lambda s, b: (0, 0))],
-        out_shape=[jax.ShapeDtypeStruct((seqs, span, width), F32), jax.ShapeDtypeStruct((1, width), F32)],
+        out_specs=row(width),
+        out_shape=jax.ShapeDtypeStruct((seqs, span, width), F32),
         compiler_params=params(),
         cost_estimate=cost(0),
         name="leave",
@@ -945,12 +980,12 @@
 
 def attend_back_body(
     pos_ref, len_ref, from_ref, q_ref, other_ref, do_near_ref, do_far_ref, o_near_ref, o_far_ref, lse_ref,
-    cos_ref, sin_ref, *rest, rows, keys, blocks, count, span, group,
+    cos_ref, sin_ref, cos0_ref, sin0_ref, *rest, rows, keys, blocks, count, span, group,
 ):
     kv_refs = rest[:count]
     dq_near_ref, dq_far_ref = rest[count : count + 2]
     dkv_refs = rest[count + 2 : 2 * count + 2]
-    kd, vd, kt, dk, dv, dq = rest[2 * count + 2 :]
+    kd, vd, kt, dk, dv, dq, score_a, grad_a, score_b, grad_b = rest[2 * count + 2 :]
     s = pl.program_id(0)
     b = pl.program_id(1)
     prep = min(512, span)
@@ -982,28 +1017,64 @@
     dq[...] = jnp.zeros_like(dq)
     whole, some = key_range(first, length, rows, keys)
 
-    def step(i, masked):
+    def scores(i, buffers, h):
         at = pl.ds(pl.multiple_of(i * keys, keys), keys)
-        mask = seen(i, first, length, rows, keys) if masked else None
-        dv_sum = dk_sum = None
+        buffers[0][h] = dot(kd[at, :], heads[h], NT)
+        buffers[1][h] = dot(vd[at, :], grads[h], NT)
+
+    def add(i, buffers, h, sums, mask=None):
+        at = pl.ds(pl.multiple_of(i * keys, keys), keys)
+        x = buffers[0][h] * SCORE2 - lse_ref[0, 4 * group + h : 4 * group + h + 1, :]
+        if mask is not None:
+            x = jnp.where(mask, x, LOWEST)
+        p = jnp.exp2(x)
+        ds = low(p * (buffers[1][h] - delta[h : h + 1]))
+        parts = dot(low(p), grads[h]), dot(ds, heads[h])
+        dq[h] += dot(kt[:, at], ds)
+        sums = parts if sums is None else (sums[0] + parts[0], sums[1] + parts[1])
+        if h == 3:
+            dv[at, :] += sums[0]
+            dk[at, :] += sums[1]
+        return sums
+
+    early, late = (score_a, grad_a), (score_b, grad_b)
+
+    def edge(i, _):
+        mask = seen(i, first, length, rows, keys)
         for h in range(4):
-            x = dot(kd[at, :], heads[h], NT) * SCORE2 - lse_ref[0, 4 * group + h : 4 * group + h + 1, :]
-            dp = dot(vd[at, :], grads[h], NT)
-            if masked:
-                x = jnp.where(mask, x, LOWEST)
-            p = jnp.exp2(x)
-            ds = low(p * (dp - delta[h : h + 1]))
-            dv_part = dot(low(p), grads[h])
-            dk_part = dot(ds, heads[h])
-            dv_sum = dv_part if dv_sum is None else dv_sum + dv_part
-            dk_sum = dk_part if dk_sum is None else dk_sum + dk_part
-            dq[h] += dot(kt[:, at], ds)
-        dv[at, :] += dv_sum
-        dk[at, :] += dk_sum
-
-    lax.fori_loop(0, whole, lambda i, _: (step(i, False), 0)[1], 0)
-    lax.fori_loop(whole, some, lambda i, _: (step(i, True), 0)[1], 0)
-    cosine, sine = cos_ref[...], sin_ref[...]
+            scores(i, early, h)
+        sums = None
+        for h in range(4):
+            sums = add(i, early, h, sums, mask)
+        return 0
+
+    lax.fori_loop(whole, some, edge, 0)
+    last = jnp.maximum(whole - 1, 0)
+    for h in range(4):
+        scores(0, early, h)
+
+    def two(i, _):
+        sums = None
+        for h in range(4):
+            scores(2 * i + 1, late, h)
+            sums = add(2 * i, early, h, sums)
+        following = jnp.minimum(2 * i + 2, last)
+        sums = None
+        for h in range(4):
+            scores(following, early, h)
+            sums = add(2 * i + 1, late, h, sums)
+        return 0
+
+    lax.fori_loop(0, whole // 2, two, 0)
+
+    @pl.when(whole % 2 == 1)
+    def _():
+        sums = None
+        for h in range(4):
+            sums = add(last, early, h, sums)
+
+    owner = jnp.where(is_near, from_ref[0], count - 1 - from_ref[0])
+    cosine, sine = turned(cos_ref[...], sin_ref[...], cos0_ref[owner][:, :1], sin0_ref[owner][:, :1])
     parts = []
     for h in range(4):
         t = dq[h] * 0.125
@@ -1031,12 +1102,12 @@
                 dkv_ref[0, i * prep : (i + 1) * prep] = low(jnp.where(lane < 64, k, v))
 
 
-def attend_backward(group, pos, lens, sources, q, other, do_near, do_far, o_near, o_far, lse, cosine, sine, kvs):
+def attend_backward(group, pos, lens, sources, q, other, do_near, do_far, o_near, o_far, lse, tables, kvs):
     seqs, span, _ = q.shape
     count = len(kvs)
     total = count * span
     rows = min(256, span // 2)
-    keys = 512
+    keys = 256
     blocks = span // rows
     lower = pl.BlockSpec((1, rows, 256), lambda s, b, *_: (s, jnp.minimum(b, blocks // 2 - 1), group))
     upper = pl.BlockSpec((1, rows, 256), lambda s, b, *_: (s, jnp.maximum(b - blocks // 2, 0), group))
@@ -1052,19 +1123,21 @@
             num_scalar_prefetch=3,
             grid=(seqs, blocks),
             in_specs=[lower, upper, lower, upper, lower, upper, stat, table, table]
+            + [full_spec(v.shape) for v in tables[2:]]
             + [pl.BlockSpec((1, span, 256), lambda s, b, *_: (s, 0, 0), pipeline_mode=pl.Buffered(1))] * count,
             out_specs=[out_lower, out_upper]
             + [pl.BlockSpec((1, span, 128), lambda s, b, *_: (s, 0, 0))] * count,
             scratch_shapes=[
                 pltpu.VMEM((total, 128), BF16), pltpu.VMEM((total, 128), BF16), pltpu.VMEM((64, total), BF16),
                 pltpu.VMEM((total, 128), F32), pltpu.VMEM((total, 128), F32), pltpu.VMEM((4, 64, rows), F32),
-            ],
+            ]
+            + [pltpu.VMEM((4, keys, rows), F32)] * 4,
         ),
         out_shape=[half, half] + [jax.ShapeDtypeStruct((seqs, span, 128), BF16)] * count,
         compiler_params=params(),
         cost_estimate=cost(1 if group else 20),
         name="attend_backward",
-    )(pos, lens, sources, q, other, do_near, do_far, o_near, o_far, lse, cosine, sine, *kvs)
+    )(pos, lens, sources, q, other, do_near, do_far, o_near, o_far, lse, *tables, *kvs)
     return outs[0], outs[1], outs[2:]
 
 
@@ -1239,15 +1312,20 @@
     )(place, *[v for left in lefts for v in left[:2]], *[v for right in rights for v in right[:2]])
 
 
-def in_place(body, args, outs, name, micros=0):
+def in_place(body, args, outs, name, columns=None):
+    def spec(shape):
+        if columns is None:
+            return full_spec(shape)
+        return pl.BlockSpec((*shape[:-1], columns), lambda i: (0,) * (len(shape) - 1) + (i,))
+
     return pl.pallas_call(
         body,
-        grid=(1,),
-        in_specs=[SCALARS if v.ndim == 1 else full_spec(v.shape) for v in args],
-        out_specs=[full_spec(v.shape) for v in outs],
+        grid=(1 if columns is None else outs[0].shape[-1] // columns,),
+        in_specs=[SCALARS if v.ndim == 1 else spec(v.shape) for v in args],
+        out_specs=[spec(v.shape) for v in outs],
         out_shape=outs,
         compiler_params=pltpu.CompilerParams(vmem_limit_bytes=VMEM_LIMIT),
-        cost_estimate=cost(micros),
+        cost_estimate=cost(0),
         name=name,
     )(*args)
 
@@ -1279,32 +1357,66 @@
     out[...] = low(near + (two[...].astype(F32) + three[...].astype(F32)))
 
 
-def unpack_body(core_ref, own, other, *outs, plan):
-    first = core_ref[0] == 0
+def unpack_body(at_ref, own, other, *rest, plan, summed, grads):
+    weights = dict(zip(summed, rest))
+    outs = rest[len(summed) : len(summed) + grads]
+    sums = dict(zip(summed, rest[len(summed) + grads :]))
+    first = at_ref[0] == 0
+    totals = {}
     for out, column, columns, half, start, rows in plan:
         at = slice(start, start + rows)
         a, b = (own, other) if half == 0 else (other, own)
-        value = jnp.where(first, a[at], b[at])
-        outs[out][:, column : column + columns] = value[:, :columns].astype(F32)
-
-
-def unpack(core, own, other, matrices):
+        value = jnp.where(first, a[at], b[at])[:, :columns].astype(F32)
+        here = slice(column, column + columns)
+        outs[out][:, here] = value
+        if out in weights:
+            part = jnp.sum(value * weights[out][:, here].astype(F32), 1, keepdims=True)
+            totals[out] = totals[out] + part if out in totals else part
+    for out, ref in sums.items():
+        ref[...] = jnp.broadcast_to(totals[out], ref.shape)
+
+
+def unpack(at, own, other, matrices):
     piece = own.shape[1]
-    plan, shapes, start = [], [], 0
-    for rows, pieces, columns in matrices:
-        ends = np.cumsum([0] + list(columns))
+    plan, shapes, weights, start = [], [], {}, 0
+    for rows, pieces, parts in matrices:
+        ends = np.cumsum([0] + [w.shape[1] for w, _ in parts])
         for half in range(2):
             for i in range(pieces):
                 column = (half * pieces + i) * piece
-                for k, size in enumerate(columns):
+                for k, (w, _) in enumerate(parts):
                     if ends[k] <= column < ends[k + 1]:
                         offset = int(column - ends[k])
                         plan.append(
-                            (len(shapes) + k, offset, min(piece, size - offset), half, start + i * rows, rows)
+                            (len(shapes) + k, offset, min(piece, w.shape[1] - offset), half, start + i * rows, rows)
                         )
-        shapes += [jax.ShapeDtypeStruct((rows, size), F32) for size in columns]
+        for w, wanted in parts:
+            if wanted:
+                weights[len(shapes)] = w
+            shapes.append(jax.ShapeDtypeStruct((rows, w.shape[1]), F32))
         start += pieces * rows
-    return in_place(functools.partial(unpack_body, plan=plan), (core, own, other), shapes, "unpack")
+    grads = len(shapes)
+    summed = list(weights)
+    shapes += [jax.ShapeDtypeStruct((shapes[k].shape[0], 128), F32) for k in summed]
+
+    def whole(shape):
+        return pl.BlockSpec(shape, lambda i, at: (0, 0))
+
+    outs = pl.pallas_call(
+        functools.partial(unpack_body, plan=plan, summed=summed, grads=grads),
+        grid_spec=pltpu.PrefetchScalarGridSpec(
+            num_scalar_prefetch=1,
+            grid=(1,),
+            in_specs=[whole(own.shape), whole(other.shape)]
+            + [pl.BlockSpec(shapes[k].shape, lambda i, at: (at[1], 0)) for k in summed],
+            out_specs=[whole(v.shape) for v in shapes],
+        ),
+        out_shape=shapes,
+        compiler_params=pltpu.CompilerParams(vmem_limit_bytes=VMEM_LIMIT),
+        cost_estimate=cost(0),
+        name="unpack",
+    )(at, own, other, *weights.values())
+    return outs[:grads], [v[:, 0] for v in outs[grads:]]
 
 
 def ring(value, steps):
@@ -1359,15 +1471,6 @@
         first_body, (after(keep_x, *done), keep_y, from_x, from_y), [like(keep_x), like(keep_y)], "first_hop"
     )
     return (*held, own, from_x, from_y)
-
-
-def with_rows(pieces, place, rows):
-    own, to_x, keep_x, to_y, keep_y = pieces
-    split = keep_x.shape[0]
-    mine, beside, below, across = [rows[jnp.bitwise_xor(place, k)] for k in range(4)]
-    own = jnp.concatenate([own[:split], mine, own[split:]], 0)
-    to_x = jnp.concatenate([to_x, jnp.stack([beside, across])], 1)
-    return own, to_x, jnp.concatenate([keep_x, below], 0), to_y, keep_y
 
 
 def second_hop(held, *done):
@@ -1407,16 +1510,8 @@
     core = (lax.axis_index("dp") % 2).astype(jnp.int32)
     first = place * span
     mirrored = (count - 1 - place) * span + half
-    inverse = 1.0 / ROPE_BASE ** (jnp.arange(0, HEAD, 2).astype(F32) / HEAD)
-
-    def tables(positions):
-        angles = positions.astype(F32)[:, None] * inverse[None, :]
-        return jnp.cos(angles), jnp.sin(angles)
-
-    cosine, sine = tables(first + jnp.arange(span))
-    cos_row = jnp.concatenate([cosine] * 4, 1)
-    sin_row = jnp.concatenate([-sine, sine] * 2, 1)
-    cos_back, sin_back = tables(jnp.concatenate([first + jnp.arange(half), mirrored + jnp.arange(half)]))
+    row_tables = rotation(span, count, "rows")
+    column_tables = rotation(span, count, "columns")
     rate = -jnp.exp(decay_log)
     pad = (0, 128 - SSM_HEADS)
     rate_row = jnp.pad(rate, pad)[None]
@@ -1440,7 +1535,7 @@
         return mine, other_core(yours), 0, mine.shape[1]
 
     halo = along(tokens[:, span - 16 :], 1)
-    hidden, q, kv = enter(after(tokens, halo), norm_one[None], w_query, w_key, w_value, cos_row, sin_row)
+    hidden, q, kv = enter(here, after(tokens, halo), norm_one[None], w_query, w_key, w_value, row_tables)
     kvs = [kv] + [ring(kv, r) for r in range(1, count)]
     q_other = mirror(q[:, half:])
     z, conv, pre, x, bk, cq, dt, sg, cum, cumt, state = mixer(
@@ -1448,15 +1543,18 @@
         step_row, rate_row * LOG2E, expand,
     )
     states = lax.all_gather(state, "seq")
-    o_near, o_far, lse = attend(blocks, lengths, sources, after(q, state), q_other, kvs)
+    skip_row, blocks, sources = [after(v, state) for v in (skip_row, blocks, sources)]
+    gated_row = after(gated_gain, state)[None]
+    gact = grad_act(pos, lengths, after(cotangent, state), w_down)
+    o_near, o_far, lse = attend(blocks, lengths, sources, after(q, gact), q_other, kvs)
     o_back = mirror(o_far)
     mixed, mix_low, held = scan_forward(
-        here, after(x, o_near), bk, cq, dt, cum, cumt, skip_row, z, gated_gain[None], expand, states
+        here, after(x, o_near), bk, cq, dt, cum, cumt, skip_row, z, gated_row, expand, states
     )
     hid = with_other(hidden)
     mix_pair = with_other(mix_low)
-    output, lefts, mine, yours, grad_mid, g_norm_two = middle(
-        pos, lengths, o_near, o_back, after(mix_low, hid[1]), tokens, cotangent, w_attn_out, w_mix_out, w_gate, w_up, w_down,
+    output, lefts, mine, yours, grad_mid = middle(
+        pos, lengths, o_near, o_back, after(mix_low, hid[1]), tokens, cotangent, gact, w_attn_out, w_mix_out, w_gate, w_up, w_down,
         norm_two[None],
     )
     square = "hops" if count == 4 else ""
@@ -1466,11 +1564,10 @@
     ffn_rights = [(*rights[:2], k * ff // 2, ff // 2) for k in range(2)]
     grad_ffn, grad_branch = [(*rights[:2], ff + k * width // 2, width // 2) for k in range(2)]
     out_lefts = ((*lefts[:2], width, ff), (*lefts[:2], width + ff, w_attn_out.shape[0]), mix_pair, hid)
-    do_near, do_far, grad_mixed, gz_m, gz_y, g_gated, adjoint = branch_back(
-        core_here, mine, yours, mixed, z, cq, cum, w_attn_out, w_mix_out, gated_gain[None], expand
+    do_near, do_far, grad_mixed, gz_m, gz_y, adjoint = branch_back(
+        core_here, mine, yours, mixed, z, cq, cum, w_attn_out, w_mix_out, gated_row, expand
     )
     adjoints = [along(adjoint, -r) for r in range(1, count)]
-    do_other = mirror(do_far)
     part_ffn = tall_grad(after(here, do_near), ffn_left, ffn_rights, 512, count, square, name="grad_ffn_in")
     part_out = wide_grad(
         after(here, part_ffn[0], *adjoints), out_lefts, (grad_ffn, grad_branch, grad_branch, with_other(gz_m, gz_y)), count,
@@ -1478,12 +1575,14 @@
     )
     ffn_held = first_hop(part_ffn, part_out[0]) if square else scatter_seq(part_ffn)
     gc_m, gc_y, tail, head, g_conv_small, g_skip, g_small = scan_backward(
-        after(x, part_out[0]), bk, cq, dt, sg, cum, cumt, grad_mixed, mixed, held, pre, conv, skip_row, rate_row,
+        after(x, part_out[0], ffn_held), bk, cq, dt, sg, cum, cumt, grad_mixed, mixed, held, pre, conv, skip_row, rate_row,
         conv_weight, expand, core_here, adjoints,
     )
-    out_held = first_hop(part_out) if square else scatter_seq(part_out)
+    do_other = mirror(after(do_far, head))
     ffn_sum = second_hop(ffn_held) if square else ffn_held
-    head = after(head, out_held, ffn_sum)
+    out_held = first_hop([after(v, ffn_held) for v in part_out]) if square else scatter_seq(part_out)
+    head = after(head, ffn_sum, out_held)
+    ffn_sum = offloaded_sum_z(ffn_sum, 0)
     returned = along(low(head), -1).astype(F32)[:, : taps - 1]
     g_conv_weight = g_conv_small[:taps]
     beside = ((0, 0), (0, 0), (0, tail.shape[2] - conv_width))
@@ -1501,13 +1600,8 @@
     part_in = tall_grad(
         here, hid, (with_other(gc_m, gc_y),), 256, count, "direct" if square else "", name="grad_conv_in"
     )
-    ffn_sum = offloaded_sum_z(ffn_sum, 0)
-    out_sum = second_hop(out_held, part_in[0]) if square else out_held
-    order = (part_in[0], out_sum)
-    out_sum = offloaded_sum_z(out_sum, 1)
-
     small = [
-        g_norm_two[0], g_gated[0], g_conv_weight.reshape(-1), g_conv_small[taps], g_skip[0],
+        g_conv_weight.reshape(-1), g_conv_small[taps], g_skip[0],
         g_small[0], g_small[1],
     ]
     sizes = [v.shape[0] for v in small]
@@ -1526,14 +1620,16 @@
     def back(group, order):
         near, far, parts = attend_backward(
             group, blocks, lengths, sources, after(q, *order), q_other, do_near, do_other, o_near, o_far, lse,
-            cos_back.T, sin_back.T, kvs,
+            column_tables, kvs,
         )
         return near, mirror(far), [parts[0]] + [ring(parts[r], -r) for r in range(1, count)]
 
-    dq_near, dq_far, pieces = back(0, order)
+    dq_near, dq_far, pieces = back(0, (part_in[0],))
+    out_sum = second_hop(out_held, dq_near) if square else out_held
     in_sum = direct_sum([after(part_in[0], dq_near), *part_in[1:]]) if square else scatter_seq(part_in)
     total = small_step(total)
-    results = back(1, (dq_near, in_sum, ffn_sum, total))
+    results = back(1, (dq_near, in_sum, ffn_sum, out_sum, total))
+    out_sum = offloaded_sum_z(out_sum, 1)
     four = lax.axis_size("dp") == 8
     in_sum = offloaded_sum_z(in_sum, 2)
     total = small_step(after(total, dq_near))
@@ -1542,57 +1638,36 @@
     )
     total = small_step(after(total, results[0]))
     heads = heads_back(
-        core_here, after(cos_row, gh, total), sin_row, (dq_near, results[0]), (dq_far, results[1]), pieces + results[2]
+        core_here, after(here, gh, total), row_tables, (dq_near, results[0]), (dq_far, results[1]), pieces + results[2]
     )
     heads_pairs = with_other(*heads[:2]), with_other(*heads[2:])
-    grad_tokens, g_norm_one = leave(
-        core_here, tokens, grad_mid, gh, heads, norm_one[None], w_query, w_key, w_value
-    )
     total = small_step(after(total, gh))
-    part_qkv = tall_grad(
-        after(here, grad_tokens, out_sum, total), hid, heads_pairs, 128, count, square, name="grad_qkv"
-    )
-    norm_rows = low(g_norm_one.reshape(count, -1))
-    columns = min(128, norm_rows.shape[1])
-    norm_rows = norm_rows.reshape(count, -1, columns)
-    norm_shape = norm_rows.shape[1:]
-    norm_rows = jnp.pad(norm_rows, ((0, 0), (0, -norm_shape[0] % 16), (0, 128 - columns)))
-    norm_at = 2 * width // count if square else part_qkv.shape[1]
-    if square:
-        part_qkv = with_rows(part_qkv, place, norm_rows)
-    else:
-        part_qkv = jnp.concatenate([part_qkv, norm_rows], 1)
+    part_qkv = tall_grad(after(here, out_sum, total), hid, heads_pairs, 128, count, square, name="grad_qkv")
+    grad_tokens = leave(
+        core_here, tokens, grad_mid, after(gh, part_qkv[0]), heads, norm_one[None], w_query, w_key, w_value
+    )
     while hops:
         total = small_step(total)
-    qkv_held = first_hop(part_qkv, out_sum, in_sum, total) if square else scatter_seq(part_qkv)
-    qkv_sum = second_hop(qkv_held, total) if square else qkv_held
+    qkv_held = first_hop(part_qkv, out_sum, total, grad_tokens) if square else scatter_seq(part_qkv)
+    qkv_sum = second_hop(qkv_held, total, in_sum) if square else qkv_held
     ffn_sum, out_sum, in_sum = [after(v, qkv_sum) for v in (ffn_sum, out_sum, in_sum)]
-    block = width // count
-
-    def rows_of(*weights):
-        return [(v.shape[0] // count, v.shape[1] // 2 // PIECE, (v.shape[1],)) for v in weights]
-
-    s_gate, s_up = unpack(core_here, ffn_sum, other_core(ffn_sum), [(block, 2, (v.shape[1],)) for v in (w_gate, w_up)])
-    s_down, s_attn_out, s_mix_out, s_gatez = unpack(
-        core_here, out_sum, other_core(out_sum), rows_of(w_down, w_attn_out, w_mix_out, w_gatez)
-    )
-    s_conv, s_step = unpack(
-        core_here, in_sum, other_core(in_sum),
-        [(block, (conv_width + 256) // 2 // PIECE, (conv_width, SSM_HEADS))],
-    )
+    at = jnp.stack([core, place])
+
+    def matrix(pieces, *weights, wanted=True):
+        return weights[0].shape[0] // count, pieces, [(w, wanted) for w in weights]
+
+    (s_gate, s_up), two_sums = unpack(at, ffn_sum, other_core(ffn_sum), [matrix(2, w_gate), matrix(2, w_up)])
+    (s_down, s_attn_out, s_mix_out, s_gatez), (gated_sum, z_sum) = unpack(
+        at, out_sum, other_core(out_sum),
+        [matrix(2, w_down, wanted=False), matrix(2, w_attn_out, wanted=False), matrix(2, w_mix_out), matrix(3, w_gatez)],
+    )
+    (s_conv, s_step), in_sums = unpack(at, in_sum, other_core(in_sum), [matrix(4, w_conv_in, w_step)])
     if four:
         qkv_sum = sum_four(qkv_sum, s_gate, s_down, s_conv)
     else:
         qkv_sum = sum_z(qkv_sum)
     got = other_core(qkv_sum)
-    norm_parts = [v[norm_at : norm_at + norm_shape[0], : norm_shape[1]].astype(F32) for v in (qkv_sum, got)]
-    s_norm_one = (norm_parts[0] + norm_parts[1]).reshape(-1)
-    qkv_sum, got = [
-        jnp.concatenate([v[:norm_at], v[norm_at + norm_rows.shape[1] :]], 0) for v in (qkv_sum, got)
-    ]
-    s_query, s_key, s_value = unpack(
-        core_here, qkv_sum, got, [(block, 2, (w_query.shape[1],)), (block, 1, (w_key.shape[1], w_value.shape[1]))]
-    )
+    (s_query, s_key, s_value), qkv_sums = unpack(at, qkv_sum, got, [matrix(2, w_query), matrix(1, w_key, w_value)])
     total = total.reshape(-1)
     starts = np.cumsum([0] + sizes)
     small = [total[a:b] for a, b in zip(starts[:-1], starts[1:])]
@@ -1601,8 +1676,10 @@
         n = v.shape[0] // count
         return lax.dynamic_slice(v, (place * n,), (n,))
 
-    s_norm_two, s_gated = [own(v) for v in small[:2]]
-    s_skip = jnp.sum(small[4].reshape(SSM_HEADS, SSM_HEAD), 1)
+    s_norm_one = (z_sum + in_sums[0] + in_sums[1] + qkv_sums[0] + qkv_sums[1] + qkv_sums[2]) / own(norm_one)
+    s_norm_two = (two_sums[0] + two_sums[1]) / own(norm_two)
+    s_gated = gated_sum / own(gated_gain)
+    s_skip = jnp.sum(small[2].reshape(SSM_HEADS, SSM_HEAD), 1)
     return (
         output,
         grad_tokens,
@@ -1613,10 +1690,10 @@
         s_gatez,
         s_conv,
         s_step,
-        small[2].reshape(taps, -1),
-        small[3],
-        small[6][:SSM_HEADS],
-        small[5][:SSM_HEADS],
+        small[0].reshape(taps, -1),
+        small[1],
+        small[4][:SSM_HEADS],
+        small[3][:SSM_HEADS],
         s_skip,
         s_gated,
         s_attn_out,

time: 544 us -> 514 us (0.945)
  waiting for transfers between devices: 41.9 us -> 29.5 us
  starting transfers between devices: 75.1 us -> 63.6 us
    pallas_call x13 -> x14, Pallas kernels: 42.4 us -> 57 us  [the longest x8 22.5 us: in_place(): pl.pallas_call(body, grid=(1 if columns is None else outs[0].shape[-1] //...]
    ppermute x17, waiting for transfers between devices: 20.9 us -> 11.1 us  [flip_seq(): return lax.ppermute(value, 'seq', [(i, i ^ bit) for i in range(n)])]
    ppermute x17, starting transfers between devices: 20.1 us -> 13 us  [flip_seq(): return lax.ppermute(value, 'seq', [(i, i ^ bit) for i in range(n)])]
    ppermute x5, waiting for transfers between devices: 6.34 us -> 0.01 us  [mirror(): return lax.ppermute(value, 'seq', [(i, n - 1 - i) for i in range(n)])]
    concatenate x6 -> x1, other arithmetic: 6.47 us -> 0.58 us  [on_device(): jnp.concatenate([base + jnp.arange(0, half, rows, dtype=jnp.int32) for ba...]
  transfers between devices with their start and end apart: 58 -> 58, of which waited for: 10 -> 9; matrix products, arithmetic and copies ran while one was open for 6% -> 5% of each run, Pallas kernels for 57% -> 60%
where the time goes in v4:
time: 514 us; the launch traced here: 507 us
  Pallas kernels  367 us (71%)
  starting transfers between devices  63.6 us (12%)
  waiting for transfers between devices  29.5 us (6%)
  local copies, waits for them, and re-layouts  18.1 us (4%)
  between operations  15.3 us (3%)
  other arithmetic  13.5 us (3%)
    pallas_call x2, Pallas kernels, attend_backward(): pl.pallas_call(functools.partial(attend_back_body, rows=rows, keys=keys,...  68.2 us
    pallas_call x1, Pallas kernels, middle(): pl.pallas_call(functools.partial(middle_body, rows=rows, blocks=blocks),...  41.1 us
    pallas_call x1, Pallas kernels, scan_backward(): pl.pallas_call(functools.partial(scan_back_body, chunks=chunks, conv_widt...  34.9 us
    pallas_call x3, Pallas kernels, tall_grad(): pl.pallas_call(functools.partial(tall_body, n=n, widths=widths, square=sq...  32.6 us
    pallas_call x1, Pallas kernels, attend(): pl.pallas_call(functools.partial(attend_body, rows=rows, keys=keys, block...  28.8 us
    ppermute x18, starting transfers between devices, flip_dp(): return lax.ppermute(value, 'dp', [(i, i ^ bit) for i in range(n)])  26.4 us
    pallas_call x8, Pallas kernels, in_place(): pl.pallas_call(body, grid=(1 if columns is None else outs[0].shape[-1] //...  22.5 us
    pallas_call x1, Pallas kernels, wide_grad(): pl.pallas_call(functools.partial(wide_body, parts=len(lefts), group=n //...  22.5 us
  transfers between devices with their start and end apart: 58, of which 9 were waited for; matrix products, arithmetic and copies ran while one was open for 5% of the time, Pallas kernels for 60%

profile of v4, /device:TPU:1, one launch (start us, length us, event | category | flops | bytes accessed | tf_op | source)
XLA Modules:
  0.0 507.4 jit_solution(11470867243013073490)
XLA Ops:
  20.6 7.3 %enter.1 = (bf16[1,1024,1024]{2,1,0:T(8,128)(2,1)}, bf16[1,1024,512]{2,1,0:T(8,128)(2,1)}, bf16[1,1024,256]{2,1,0:T(8,128)(2,1)}) custom-call(s32[1]{0:T(128)} %bitcast.2.place_ref, bf16[1,1024,1024]{2,1,0:T(8,128)(2,1)} %tok_ref.4, f32[1,1024]{1,0:T(1,128)} %bitcast.60, bf16[1024,512]{1,0:T(8,128)(2,1)} %rest_0_.7, bf16[1024,128]{1,0:T(8,128)(2,1)} %rest_1_.6, ...), custom_call_target="tpu_custom_call" | custom-call | flops 24000000000 | bytes 800000 | tf_op jit(solution)/shard_map/enter/pallas_call | solution.py:166
  33.6 21.5 %mixer.1 = (bf16[1,1024,1536]{2,1,0:T(8,128)(2,1)}, bf16[1,1024,1792]{2,1,0:T(8,128)(2,1)}, bf16[1,1024,1792]{2,1,0:T(8,128)(2,1)}, bf16[1,1024,1536]{2,1,0:T(8,...) custom-call(s32[2]{0:T(128)} %pad_add_fusion.pos_ref, ...), custom_call_target="tpu_custom_call" | custom-call | flops 60000002048 | bytes 2000000 | tf_op jit(solution)/shard_map/mixer/pallas_call | solution.py:257
  55.4 9.4 %grad_act.1.gact_ref = bf16[1,1024,2048]{2,1,0:T(8,128)(2,1)} custom-call(s32[2]{0:T(128)} %pad_add_fusion.pos_ref, s32[1]{0:T(128)S(6)} %copy.73.len_ref, bf16[1,1024,1024]{2,1,0:T(8,128)(2,1)} %cot_ref.2, bf16[2048,1024]{1,0:T(8,128)(2,1)} %wd_ref.3), custom_call_target="tpu_custom_call" | custom-call | tf_op jit(solution)/shard_map/grad_act/pallas_call | solution.py:388
  67.5 28.8 %attend.1 = (bf16[1,512,512]{2,1,0:T(8,128)(2,1)}, bf16[1,512,512]{2,1,0:T(8,128)(2,1)}, f32[1,8,1024]{2,1,0:T(8,128)}) custom-call(s32[4]{0:T(128)} %pad_add_fusion.1.pos_ref, s32[1]{0:T(128)S(6)} %copy.73.len_ref, s32[4]{0:T(128)} %compare_select_fusion.from_ref, bf16[1,1024,512]{2,1,0:T(8,128)(2,1)} %get-tuple-element.273.q_ref, ...), custom_call_target="tpu_custom_call" | custom-call | flops 77999996928 | bytes 2600000 | tf_op jit(solution)/shard_map/attend/pallas_call | solution.py:959
  98.4 16.1 %scan_forward.1 = (f32[1,1024,1536]{2,1,0:T(8,128)}, bf16[1,1024,1536]{2,1,0:T(8,128)(2,1)}, bf16[1,8,128,1536]{3,2,1,0:T(8,128)(2,1)}) custom-call(s32[1]{0:T(128)} %bitcast.2.place_ref, bf16[1,1024,1536]{2,1,0:T(8,128)(2,1)} %get-tuple-element.237.x_ref, bf16[1,1024,128]{2,1,0:T(8,128)(2,1)} %get-tuple-element.206.bk_ref, ...), custom_call_target="tpu_custom_call" | custom-call | flops 48000000000 | bytes 1600000 | tf_op jit(solution)/shard_map/scan_forward/pallas_call | solution.py:353
  114.5 41.1 %middle.1 = (bf16[1,1024,1024]{2,1,0:T(8,128)(2,1)}, bf16[1,1024,3584]{2,1,0:T(8,128)(2,1)}, bf16[1,1024,3072]{2,1,0:T(8,128)(2,1)}, bf16[1,1024,3072]{2,1,0:T(8,128)(2,1)}, f32[1,1024,1024]{2,1,0:T(8,128)}) custom-call(s32[2]{0:T(128)} %pad_add_fusion.pos_ref, s32[1]{0:T(128)S(6)} %copy.73.len_ref, ...), custom_call_target="tpu_custom_call" | custom-call | flops 134999998464 | bytes 4500000 | tf_op jit(solution)/shard_map/middle/pallas_call | solution.py:453
  156.4 17.7 %branch_back.1 = (bf16[1,512,512]{2,1,0:T(8,128)(2,1)}, bf16[1,512,512]{2,1,0:T(8,128)(2,1)}, bf16[1,1024,1536]{2,1,0:T(8,128)(2,1)}, bf16[1,1024,768]{2,1,0:T(8...) custom-call(s32[1]{0:T(128)} %bitcast.1.core_ref, ...), custom_call_target="tpu_custom_call" | custom-call | flops 17999998976 | bytes 600000 | tf_op jit(solution)/shard_map/branch_back/pallas_call | solution.py:541
  179.2 15.5 %grad_ffn_in.1 = (bf16[1024,512]{1,0:T(8,128)(2,1)}, bf16[2,512,512]{2,1,0:T(8,128)(2,1)}, bf16[512,512]{1,0:T(8,128)(2,1)}, bf16[2,512,512]{2,1,0:T(8,128)(2,1)}, bf16[512,512]{1,0:T(8,128)(2,1)}) custom-call(s32[1]{0:T(128)} %bitcast.2.place_ref, bf16[1024,3584]{1,0:T(8,128)(2,1)} %bitcast.50, ...), custom_call_target="tpu_custom_call" | custom-call | tf_op jit(solution)/shard_map/grad_ffn_in/pallas_call | solution.py:1220
  194.7 5.0 collective-permute-done.10.rest_1_
  199.8 22.5 %grad_outs.1 = (bf16[2816,256]{1,0:T(8,128)(2,1)}, bf16[2,1280,256]{2,1,0:T(8,128)(2,1)}, bf16[1280,256]{1,0:T(8,128)(2,1)}, bf16[2,1536,256]{2,1,0:T(8,128)(2,1)}, bf16[1536,256]{1,0:T(8,128)(2,1)}) custom-call(s32[1]{0:T(128)} %bitcast.2.place_ref, bf16[1024,3584]{1,0:T(8,128)(2,1)} %bitcast.51, ...), custom_call_target="tpu_custom_call" | custom-call | flops 48000000000 | bytes 1600000 | tf_op jit(solution)/shard_map/grad_outs/pallas_call | solution.py:1300
  229.5 34.9 %scan_backward.1 = (bf16[1,1024,1024]{2,1,0:T(8,128)(2,1)}, bf16[1,1024,1024]{2,1,0:T(8,128)(2,1)}, f32[1,8,2048]{2,1,0:T(8,128)}, f32[1,8,1792]{2,1,0:T(8,128)}...) custom-call(bf16[1,1024,1536]{2,1,0:T(8,128)(2,1)} %get-tuple-element.237.x_ref, ...), custom_call_target="tpu_custom_call" | custom-call | flops 12000000000 | bytes 400000 | tf_op jit(solution)/shard_map/scan_backward/pallas_call | solution.py:678
  264.4 7.6 %collective-permute-done.16.late_y = bf16[512,512]{1,0:T(8,128)(2,1)} collective-permute-done((bf16[512,512]{1,0:T(8,128)(2,1)}, bf16[512,512]{1,0:T(8,128)(2,1)}, u32[]{:S(2)}, u32[]{:S(2)}) %collective-permute-start.16) | collective-permute-done | bytes 524320 | tf_op jit(solution)/shard_map/ppermute | solution.py:1456
  285.3 4.4 collective-permute-start.21
  296.2 9.2 %grad_conv_in.1 = (bf16[1024,256]{1,0:T(8,128)(2,1)}, bf16[1024,256]{1,0:T(8,128)(2,1)}, bf16[1024,256]{1,0:T(8,128)(2,1)}, bf16[1024,256]{1,0:T(8,128)(2,1)}) custom-call(s32[1]{0:T(128)} %bitcast.2.place_ref, bf16[1024,1024]{1,0:T(8,128)(2,1)} %bitcast.46, bf16[1024,1024]{1,0:T(8,128)(2,1)} %collective-permute-done.6.rest_7_.left_b, ...), custom_call_target="tpu_custom_call" | custom-call | tf_op jit(solution)/shard_map/grad_conv_in/pallas_call | solution.py:1220
  308.1 34.1 %attend_backward.2 = (bf16[1,512,256]{2,1,0:T(8,128)(2,1)}, bf16[1,512,256]{2,1,0:T(8,128)(2,1)}, bf16[1,1024,128]{2,1,0:T(8,128)(2,1)}, bf16[1,1024,128]{2,1,0:...) custom-call(s32[4]{0:T(128)} %pad_add_fusion.1.pos_ref, s32[1]{0:T(128)S(6)} %copy.73.len_ref, ...), custom_call_target="tpu_custom_call" | custom-call | flops 60000002048 | bytes 2000000 | tf_op jit(solution)/shard_map/attend_backward/pallas_call | solution.py:1118
  353.3 34.1 %attend_backward.3 = (bf16[1,512,256]{2,1,0:T(8,128)(2,1)}, bf16[1,512,256]{2,1,0:T(8,128)(2,1)}, bf16[1,1024,128]{2,1,0:T(8,128)(2,1)}, bf16[1,1024,128]{2,1,0:...) custom-call(s32[4]{0:T(128)} %pad_add_fusion.1.pos_ref, s32[1]{0:T(128)S(6)} %copy.73.len_ref, ...), custom_call_target="tpu_custom_call" | custom-call | flops 3000000000 | bytes 100000 | tf_op jit(solution)/shard_map/attend_backward/pallas_call | solution.py:1118
  392.7 13.4 %leave_mixer.1.gh_ref = f32[1,1024,1024]{2,1,0:T(8,128)} custom-call(s32[1]{0:T(128)} %bitcast.1.core_ref, bf16[1,1024,768]{2,1,0:T(8,128)(2,1)} %get-tuple-element.281.gz_m, bf16[1,1024,768]{2,1,0:T(8,128)(2,1)} %get-tuple-element.228.gz_y, bf16[1,1024,1024]{2,1,0:T(8,128)(2,1)} %get-tuple-element.403.gc_m, bf16[1,1024,1024]{2,1,0:T(8,128)(2,1)} %get-tuple-element.402.gc_y, ...), custom_call_target="tpu_custom_call" | custom-call | tf_op jit(solution)/shard_map/leave_mixer/pallas_call | solution.py:731
  406.2 4.5 heads_back.1
  410.6 7.1 %collective-permute-start.40 = (bf16[1024,256]{1,0:T(8,128)(2,1)}, bf16[1024,256]{1,0:T(8,128)(2,1)}, u32[]{:S(2)}, u32[]{:S(2)}) collective-permute-start(bf16[1024,256]{1,0:T(8,128)(2,1)} %bitcast.58), channel_id=1, source_target_pairs={{0,4},{4,0},{8,12},{12,8},{16,20},{20,16},{24,28},{28,24},{1,5},{5... | collective-permute-start | bytes 1572872 | tf_op jit(solution)/shard_map/ppermute | solution.py:1439
  423.7 8.0 %grad_qkv.1 = (bf16[768,128]{1,0:T(8,128)(2,1)}, bf16[2,512,128]{2,1,0:T(8,128)(2,1)}, bf16[512,128]{1,0:T(8,128)(2,1)}, bf16[2,256,128]{2,1,0:T(8,128)(2,1)}, bf16[256,128]{1,0:T(8,128)(2,1)}) custom-call(s32[1]{0:T(128)} %bitcast.2.place_ref, bf16[1024,1024]{1,0:T(8,128)(2,1)} %bitcast.47, bf16[1024,1024]{1,0:T(8,128)(2,1)} %collective-permute-done.6.rest_7_.left_b, ...), custom_call_target="tpu_custom_call" | custom-call | tf_op jit(solution)/shard_map/grad_qkv/pallas_call | solution.py:1220
  436.2 9.2 %leave.1 = f32[1,1024,1024]{2,1,0:T(8,128)} custom-call(s32[1]{0:T(128)} %bitcast.1.core_ref, bf16[1,1024,1024]{2,1,0:T(8,128)(2,1)} %tok_ref.4, f32[1,1024,1024]{2,1,0:T(8,128)} %get-tuple-element.217.gmid_ref, f32[1,1024,1024]{2,1,0:T(8,128)} %leave_mixer.1.gh_ref, bf16[1,1024,256]{2,1,0:T(8,128)(2,1)} %get-tuple-element.291.gq_m, ...), custom_call_target="tpu_custom_call" | custom-call | tf_op jit(solution)/shard_map/leave/pallas_call | solution.py:814
  449.7 7.6 %all-reduce.18.cloned.1.call-done.own = bf16[1024,256]{1,0:T(8,128)(2,1)} async-done(((bf16[1024,256]{1,0:T(8,128)(2,1)}), bf16[1024,256]{1,0:T(8,128)(2,1)}) %all-reduce.18.cloned.1.call-update) | async-done | bytes 524304 | tf_op jit(solution)/shard_map/psum | solution.py:1485
  475.0 5.2 %unpack.6 = (f32[256,2048]{1,0:T(8,128)}, f32[256,2048]{1,0:T(8,128)}, f32[256,128]{1,0:T(8,128)}, f32[256,128]{1,0:T(8,128)}) custom-call(s32[2]{0:T(128)} %pad_add_fusion.2.at_ref, bf16[1024,512]{1,0:T(8,128)(2,1)} %all-reduce.14.cloned.1.call-done.own, bf16[1024,512]{1,0:T(8,128)(2,1)} %collective-permute-done.49.other, bf16[1024,2048]{1,0:T(8,128)(2,1)} %rest_0_.6, ...), custom_call_target="tpu_custom_call" | custom-call | tf_op jit(solution)/shard_map/unpack/pallas_call | solution.py:1405
  482.6 6.0 %unpack.4 = (f32[512,1024]{1,0:T(8,128)}, f32[128,1024]{1,0:T(8,128)}, f32[384,1024]{1,0:T(8,128)}, f32[256,1536]{1,0:T(8,128)}, f32[384,128]{1,0:T(8,128)}, /*index=5*/f32[256,128]{1,0:T(8,128)}) custom-call(s32[2]{0:T(128)} %pad_add_fusion.2.at_ref, bf16[2816,256]{1,0:T(8,128)(2,1)} %all-reduce.16.cloned.1.call-done.own, ...), custom_call_target="tpu_custom_call" | custom-call | tf_op jit(solution)/shard_map/unpack/pallas_call | solution.py:1405
  (225 shorter events, 122.1 us)
Async XLA Ops:
  7.2 91.2 %all-gather.3.cloned.1.call-start = ((), (), s32[]{:S(2)}) async-start(), calls=%async_computation.3 | async-start | bytes 2211840 | tf_op jit(solution)/shard_map/all_gather | solution.py:1545
  27.9 39.6 %collective-permute-start.2 = (bf16[1,1024,256]{2,1,0:T(8,128)(2,1)}, bf16[1,1024,256]{2,1,0:T(8,128)(2,1)}, u32[]{:S(2)}, u32[]{:S(2)}) collective-permute-start(bf16[1,1024,256]{2,1,0:T(8,128)(2,1)} %get-tuple-element.201.rest_0_), channel_id=1, source_target_pairs={{0,1},{1,2},{2,3},{3,0},{4,5},{5,6},{6,7},{7,4},{8,9},{9,10},{10,1... | collective-permute-start | bytes 1572872 | tf_op jit(solution)/shard_map/ppermute | solution.py:1424
  29.1 38.3 %collective-permute-start.3 = (bf16[1,1024,256]{2,1,0:T(8,128)(2,1)}, bf16[1,1024,256]{2,1,0:T(8,128)(2,1)}, u32[]{:S(2)}, u32[]{:S(2)}) collective-permute-start(bf16[1,1024,256]{2,1,0:T(8,128)(2,1)} %get-tuple-element.201.rest_0_), channel_id=1, source_target_pairs={{0,2},{1,3},{2,0},{3,1},{4,6},{5,7},{6,4},{7,5},{8,10},{9,11},{10,... | collective-permute-start | bytes 1572872 | tf_op jit(solution)/shard_map/ppermute | solution.py:1424
  29.2 38.2 %collective-permute-start.4 = (bf16[1,1024,256]{2,1,0:T(8,128)(2,1)}, bf16[1,1024,256]{2,1,0:T(8,128)(2,1)}, u32[]{:S(2)}, u32[]{:S(2)}) collective-permute-start(bf16[1,1024,256]{2,1,0:T(8,128)(2,1)} %get-tuple-element.201.rest_0_), channel_id=1, source_target_pairs={{0,3},{1,0},{2,1},{3,2},{4,7},{5,4},{6,5},{7,6},{8,11},{9,8},{10,9... | collective-permute-start | bytes 1572872 | tf_op jit(solution)/shard_map/ppermute | solution.py:1424
  33.4 34.1 %collective-permute-start.1 = (bf16[1,512,512]{2,1,0:T(8,128)(2,1)}, bf16[1,512,512]{2,1,0:T(8,128)(2,1)}, u32[]{:S(2)}, u32[]{:S(2)}) collective-permute-start(bf16[1,512,512]{2,1,0:T(8,128)(2,1)} %slice.161), channel_id=1, source_target_pairs={{0,3},{1,2},{2,1},{3,0},{4,7},{5,6},{6,5},{7,4},{8,11},{9,10},{10,... | collective-permute-start | bytes 1572872 | tf_op jit(solution)/shard_map/ppermute | solution.py:1434
  55.2 293.9 %all-reduce.14.cloned.1.call-start = ((), (), s32[]{:S(2)}) async-start(), calls=%async_computation | async-start | bytes 2097152 | tf_op jit(solution)/shard_map/psum | solution.py:1485
  65.4 49.1 %collective-permute-start.6 = (bf16[1024,1024]{1,0:T(8,128)(2,1)}, bf16[1024,1024]{1,0:T(8,128)(2,1)}, u32[]{:S(2)}, u32[]{:S(2)}) collective-permute-start(bf16[1024,1024]{1,0:T(8,128)(2,1)} %bitcast.44), channel_id=1, source_target_pairs={{0,4},{4,0},{8,12},{12,8},{16,20},{20,16},{24,28},{28,24},{1,5},{5... | collective-permute-start | bytes 6291464 | tf_op jit(solution)/shard_map/ppermute | solution.py:1439
  156.1 43.7 %collective-permute-start.12 = (bf16[1024,1536]{1,0:T(8,128)(2,1)}, bf16[1024,1536]{1,0:T(8,128)(2,1)}, u32[]{:S(2)}, u32[]{:S(2)}) collective-permute-start(bf16[1024,1536]{1,0:T(8,128)(2,1)} %bitcast.65), channel_id=1, source_target_pairs={{0,4},{4,0},{8,12},{12,8},{16,20},{20,16},{24,28},{28,24},{1,5},{5... | collective-permute-start | bytes 9437192 | tf_op jit(solution)/shard_map/ppermute | solution.py:1439
  226.6 48.9 %collective-permute-start.19 = (bf16[2,1536,256]{2,1,0:T(8,128)(2,1)}, bf16[2,1536,256]{2,1,0:T(8,128)(2,1)}, u32[]{:S(2)}, u32[]{:S(2)}) collective-permute-start(bf16[2,1536,256]{2,1,0:T(8,128)(2,1)} %get-tuple-element.253), channel_id=1, source_target_pairs={{0,2},{1,3},{2,0},{3,1},{4,6},{5,7},{6,4},{7,5},{8,10},{9,11},{10,... | collective-permute-start | bytes 4718600 | tf_op jit(solution)/shard_map/ppermute | solution.py:1456
  226.8 48.8 %collective-permute-start.18 = (bf16[2,1280,256]{2,1,0:T(8,128)(2,1)}, bf16[2,1280,256]{2,1,0:T(8,128)(2,1)}, u32[]{:S(2)}, u32[]{:S(2)}) collective-permute-start(bf16[2,1280,256]{2,1,0:T(8,128)(2,1)} %get-tuple-element.251), channel_id=1, source_target_pairs={{0,1},{1,0},{2,3},{3,2},{4,5},{5,4},{6,7},{7,6},{8,9},{9,8},{10,11... | collective-permute-start | bytes 3932168 | tf_op jit(solution)/shard_map/ppermute | solution.py:1456
  228.1 43.9 %collective-permute-start.16 = (bf16[512,512]{1,0:T(8,128)(2,1)}, bf16[512,512]{1,0:T(8,128)(2,1)}, u32[]{:S(2)}, u32[]{:S(2)}) collective-permute-start(bf16[512,512]{1,0:T(8,128)(2,1)} %get-tuple-element.235), channel_id=1, source_target_pairs={{0,2},{1,3},{2,0},{3,1},{4,6},{5,7},{6,4},{7,5},{8,10},{9,11},{10,... | collective-permute-start | bytes 1572872 | tf_op jit(solution)/shard_map/ppermute | solution.py:1456
  229.3 42.8 %collective-permute-start.17 = (bf16[512,512]{1,0:T(8,128)(2,1)}, bf16[512,512]{1,0:T(8,128)(2,1)}, u32[]{:S(2)}, u32[]{:S(2)}) collective-permute-start(bf16[512,512]{1,0:T(8,128)(2,1)} %get-tuple-element.236), channel_id=1, source_target_pairs={{0,1},{1,0},{2,3},{3,2},{4,5},{5,4},{6,7},{7,6},{8,9},{9,8},{10,11... | collective-permute-start | bytes 1572872 | tf_op jit(solution)/shard_map/ppermute | solution.py:1456
  293.8 129.2 %all-reduce.16.cloned.1.call-start = ((), (), s32[]{:S(2)}) async-start(), calls=%async_computation.1 | async-start | bytes 2883584 | tf_op jit(solution)/shard_map/psum | solution.py:1485
  293.9 48.4 %collective-permute-start.26 = (bf16[1280,256]{1,0:T(8,128)(2,1)}, bf16[1280,256]{1,0:T(8,128)(2,1)}, u32[]{:S(2)}, u32[]{:S(2)}) collective-permute-start(bf16[1280,256]{1,0:T(8,128)(2,1)} %get-tuple-element.254), channel_id=1, source_target_pairs={{0,2},{1,3},{2,0},{3,1},{4,6},{5,7},{6,4},{7,5},{8,10},{9,11},{10,... | collective-permute-start | bytes 1966088 | tf_op jit(solution)/shard_map/ppermute | solution.py:1456
  293.9 48.3 %collective-permute-start.27 = (bf16[1536,256]{1,0:T(8,128)(2,1)}, bf16[1536,256]{1,0:T(8,128)(2,1)}, u32[]{:S(2)}, u32[]{:S(2)}) collective-permute-start(bf16[1536,256]{1,0:T(8,128)(2,1)} %get-tuple-element.255), channel_id=1, source_target_pairs={{0,1},{1,0},{2,3},{3,2},{4,5},{5,4},{6,7},{7,6},{8,9},{9,8},{10,11... | collective-permute-start | bytes 2359304 | tf_op jit(solution)/shard_map/ppermute | solution.py:1456
  305.3 41.2 %collective-permute-start.23 = (bf16[1024,256]{1,0:T(8,128)(2,1)}, bf16[1024,256]{1,0:T(8,128)(2,1)}, u32[]{:S(2)}, u32[]{:S(2)}) collective-permute-start(bf16[1024,256]{1,0:T(8,128)(2,1)} %get-tuple-element.266), channel_id=1, source_target_pairs={{0,1},{1,0},{2,3},{3,2},{4,5},{5,4},{6,7},{7,6},{8,9},{9,8},{10,11... | collective-permute-start | bytes 1572872 | tf_op jit(solution)/shard_map/ppermute | solution.py:1456
  306.8 39.7 %collective-permute-start.24 = (bf16[1024,256]{1,0:T(8,128)(2,1)}, bf16[1024,256]{1,0:T(8,128)(2,1)}, u32[]{:S(2)}, u32[]{:S(2)}) collective-permute-start(bf16[1024,256]{1,0:T(8,128)(2,1)} %get-tuple-element.267), channel_id=1, source_target_pairs={{0,2},{1,3},{2,0},{3,1},{4,6},{5,7},{6,4},{7,5},{8,10},{9,11},{10,... | collective-permute-start | bytes 1572872 | tf_op jit(solution)/shard_map/ppermute | solution.py:1456
  306.9 39.7 %collective-permute-start.25 = (bf16[1024,256]{1,0:T(8,128)(2,1)}, bf16[1024,256]{1,0:T(8,128)(2,1)}, u32[]{:S(2)}, u32[]{:S(2)}) collective-permute-start(bf16[1024,256]{1,0:T(8,128)(2,1)} %get-tuple-element.268), channel_id=1, source_target_pairs={{0,3},{1,2},{2,1},{3,0},{4,7},{5,6},{6,5},{7,4},{8,11},{9,10},{10,... | collective-permute-start | bytes 1572872 | tf_op jit(solution)/shard_map/ppermute | solution.py:1456
  349.1 108.2 %all-reduce.18.cloned.1.call-start = ((), (), s32[]{:S(2)}) async-start(), calls=%async_computation.2 | async-start | bytes 1048576 | tf_op jit(solution)/shard_map/psum | solution.py:1485
  349.2 40.4 %collective-permute-start.29 = (bf16[1,512,256]{2,1,0:T(8,128)(2,1)}, bf16[1,512,256]{2,1,0:T(8,128)(2,1)S(1)}, u32[]{:S(2)}, u32[]{:S(2)}) collective-permute-start(bf16[1,512,256]{2,1,0:T(8,128)(2,1)} %get-tuple-element.275), channel_id=1, source_target_pairs={{0,3},{1,2},{2,1},{3,0},{4,7},{5,6},{6,5},{7,4},{8,11},{9,10},{10,... | collective-permute-start | bytes 786440 | tf_op jit(solution)/shard_map/ppermute | solution.py:1434
  350.3 37.0 %collective-permute-start.30 = (f32[88,128]{1,0:T(8,128)S(1)}, f32[88,128]{1,0:T(8,128)S(1)}, u32[]{:S(2)}, u32[]{:S(2)}) collective-permute-start(f32[88,128]{1,0:T(8,128)S(1)} %fusion.6), channel_id=1, source_target_pairs={{0,2},{1,3},{2,0},{3,1},{4,6},{5,7},{6,4},{7,5},{8,10},{9,11},{10,... | collective-permute-start | bytes 135176 | tf_op jit(solution)/shard_map/ppermute | solution.py:1456
  351.8 38.0 %collective-permute-start.31 = (bf16[1,1024,128]{2,1,0:T(8,128)(2,1)}, bf16[1,1024,128]{2,1,0:T(8,128)(2,1)}, u32[]{:S(2)}, u32[]{:S(2)}) collective-permute-start(bf16[1,1024,128]{2,1,0:T(8,128)(2,1)} %get-tuple-element.278), channel_id=1, source_target_pairs={{0,3},{1,0},{2,1},{3,2},{4,7},{5,4},{6,5},{7,6},{8,11},{9,8},{10,9... | collective-permute-start | bytes 786440 | tf_op jit(solution)/shard_map/ppermute | solution.py:1424
  351.9 39.4 %collective-permute-start.32 = (bf16[1,1024,128]{2,1,0:T(8,128)(2,1)}, bf16[1,1024,128]{2,1,0:T(8,128)(2,1)}, u32[]{:S(2)}, u32[]{:S(2)}) collective-permute-start(bf16[1,1024,128]{2,1,0:T(8,128)(2,1)} %get-tuple-element.279), channel_id=1, source_target_pairs={{0,2},{1,3},{2,0},{3,1},{4,6},{5,7},{6,4},{7,5},{8,10},{9,11},{10,... | collective-permute-start | bytes 786440 | tf_op jit(solution)/shard_map/ppermute | solution.py:1424
  353.1 38.3 %collective-permute-start.33 = (bf16[1,1024,128]{2,1,0:T(8,128)(2,1)}, bf16[1,1024,128]{2,1,0:T(8,128)(2,1)}, u32[]{:S(2)}, u32[]{:S(2)}) collective-permute-start(bf16[1,1024,128]{2,1,0:T(8,128)(2,1)} %get-tuple-element.280), channel_id=1, source_target_pairs={{0,1},{1,2},{2,3},{3,0},{4,5},{5,6},{6,7},{7,4},{8,9},{9,10},{10,1... | collective-permute-start | bytes 786440 | tf_op jit(solution)/shard_map/ppermute | solution.py:1424
  (55 other events, 644.3 us)
Sparse Core Ops, SparseCore 0:
  55.3 35.2 all-gather.2
  293.9 50.9 all-reduce.13
  349.2 68.3 all-reduce.15
  420.0 37.2 all-reduce.17

commit v5 on v4

--- a/solution.py
+++ b/solution.py
@@ -432,7 +432,7 @@
     gh2 = dot(gg, wg_ref[...], NT) + dot(gu, wu_ref[...], NT)
     g = gh2 * gain
     gmid = cot + scale * (g - unit * jnp.mean(g * unit, -1, keepdims=True))
-    gmid_ref[0] = gmid
+    gmid_ref[0] = low(gmid)
     halves_out(pos_ref[1], (gg, gu, gffn, low(live * gmid)), mine_ref, yours_ref)
 
 
@@ -463,7 +463,7 @@
         ),
         out_shape=[
             shape(width, BF16), shape(width + ff + 512, BF16), shape(width + ff, BF16), shape(width + ff, BF16),
-            shape(width, F32),
+            shape(width, BF16),
         ],
         compiler_params=params(),
         cost_estimate=cost(45),
@@ -717,7 +717,7 @@
     gz = halves_in(core, gz_m[0], gz_y[0])
     gc = halves_in(core, gc_m[0], gc_y[0])
     gh = dot(gz, wz_ref[...], NT) + dot(gc[:, :conv_width], wc_ref[...], NT)
-    gh_ref[0] = gh + dot(gc[:, conv_width : conv_width + 128], ws_ref[...], NT)
+    gh_ref[0] = low(gh + dot(gc[:, conv_width : conv_width + 128], ws_ref[...], NT))
 
 
 def leave_mixer(core, gz, gc, wz, wc, ws):
@@ -735,7 +735,7 @@
         + [row(v.shape[2]) for v in (*gz, *gc)]
         + [full_spec(v.shape) for v in (wz, wc, ws)],
         out_specs=row(width),
-        out_shape=jax.ShapeDtypeStruct((seqs, span, width), F32),
+        out_shape=jax.ShapeDtypeStruct((seqs, span, width), BF16),
         compiler_params=params(),
         cost_estimate=cost(0),
         name="leave_mixer",
@@ -794,14 +794,14 @@
     core_ref, tok_ref, gmid_ref, gh_ref, gq_m, gq_y, gkv_m, gkv_y, gain_ref, wq_ref, wk_ref, wv_ref, gt_ref
 ):
     core = core_ref[0]
-    gh = gh_ref[0] + dot(halves_in(core, gq_m[0], gq_y[0]), wq_ref[...], NT)
+    gh = gh_ref[0].astype(F32) + dot(halves_in(core, gq_m[0], gq_y[0]), wq_ref[...], NT)
     gkv = halves_in(core, gkv_m[0], gkv_y[0])
     gh = gh + dot(gkv[:, :128], wk_ref[...], NT) + dot(gkv[:, 128:], wv_ref[...], NT)
     v = tok_ref[0].astype(F32)
     scale = lax.rsqrt(jnp.mean(v * v, -1, keepdims=True) + EPS)
     unit = v * scale
     g = gh * gain_ref[...]
-    gt_ref[0] = gmid_ref[0] + scale * (g - unit * jnp.mean(g * unit, -1, keepdims=True))
+    gt_ref[0] = gmid_ref[0].astype(F32) + scale * (g - unit * jnp.mean(g * unit, -1, keepdims=True))
 
 
 def leave(core, tokens, gmid, gh, heads, gain, wq, wk, wv):
@@ -1627,11 +1627,9 @@
     dq_near, dq_far, pieces = back(0, (part_in[0],))
     out_sum = second_hop(out_held, dq_near) if square else out_held
     in_sum = direct_sum([after(part_in[0], dq_near), *part_in[1:]]) if square else scatter_seq(part_in)
-    total = small_step(total)
-    results = back(1, (dq_near, in_sum, ffn_sum, out_sum, total))
-    out_sum = offloaded_sum_z(out_sum, 1)
+    results = back(1, (dq_near, in_sum, ffn_sum, out_sum))
     four = lax.axis_size("dp") == 8
-    in_sum = offloaded_sum_z(in_sum, 2)
+    out_sum, in_sum = offloaded_sum_z((out_sum, in_sum), 1)
     total = small_step(after(total, dq_near))
     gh = leave_mixer(
         core_here, (after(gz_m, results[0], dq_far, total, *pieces), gz_y), (gc_m, gc_y), w_gatez, w_conv_in, w_step_wide
@@ -1641,32 +1639,40 @@
         core_here, after(here, gh, total), row_tables, (dq_near, results[0]), (dq_far, results[1]), pieces + results[2]
     )
     heads_pairs = with_other(*heads[:2]), with_other(*heads[2:])
-    total = small_step(after(total, gh))
-    part_qkv = tall_grad(after(here, out_sum, total), hid, heads_pairs, 128, count, square, name="grad_qkv")
+    part_qkv = tall_grad(here, hid, heads_pairs, 128, count, square, name="grad_qkv")
     grad_tokens = leave(
-        core_here, tokens, grad_mid, after(gh, part_qkv[0]), heads, norm_one[None], w_query, w_key, w_value
-    )
-    while hops:
-        total = small_step(total)
-    qkv_held = first_hop(part_qkv, out_sum, total, grad_tokens) if square else scatter_seq(part_qkv)
-    qkv_sum = second_hop(qkv_held, total, in_sum) if square else qkv_held
-    ffn_sum, out_sum, in_sum = [after(v, qkv_sum) for v in (ffn_sum, out_sum, in_sum)]
+        core_here, tokens, grad_mid, after(gh, part_qkv[0], out_sum, in_sum), heads, norm_one[None], w_query, w_key, w_value
+    )
+    total = small_step(after(total, part_qkv[0]))
     at = jnp.stack([core, place])
 
     def matrix(pieces, *weights, wanted=True):
         return weights[0].shape[0] // count, pieces, [(w, wanted) for w in weights]
 
-    (s_gate, s_up), two_sums = unpack(at, ffn_sum, other_core(ffn_sum), [matrix(2, w_gate), matrix(2, w_up)])
+    done = (total, grad_tokens)
+    qkv_held = first_hop(part_qkv, *done) if square else scatter_seq(part_qkv)
+    ffn_sum = after(ffn_sum, heads[0])
+    (s_gate, s_up), two_sums = unpack(
+        at, after(ffn_sum, qkv_held), other_core(ffn_sum), [matrix(2, w_gate), matrix(2, w_up)]
+    )
+    total = small_step(after(total, qkv_held))
+    qkv_sum = second_hop(qkv_held, total, s_gate) if square else qkv_held
+    out_sum, in_sum = [after(v, qkv_held) for v in (out_sum, in_sum)]
     (s_down, s_attn_out, s_mix_out, s_gatez), (gated_sum, z_sum) = unpack(
-        at, out_sum, other_core(out_sum),
+        at, after(out_sum, qkv_sum), other_core(out_sum),
         [matrix(2, w_down, wanted=False), matrix(2, w_attn_out, wanted=False), matrix(2, w_mix_out), matrix(3, w_gatez)],
     )
-    (s_conv, s_step), in_sums = unpack(at, in_sum, other_core(in_sum), [matrix(4, w_conv_in, w_step)])
+    (s_conv, s_step), in_sums = unpack(
+        at, after(in_sum, qkv_sum), other_core(in_sum), [matrix(4, w_conv_in, w_step)]
+    )
     if four:
-        qkv_sum = sum_four(qkv_sum, s_gate, s_down, s_conv)
+        total = small_step(after(total, qkv_sum))
+        qkv_sum = sum_four(qkv_sum, s_conv, s_down, total)
     else:
         qkv_sum = sum_z(qkv_sum)
     got = other_core(qkv_sum)
+    while hops:
+        total = small_step(total)
     (s_query, s_key, s_value), qkv_sums = unpack(at, qkv_sum, got, [matrix(2, w_query), matrix(1, w_key, w_value)])
     total = total.reshape(-1)
     starts = np.cumsum([0] + sizes)

time: 514 us -> 505 us (0.982)
  waiting for transfers between devices: 29.5 us -> 22.4 us
    psum x3 -> x2, waiting for transfers between devices: 7.65 us -> 0.01 us  [offloaded_sum_z(): lax.psum(value, 'dp', axis_index_groups=groups[::-1 if which & 2 else 1])]
  transfers between devices with their start and end apart: 58 -> 57, of which waited for: 9 -> 8; matrix products, arithmetic and copies ran while one was open for 5% -> 5% of each run, Pallas kernels for 60% -> 62%
where the time goes in v5:
time: 505 us; the launch traced here: 497 us
  Pallas kernels  367 us (73%)
  starting transfers between devices  60.2 us (12%)
  waiting for transfers between devices  22.4 us (4%)
  local copies, waits for them, and re-layouts  18.2 us (4%)
  between operations  15.3 us (3%)
  other arithmetic  14.9 us (3%)
    pallas_call x2, Pallas kernels, attend_backward(): pl.pallas_call(functools.partial(attend_back_body, rows=rows, keys=keys,...  68.6 us
    pallas_call x1, Pallas kernels, middle(): pl.pallas_call(functools.partial(middle_body, rows=rows, blocks=blocks),...  41 us
    pallas_call x1, Pallas kernels, scan_backward(): pl.pallas_call(functools.partial(scan_back_body, chunks=chunks, conv_widt...  34.9 us
    pallas_call x3, Pallas kernels, tall_grad(): pl.pallas_call(functools.partial(tall_body, n=n, widths=widths, square=sq...  32.6 us
    pallas_call x1, Pallas kernels, attend(): pl.pallas_call(functools.partial(attend_body, rows=rows, keys=keys, block...  28.8 us
    ppermute x18, starting transfers between devices, flip_dp(): return lax.ppermute(value, 'dp', [(i, i ^ bit) for i in range(n)])  22.6 us
    pallas_call x1, Pallas kernels, wide_grad(): pl.pallas_call(functools.partial(wide_body, parts=len(lefts), group=n //...  22.6 us
    pallas_call x8, Pallas kernels, in_place(): pl.pallas_call(body, grid=(1 if columns is None else outs[0].shape[-1] //...  22.5 us
  transfers between devices with their start and end apart: 57, of which 8 were waited for; matrix products, arithmetic and copies ran while one was open for 5% of the time, Pallas kernels for 62%

profile of v5, /device:TPU:1, one launch (start us, length us, event | category | flops | bytes accessed | tf_op | source)
XLA Modules:
  0.0 497.5 jit_solution(17920472046186849817)
XLA Ops:
  8.0 3.9 collective-permute-start
  20.6 7.3 %enter.1 = (bf16[1,1024,1024]{2,1,0:T(8,128)(2,1)}, bf16[1,1024,512]{2,1,0:T(8,128)(2,1)}, bf16[1,1024,256]{2,1,0:T(8,128)(2,1)}) custom-call(s32[1]{0:T(128)} %bitcast.2.place_ref, bf16[1,1024,1024]{2,1,0:T(8,128)(2,1)} %tok_ref.4, f32[1,1024]{1,0:T(1,128)} %bitcast.58, bf16[1024,512]{1,0:T(8,128)(2,1)} %rest_0_.7, bf16[1024,128]{1,0:T(8,128)(2,1)} %rest_1_.6, ...), custom_call_target="tpu_custom_call" | custom-call | flops 24000000000 | bytes 800000 | tf_op jit(solution)/shard_map/enter/pallas_call | solution.py:166
  33.7 21.5 %mixer.1 = (bf16[1,1024,1536]{2,1,0:T(8,128)(2,1)}, bf16[1,1024,1792]{2,1,0:T(8,128)(2,1)}, bf16[1,1024,1792]{2,1,0:T(8,128)(2,1)}, bf16[1,1024,1536]{2,1,0:T(8,...) custom-call(s32[2]{0:T(128)} %pad_add_fusion.pos_ref, ...), custom_call_target="tpu_custom_call" | custom-call | flops 60000002048 | bytes 2000000 | tf_op jit(solution)/shard_map/mixer/pallas_call | solution.py:257
  55.4 9.4 %grad_act.1.gact_ref = bf16[1,1024,2048]{2,1,0:T(8,128)(2,1)} custom-call(s32[2]{0:T(128)} %pad_add_fusion.pos_ref, s32[1]{0:T(128)S(6)} %copy.73.len_ref, bf16[1,1024,1024]{2,1,0:T(8,128)(2,1)} %cot_ref.2, bf16[2048,1024]{1,0:T(8,128)(2,1)} %wd_ref.3), custom_call_target="tpu_custom_call" | custom-call | tf_op jit(solution)/shard_map/grad_act/pallas_call | solution.py:388
  67.5 28.8 %attend.1 = (bf16[1,512,512]{2,1,0:T(8,128)(2,1)}, bf16[1,512,512]{2,1,0:T(8,128)(2,1)}, f32[1,8,1024]{2,1,0:T(8,128)}) custom-call(s32[4]{0:T(128)} %pad_add_fusion.1.pos_ref, s32[1]{0:T(128)S(6)} %copy.73.len_ref, s32[4]{0:T(128)} %compare_select_fusion.from_ref, bf16[1,1024,512]{2,1,0:T(8,128)(2,1)} %get-tuple-element.274.q_ref, ...), custom_call_target="tpu_custom_call" | custom-call | flops 77999996928 | bytes 2600000 | tf_op jit(solution)/shard_map/attend/pallas_call | solution.py:959
  98.4 16.1 %scan_forward.1 = (f32[1,1024,1536]{2,1,0:T(8,128)}, bf16[1,1024,1536]{2,1,0:T(8,128)(2,1)}, bf16[1,8,128,1536]{3,2,1,0:T(8,128)(2,1)}) custom-call(s32[1]{0:T(128)} %bitcast.2.place_ref, bf16[1,1024,1536]{2,1,0:T(8,128)(2,1)} %get-tuple-element.241.x_ref, bf16[1,1024,128]{2,1,0:T(8,128)(2,1)} %get-tuple-element.210.bk_ref, ...), custom_call_target="tpu_custom_call" | custom-call | flops 48000000000 | bytes 1600000 | tf_op jit(solution)/shard_map/scan_forward/pallas_call | solution.py:353
  114.5 41.0 %middle.1 = (bf16[1,1024,1024]{2,1,0:T(8,128)(2,1)}, bf16[1,1024,3584]{2,1,0:T(8,128)(2,1)}, bf16[1,1024,3072]{2,1,0:T(8,128)(2,1)}, bf16[1,1024,3072]{2,1,0:T(8,128)(2,1)}, bf16[1,1024,1024]{2,1,0:T(8,128)(2,1)}) custom-call(s32[2]{0:T(128)} %pad_add_fusion.pos_ref, s32[1]{0:T(128)S(6)} %copy.73.len_ref, ...), custom_call_target="tpu_custom_call" | custom-call | flops 134999998464 | bytes 4500000 | tf_op jit(solution)/shard_map/middle/pallas_call | solution.py:453
  156.3 17.7 %branch_back.1 = (bf16[1,512,512]{2,1,0:T(8,128)(2,1)}, bf16[1,512,512]{2,1,0:T(8,128)(2,1)}, bf16[1,1024,1536]{2,1,0:T(8,128)(2,1)}, bf16[1,1024,768]{2,1,0:T(8...) custom-call(s32[1]{0:T(128)} %bitcast.1.core_ref, ...), custom_call_target="tpu_custom_call" | custom-call | flops 17999998976 | bytes 600000 | tf_op jit(solution)/shard_map/branch_back/pallas_call | solution.py:541
  179.1 15.5 %grad_ffn_in.1 = (bf16[1024,512]{1,0:T(8,128)(2,1)}, bf16[2,512,512]{2,1,0:T(8,128)(2,1)}, bf16[512,512]{1,0:T(8,128)(2,1)}, bf16[2,512,512]{2,1,0:T(8,128)(2,1)}, bf16[512,512]{1,0:T(8,128)(2,1)}) custom-call(s32[1]{0:T(128)} %bitcast.2.place_ref, bf16[1024,3584]{1,0:T(8,128)(2,1)} %bitcast.48, ...), custom_call_target="tpu_custom_call" | custom-call | tf_op jit(solution)/shard_map/grad_ffn_in/pallas_call | solution.py:1220
  194.7 5.0 %collective-permute-done.10.rest_1_ = bf16[1,144,1536]{2,1,0:T(8,128)(2,1)} collective-permute-done((bf16[1,144,1536]{2,1,0:T(8,128)(2,1)}, bf16[1,144,1536]{2,1,0:T(8,128)(2,1)}, u32[]{:S(2)}, u32[]{:S(2)}) %collective-permute-start.10) | collective-permute-done | bytes 442400 | tf_op jit(solution)/shard_map/ppermute | solution.py:1429
  199.7 22.6 %grad_outs.1 = (bf16[2816,256]{1,0:T(8,128)(2,1)}, bf16[2,1280,256]{2,1,0:T(8,128)(2,1)}, bf16[1280,256]{1,0:T(8,128)(2,1)}, bf16[2,1536,256]{2,1,0:T(8,128)(2,1)}, bf16[1536,256]{1,0:T(8,128)(2,1)}) custom-call(s32[1]{0:T(128)} %bitcast.2.place_ref, bf16[1024,3584]{1,0:T(8,128)(2,1)} %bitcast.49, ...), custom_call_target="tpu_custom_call" | custom-call | flops 48000000000 | bytes 1600000 | tf_op jit(solution)/shard_map/grad_outs/pallas_call | solution.py:1300
  229.4 34.9 %scan_backward.1 = (bf16[1,1024,1024]{2,1,0:T(8,128)(2,1)}, bf16[1,1024,1024]{2,1,0:T(8,128)(2,1)}, f32[1,8,2048]{2,1,0:T(8,128)}, f32[1,8,1792]{2,1,0:T(8,128)}...) custom-call(bf16[1,1024,1536]{2,1,0:T(8,128)(2,1)} %get-tuple-element.241.x_ref, ...), custom_call_target="tpu_custom_call" | custom-call | flops 12000000000 | bytes 400000 | tf_op jit(solution)/shard_map/scan_backward/pallas_call | solution.py:678
  264.4 7.6 %collective-permute-done.16.late_y = bf16[512,512]{1,0:T(8,128)(2,1)} collective-permute-done((bf16[512,512]{1,0:T(8,128)(2,1)}, bf16[512,512]{1,0:T(8,128)(2,1)}, u32[]{:S(2)}, u32[]{:S(2)}) %collective-permute-start.16) | collective-permute-done | bytes 524320 | tf_op jit(solution)/shard_map/ppermute | solution.py:1456
  285.2 4.1 collective-permute-start.21
  293.4 9.1 %grad_conv_in.1 = (bf16[1024,256]{1,0:T(8,128)(2,1)}, bf16[1024,256]{1,0:T(8,128)(2,1)}, bf16[1024,256]{1,0:T(8,128)(2,1)}, bf16[1024,256]{1,0:T(8,128)(2,1)}) custom-call(s32[1]{0:T(128)} %bitcast.2.place_ref, bf16[1024,1024]{1,0:T(8,128)(2,1)} %bitcast.44, bf16[1024,1024]{1,0:T(8,128)(2,1)} %collective-permute-done.6.rest_7_.left_b, ...), custom_call_target="tpu_custom_call" | custom-call | tf_op jit(solution)/shard_map/grad_conv_in/pallas_call | solution.py:1220
  305.9 34.2 %attend_backward.2 = (bf16[1,512,256]{2,1,0:T(8,128)(2,1)}, bf16[1,512,256]{2,1,0:T(8,128)(2,1)}, bf16[1,1024,128]{2,1,0:T(8,128)(2,1)}, bf16[1,1024,128]{2,1,0:...) custom-call(s32[4]{0:T(128)} %pad_add_fusion.1.pos_ref, s32[1]{0:T(128)S(6)} %copy.73.len_ref, ...), custom_call_target="tpu_custom_call" | custom-call | flops 60000002048 | bytes 2000000 | tf_op jit(solution)/shard_map/attend_backward/pallas_call | solution.py:1118
  340.1 4.2 second_hop.4
  352.5 34.4 %attend_backward.3 = (bf16[1,512,256]{2,1,0:T(8,128)(2,1)}, bf16[1,512,256]{2,1,0:T(8,128)(2,1)}, bf16[1,1024,128]{2,1,0:T(8,128)(2,1)}, bf16[1,1024,128]{2,1,0:...) custom-call(s32[4]{0:T(128)} %pad_add_fusion.1.pos_ref, s32[1]{0:T(128)S(6)} %copy.73.len_ref, ...), custom_call_target="tpu_custom_call" | custom-call | flops 3000000000 | bytes 100000 | tf_op jit(solution)/shard_map/attend_backward/pallas_call | solution.py:1118
  392.1 13.3 %leave_mixer.1.gh_ref = bf16[1,1024,1024]{2,1,0:T(8,128)(2,1)} custom-call(s32[1]{0:T(128)} %bitcast.1.core_ref, bf16[1,1024,768]{2,1,0:T(8,128)(2,1)} %get-tuple-element.285.gz_m, bf16[1,1024,768]{2,1,0:T(8,128)(2,1)} %get-tuple-element.232.gz_y, bf16[1,1024,1024]{2,1,0:T(8,128)(2,1)} %get-tuple-element.413.gc_m, ...), custom_call_target="tpu_custom_call" | custom-call | tf_op jit(solution)/shard_map/leave_mixer/pallas_call | solution.py:731
  405.5 4.5 heads_back.1
  416.9 7.9 %grad_qkv.1 = (bf16[768,128]{1,0:T(8,128)(2,1)}, bf16[2,512,128]{2,1,0:T(8,128)(2,1)}, bf16[512,128]{1,0:T(8,128)(2,1)}, bf16[2,256,128]{2,1,0:T(8,128)(2,1)}, bf16[256,128]{1,0:T(8,128)(2,1)}) custom-call(s32[1]{0:T(128)} %bitcast.2.place_ref, bf16[1024,1024]{1,0:T(8,128)(2,1)} %bitcast.45, bf16[1024,1024]{1,0:T(8,128)(2,1)} %collective-permute-done.6.rest_7_.left_b, ...), custom_call_target="tpu_custom_call" | custom-call | tf_op jit(solution)/shard_map/grad_qkv/pallas_call | solution.py:1220
  431.3 8.2 %leave.1 = f32[1,1024,1024]{2,1,0:T(8,128)} custom-call(s32[1]{0:T(128)} %bitcast.1.core_ref, bf16[1,1024,1024]{2,1,0:T(8,128)(2,1)} %tok_ref.4, bf16[1,1024,1024]{2,1,0:T(8,128)(2,1)} %get-tuple-element.221.gmid_ref, bf16[1,1024,1024]{2,1,0:T(8,128)(2,1)} %leave_mixer.1.gh_ref, bf16[1,1024,256]{2,1,0:T(8,128)(2,1)} %get-tuple-element.293.gq_m, ...), custom_call_target="tpu_custom_call" | custom-call | tf_op jit(solution)/shard_map/leave/pallas_call | solution.py:814
  448.4 5.2 %unpack.4 = (f32[256,2048]{1,0:T(8,128)}, f32[256,2048]{1,0:T(8,128)}, f32[256,128]{1,0:T(8,128)}, f32[256,128]{1,0:T(8,128)}) custom-call(s32[2]{0:T(128)} %pad_add_fusion.2.at_ref, bf16[1024,512]{1,0:T(8,128)(2,1)} %all-reduce.14.cloned.1.call-done.own, bf16[1024,512]{1,0:T(8,128)(2,1)} %collective-permute-done.44.other, bf16[1024,2048]{1,0:T(8,128)(2,1)} %rest_0_.4, ...), custom_call_target="tpu_custom_call" | custom-call | tf_op jit(solution)/shard_map/unpack/pallas_call | solution.py:1405
  472.0 6.0 %unpack.5 = (f32[512,1024]{1,0:T(8,128)}, f32[128,1024]{1,0:T(8,128)}, f32[384,1024]{1,0:T(8,128)}, f32[256,1536]{1,0:T(8,128)}, f32[384,128]{1,0:T(8,128)}, /*index=5*/f32[256,128]{1,0:T(8,128)}) custom-call(s32[2]{0:T(128)} %pad_add_fusion.2.at_ref, bf16[2816,256]{1,0:T(8,128)(2,1)} %get-tuple-element.313.own, ...), custom_call_target="tpu_custom_call" | custom-call | tf_op jit(solution)/shard_map/unpack/pallas_call | solution.py:1405
  (222 shorter events, 120.0 us)
Async XLA Ops:
  7.2 91.2 %all-gather.3.cloned.1.call-start = ((), (), s32[]{:S(2)}) async-start(), calls=%async_computation.1 | async-start | bytes 2211840 | tf_op jit(solution)/shard_map/all_gather | solution.py:1545
  27.9 39.6 %collective-permute-start.2 = (bf16[1,1024,256]{2,1,0:T(8,128)(2,1)}, bf16[1,1024,256]{2,1,0:T(8,128)(2,1)}, u32[]{:S(2)}, u32[]{:S(2)}) collective-permute-start(bf16[1,1024,256]{2,1,0:T(8,128)(2,1)} %get-tuple-element.205.rest_0_), channel_id=1, source_target_pairs={{0,1},{1,2},{2,3},{3,0},{4,5},{5,6},{6,7},{7,4},{8,9},{9,10},{10,1... | collective-permute-start | bytes 1572872 | tf_op jit(solution)/shard_map/ppermute | solution.py:1424
  29.2 38.3 %collective-permute-start.3 = (bf16[1,1024,256]{2,1,0:T(8,128)(2,1)}, bf16[1,1024,256]{2,1,0:T(8,128)(2,1)}, u32[]{:S(2)}, u32[]{:S(2)}) collective-permute-start(bf16[1,1024,256]{2,1,0:T(8,128)(2,1)} %get-tuple-element.205.rest_0_), channel_id=1, source_target_pairs={{0,2},{1,3},{2,0},{3,1},{4,6},{5,7},{6,4},{7,5},{8,10},{9,11},{10,... | collective-permute-start | bytes 1572872 | tf_op jit(solution)/shard_map/ppermute | solution.py:1424
  29.3 38.2 %collective-permute-start.4 = (bf16[1,1024,256]{2,1,0:T(8,128)(2,1)}, bf16[1,1024,256]{2,1,0:T(8,128)(2,1)}, u32[]{:S(2)}, u32[]{:S(2)}) collective-permute-start(bf16[1,1024,256]{2,1,0:T(8,128)(2,1)} %get-tuple-element.205.rest_0_), channel_id=1, source_target_pairs={{0,3},{1,0},{2,1},{3,2},{4,7},{5,4},{6,5},{7,6},{8,11},{9,8},{10,9... | collective-permute-start | bytes 1572872 | tf_op jit(solution)/shard_map/ppermute | solution.py:1424
  33.4 34.0 %collective-permute-start.1 = (bf16[1,512,512]{2,1,0:T(8,128)(2,1)}, bf16[1,512,512]{2,1,0:T(8,128)(2,1)}, u32[]{:S(2)}, u32[]{:S(2)}) collective-permute-start(bf16[1,512,512]{2,1,0:T(8,128)(2,1)} %slice.161), channel_id=1, source_target_pairs={{0,3},{1,2},{2,1},{3,0},{4,7},{5,6},{6,5},{7,4},{8,11},{9,10},{10,... | collective-permute-start | bytes 1572872 | tf_op jit(solution)/shard_map/ppermute | solution.py:1434
  55.2 291.7 %all-reduce.14.cloned.1.call-start = ((), (), s32[]{:S(2)}) async-start(), calls=%async_computation | async-start | bytes 2097152 | tf_op jit(solution)/shard_map/psum | solution.py:1485
  65.4 49.1 %collective-permute-start.6 = (bf16[1024,1024]{1,0:T(8,128)(2,1)}, bf16[1024,1024]{1,0:T(8,128)(2,1)}, u32[]{:S(2)}, u32[]{:S(2)}) collective-permute-start(bf16[1024,1024]{1,0:T(8,128)(2,1)} %bitcast.42), channel_id=1, source_target_pairs={{0,4},{4,0},{8,12},{12,8},{16,20},{20,16},{24,28},{28,24},{1,5},{5... | collective-permute-start | bytes 6291464 | tf_op jit(solution)/shard_map/ppermute | solution.py:1439
  156.0 43.7 %collective-permute-start.12 = (bf16[1024,1536]{1,0:T(8,128)(2,1)}, bf16[1024,1536]{1,0:T(8,128)(2,1)}, u32[]{:S(2)}, u32[]{:S(2)}) collective-permute-start(bf16[1024,1536]{1,0:T(8,128)(2,1)} %bitcast.63), channel_id=1, source_target_pairs={{0,4},{4,0},{8,12},{12,8},{16,20},{20,16},{24,28},{28,24},{1,5},{5... | collective-permute-start | bytes 9437192 | tf_op jit(solution)/shard_map/ppermute | solution.py:1439
  226.5 48.9 %collective-permute-start.19 = (bf16[2,1536,256]{2,1,0:T(8,128)(2,1)}, bf16[2,1536,256]{2,1,0:T(8,128)(2,1)}, u32[]{:S(2)}, u32[]{:S(2)}) collective-permute-start(bf16[2,1536,256]{2,1,0:T(8,128)(2,1)} %get-tuple-element.257), channel_id=1, source_target_pairs={{0,2},{1,3},{2,0},{3,1},{4,6},{5,7},{6,4},{7,5},{8,10},{9,11},{10,... | collective-permute-start | bytes 4718600 | tf_op jit(solution)/shard_map/ppermute | solution.py:1456
  226.7 48.8 %collective-permute-start.18 = (bf16[2,1280,256]{2,1,0:T(8,128)(2,1)}, bf16[2,1280,256]{2,1,0:T(8,128)(2,1)}, u32[]{:S(2)}, u32[]{:S(2)}) collective-permute-start(bf16[2,1280,256]{2,1,0:T(8,128)(2,1)} %get-tuple-element.255), channel_id=1, source_target_pairs={{0,1},{1,0},{2,3},{3,2},{4,5},{5,4},{6,7},{7,6},{8,9},{9,8},{10,11... | collective-permute-start | bytes 3932168 | tf_op jit(solution)/shard_map/ppermute | solution.py:1456
  228.1 43.8 %collective-permute-start.16 = (bf16[512,512]{1,0:T(8,128)(2,1)}, bf16[512,512]{1,0:T(8,128)(2,1)}, u32[]{:S(2)}, u32[]{:S(2)}) collective-permute-start(bf16[512,512]{1,0:T(8,128)(2,1)} %get-tuple-element.239), channel_id=1, source_target_pairs={{0,2},{1,3},{2,0},{3,1},{4,6},{5,7},{6,4},{7,5},{8,10},{9,11},{10,... | collective-permute-start | bytes 1572872 | tf_op jit(solution)/shard_map/ppermute | solution.py:1456
  229.2 42.8 %collective-permute-start.17 = (bf16[512,512]{1,0:T(8,128)(2,1)}, bf16[512,512]{1,0:T(8,128)(2,1)}, u32[]{:S(2)}, u32[]{:S(2)}) collective-permute-start(bf16[512,512]{1,0:T(8,128)(2,1)} %get-tuple-element.240), channel_id=1, source_target_pairs={{0,1},{1,0},{2,3},{3,2},{4,5},{5,4},{6,7},{7,6},{8,9},{9,8},{10,11... | collective-permute-start | bytes 1572872 | tf_op jit(solution)/shard_map/ppermute | solution.py:1456
  289.3 142.0 %all-reduce.16.cloned.1.call-start = ((), (), s32[]{:S(2)}) async-start(), calls=%async_computation.2 | async-start | bytes 3932160 | tf_op jit(solution)/shard_map/psum | solution.py:1485
  289.4 50.7 %collective-permute-start.26 = (bf16[1280,256]{1,0:T(8,128)(2,1)}, bf16[1280,256]{1,0:T(8,128)(2,1)}, u32[]{:S(2)}, u32[]{:S(2)}) collective-permute-start(bf16[1280,256]{1,0:T(8,128)(2,1)} %get-tuple-element.258), channel_id=1, source_target_pairs={{0,2},{1,3},{2,0},{3,1},{4,6},{5,7},{6,4},{7,5},{8,10},{9,11},{10,... | collective-permute-start | bytes 1966088 | tf_op jit(solution)/shard_map/ppermute | solution.py:1456
  292.7 47.4 %collective-permute-start.27 = (bf16[1536,256]{1,0:T(8,128)(2,1)}, bf16[1536,256]{1,0:T(8,128)(2,1)}, u32[]{:S(2)}, u32[]{:S(2)}) collective-permute-start(bf16[1536,256]{1,0:T(8,128)(2,1)} %get-tuple-element.259), channel_id=1, source_target_pairs={{0,1},{1,0},{2,3},{3,2},{4,5},{5,4},{6,7},{7,6},{8,9},{9,8},{10,11... | collective-permute-start | bytes 2359304 | tf_op jit(solution)/shard_map/ppermute | solution.py:1456
  302.5 41.8 %collective-permute-start.23 = (bf16[1024,256]{1,0:T(8,128)(2,1)}, bf16[1024,256]{1,0:T(8,128)(2,1)}, u32[]{:S(2)}, u32[]{:S(2)}) collective-permute-start(bf16[1024,256]{1,0:T(8,128)(2,1)} %get-tuple-element.270), channel_id=1, source_target_pairs={{0,1},{1,0},{2,3},{3,2},{4,5},{5,4},{6,7},{7,6},{8,9},{9,8},{10,11... | collective-permute-start | bytes 1572872 | tf_op jit(solution)/shard_map/ppermute | solution.py:1456
  304.6 39.7 %collective-permute-start.24 = (bf16[1024,256]{1,0:T(8,128)(2,1)}, bf16[1024,256]{1,0:T(8,128)(2,1)}, u32[]{:S(2)}, u32[]{:S(2)}) collective-permute-start(bf16[1024,256]{1,0:T(8,128)(2,1)} %get-tuple-element.271), channel_id=1, source_target_pairs={{0,2},{1,3},{2,0},{3,1},{4,6},{5,7},{6,4},{7,5},{8,10},{9,11},{10,... | collective-permute-start | bytes 1572872 | tf_op jit(solution)/shard_map/ppermute | solution.py:1456
  304.6 39.7 %collective-permute-start.25 = (bf16[1024,256]{1,0:T(8,128)(2,1)}, bf16[1024,256]{1,0:T(8,128)(2,1)}, u32[]{:S(2)}, u32[]{:S(2)}) collective-permute-start(bf16[1024,256]{1,0:T(8,128)(2,1)} %get-tuple-element.272), channel_id=1, source_target_pairs={{0,3},{1,2},{2,1},{3,0},{4,7},{5,6},{6,5},{7,4},{8,11},{9,10},{10,... | collective-permute-start | bytes 1572872 | tf_op jit(solution)/shard_map/ppermute | solution.py:1456
  348.3 40.7 %collective-permute-start.28 = (bf16[1,512,256]{2,1,0:T(8,128)(2,1)}, bf16[1,512,256]{2,1,0:T(8,128)(2,1)S(1)}, u32[]{:S(2)}, u32[]{:S(2)}) collective-permute-start(bf16[1,512,256]{2,1,0:T(8,128)(2,1)} %get-tuple-element.276), channel_id=1, source_target_pairs={{0,3},{1,2},{2,1},{3,0},{4,7},{5,6},{6,5},{7,4},{8,11},{9,10},{10,... | collective-permute-start | bytes 786440 | tf_op jit(solution)/shard_map/ppermute | solution.py:1434
  349.5 37.4 %collective-permute-start.29 = (f32[88,128]{1,0:T(8,128)S(1)}, f32[88,128]{1,0:T(8,128)S(1)}, u32[]{:S(2)}, u32[]{:S(2)}) collective-permute-start(f32[88,128]{1,0:T(8,128)S(1)} %pad_bitcast_fusion), channel_id=1, source_target_pairs={{0,1},{1,0},{2,3},{3,2},{4,5},{5,4},{6,7},{7,6},{8,9},{9,8},{10,11... | collective-permute-start | bytes 135176 | tf_op jit(solution)/shard_map/ppermute | solution.py:1456
  351.0 38.4 %collective-permute-start.30 = (bf16[1,1024,128]{2,1,0:T(8,128)(2,1)}, bf16[1,1024,128]{2,1,0:T(8,128)(2,1)}, u32[]{:S(2)}, u32[]{:S(2)}) collective-permute-start(bf16[1,1024,128]{2,1,0:T(8,128)(2,1)} %get-tuple-element.282), channel_id=1, source_target_pairs={{0,3},{1,0},{2,1},{3,2},{4,7},{5,4},{6,5},{7,6},{8,11},{9,8},{10,9... | collective-permute-start | bytes 786440 | tf_op jit(solution)/shard_map/ppermute | solution.py:1424
  352.1 38.7 %collective-permute-start.31 = (bf16[1,1024,128]{2,1,0:T(8,128)(2,1)}, bf16[1,1024,128]{2,1,0:T(8,128)(2,1)}, u32[]{:S(2)}, u32[]{:S(2)}) collective-permute-start(bf16[1,1024,128]{2,1,0:T(8,128)(2,1)} %get-tuple-element.283), channel_id=1, source_target_pairs={{0,2},{1,3},{2,0},{3,1},{4,6},{5,7},{6,4},{7,5},{8,10},{9,11},{10,... | collective-permute-start | bytes 786440 | tf_op jit(solution)/shard_map/ppermute | solution.py:1424
  352.2 39.5 %collective-permute-start.32 = (bf16[1,1024,128]{2,1,0:T(8,128)(2,1)}, bf16[1,1024,128]{2,1,0:T(8,128)(2,1)}, u32[]{:S(2)}, u32[]{:S(2)}) collective-permute-start(bf16[1,1024,128]{2,1,0:T(8,128)(2,1)} %get-tuple-element.284), channel_id=1, source_target_pairs={{0,1},{1,2},{2,3},{3,0},{4,5},{5,6},{6,7},{7,4},{8,9},{9,10},{10,1... | collective-permute-start | bytes 786440 | tf_op jit(solution)/shard_map/ppermute | solution.py:1424
  413.8 33.8 %collective-permute-start.44 = (bf16[1024,512]{1,0:T(8,128)(2,1)}, bf16[1024,512]{1,0:T(8,128)(2,1)}, u32[]{:S(2)}, u32[]{:S(2)}) collective-permute-start(bf16[1024,512]{1,0:T(8,128)(2,1)} %all-reduce.14.cloned.1.call-done.own), channel_id=1, source_target_pairs={{0,4},{4,0},{8,12},{12,8},{16,20},{20,16},{24,28},{28,24},{1,5},{5... | collective-permute-start | bytes 3145736 | tf_op jit(solution)/shard_map/ppermute | solution.py:1439
  (54 other events, 649.3 us)
Sparse Core Ops, SparseCore 0:
  55.3 35.2 all-gather.2
  289.5 53.9 all-reduce.13
  347.0 83.5 all-reduce.15

commit v6 on v5

--- a/solution.py
+++ b/solution.py
@@ -157,7 +157,7 @@
 
 def enter(place, tokens, gain, wq, wk, wv, tables):
     seqs, span, width = tokens.shape
-    rows = min(256, span)
+    rows = min(512, span)
 
     def row(n):
         return pl.BlockSpec((1, rows, n), lambda s, b: (s, b, 0))
@@ -1273,7 +1273,7 @@
     steps = min(n, 4)
     rows = [v[3] // n * (g[3] // PIECE) for v, g in zip(lefts, rights)]
     total = sum(rows)
-    split = sum(rows[:2])
+    split = total // 32 * 16
 
     def turn(i, place):
         return jnp.bitwise_xor(place[0], i) if square else i
@@ -1613,9 +1613,9 @@
     def flip(value, axis, bit):
         return flip_seq(value, bit) if axis == "seq" else flip_dp(value, bit)
 
-    def small_step(total):
+    def small_step(total, *done):
         axis, bit = hops.pop(0)
-        return total + flip(total, axis, bit)
+        return after(total, *done) + flip(total, axis, bit)
 
     def back(group, order):
         near, far, parts = attend_backward(
@@ -1643,7 +1643,7 @@
     grad_tokens = leave(
         core_here, tokens, grad_mid, after(gh, part_qkv[0], out_sum, in_sum), heads, norm_one[None], w_query, w_key, w_value
     )
-    total = small_step(after(total, part_qkv[0]))
+    total = small_step(after(total, part_qkv[0]), grad_tokens)
     at = jnp.stack([core, place])
 
     def matrix(pieces, *weights, wanted=True):

time: 505 us -> 501 us (level)
  transfers between devices with their start and end apart: 57 -> 57, of which waited for: 8 -> 9; matrix products, arithmetic and copies ran while one was open for 5% -> 5% of each run, Pallas kernels for 62% -> 62%
where the time goes in v6:
time: 501 us; the launch traced here: 494 us
  Pallas kernels  366 us (73%)
  starting transfers between devices  59.1 us (12%)
  waiting for transfers between devices  21.1 us (4%)
  local copies, waits for them, and re-layouts  18.2 us (4%)
  between operations  15.2 us (3%)
  other arithmetic  14.1 us (3%)
    pallas_call x2, Pallas kernels, attend_backward(): pl.pallas_call(functools.partial(attend_back_body, rows=rows, keys=keys,...  68.5 us
    pallas_call x1, Pallas kernels, middle(): pl.pallas_call(functools.partial(middle_body, rows=rows, blocks=blocks),...  41.3 us
    pallas_call x1, Pallas kernels, scan_backward(): pl.pallas_call(functools.partial(scan_back_body, chunks=chunks, conv_widt...  35.2 us
    pallas_call x3, Pallas kernels, tall_grad(): pl.pallas_call(functools.partial(tall_body, n=n, widths=widths, square=sq...  32.3 us
    pallas_call x1, Pallas kernels, attend(): pl.pallas_call(functools.partial(attend_body, rows=rows, keys=keys, block...  28.8 us
    pallas_call x1, Pallas kernels, wide_grad(): pl.pallas_call(functools.partial(wide_body, parts=len(lefts), group=n //...  22.6 us
    pallas_call x8, Pallas kernels, in_place(): pl.pallas_call(body, grid=(1 if columns is None else outs[0].shape[-1] //...  22.5 us
    ppermute x18, starting transfers between devices, flip_dp(): return lax.ppermute(value, 'dp', [(i, i ^ bit) for i in range(n)])  21.7 us
  transfers between devices with their start and end apart: 57, of which 9 were waited for; matrix products, arithmetic and copies ran while one was open for 5% of the time, Pallas kernels for 62%

profile of v6, /device:TPU:1, one launch (start us, length us, event | category | flops | bytes accessed | tf_op | source)
XLA Modules:
  0.0 493.9 jit_solution(4197609034705512317)
XLA Ops:
  20.6 6.7 %enter.1 = (bf16[1,1024,1024]{2,1,0:T(8,128)(2,1)}, bf16[1,1024,512]{2,1,0:T(8,128)(2,1)}, bf16[1,1024,256]{2,1,0:T(8,128)(2,1)}) custom-call(s32[1]{0:T(128)} %bitcast.2.place_ref, bf16[1,1024,1024]{2,1,0:T(8,128)(2,1)} %tok_ref.4, f32[1,1024]{1,0:T(1,128)} %bitcast.58, bf16[1024,512]{1,0:T(8,128)(2,1)} %rest_0_.7, bf16[1024,128]{1,0:T(8,128)(2,1)} %rest_1_.6, ...), custom_call_target="tpu_custom_call" | custom-call | flops 24000000000 | bytes 800000 | tf_op jit(solution)/shard_map/enter/pallas_call | solution.py:166
  33.1 21.5 %mixer.1 = (bf16[1,1024,1536]{2,1,0:T(8,128)(2,1)}, bf16[1,1024,1792]{2,1,0:T(8,128)(2,1)}, bf16[1,1024,1792]{2,1,0:T(8,128)(2,1)}, bf16[1,1024,1536]{2,1,0:T(8,...) custom-call(s32[2]{0:T(128)} %pad_add_fusion.pos_ref, ...), custom_call_target="tpu_custom_call" | custom-call | flops 60000002048 | bytes 2000000 | tf_op jit(solution)/shard_map/mixer/pallas_call | solution.py:257
  55.0 9.4 %grad_act.1.gact_ref = bf16[1,1024,2048]{2,1,0:T(8,128)(2,1)} custom-call(s32[2]{0:T(128)} %pad_add_fusion.pos_ref, s32[1]{0:T(128)S(6)} %copy.73.len_ref, bf16[1,1024,1024]{2,1,0:T(8,128)(2,1)} %cot_ref.2, bf16[2048,1024]{1,0:T(8,128)(2,1)} %wd_ref.3), custom_call_target="tpu_custom_call" | custom-call | tf_op jit(solution)/shard_map/grad_act/pallas_call | solution.py:388
  67.1 28.8 %attend.1 = (bf16[1,512,512]{2,1,0:T(8,128)(2,1)}, bf16[1,512,512]{2,1,0:T(8,128)(2,1)}, f32[1,8,1024]{2,1,0:T(8,128)}) custom-call(s32[4]{0:T(128)} %pad_add_fusion.1.pos_ref, s32[1]{0:T(128)S(6)} %copy.73.len_ref, s32[4]{0:T(128)} %compare_select_fusion.from_ref, bf16[1,1024,512]{2,1,0:T(8,128)(2,1)} %get-tuple-element.275.q_ref, ...), custom_call_target="tpu_custom_call" | custom-call | flops 77999996928 | bytes 2600000 | tf_op jit(solution)/shard_map/attend/pallas_call | solution.py:959
  98.0 16.1 %scan_forward.1 = (f32[1,1024,1536]{2,1,0:T(8,128)}, bf16[1,1024,1536]{2,1,0:T(8,128)(2,1)}, bf16[1,8,128,1536]{3,2,1,0:T(8,128)(2,1)}) custom-call(s32[1]{0:T(128)} %bitcast.2.place_ref, bf16[1,1024,1536]{2,1,0:T(8,128)(2,1)} %get-tuple-element.242.x_ref, bf16[1,1024,128]{2,1,0:T(8,128)(2,1)} %get-tuple-element.211.bk_ref, ...), custom_call_target="tpu_custom_call" | custom-call | flops 48000000000 | bytes 1600000 | tf_op jit(solution)/shard_map/scan_forward/pallas_call | solution.py:353
  114.1 41.3 %middle.1 = (bf16[1,1024,1024]{2,1,0:T(8,128)(2,1)}, bf16[1,1024,3584]{2,1,0:T(8,128)(2,1)}, bf16[1,1024,3072]{2,1,0:T(8,128)(2,1)}, bf16[1,1024,3072]{2,1,0:T(8,128)(2,1)}, bf16[1,1024,1024]{2,1,0:T(8,128)(2,1)}) custom-call(s32[2]{0:T(128)} %pad_add_fusion.pos_ref, s32[1]{0:T(128)S(6)} %copy.73.len_ref, ...), custom_call_target="tpu_custom_call" | custom-call | flops 134999998464 | bytes 4500000 | tf_op jit(solution)/shard_map/middle/pallas_call | solution.py:453
  156.2 17.7 %branch_back.1 = (bf16[1,512,512]{2,1,0:T(8,128)(2,1)}, bf16[1,512,512]{2,1,0:T(8,128)(2,1)}, bf16[1,1024,1536]{2,1,0:T(8,128)(2,1)}, bf16[1,1024,768]{2,1,0:T(8...) custom-call(s32[1]{0:T(128)} %bitcast.1.core_ref, ...), custom_call_target="tpu_custom_call" | custom-call | flops 17999998976 | bytes 600000 | tf_op jit(solution)/shard_map/branch_back/pallas_call | solution.py:541
  179.0 15.2 %grad_ffn_in.1 = (bf16[1024,512]{1,0:T(8,128)(2,1)}, bf16[2,512,512]{2,1,0:T(8,128)(2,1)}, bf16[512,512]{1,0:T(8,128)(2,1)}, bf16[2,512,512]{2,1,0:T(8,128)(2,1)}, bf16[512,512]{1,0:T(8,128)(2,1)}) custom-call(s32[1]{0:T(128)} %bitcast.2.place_ref, bf16[1024,3584]{1,0:T(8,128)(2,1)} %bitcast.48, ...), custom_call_target="tpu_custom_call" | custom-call | tf_op jit(solution)/shard_map/grad_ffn_in/pallas_call | solution.py:1220
  194.3 5.3 %collective-permute-done.10.rest_1_ = bf16[1,144,1536]{2,1,0:T(8,128)(2,1)} collective-permute-done((bf16[1,144,1536]{2,1,0:T(8,128)(2,1)}, bf16[1,144,1536]{2,1,0:T(8,128)(2,1)}, u32[]{:S(2)}, u32[]{:S(2)}) %collective-permute-start.10) | collective-permute-done | bytes 442400 | tf_op jit(solution)/shard_map/ppermute | solution.py:1429
  199.6 22.6 %grad_outs.1 = (bf16[2816,256]{1,0:T(8,128)(2,1)}, bf16[2,1408,256]{2,1,0:T(8,128)(2,1)}, bf16[1408,256]{1,0:T(8,128)(2,1)}, bf16[2,1408,256]{2,1,0:T(8,128)(2,1)}, bf16[1408,256]{1,0:T(8,128)(2,1)}) custom-call(s32[1]{0:T(128)} %bitcast.2.place_ref, bf16[1024,3584]{1,0:T(8,128)(2,1)} %bitcast.49, ...), custom_call_target="tpu_custom_call" | custom-call | flops 48000000000 | bytes 1600000 | tf_op jit(solution)/shard_map/grad_outs/pallas_call | solution.py:1300
  229.3 35.2 %scan_backward.1 = (bf16[1,1024,1024]{2,1,0:T(8,128)(2,1)}, bf16[1,1024,1024]{2,1,0:T(8,128)(2,1)}, f32[1,8,2048]{2,1,0:T(8,128)}, f32[1,8,1792]{2,1,0:T(8,128)}...) custom-call(bf16[1,1024,1536]{2,1,0:T(8,128)(2,1)} %get-tuple-element.242.x_ref, ...), custom_call_target="tpu_custom_call" | custom-call | flops 12000000000 | bytes 400000 | tf_op jit(solution)/shard_map/scan_backward/pallas_call | solution.py:678
  264.5 5.1 %collective-permute-done.16.late_y = bf16[512,512]{1,0:T(8,128)(2,1)} collective-permute-done((bf16[512,512]{1,0:T(8,128)(2,1)}, bf16[512,512]{1,0:T(8,128)(2,1)}, u32[]{:S(2)}, u32[]{:S(2)}) %collective-permute-start.16) | collective-permute-done | bytes 524320 | tf_op jit(solution)/shard_map/ppermute | solution.py:1456
  282.9 4.7 collective-permute-start.21
  291.7 9.1 %grad_conv_in.1 = (bf16[1024,256]{1,0:T(8,128)(2,1)}, bf16[1024,256]{1,0:T(8,128)(2,1)}, bf16[1024,256]{1,0:T(8,128)(2,1)}, bf16[1024,256]{1,0:T(8,128)(2,1)}) custom-call(s32[1]{0:T(128)} %bitcast.2.place_ref, bf16[1024,1024]{1,0:T(8,128)(2,1)} %bitcast.44, bf16[1024,1024]{1,0:T(8,128)(2,1)} %collective-permute-done.6.rest_7_.left_b, ...), custom_call_target="tpu_custom_call" | custom-call | tf_op jit(solution)/shard_map/grad_conv_in/pallas_call | solution.py:1220
  303.5 34.1 %attend_backward.2 = (bf16[1,512,256]{2,1,0:T(8,128)(2,1)}, bf16[1,512,256]{2,1,0:T(8,128)(2,1)}, bf16[1,1024,128]{2,1,0:T(8,128)(2,1)}, bf16[1,1024,128]{2,1,0:...) custom-call(s32[4]{0:T(128)} %pad_add_fusion.1.pos_ref, s32[1]{0:T(128)S(6)} %copy.73.len_ref, ...), custom_call_target="tpu_custom_call" | custom-call | flops 60000002048 | bytes 2000000 | tf_op jit(solution)/shard_map/attend_backward/pallas_call | solution.py:1118
  337.6 4.2 second_hop.4
  350.0 34.4 %attend_backward.3 = (bf16[1,512,256]{2,1,0:T(8,128)(2,1)}, bf16[1,512,256]{2,1,0:T(8,128)(2,1)}, bf16[1,1024,128]{2,1,0:T(8,128)(2,1)}, bf16[1,1024,128]{2,1,0:...) custom-call(s32[4]{0:T(128)} %pad_add_fusion.1.pos_ref, s32[1]{0:T(128)S(6)} %copy.73.len_ref, ...), custom_call_target="tpu_custom_call" | custom-call | flops 3000000000 | bytes 100000 | tf_op jit(solution)/shard_map/attend_backward/pallas_call | solution.py:1118
  389.7 13.3 %leave_mixer.1.gh_ref = bf16[1,1024,1024]{2,1,0:T(8,128)(2,1)} custom-call(s32[1]{0:T(128)} %bitcast.1.core_ref, bf16[1,1024,768]{2,1,0:T(8,128)(2,1)} %get-tuple-element.286.gz_m, bf16[1,1024,768]{2,1,0:T(8,128)(2,1)} %get-tuple-element.233.gz_y, bf16[1,1024,1024]{2,1,0:T(8,128)(2,1)} %get-tuple-element.415.gc_m, ...), custom_call_target="tpu_custom_call" | custom-call | tf_op jit(solution)/shard_map/leave_mixer/pallas_call | solution.py:731
  403.1 4.5 heads_back.1
  407.6 4.0 collective-permute-start.38
  414.7 7.9 %grad_qkv.1 = (bf16[768,128]{1,0:T(8,128)(2,1)}, bf16[2,512,128]{2,1,0:T(8,128)(2,1)}, bf16[512,128]{1,0:T(8,128)(2,1)}, bf16[2,256,128]{2,1,0:T(8,128)(2,1)}, bf16[256,128]{1,0:T(8,128)(2,1)}) custom-call(s32[1]{0:T(128)} %bitcast.2.place_ref, bf16[1024,1024]{1,0:T(8,128)(2,1)} %bitcast.45, bf16[1024,1024]{1,0:T(8,128)(2,1)} %collective-permute-done.6.rest_7_.left_b, ...), custom_call_target="tpu_custom_call" | custom-call | tf_op jit(solution)/shard_map/grad_qkv/pallas_call | solution.py:1220
  428.0 8.2 %leave.1 = f32[1,1024,1024]{2,1,0:T(8,128)} custom-call(s32[1]{0:T(128)} %bitcast.1.core_ref, bf16[1,1024,1024]{2,1,0:T(8,128)(2,1)} %tok_ref.4, bf16[1,1024,1024]{2,1,0:T(8,128)(2,1)} %get-tuple-element.222.gmid_ref, bf16[1,1024,1024]{2,1,0:T(8,128)(2,1)} %leave_mixer.1.gh_ref, bf16[1,1024,256]{2,1,0:T(8,128)(2,1)} %get-tuple-element.294.gq_m, ...), custom_call_target="tpu_custom_call" | custom-call | tf_op jit(solution)/shard_map/leave/pallas_call | solution.py:814
  446.3 5.2 %unpack.4 = (f32[256,2048]{1,0:T(8,128)}, f32[256,2048]{1,0:T(8,128)}, f32[256,128]{1,0:T(8,128)}, f32[256,128]{1,0:T(8,128)}) custom-call(s32[2]{0:T(128)} %pad_add_fusion.2.at_ref, bf16[1024,512]{1,0:T(8,128)(2,1)} %all-reduce.14.cloned.1.call-done.own, bf16[1024,512]{1,0:T(8,128)(2,1)} %collective-permute-done.44.other, bf16[1024,2048]{1,0:T(8,128)(2,1)} %rest_0_.4, ...), custom_call_target="tpu_custom_call" | custom-call | tf_op jit(solution)/shard_map/unpack/pallas_call | solution.py:1405
  468.5 6.0 %unpack.5 = (f32[512,1024]{1,0:T(8,128)}, f32[128,1024]{1,0:T(8,128)}, f32[384,1024]{1,0:T(8,128)}, f32[256,1536]{1,0:T(8,128)}, f32[384,128]{1,0:T(8,128)}, /*index=5*/f32[256,128]{1,0:T(8,128)}) custom-call(s32[2]{0:T(128)} %pad_add_fusion.2.at_ref, bf16[2816,256]{1,0:T(8,128)(2,1)} %get-tuple-element.315.own, ...), custom_call_target="tpu_custom_call" | custom-call | tf_op jit(solution)/shard_map/unpack/pallas_call | solution.py:1405
  (222 shorter events, 118.4 us)
Async XLA Ops:
  7.2 90.8 %all-gather.3.cloned.1.call-start = ((), (), s32[]{:S(2)}) async-start(), calls=%async_computation.1 | async-start | bytes 2211840 | tf_op jit(solution)/shard_map/all_gather | solution.py:1545
  27.4 39.7 %collective-permute-start.2 = (bf16[1,1024,256]{2,1,0:T(8,128)(2,1)}, bf16[1,1024,256]{2,1,0:T(8,128)(2,1)}, u32[]{:S(2)}, u32[]{:S(2)}) collective-permute-start(bf16[1,1024,256]{2,1,0:T(8,128)(2,1)} %get-tuple-element.206.rest_0_), channel_id=1, source_target_pairs={{0,1},{1,2},{2,3},{3,0},{4,5},{5,6},{6,7},{7,4},{8,9},{9,10},{10,1... | collective-permute-start | bytes 1572872 | tf_op jit(solution)/shard_map/ppermute | solution.py:1424
  28.6 38.4 %collective-permute-start.3 = (bf16[1,1024,256]{2,1,0:T(8,128)(2,1)}, bf16[1,1024,256]{2,1,0:T(8,128)(2,1)}, u32[]{:S(2)}, u32[]{:S(2)}) collective-permute-start(bf16[1,1024,256]{2,1,0:T(8,128)(2,1)} %get-tuple-element.206.rest_0_), channel_id=1, source_target_pairs={{0,2},{1,3},{2,0},{3,1},{4,6},{5,7},{6,4},{7,5},{8,10},{9,11},{10,... | collective-permute-start | bytes 1572872 | tf_op jit(solution)/shard_map/ppermute | solution.py:1424
  28.7 38.3 %collective-permute-start.4 = (bf16[1,1024,256]{2,1,0:T(8,128)(2,1)}, bf16[1,1024,256]{2,1,0:T(8,128)(2,1)}, u32[]{:S(2)}, u32[]{:S(2)}) collective-permute-start(bf16[1,1024,256]{2,1,0:T(8,128)(2,1)} %get-tuple-element.206.rest_0_), channel_id=1, source_target_pairs={{0,3},{1,0},{2,1},{3,2},{4,7},{5,4},{6,5},{7,6},{8,11},{9,8},{10,9... | collective-permute-start | bytes 1572872 | tf_op jit(solution)/shard_map/ppermute | solution.py:1424
  32.9 34.2 %collective-permute-start.1 = (bf16[1,512,512]{2,1,0:T(8,128)(2,1)}, bf16[1,512,512]{2,1,0:T(8,128)(2,1)}, u32[]{:S(2)}, u32[]{:S(2)}) collective-permute-start(bf16[1,512,512]{2,1,0:T(8,128)(2,1)} %slice.161), channel_id=1, source_target_pairs={{0,3},{1,2},{2,1},{3,0},{4,7},{5,6},{6,5},{7,4},{8,11},{9,10},{10,... | collective-permute-start | bytes 1572872 | tf_op jit(solution)/shard_map/ppermute | solution.py:1434
  54.7 289.8 %all-reduce.14.cloned.1.call-start = ((), (), s32[]{:S(2)}) async-start(), calls=%async_computation | async-start | bytes 2097152 | tf_op jit(solution)/shard_map/psum | solution.py:1485
  65.0 49.1 %collective-permute-start.6 = (bf16[1024,1024]{1,0:T(8,128)(2,1)}, bf16[1024,1024]{1,0:T(8,128)(2,1)}, u32[]{:S(2)}, u32[]{:S(2)}) collective-permute-start(bf16[1024,1024]{1,0:T(8,128)(2,1)} %bitcast.42), channel_id=1, source_target_pairs={{0,4},{4,0},{8,12},{12,8},{16,20},{20,16},{24,28},{28,24},{1,5},{5... | collective-permute-start | bytes 6291464 | tf_op jit(solution)/shard_map/ppermute | solution.py:1439
  155.9 43.7 %collective-permute-start.12 = (bf16[1024,1536]{1,0:T(8,128)(2,1)}, bf16[1024,1536]{1,0:T(8,128)(2,1)}, u32[]{:S(2)}, u32[]{:S(2)}) collective-permute-start(bf16[1024,1536]{1,0:T(8,128)(2,1)} %bitcast.63), channel_id=1, source_target_pairs={{0,4},{4,0},{8,12},{12,8},{16,20},{20,16},{24,28},{28,24},{1,5},{5... | collective-permute-start | bytes 9437192 | tf_op jit(solution)/shard_map/ppermute | solution.py:1439
  226.4 46.8 %collective-permute-start.18 = (bf16[2,1408,256]{2,1,0:T(8,128)(2,1)}, bf16[2,1408,256]{2,1,0:T(8,128)(2,1)}, u32[]{:S(2)}, u32[]{:S(2)}) collective-permute-start(bf16[2,1408,256]{2,1,0:T(8,128)(2,1)} %get-tuple-element.256), channel_id=1, source_target_pairs={{0,1},{1,0},{2,3},{3,2},{4,5},{5,4},{6,7},{7,6},{8,9},{9,8},{10,11... | collective-permute-start | bytes 4325384 | tf_op jit(solution)/shard_map/ppermute | solution.py:1456
  227.6 45.6 %collective-permute-start.19 = (bf16[2,1408,256]{2,1,0:T(8,128)(2,1)}, bf16[2,1408,256]{2,1,0:T(8,128)(2,1)}, u32[]{:S(2)}, u32[]{:S(2)}) collective-permute-start(bf16[2,1408,256]{2,1,0:T(8,128)(2,1)} %get-tuple-element.258), channel_id=1, source_target_pairs={{0,2},{1,3},{2,0},{3,1},{4,6},{5,7},{6,4},{7,5},{8,10},{9,11},{10,... | collective-permute-start | bytes 4325384 | tf_op jit(solution)/shard_map/ppermute | solution.py:1456
  228.0 41.7 %collective-permute-start.16 = (bf16[512,512]{1,0:T(8,128)(2,1)}, bf16[512,512]{1,0:T(8,128)(2,1)}, u32[]{:S(2)}, u32[]{:S(2)}) collective-permute-start(bf16[512,512]{1,0:T(8,128)(2,1)} %get-tuple-element.240), channel_id=1, source_target_pairs={{0,2},{1,3},{2,0},{3,1},{4,6},{5,7},{6,4},{7,5},{8,10},{9,11},{10,... | collective-permute-start | bytes 1572872 | tf_op jit(solution)/shard_map/ppermute | solution.py:1456
  229.1 40.6 %collective-permute-start.17 = (bf16[512,512]{1,0:T(8,128)(2,1)}, bf16[512,512]{1,0:T(8,128)(2,1)}, u32[]{:S(2)}, u32[]{:S(2)}) collective-permute-start(bf16[512,512]{1,0:T(8,128)(2,1)} %get-tuple-element.241), channel_id=1, source_target_pairs={{0,1},{1,0},{2,3},{3,2},{4,5},{5,4},{6,7},{7,6},{8,9},{9,8},{10,11... | collective-permute-start | bytes 1572872 | tf_op jit(solution)/shard_map/ppermute | solution.py:1456
  287.6 140.3 %all-reduce.16.cloned.1.call-start = ((), (), s32[]{:S(2)}) async-start(), calls=%async_computation.2 | async-start | bytes 3932160 | tf_op jit(solution)/shard_map/psum | solution.py:1485
  287.7 49.9 %collective-permute-start.26 = (bf16[1408,256]{1,0:T(8,128)(2,1)}, bf16[1408,256]{1,0:T(8,128)(2,1)}, u32[]{:S(2)}, u32[]{:S(2)}) collective-permute-start(bf16[1408,256]{1,0:T(8,128)(2,1)} %get-tuple-element.259), channel_id=1, source_target_pairs={{0,2},{1,3},{2,0},{3,1},{4,6},{5,7},{6,4},{7,5},{8,10},{9,11},{10,... | collective-permute-start | bytes 2162696 | tf_op jit(solution)/shard_map/ppermute | solution.py:1456
  290.1 47.5 %collective-permute-start.27 = (bf16[1408,256]{1,0:T(8,128)(2,1)}, bf16[1408,256]{1,0:T(8,128)(2,1)}, u32[]{:S(2)}, u32[]{:S(2)}) collective-permute-start(bf16[1408,256]{1,0:T(8,128)(2,1)} %get-tuple-element.260), channel_id=1, source_target_pairs={{0,1},{1,0},{2,3},{3,2},{4,5},{5,4},{6,7},{7,6},{8,9},{9,8},{10,11... | collective-permute-start | bytes 2162696 | tf_op jit(solution)/shard_map/ppermute | solution.py:1456
  300.8 41.0 %collective-permute-start.23 = (bf16[1024,256]{1,0:T(8,128)(2,1)}, bf16[1024,256]{1,0:T(8,128)(2,1)}, u32[]{:S(2)}, u32[]{:S(2)}) collective-permute-start(bf16[1024,256]{1,0:T(8,128)(2,1)} %get-tuple-element.271), channel_id=1, source_target_pairs={{0,1},{1,0},{2,3},{3,2},{4,5},{5,4},{6,7},{7,6},{8,9},{9,8},{10,11... | collective-permute-start | bytes 1572872 | tf_op jit(solution)/shard_map/ppermute | solution.py:1456
  302.0 39.8 %collective-permute-start.24 = (bf16[1024,256]{1,0:T(8,128)(2,1)}, bf16[1024,256]{1,0:T(8,128)(2,1)}, u32[]{:S(2)}, u32[]{:S(2)}) collective-permute-start(bf16[1024,256]{1,0:T(8,128)(2,1)} %get-tuple-element.272), channel_id=1, source_target_pairs={{0,2},{1,3},{2,0},{3,1},{4,6},{5,7},{6,4},{7,5},{8,10},{9,11},{10,... | collective-permute-start | bytes 1572872 | tf_op jit(solution)/shard_map/ppermute | solution.py:1456
  302.4 39.5 %collective-permute-start.25 = (bf16[1024,256]{1,0:T(8,128)(2,1)}, bf16[1024,256]{1,0:T(8,128)(2,1)}, u32[]{:S(2)}, u32[]{:S(2)}) collective-permute-start(bf16[1024,256]{1,0:T(8,128)(2,1)} %get-tuple-element.273), channel_id=1, source_target_pairs={{0,3},{1,2},{2,1},{3,0},{4,7},{5,6},{6,5},{7,4},{8,11},{9,10},{10,... | collective-permute-start | bytes 1572872 | tf_op jit(solution)/shard_map/ppermute | solution.py:1456
  345.8 40.8 %collective-permute-start.28 = (bf16[1,512,256]{2,1,0:T(8,128)(2,1)}, bf16[1,512,256]{2,1,0:T(8,128)(2,1)S(1)}, u32[]{:S(2)}, u32[]{:S(2)}) collective-permute-start(bf16[1,512,256]{2,1,0:T(8,128)(2,1)} %get-tuple-element.277), channel_id=1, source_target_pairs={{0,3},{1,2},{2,1},{3,0},{4,7},{5,6},{6,5},{7,4},{8,11},{9,10},{10,... | collective-permute-start | bytes 786440 | tf_op jit(solution)/shard_map/ppermute | solution.py:1434
  347.2 37.2 %collective-permute-start.29 = (f32[88,128]{1,0:T(8,128)S(1)}, f32[88,128]{1,0:T(8,128)S(1)}, u32[]{:S(2)}, u32[]{:S(2)}) collective-permute-start(f32[88,128]{1,0:T(8,128)S(1)} %pad_bitcast_fusion), channel_id=1, source_target_pairs={{0,1},{1,0},{2,3},{3,2},{4,5},{5,4},{6,7},{7,6},{8,9},{9,8},{10,11... | collective-permute-start | bytes 135176 | tf_op jit(solution)/shard_map/ppermute | solution.py:1456
  348.4 38.5 %collective-permute-start.30 = (bf16[1,1024,128]{2,1,0:T(8,128)(2,1)}, bf16[1,1024,128]{2,1,0:T(8,128)(2,1)}, u32[]{:S(2)}, u32[]{:S(2)}) collective-permute-start(bf16[1,1024,128]{2,1,0:T(8,128)(2,1)} %get-tuple-element.283), channel_id=1, source_target_pairs={{0,3},{1,0},{2,1},{3,2},{4,7},{5,4},{6,5},{7,6},{8,11},{9,8},{10,9... | collective-permute-start | bytes 786440 | tf_op jit(solution)/shard_map/ppermute | solution.py:1424
  349.5 38.7 %collective-permute-start.31 = (bf16[1,1024,128]{2,1,0:T(8,128)(2,1)}, bf16[1,1024,128]{2,1,0:T(8,128)(2,1)}, u32[]{:S(2)}, u32[]{:S(2)}) collective-permute-start(bf16[1,1024,128]{2,1,0:T(8,128)(2,1)} %get-tuple-element.284), channel_id=1, source_target_pairs={{0,2},{1,3},{2,0},{3,1},{4,6},{5,7},{6,4},{7,5},{8,10},{9,11},{10,... | collective-permute-start | bytes 786440 | tf_op jit(solution)/shard_map/ppermute | solution.py:1424
  349.8 39.2 %collective-permute-start.32 = (bf16[1,1024,128]{2,1,0:T(8,128)(2,1)}, bf16[1,1024,128]{2,1,0:T(8,128)(2,1)}, u32[]{:S(2)}, u32[]{:S(2)}) collective-permute-start(bf16[1,1024,128]{2,1,0:T(8,128)(2,1)} %get-tuple-element.285), channel_id=1, source_target_pairs={{0,1},{1,2},{2,3},{3,0},{4,5},{5,6},{6,7},{7,4},{8,9},{9,10},{10,1... | collective-permute-start | bytes 786440 | tf_op jit(solution)/shard_map/ppermute | solution.py:1424
  411.6 33.8 %collective-permute-start.44 = (bf16[1024,512]{1,0:T(8,128)(2,1)}, bf16[1024,512]{1,0:T(8,128)(2,1)}, u32[]{:S(2)}, u32[]{:S(2)}) collective-permute-start(bf16[1024,512]{1,0:T(8,128)(2,1)} %all-reduce.14.cloned.1.call-done.own), channel_id=1, source_target_pairs={{0,4},{4,0},{8,12},{12,8},{16,20},{20,16},{24,28},{28,24},{1,5},{5... | collective-permute-start | bytes 3145736 | tf_op jit(solution)/shard_map/ppermute | solution.py:1439
  (54 other events, 643.5 us)
Sparse Core Ops, SparseCore 0:
  54.8 35.1 all-gather.2
  287.8 53.0 all-reduce.13
  344.6 83.3 all-reduce.15
